TPU v7x, 32 devices: a whole 2x2x4 slice. The times are simulated.
32 devices in a mesh: case: 2 (over x), space: 16 (over z, y, core).
Axes of the slice: x: 2, y: 2, z: 4, core: 2. Of those that a mesh axis runs over, the one named last changes fastest.
Arguments:
- ensemble: bfloat16 [160, 2048, 256], P('case', 'space'), parts along dimension 0, may hold values from -0.66796875 to 0.66796875
- innovation: bfloat16 [36864, 256], P(('case', 'space')), parts along dimension 0, may hold values from -6 to 6
- obs_weight: bfloat16 [36864, 256], P(('case', 'space')), parts along dimension 0, may hold values from 0.19921875 to 2
- interp_weight: float32 [8, 18432], P('case', 'space'), parts along dimension 0, may hold values from 0.1 to 0.5
- slot_of: int32 [8, 18432], P('case', 'space'), parts along dimension 0, may hold values from 0 to 2047, as said below
- intersection_list: int32 [32, 16, 128], P(('case', 'space')), parts along dimension 0, may hold values from 0 to 128, as said below
Outputs:
- control: float32 [160, 131072], P('case', 'space'), parts along dimension 0
- increment: float32 [36864, 256], P(('case', 'space')), parts along dimension 0
There are 2 independent parts, one for each index of `case`. A program takes and returns all parts, laid end to end along the dimension named above; each array names one. Nothing has to cross between parts.
Inputs may be any that keep to these rules, and one draw needn't show every extreme that they name: `slot_of`: every slot named is live: its intersection_list entry is a column, never 128. `intersection_list`: each list of one owner and one fine device holds 0 to 128 distinct columns in its first slots, then 128; lists are nonempty only for the 16 owners o with (o - s + 8) mod 16 < 16; every live slot is named by some slot_of entry of that fine device; owner s holds a full list of 128 for fine device s.
All inputs are finite; a program needn't handle non-finite values.
Results may differ from a plain program's by a relative error of at most 0.0031.
Values may be sent and summed in bfloat16 or wider, within the bound.
No kernel may reach another device: no remote copies, remote signals or barrier semaphores. Data moves between devices by JAX's collectives and lax.ppermute only.
A program may use at most 128 MiB of HBM per device.

v0:
```python
import jax
import jax.numpy as jnp
from jax import lax
from jax.sharding import PartitionSpec as P

VAR = 4
ITERS = 2


loc_scale = 3.0


def vertical_taper(levels):
    heights = jnp.arange(levels).astype(jnp.float32)
    spread = (heights[:, None] - heights[None, :]) / loc_scale
    return jnp.exp(-0.5 * spread * spread)


def on_device(ensemble, innovation, obs_weight, interp_weight, slot_of, intersection_list):
    members, columns, width = ensemble.shape
    levels = width // VAR
    devices = lax.axis_size("space")
    capacity = intersection_list.shape[2]
    taper = vertical_taper(levels)
    receive_index = intersection_list[0]
    weight_obs = obs_weight.astype(jnp.float32)
    target = innovation.astype(jnp.float32)
    mine = lax.all_to_all(intersection_list, "space", split_axis=1, concat_axis=0, tiled=True)
    placed = jnp.arange(devices, dtype=jnp.int32)[:, None] * columns + mine[:, 0, :]
    lookup = placed.reshape(-1)[slot_of]
    control = jnp.zeros((members, columns * levels), jnp.float32)
    increment = jnp.zeros(innovation.shape, jnp.float32)
    for sweep in range(ITERS):
        weighted = weight_obs * (increment - target)
        spread = interp_weight[:, :, None] * weighted[None, :, :]
        packed = jax.ops.segment_sum(
            spread.reshape(-1, width), slot_of.reshape(-1), num_segments=devices * capacity
        )
        packed = packed.reshape(devices, capacity, width)
        received = lax.all_to_all(packed, "space", split_axis=0, concat_axis=0, tiled=True)
        summed = jax.ops.segment_sum(
            received.reshape(-1, width), receive_index.reshape(-1), num_segments=columns + 1
        )
        shaped = summed[:columns].reshape(columns, VAR, levels)
        inner = jnp.sum(
            ensemble.astype(jnp.float32).reshape(members, columns, VAR, levels) * shaped[None],
            axis=2,
        )
        result = jnp.dot(
            inner.reshape(members * columns, levels), taper, precision=lax.Precision.HIGHEST
        )
        gradient = control + result.reshape(members, columns * levels)
        tapered = jnp.dot(
            gradient.reshape(members * columns, levels), taper.T, precision=lax.Precision.HIGHEST
        )
        tapered = tapered.reshape(members, columns, levels)
        source = lax.all_gather(
            jnp.sum(ensemble.astype(jnp.float32) * jnp.tile(tapered, (1, 1, VAR)), axis=0).astype(
                jnp.bfloat16
            ),
            "space",
            axis=0,
            tiled=True,
        )
        picked = source[lookup].astype(jnp.float32)
        image = jnp.sum(interp_weight[:, :, None] * picked, axis=0)
        grad_norm, image_norm = lax.psum(
            (jnp.sum(gradient * gradient), jnp.sum(weight_obs * image * image)), "space"
        )
        length = grad_norm / (grad_norm + image_norm)
        control = control - length * gradient
        increment = increment - length * image
    return (control, increment)


def solution(mesh):
    placed = (
        P("case", "space", None),
        P(("case", "space"), None),
        P(("case", "space"), None),
        P("case", "space"),
        P("case", "space"),
        P(("case", "space"), None, None),
    )
    return jax.shard_map(
        on_device,
        mesh=mesh,
        in_specs=placed,
        out_specs=(P("case", "space"), P(("case", "space"), None)),
        check_vma=False,
    )
```

profile of v0, /device:TPU:0, one launch (start us, length us, event | category | flops | bytes accessed | tf_op | source)
XLA Modules:
  0.0 432.6 jit_solution(10710715177364128569)
XLA Ops:
  10.1 2.8 bitcast_multiply_fusion.3
  12.9 27.0 %scatter_custom_fusion = f32[2048,256]{1,0:T(8,128)} fusion(s32[4608]{0:T(1024)S(1)} %reshape.200, f32[4608,256]{1,0:T(8,128)} %bitcast_multiply_fusion.3, f32[]{:T(128)} %constant.6.clone.1), kind=kCustom, calls=%fused_computation.49 | custom fusion | flops 1179648 | bytes 2097664 | tf_op jit(solution)/shard_map/scatter-add | solution.py:36
  39.8 7.4 %all-to-all-start = ((f32[16,128,256]{2,1,0:T(8,128)}), f32[16,128,256]{2,1,0:T(8,128)S(1)}, u32[]{:S(2)}, u32[]{:S(2)}) async-start(f32[16,128,256]{2,1,0:T(8,128)} %bitcast.3), calls=%async_computation | async-start | bytes 4194304 | tf_op jit(solution)/shard_map/all_to_all | solution.py:40
  47.3 7.9 %copy.35 = bf16[80,128,256]{1,2,0:T(8,128)(2,1)} copy(bf16[80,128,256]{2,1,0:T(8,128)(2,1)} %param.6) | data formatting | bytes 10485760 | tf_op args[0]
  55.2 33.1 %all-to-all-done = f32[16,128,256]{2,1,0:T(8,128)S(1)} async-done(((f32[16,128,256]{2,1,0:T(8,128)}), f32[16,128,256]{2,1,0:T(8,128)S(1)}, u32[]{:S(2)}, u32[]{:S(2)}) %all-to-all-start) | async-done | bytes 2097184 | tf_op jit(solution)/shard_map/all_to_all | solution.py:40
  88.3 12.7 %scatter_custom_fusion.1 = f32[129,256]{1,0:T(8,128)S(1)} fusion(s32[2048]{0:T(1024)} %bitcast.1, f32[2048,256]{1,0:T(8,128)S(1)} %bitcast.72, f32[]{:T(128)} %constant.6.clone.1), kind=kCustom, calls=%fused_computation.53 | custom fusion | flops 524288 | bytes 132608 | tf_op jit(solution)/shard_map/scatter-add | solution.py:41
  101.2 8.5 %multiply_reduce_fusion.1 = (f32[80,128,64]{1,2,0:T(8,128)S(1)}, f32[80,128,4,64]{1,3,2,0:T(8,128)}) fusion(f32[128,4,64]{0,2,1:T(8,128)S(1)} %bitcast.74, bf16[80,128,4,64]{1,3,2,0:T(8,128)(2,1)} %bitcast.63), kind=kLoop, calls=%fused_computation.12 | loop fusion | flops 7208960 | bytes 18481152 | tf_op jit(solution)/shard_map/reduce_sum | solution.py:45
  109.7 3.5 multiply_reduce_fusion.3
  114.7 2.6 convolution_bitcast_fusion
  120.2 11.3 %all-to-all-start.1 = ((s32[1,16,128]{2,0,1:T(1,128)}), s32[1,16,128]{2,0,1:T(1,128)S(1)}, u32[]{:S(2)}, u32[]{:S(2)}) async-start(s32[1,16,128]{2,0,1:T(1,128)} %bitcast.8), calls=%async_computation.1 | async-start | bytes 16384 | tf_op jit(solution)/shard_map/all_to_all | solution.py:28
  131.6 6.2 %all-to-all-done.1 = s32[1,16,128]{2,0,1:T(1,128)S(1)} async-done(((s32[1,16,128]{2,0,1:T(1,128)}), s32[1,16,128]{2,0,1:T(1,128)S(1)}, u32[]{:S(2)}, u32[]{:S(2)}) %all-to-all-start.1) | async-done | bytes 8224 | tf_op jit(solution)/shard_map/all_to_all | solution.py:28
  137.9 24.1 %gather_fusion = s32[4608]{0:T(1024)S(1)} fusion(s32[2048]{0:T(1024)S(1)} %bitcast_add_fusion, s32[5120]{0:T(1024)S(1)} %pad_clamp_fusion.1), kind=kCustom, calls=%fused_computation | custom fusion | bytes 55296 | tf_op jit(solution)/shard_map/gather | solution.py:30
  162.1 4.5 %all-gather.3.cloned.1.call-done = bf16[2048,256]{1,0:T(8,128)(2,1)} async-done(((bf16[128,256]{1,0:T(8,128)(2,1)}), bf16[2048,256]{1,0:T(8,128)(2,1)}) %all-gather.3.cloned.1.call-update) | async-done | bytes 1048592 | tf_op jit(solution)/shard_map/all_gather | solution.py:57
  166.6 11.3 %gather_fusion.1 = bf16[4608,256]{1,0:T(8,128)(2,1)S(1)} fusion(bf16[2048,256]{1,0:T(8,128)(2,1)} %all-gather.3.cloned.1.call-done, s32[5120]{0:T(1024)S(1)} %pad_clamp_fusion), kind=kCustom, calls=%fused_computation.1 | custom fusion | bytes 4737024 | tf_op jit(solution)/shard_map/gather | solution.py:65
  180.5 32.4 %all-reduce.1 = (f32[]{:T(128)}, f32[]{:T(128)}) all-reduce(f32[]{:T(128)} %get-tuple-element.10, f32[]{:T(128)} %fusion.16), channel_id=1, replica_groups=mesh['case'=2,'space'=16] {'space'}, use_global_device_ids=true, to_apply=%region_4.0 | all-reduce | flops 2 | bytes 16 | tf_op jit(solution)/shard_map/psum | solution.py:67
  216.3 2.8 bitcast_multiply_fusion.2
  219.1 26.1 %scatter_custom_fusion.2 = f32[2048,256]{1,0:T(8,128)S(1)} fusion(s32[4608]{0:T(1024)} %copy-done.13, f32[4608,256]{1,0:T(8,128)} %bitcast_multiply_fusion.2, f32[]{:T(128)} %constant.6.clone.1), kind=kCustom, calls=%fused_computation.47 | custom fusion | flops 1179648 | bytes 2097664 | tf_op jit(solution)/shard_map/scatter-add | solution.py:36
  245.2 50.6 %all_to_all.19 = f32[16,128,256]{2,1,0:T(8,128)} all-to-all(f32[16,128,256]{2,1,0:T(8,128)S(1)} %bitcast.71), channel_id=1, replica_groups=mesh['case'=2,'space'=16] {'space'}, dimensions={0} | all-to-all | bytes 4194304 | tf_op jit(solution)/shard_map/all_to_all | solution.py:40
  295.8 12.7 %scatter_custom_fusion.3 = f32[129,256]{1,0:T(8,128)S(1)} fusion(s32[2048]{0:T(1024)} %bitcast.1, f32[2048,256]{1,0:T(8,128)} %bitcast.73, f32[]{:T(128)} %constant.6.clone.1), kind=kCustom, calls=%fused_computation.51 | custom fusion | flops 524288 | bytes 132608 | tf_op jit(solution)/shard_map/scatter-add | solution.py:41
  308.7 5.9 %multiply_reduce_fusion = f32[80,128,64]{1,2,0:T(8,128)S(1)} fusion(f32[80,128,4,64]{1,3,2,0:T(8,128)} %get-tuple-element.9, f32[128,4,64]{0,2,1:T(8,128)S(1)} %bitcast.75), kind=kLoop, calls=%fused_computation.11 | loop fusion | flops 4587520 | bytes 13238272 | tf_op jit(solution)/shard_map/reduce_sum | solution.py:45
  314.6 2.5 fusion.4
  319.0 2.5 fusion.10
  324.1 4.0 copy.46
  328.0 5.4 %reshape.173 = f32[80,8192]{1,0:T(8,128)} reshape(f32[10240,64]{1,0:T(8,128)} %copy.46) | data formatting | bytes 5242880 | tf_op jit(solution)/shard_map/reshape | solution.py:52
  333.4 5.3 %copy.41 = f32[10240,64]{1,0:T(8,128)} copy(f32[10240,64]{0,1:T(8,128)} %get-tuple-element.7) | data formatting | bytes 5242880 | tf_op jit(solution)/shard_map/sub | solution.py:71
  338.7 3.1 multiply_reduce_fusion.2
  341.8 22.4 %all-gather.5.cloned.1.call-done = bf16[2048,256]{1,0:T(8,128)(2,1)} async-done(((bf16[128,256]{1,0:T(8,128)(2,1)}), bf16[2048,256]{1,0:T(8,128)(2,1)}) %all-gather.5.cloned.1.call-update) | async-done | bytes 1048592 | tf_op jit(solution)/shard_map/all_gather | solution.py:57
  364.1 12.8 %gather_fusion.2 = bf16[4608,256]{1,0:T(8,128)(2,1)} fusion(bf16[2048,256]{1,0:T(8,128)(2,1)} %all-gather.5.cloned.1.call-done, s32[5120]{0:T(1024)S(1)} %copy-done.11), kind=kCustom, calls=%fused_computation.2 | custom fusion | bytes 4737024 | tf_op jit(solution)/shard_map/gather | solution.py:65
  376.9 2.2 fusion.2
  380.1 5.5 %sub.73 = f32[80,8192]{1,0:T(8,128)} reshape(f32[10240,64]{1,0:T(8,128)} %copy.41) | data formatting | bytes 5242880 | tf_op jit(solution)/shard_map/sub | solution.py:71
  385.5 32.3 %all-reduce = (f32[]{:T(128)}, f32[]{:T(128)}) all-reduce(f32[]{:T(128)} %multiply_reduce_fusion.2, f32[]{:T(128)} %fusion.15), channel_id=1, replica_groups=mesh['case'=2,'space'=16] {'space'}, use_global_device_ids=true, to_apply=%region_13.0 | all-reduce | flops 2 | bytes 16 | tf_op jit(solution)/shard_map/psum | solution.py:67
  421.9 3.6 multiply_subtract_fusion
  (70 shorter events, 19.3 us)
Async XLA Ops:
  7.9 5.0 %copy-start.13 = (s32[4608]{0:T(1024)}, s32[4608]{0:T(1024)S(1)}, u32[]{:S(2)}) copy-start(s32[4608]{0:T(1024)S(1)} %reshape.200) | copy-start | bytes 55300
  8.6 4.2 copy-start.7
  39.8 48.5 %all-to-all-start = ((f32[16,128,256]{2,1,0:T(8,128)}), f32[16,128,256]{2,1,0:T(8,128)S(1)}, u32[]{:S(2)}, u32[]{:S(2)}) async-start(f32[16,128,256]{2,1,0:T(8,128)} %bitcast.3), calls=%async_computation | async-start | bytes 4194304 | tf_op jit(solution)/shard_map/all_to_all | solution.py:40
  47.2 119.3 %all-gather.3.cloned.1.call-start = ((), (), s32[]{:S(2)}) async-start(), calls=%async_computation.3 | async-start | bytes 1114112 | tf_op jit(solution)/shard_map/all_gather | solution.py:57
  113.2 1.5 copy-start
  113.2 4.4 %slice-start = ((s8[5242880]{0:T(1024)(128)(4,1)}), s8[4194304]{0:T(1024)(128)(4,1)S(1)}, s32[]{:S(2)}) async-start(s8[5242880]{0:T(1024)(128)(4,1)} %bitcast.64), calls=%async_computation.5 | async-start | bytes 8388608
  114.7 2.9 slice-start.1
  117.6 13.9 %copy-start.12 = (s32[4,1152]{1,0:T(4,128)S(1)}, s32[4,1152]{1,0:T(4,128)}, u32[]{:S(2)}) copy-start(s32[4,1152]{1,0:T(4,128)} %param.10) | copy-start | bytes 55300
  120.2 17.7 %all-to-all-start.1 = ((s32[1,16,128]{2,0,1:T(1,128)}), s32[1,16,128]{2,0,1:T(1,128)S(1)}, u32[]{:S(2)}, u32[]{:S(2)}) async-start(s32[1,16,128]{2,0,1:T(1,128)} %bitcast.8), calls=%async_computation.1 | async-start | bytes 16384 | tf_op jit(solution)/shard_map/all_to_all | solution.py:28
  131.5 232.6 %all-gather.5.cloned.1.call-start = ((), (), s32[]{:S(2)}) async-start(), calls=%async_computation.4 | async-start | bytes 1114112 | tf_op jit(solution)/shard_map/all_gather | solution.py:57
  162.0 15.8 %copy-start.10 = (s32[5120]{0:T(1024)}, s32[5120]{0:T(1024)S(1)}, u32[]{:S(2)}) copy-start(s32[5120]{0:T(1024)S(1)} %pad_clamp_fusion) | copy-start | bytes 61444
  177.8 1.7 copy-start.5
  179.5 36.8 %copy-start.2 = (f32[1152,256]{1,0:T(8,128)}, f32[1152,256]{1,0:T(8,128)S(1)}, u32[]{:S(2)}) copy-start(f32[1152,256]{1,0:T(8,128)S(1)} %fusion.3) | copy-start | bytes 3538948
  179.5 36.8 %copy-start.8 = (f32[4608]{0:T(1024)S(1)}, f32[4608]{0:T(1024)}, u32[]{:S(2)}) copy-start(f32[4608]{0:T(1024)} %copy-done.7) | copy-start | bytes 55300
  308.7 8.5 %copy-start.1 = (f32[10240,64]{0,1:T(8,128)S(1)}, f32[10240,64]{0,1:T(8,128)}, u32[]{:S(2)}) copy-start(f32[10240,64]{0,1:T(8,128)} %copy-done) | copy-start | bytes 7864324
  314.6 6.9 %slice-start.2 = ((s8[5242880]{0:T(1024)(128)(4,1)}), s8[4194304]{0:T(1024)(128)(4,1)S(1)}, s32[]{:S(2)}) async-start(s8[5242880]{0:T(1024)(128)(4,1)} %bitcast.66), calls=%async_computation.7 | async-start | bytes 8388608
  317.2 4.4 %slice-start.3 = ((s8[5242880]{0:T(1024)(128)(4,1)}), s8[1048576]{0:T(1024)(128)(4,1)S(1)}, s32[]{:S(2)}) async-start(s8[5242880]{0:T(1024)(128)(4,1)} %bitcast.66), calls=%async_computation.8 | async-start | bytes 2097152
  338.7 25.4 %copy-start.11 = (s32[5120]{0:T(1024)S(1)}, s32[5120]{0:T(1024)}, u32[]{:S(2)}) copy-start(s32[5120]{0:T(1024)} %copy-done.10) | copy-start | bytes 61444
  341.8 35.1 %copy-start.9 = (f32[4,1152]{1,0:T(4,128)S(1)}, f32[4,1152]{1,0:T(4,128)}, u32[]{:S(2)}) copy-start(f32[4,1152]{1,0:T(4,128)} %param.9) | copy-start | bytes 55300
  376.9 2.2 copy-start.6
  380.1 39.6 %copy-start.3 = (f32[1152,256]{1,0:T(8,128)S(1)}, f32[1152,256]{1,0:T(8,128)}, u32[]{:S(2)}) copy-start(f32[1152,256]{1,0:T(8,128)} %copy-done.2) | copy-start | bytes 3538948
  419.7 2.2 copy-start.4
Sparse Core Ops, SparseCore 0:
  120.3 46.2 all-gather.2
  324.2 39.9 all-gather.4
where the time goes:
time: 439 us; the launch traced here: 433 us
  other arithmetic  120 us (27%)
  blocking collectives  115 us (26%)
  local copies, waits for them, and re-layouts  82.2 us (19%)
  waiting for transfers between devices  66.2 us (15%)
  starting transfers between devices  18.8 us (4%)
  between operations  18.5 us (4%)
  matrix products  11.1 us (3%)
    psum x2, blocking collectives, on_device(): lax.psum((jnp.sum(gradient * gradient), jnp.sum(weight_obs * image * imag...  64.7 us
    scatter-add x2, other arithmetic, on_device(): jax.ops.segment_sum(spread.reshape(-1, width), slot_of.reshape(-1), num_s...  53 us
    all_to_all x1, blocking collectives, on_device(): lax.all_to_all(packed, 'space', split_axis=0, concat_axis=0, tiled=True)  50.6 us
    all_to_all x1, waiting for transfers between devices, on_device(): lax.all_to_all(packed, 'space', split_axis=0, concat_axis=0, tiled=True)  33.1 us
    all_gather x2, waiting for transfers between devices, on_device(): lax.all_gather(jnp.sum(ensemble.astype(jnp.float32) * jnp.tile(tapered, (...  26.9 us
    scatter-add x2, other arithmetic, on_device(): jax.ops.segment_sum(received.reshape(-1, width), receive_index.reshape(-1...  25.5 us
    gather x2, local copies, waits for them, and re-layouts, on_device(): lookup = placed.reshape(-1)[slot_of]  24.1 us
    gather x2, local copies, waits for them, and re-layouts, on_device(): picked = source[lookup].astype(jnp.float32)  24 us
  transfers between devices with their start and end apart: 4, of which 4 were waited for; matrix products, arithmetic and copies ran while one was open for 12% of the time, Pallas kernels for 0%

commit v1 on v0

v1 whole, which is shorter than its diff:
```python
import functools

import jax
import jax.numpy as jnp
import ml_dtypes
import numpy as np
from jax import lax
from jax.experimental import pallas as pl
from jax.experimental.pallas import tpu as pltpu
from jax.sharding import PartitionSpec as P

VAR = 4
LOC_SCALE = 3.0
BF = jnp.bfloat16
F32 = jnp.float32
LANES = 128
GROUP = 16
VMEM = pl.BlockSpec(memory_space=pltpu.VMEM)
SMEM = pl.BlockSpec(memory_space=pltpu.SMEM)
ANY = pl.BlockSpec(memory_space=pl.ANY)


def vertical_taper(levels):
    heights = np.arange(levels).astype(np.float32)
    spread = (heights[:, None] - heights[None, :]) / np.float32(LOC_SCALE)
    return np.exp(np.float32(-0.5) * spread * spread)


def host_halves(x):
    high = x.astype(ml_dtypes.bfloat16)
    return [high, (x - high.astype(x.dtype)).astype(ml_dtypes.bfloat16)]


def params(mib):
    return pltpu.CompilerParams(vmem_limit_bytes=mib << 20)


def cost(flops, nbytes):
    return pl.CostEstimate(flops=int(flops), bytes_accessed=int(nbytes), transcendentals=0)


def dot(a, b):
    return jnp.dot(a, b, preferred_element_type=F32)


def halves(x):
    high = x.astype(BF)
    return high, (x - high.astype(F32)).astype(BF)


def shape(dims, dtype):
    return jax.ShapeDtypeStruct(dims, dtype)


def adjoint_kernel(slot_ref, weight_ref, target_ref, obs_ref, at_ref, y_ref, wh_s, wl_s, lo_s):
    step = pl.program_id(0)
    rows, fine = at_ref.shape

    @pl.when(step == 0)
    def _():
        w = -(obs_ref[...].astype(F32) * target_ref[...].astype(F32))
        wh_s[...], wl_s[...] = halves(w)

    row = lax.broadcasted_iota(jnp.int32, (rows, LANES), 0)
    for j in range(fine // LANES):
        lanes = pl.ds(j * LANES, LANES)
        total = None
        for b in range(slot_ref.shape[0]):
            slots = slot_ref[b : b + 1, lanes] - step * rows
            term = jnp.where(row == slots, weight_ref[b : b + 1, lanes], 0.0)
            total = term if total is None else total + term
        at_ref[:, lanes], lo_s[:, lanes] = halves(total)
    y_ref[...] = dot(at_ref[...], wh_s[...]) + dot(at_ref[...], wl_s[...]) + dot(lo_s[...], wh_s[...])


def adjoint_first(slot_of, weight, target, obs, slots):
    sources, fine = slot_of.shape
    width = target.shape[1]
    rows = slots // 8
    full = lambda i: (0, 0)
    return pl.pallas_call(
        adjoint_kernel,
        grid=(8,),
        in_specs=[
            pl.BlockSpec((sources, fine), full),
            pl.BlockSpec((sources, fine), full),
            pl.BlockSpec((fine, width), full),
            pl.BlockSpec((fine, width), full),
        ],
        out_specs=[
            pl.BlockSpec((rows, fine), lambda i: (i, 0)),
            pl.BlockSpec((rows, width), lambda i: (i, 0)),
        ],
        out_shape=[shape((slots, fine), BF), shape((slots, width), F32)],
        scratch_shapes=[pltpu.VMEM((fine, width), BF)] * 2 + [pltpu.VMEM((rows, fine), BF)],
        compiler_params=params(24),
        cost_estimate=cost(2 * slots * fine * width, 8e6),
        name="adjoint_first",
    )(slot_of, weight, target, obs)


PARTS = ((0, 0), (1, 0), (0, 1), (1, 1))
STEPS = 4
HEAD = 16
TOP = 32512.0


def owner(me_ref, k, dy, dc):
    z, y, c = me_ref[0], me_ref[1], me_ref[2]
    y = y if dy == 0 else 1 - y
    c = c if dc == 0 else 1 - c
    return (lax.rem(z + k, STEPS) * 2 + y) * 2 + c


def sources_of(me_ref):
    return [owner(me_ref, (STEPS - k) % STEPS, dy, dc) for dy, dc in PARTS for k in range(STEPS)]


def hits(lists_ref, o):
    column = lax.broadcasted_iota(jnp.int32, (LANES, LANES), 0)
    return jnp.where(column == lists_ref[pl.ds(o, 1), :], 1.0, 0.0)


def forward_matrix_kernel(grouped, me_ref, slot_ref, weight_ref, lists_ref, a_ref, raw_s, p_s):
    rows, slots = a_ref.shape
    if grouped:

        @pl.when(pl.program_id(0) == 0)
        def _():
            for i, o in enumerate(sources_of(me_ref)):
                p_s[i] = hits(lists_ref, o).T.astype(BF)

    out = raw_s if grouped else a_ref
    lane = lax.broadcasted_iota(jnp.int32, (32, LANES), 1)
    for r in range(rows // 32):
        some = pl.ds(r * 32, 32)
        picked = slot_ref[some, :]
        scale = weight_ref[some, :]
        ids = [jnp.broadcast_to(picked[:, b : b + 1], (32, LANES)) for b in range(picked.shape[1])]
        ws = [jnp.broadcast_to(scale[:, b : b + 1], (32, LANES)) for b in range(picked.shape[1])]
        for j in range(slots // LANES):
            here = lane + j * LANES
            total = None
            for i, w in zip(ids, ws):
                term = jnp.where(here == i, w, 0.0)
                total = term if total is None else total + term
            out[some, pl.ds(j * LANES, LANES)] = total.astype(BF)
    if grouped:
        for i, o in enumerate(sources_of(me_ref)):
            held = raw_s[:, pl.ds(pl.multiple_of(o * LANES, LANES), LANES)]
            a_ref[:, pl.ds(i * LANES, LANES)] = dot(held, p_s[i]).astype(BF)


def forward_matrix(me, slot_rows, weight_rows, lists, slots, grouped):
    fine, sources = slot_rows.shape
    rows = fine // 4 if fine % 128 == 0 and fine % 4 == 0 else fine
    return pl.pallas_call(
        functools.partial(forward_matrix_kernel, grouped),
        grid=(fine // rows,),
        in_specs=[
            SMEM,
            pl.BlockSpec((rows, sources), lambda i: (i, 0)),
            pl.BlockSpec((rows, sources), lambda i: (i, 0)),
            pl.BlockSpec(lists.shape, lambda i: (0, 0)),
        ],
        out_specs=pl.BlockSpec((rows, slots), lambda i: (i, 0)),
        out_shape=shape((fine, slots), BF),
        scratch_shapes=[
            pltpu.VMEM((rows, slots), BF),
            pltpu.VMEM((16, LANES, LANES), BF),
        ],
        compiler_params=params(16),
        cost_estimate=cost(2 * slots * fine * LANES * 16, 5e6),
        name="forward_matrix",
    )(me, slot_rows, weight_rows, lists)


def place_kernel(me_ref, lists_ref, at_ref, out_ref):
    for i, (dy, dc) in enumerate(PARTS):
        for k in range(STEPS):
            o = owner(me_ref, k, dy, dc)
            held = at_ref[pl.ds(pl.multiple_of(o * LANES, LANES), LANES), :]
            out = pl.ds((i * STEPS + k) * LANES, LANES)
            out_ref[out, :] = dot(hits(lists_ref, o).astype(BF), held).astype(BF)


def place_rows(me, lists, at):
    slots, fine = at.shape
    return pl.pallas_call(
        place_kernel,
        in_specs=[SMEM, VMEM, VMEM],
        out_specs=VMEM,
        out_shape=shape((slots, fine), BF),
        compiler_params=params(16),
        cost_estimate=cost(2 * slots * fine * LANES * 4, 1e7),
        name="place_rows",
    )(me, lists, at)


def split_kernel(me_ref, lists_ref, y_ref, *outs):
    for out, (dy, dc) in zip(outs, PARTS):
        for k in range(STEPS):
            o = owner(me_ref, k, dy, dc)
            hit = hits(lists_ref, o).astype(BF)
            high, low = halves(y_ref[pl.ds(pl.multiple_of(o * LANES, LANES), LANES), :])
            out[pl.ds(k * LANES, LANES), :] = dot(hit, high) + dot(hit, low)


def split_first(me, lists, y):
    width = y.shape[1]
    return pl.pallas_call(
        split_kernel,
        in_specs=[SMEM, VMEM, VMEM],
        out_specs=[VMEM] * 4,
        out_shape=[shape((STEPS * LANES, width), F32)] * 4,
        compiler_params=params(16),
        cost_estimate=cost(2 * y.shape[0] * LANES * width, 2e6),
        name="split_first",
    )(me, lists, y)


def exponent(m):
    return jnp.clip(jnp.ceil(jnp.log2(jnp.maximum(m, 1e-30))), -100.0, 100.0)


def whole16(x):
    return x.astype(jnp.int32).astype(jnp.int16)


def wide(x):
    return x.astype(jnp.int32).astype(F32)


def pack(out_ref, t, sums=None):
    rows, width = t.shape
    e = exponent(jnp.max(jnp.abs(t), axis=0, keepdims=True))
    out_ref[pl.ds(0, rows), :] = whole16(jnp.round(t * (jnp.exp2(-e) * TOP)))
    head = [e]
    if sums is not None:
        for i in range(2):
            v = sums[i : i + 1, :]
            f = exponent(v)
            v = v * (jnp.exp2(-f) * 16384.0)
            first = jnp.floor(v)
            head += [f, first, jnp.floor((v - first) * 16384.0)]
    row = lax.broadcasted_iota(jnp.int32, (HEAD, width), 0)
    total = jnp.zeros((HEAD, width), F32)
    for i, h in enumerate(head):
        total = jnp.where(row == i, h, total)
    out_ref[pl.ds(rows, HEAD), :] = whole16(total)


def unpack(ref):
    rows = ref.shape[0] - HEAD
    head = wide(ref[pl.ds(rows, HEAD), :])
    return wide(ref[pl.ds(0, rows), :]) * (jnp.exp2(head[0:1, :]) * (1.0 / TOP))


def unpack_sums(ref):
    head = wide(ref[pl.ds(ref.shape[0] - HEAD, HEAD), :])
    row = lax.broadcasted_iota(jnp.int32, (8, head.shape[1]), 0)
    total = jnp.zeros(row.shape, F32)
    for i in range(2):
        f, first, second = [head[1 + 3 * i + j : 2 + 3 * i + j, :] for j in range(3)]
        v = (first + second * (1.0 / 16384.0)) * (jnp.exp2(f) * (1.0 / 16384.0))
        total = jnp.where(row == i, v, total)
    return total


def merge_y_kernel(with_sums, *refs):
    if with_sums:
        a_ref, b_ref, mine_ref, out_ref, s_ref = refs
        sums = mine_ref[...] + b_ref[pl.ds(a_ref.shape[0], 8), :]
        s_ref[...] = sums
    else:
        a_ref, b_ref, out_ref = refs
        sums = None
    pack(out_ref, a_ref[...] + b_ref[pl.ds(0, a_ref.shape[0]), :], sums)


def merge_y(a, b, sums):
    rows, width = a.shape
    out = [shape((rows + HEAD, width), jnp.int16)]
    args = [a, b]
    if sums is not None:
        out.append(shape((8, width), F32))
        args.append(sums)
    return pl.pallas_call(
        functools.partial(merge_y_kernel, sums is not None),
        in_specs=[VMEM] * len(args),
        out_specs=[VMEM] * len(out),
        out_shape=out,
        compiler_params=params(8),
        cost_estimate=cost(5 * rows * width, 1e6),
        name="merge_y",
    )(*args)


def merge_z_kernel(with_sums, *refs):
    if with_sums:
        a_ref, b_ref, p_ref, mine_ref, own_ref, *outs, s_ref = refs
        sums = mine_ref[...] + unpack_sums(p_ref)
        s_ref[...] = sums
    else:
        a_ref, b_ref, p_ref, own_ref, *outs = refs
        sums = None
    t = a_ref[...] + b_ref[...] + unpack(p_ref)
    own_ref[...] = t[:LANES]
    for k in range(1, STEPS):
        pack(outs[k - 1], t[k * LANES : (k + 1) * LANES], sums)


def merge_z(a, b, p, sums):
    width = a.shape[1]
    out = [shape((LANES, width), F32)]
    out += [shape((LANES + HEAD, width), jnp.int16)] * (STEPS - 1)
    args = [a, b, p]
    if sums is not None:
        out.append(shape((8, width), F32))
        args.append(sums)
    return pl.pallas_call(
        functools.partial(merge_z_kernel, sums is not None),
        in_specs=[VMEM] * len(args),
        out_specs=[VMEM] * len(out),
        out_shape=out,
        compiler_params=params(8),
        cost_estimate=cost(5 * STEPS * LANES * width, 1e6),
        name="merge_z",
    )(*args)


def fold(a):
    return jnp.sum(a, axis=0, keepdims=True)


def length_of(sums):
    grad = jnp.sum(sums[0:1, :], axis=1, keepdims=True)
    image = jnp.sum(sums[1:2, :], axis=1, keepdims=True)
    return grad / (grad + image), image / (grad + image)


def products(e, y, held, rows):
    p = e.astype(F32) * y
    q = p[:, :LANES] + p[:, LANES:]
    q = q + pltpu.roll(q, LANES // 2, 1)
    high, low = halves(q)
    held[rows, :LANES] = high
    held[rows, LANES:] = low


BATCH = 16


def coarse_kernel(packed, second, e_ref, k_ref, *refs):
    refs = list(refs)
    y = refs.pop(0)[...]
    got = [refs.pop(0) for _ in range(packed)]
    for r in got:
        y = y + unpack(r)
    if second:
        y0_ref, s_ref = refs.pop(0), refs.pop(0)
        sums = s_ref[...]
        for r in got:
            sums = sums + unpack_sums(r)
        l0, keep = length_of(sums)
        y = keep * y0_ref[...] - l0 * y
        refs.pop(0)
        refs.pop(2)[...] = jnp.broadcast_to(l0, (8, LANES))
    else:
        refs.pop(0)
    x_ref, y_ref, sum_ref, p_s = refs
    columns, members, width = e_ref.shape
    y_ref[...] = y
    sum_ref[...] = jnp.zeros_like(sum_ref)

    @pl.loop(0, columns // BATCH)
    def _(i):
        base = pl.multiple_of(i * BATCH, BATCH)
        yb = y_ref[pl.ds(base, BATCH), :]
        for c in range(BATCH):
            products(e_ref[base + c], yb[c : c + 1, :], p_s, pl.ds(c * members, members))
        t = dot(p_s[...], k_ref[...])
        parts = []
        for c in range(BATCH):
            parts.append(fold(t[c * members : (c + 1) * members] * e_ref[base + c].astype(F32)))
        x = jnp.concatenate(parts, axis=0)
        x_ref[pl.ds(base, BATCH), :] = x.astype(BF)
        sum_ref[0:1, :] += fold(x * yb)


def coarse_image(ens, kern, own, got, after, y0=None, sums=None):
    columns, members, width = ens.shape
    second = y0 is not None
    args = [ens, kern, own, *got] + ([y0, sums] if second else []) + [after]
    out = [shape((columns, width), BF), shape((columns, width), F32)]
    out += [shape((8, LANES), F32)] if second else []
    out += [shape((8, width), F32)]
    return pl.pallas_call(
        functools.partial(coarse_kernel, len(got), second),
        in_specs=[VMEM] * (len(args) - 1) + [ANY],
        out_specs=[VMEM] * len(out),
        out_shape=out,
        scratch_shapes=[pltpu.VMEM((BATCH * members, width), BF)],
        compiler_params=params(16),
        cost_estimate=cost(2 * columns * members * width * width, 5e6),
        name="coarse_second" if second else "coarse_first",
    )(*args)


def project_kernel(e_ref, y_ref, t_ref, g_ref, even_s, odd_s):
    columns, members, width = e_ref.shape
    lanes = BATCH // 2 * LANES

    @pl.loop(0, columns // BATCH)
    def _(i):
        base = pl.multiple_of(i * BATCH, BATCH)
        yb = y_ref[pl.ds(base, BATCH), :]
        for c in range(BATCH):
            held = odd_s if c % 2 else even_s
            rows = pl.ds((c // 2) * members, members)
            products(e_ref[base + c], yb[c : c + 1, :], held, rows)
        r = dot(even_s[...], t_ref[0]) + dot(odd_s[...], t_ref[1])
        for pair in range(BATCH // 2):
            at = pl.multiple_of(i * lanes + pair * LANES, LANES)
            g_ref[:, pl.ds(at, LANES)] = r[pair * members : (pair + 1) * members]


def project(ens, y, taps):
    columns, members, width = ens.shape
    levels = width // VAR
    return pl.pallas_call(
        project_kernel,
        in_specs=[VMEM] * 3,
        out_specs=VMEM,
        out_shape=shape((members, columns * levels), F32),
        scratch_shapes=[pltpu.VMEM((BATCH // 2 * members, width), BF)] * 2,
        compiler_params=params(16),
        cost_estimate=cost(2 * columns * members * width * width, 8e6),
        name="project",
    )(ens, y, taps)


def lay_out(x_refs, xs):
    at = 0
    for x in x_refs:
        xs[pl.ds(at, x.shape[0]), :] = x[...]
        at += x.shape[0]


CUTS = 3


def image_kernel(count, n, *refs):
    x_refs, refs = refs[:count], refs[count:]
    a_ref, at_ref, obs_ref, g_ref, im_ref, sum_ref = refs[:6]
    outs, (xs, v_s) = refs[6 : 6 + n], refs[6 + n :]
    lay_out(x_refs, xs)
    fine, slots = a_ref.shape
    rows = fine // CUTS
    sums = g_ref[...]
    row = lax.broadcasted_iota(jnp.int32, sums.shape, 0)
    for i in range(CUTS):
        some = pl.ds(i * rows, rows)
        im = dot(a_ref[some, :], xs[...])
        im_ref[some, :] = im
        v = obs_ref[some, :].astype(F32) * im
        v_s[some, :] = v.astype(BF)
        sums = sums + jnp.where(row == 1, fold(v * im), 0.0)
    sum_ref[...] = sums
    rows = slots // n
    for i, out in enumerate(outs):
        out[pl.ds(0, rows), :] = dot(at_ref[pl.ds(i * rows, rows), :], v_s[...])
    if n > 1:
        outs[n - 1][pl.ds(rows, 8), :] = sums


def image_first(xs, a, at, obs, g_sums, n):
    fine, slots = a.shape
    width = obs.shape[1]
    z_rows = [slots // n] * n
    if n > 1:
        z_rows[-1] += 8
    return pl.pallas_call(
        functools.partial(image_kernel, len(xs), n),
        in_specs=[VMEM] * (len(xs) + 4),
        out_specs=[VMEM] * (2 + n),
        out_shape=[shape((fine, width), F32), shape((8, width), F32)]
        + [shape((r, width), F32) for r in z_rows],
        scratch_shapes=[pltpu.VMEM((slots, width), BF), pltpu.VMEM((fine, width), BF)],
        compiler_params=params(16),
        cost_estimate=cost(4 * slots * fine * width, 13e6),
        name="image_first",
    )(*xs, a, at, obs, g_sums)


def second_kernel(count, *refs):
    x_refs, refs = refs[:count], refs[count:]
    a_ref, obs_ref, g_ref, after_ref, im_ref, sum_ref, xs = refs
    lay_out(x_refs, xs)
    fine = a_ref.shape[0]
    rows = fine // CUTS
    sums = g_ref[...]
    row = lax.broadcasted_iota(jnp.int32, sums.shape, 0)
    for i in range(CUTS):
        some = pl.ds(i * rows, rows)
        im = dot(a_ref[some, :], xs[...])
        im_ref[some, :] = im
        v = obs_ref[some, :].astype(F32) * im
        sums = sums + jnp.where(row == 1, fold(v * im), 0.0)
    sum_ref[...] = sums


def image_second(xs, a, obs, g_sums, after):
    fine, slots = a.shape
    width = obs.shape[1]
    return pl.pallas_call(
        functools.partial(second_kernel, len(xs)),
        in_specs=[VMEM] * (len(xs) + 3) + [ANY],
        out_specs=[VMEM] * 2,
        out_shape=[shape((fine, width), F32), shape((8, width), F32)],
        scratch_shapes=[pltpu.VMEM((slots, width), BF)],
        compiler_params=params(16),
        cost_estimate=cost(2 * slots * fine * width, 8e6),
        name="image_second",
    )(*xs, a, obs, g_sums, after)


def over_core(x):
    return lax.ppermute(x, "space", [(i, i ^ 1) for i in range(GROUP)])


def over_y(x):
    return lax.ppermute(x, "space", [(i, i ^ 2) for i in range(GROUP)])


def over_z(x, k):
    return lax.ppermute(x, "space", [(i, (i + 4 * k) % GROUP) for i in range(GROUP)])


def scatter_sums(parts, sums=None):
    near, far_y, near_c, far_yc = parts
    got_yc = over_core(far_yc)
    got_c = over_core(near_c)
    out, *s = merge_y(far_y, got_yc, sums)
    got_y = over_y(out)
    own, *out = merge_z(near, got_c, got_y, s[0] if s else None)
    s = out[STEPS - 1 :]
    got = [over_z(out[k - 1], k) for k in range(1, STEPS)]
    return own, got, (s[0] if s else None)


def gather_columns(x):
    zs = [over_z(x, k) for k in range(1, STEPS)]
    y_own = over_y(x)
    c_own = over_core(x)
    rest = jnp.concatenate(zs, axis=0)
    y_rest = over_y(rest)
    c_rest = over_core(rest)
    return [x, rest, y_own, y_rest, c_own, c_rest, over_core(y_own), over_core(y_rest)]


def sum_all(x):
    x = x + over_core(x)
    x = x + over_y(x)
    return x + over_z(x, 1) + over_z(x, 2) + over_z(x, 3)


def on_device(ensemble, innovation, obs_weight, interp_weight, slot_of, intersection_list):
    members, columns, width = ensemble.shape
    levels = width // VAR
    devices = lax.axis_size("space")
    capacity = intersection_list.shape[2]
    slots = devices * capacity
    grouped = devices == GROUP and capacity == columns == LANES

    taper = vertical_taper(levels)
    both = taper.astype(np.float64) @ taper.T.astype(np.float64)
    kern = np.tile(np.concatenate(host_halves(both), axis=0), (2, VAR))
    tall = np.tile(np.concatenate(host_halves(taper), axis=0), (2, 1))
    none = np.zeros_like(tall)
    taps = np.stack(
        [np.concatenate([tall, none], axis=1), np.concatenate([none, tall], axis=1)]
    )
    kern, taps = jnp.asarray(kern), jnp.asarray(taps)

    ens = jnp.transpose(ensemble, (1, 0, 2))
    at, y_slots = adjoint_first(slot_of, interp_weight, innovation, obs_weight, slots)
    index = lax.axis_index("space").astype(jnp.int32)
    me = jnp.stack([index // 4, index // 2 % 2, index % 2, index])
    if grouped:
        lists = lax.all_to_all(
            intersection_list, "space", split_axis=1, concat_axis=0, tiled=True
        ).reshape(devices, capacity)
        scatter, gather, add_up = scatter_sums, gather_columns, sum_all
        first = split_first(me, lists, y_slots)
        at = place_rows(me, lists, at)
        n = 4
    else:
        lists = intersection_list[0]
        hit = (lists.reshape(-1, 1) == jnp.arange(columns, dtype=jnp.int32)).astype(BF)

        def swap(x):
            x = x.reshape(devices, capacity, width)
            x = lax.all_to_all(x, "space", split_axis=0, concat_axis=0, tiled=True)
            return x.reshape(slots, width)

        def scatter(parts, sums=None):
            got = swap(parts[0])
            high = lax.reduce_precision(got, 8, 7)
            high, low = high.astype(BF), (got - high).astype(BF)
            if sums is not None:
                sums = lax.psum(sums, "space")
            return dot(hit.T, high) + dot(hit.T, low), [], sums

        def gather(x):
            return [swap(dot(hit, x).astype(BF))]

        def add_up(x):
            return lax.psum(x, "space")

        first = [y_slots]
        n = 1

    a = forward_matrix(me, slot_of.T, interp_weight.T, lists, slots, grouped)
    own, got, _ = scatter(first)
    x0, y0, g_sums = coarse_image(ens, kern, own, got, at)
    im0, sums, *second = image_first(gather(x0), a, at, obs_weight, g_sums, n)
    g0 = project(ens, y0, taps)
    own, got, sums = scatter(second, sums)
    x1, y1, l0, g_sums = coarse_image(ens, kern, own, got, g0, y0, sums)
    g1 = project(ens, y1, taps)
    im1, sums = image_second(gather(x1), a, obs_weight, g_sums, g1)
    l0 = l0[:1, :1]
    l1, _ = length_of(add_up(sums))
    return (-(l0 * g0 + l1 * g1), -(l0 * im0 + l1 * im1))


def solution(mesh):
    placed = (
        P("case", "space", None),
        P(("case", "space"), None),
        P(("case", "space"), None),
        P("case", "space"),
        P("case", "space"),
        P(("case", "space"), None, None),
    )
    return jax.shard_map(
        on_device,
        mesh=mesh,
        in_specs=placed,
        out_specs=(P("case", "space"), P(("case", "space"), None)),
        check_vma=False,
    )
```

time: 439 us -> 144 us (0.33); the launches traced: 433 us -> 144 us
  other arithmetic: 120 us -> 4.96 us
  blocking collectives: 115 us -> 0 us
  local copies, waits for them, and re-layouts: 82.2 us -> 12.4 us
  Pallas kernels: 0 us -> 42.1 us
  waiting for transfers between devices: 66.2 us -> 38.1 us
  starting transfers between devices: 18.8 us -> 43 us
  between operations: 18.5 us -> 3.06 us
  matrix products: 11.1 us -> 0 us
    scatter-add x4 -> x0, other arithmetic: 78.5 us -> none  [the longest x2 53 us: on_device(): jax.ops.segment_sum(spread.reshape(-1, width), slot_of.reshape(-1), num_s...]
    psum x2 -> x0, blocking collectives: 64.7 us -> none  [on_device(): lax.psum((jnp.sum(gradient * gradient), jnp.sum(weight_obs * image * imag...]
    all_to_all x1 -> x0, blocking collectives: 50.6 us -> none  [on_device(): lax.all_to_all(packed, 'space', split_axis=0, concat_axis=0, tiled=True)]
    gather x4 -> x0, local copies, waits for them, and re-layouts: 48.1 us -> none  [the longest x2 24.1 us: on_device(): lookup = placed.reshape(-1)[slot_of]]
    pallas_call x0 -> x14, Pallas kernels: none -> 42.1 us  [the longest x1 9.48 us: adjoint_first(): pl.pallas_call(adjoint_kernel, grid=(8,), in_specs=[pl.BlockSpec((sources...]
    ppermute x0 -> x35, waiting for transfers between devices: none -> 38.1 us  [the longest x7 21.8 us: over_y(): return lax.ppermute(x, 'space', [(i, i ^ 2) for i in range(GROUP)])]
    ppermute x0 -> x35, starting transfers between devices: none -> 35.6 us  [the longest x15 23.2 us: over_z(): lax.ppermute(x, 'space', [(i, (i + 4 * k) % GROUP) for i in range(GROUP)])]
    all_to_all x1 -> x0, waiting for transfers between devices: 33.1 us -> none  [on_device(): lax.all_to_all(packed, 'space', split_axis=0, concat_axis=0, tiled=True)]
  transfers between devices with their start and end apart: 4 -> 36, of which waited for: 4 -> 18; matrix products, arithmetic and copies ran while one was open for 12% -> 5% of each run, Pallas kernels for 0% -> 19%
where the time goes in v1:
time: 144 us
  starting transfers between devices  43 us (30%)
  Pallas kernels  42.1 us (29%)
  waiting for transfers between devices  38.1 us (26%)
  local copies, waits for them, and re-layouts  12.4 us (9%)
  other arithmetic  4.96 us (3%)
  between operations  3.06 us (2%)
    ppermute x15, starting transfers between devices, over_z(): lax.ppermute(x, 'space', [(i, (i + 4 * k) % GROUP) for i in range(GROUP)])  23.2 us
    ppermute x7, waiting for transfers between devices, over_y(): return lax.ppermute(x, 'space', [(i, i ^ 2) for i in range(GROUP)])  21.8 us
    ppermute x15, waiting for transfers between devices, over_z(): lax.ppermute(x, 'space', [(i, (i + 4 * k) % GROUP) for i in range(GROUP)])  12.6 us
    unnamed x43, local copies, waits for them, and re-layouts  11.8 us
    pallas_call x1, Pallas kernels, adjoint_first(): pl.pallas_call(adjoint_kernel, grid=(8,), in_specs=[pl.BlockSpec((sources...  9.48 us
    ppermute x7, starting transfers between devices, over_y(): return lax.ppermute(x, 'space', [(i, i ^ 2) for i in range(GROUP)])  9.38 us
    pallas_call x1, Pallas kernels, forward_matrix(): pl.pallas_call(functools.partial(forward_matrix_kernel, grouped), grid=(f...  8.33 us
    pallas_call x2, Pallas kernels, coarse_image(): pl.pallas_call(functools.partial(coarse_kernel, len(got), second), in_spe...  8.17 us
  transfers between devices with their start and end apart: 36, of which 18 were waited for; matrix products, arithmetic and copies ran while one was open for 5% of the time, Pallas kernels for 19%

profile of v1, /device:TPU:0, one launch (start us, length us, event | category | flops | bytes accessed | tf_op | source)
XLA Modules:
  0.0 143.6 jit_solution(4042351021166541628)
XLA Ops:
  0.6 7.4 %all-to-all-start = ((s32[1,16,128]{2,0,1:T(1,128)}), s32[1,16,128]{2,0,1:T(1,128)S(1)}, u32[]{:S(2)}, u32[]{:S(2)}) async-start(s32[1,16,128]{2,0,1:T(1,128)} %bitcast.30), calls=%async_computation | async-start | bytes 16384 | tf_op jit(solution)/shard_map/all_to_all | solution.py:591
  11.7 9.5 %adjoint_first.1 = (bf16[2048,1152]{1,0:T(8,128)(2,1)S(1)}, f32[2048,256]{1,0:T(8,128)S(1)}) custom-call(s32[4,1152]{1,0:T(4,128)S(1)} %copy-done.7, f32[4,1152]{1,0:T(4,128)S(1)} %copy-done.9, bf16[1152,256]{1,0:T(8,128)(2,1)S(1)} %copy-done.11, bf16[1152,256]{1,0:T(8,128)(2,1)S(1)} %copy-done.3), custom_call_target="tpu_custom_call" | custom-call | flops 1207959552 | bytes 8000000 | tf_op jit(solution)/shard_map/adjoint_first/pallas_call | solution.py:81
  21.2 2.2 %copy-done.2 = bf16[2048,1152]{1,0:T(8,128)(2,1)} copy-done((bf16[2048,1152]{1,0:T(8,128)(2,1)}, bf16[2048,1152]{1,0:T(8,128)(2,1)S(1)}, u32[]{:S(2)}) %copy-start.2) | copy-done | bytes 4718616
  26.8 1.9 %collective-permute-start.2 = (s16[528,256]{1,0:T(8,128)(2,1)S(1)}, s16[528,256]{1,0:T(8,128)(2,1)S(1)}, u32[]{:S(2)}, u32[]{:S(2)}) collective-permute-start(s16[528,256]{1,0:T(8,128)(2,1)S(1)} %merge_y.2), channel_id=1, source_target_pairs={{0,2},{1,3},{2,0},{3,1},{4,6},{5,7},{6,4},{7,5},{8,10},{9,11},{10,... | collective-permute-start | bytes 811016 | tf_op jit(solution)/shard_map/ppermute | solution.py:533
  28.8 5.5 %copy.18 = bf16[80,128,256]{2,0,1:T(8,128)(2,1)S(1)} copy(bf16[80,128,256]{2,1,0:T(8,128)(2,1)} %param.8) | data formatting | bytes 10485760 | tf_op args[0]
  35.8 1.7 %collective-permute-start.3 = (s16[144,256]{1,0:T(8,128)(2,1)S(1)}, s16[144,256]{1,0:T(8,128)(2,1)S(1)}, u32[]{:S(2)}, u32[]{:S(2)}) collective-permute-start(s16[144,256]{1,0:T(8,128)(2,1)S(1)} %get-tuple-element.40), channel_id=1, source_target_pairs={{0,4},{1,5},{2,6},{3,7},{4,8},{5,9},{6,10},{7,11},{8,12},{9,13},{1... | collective-permute-start | bytes 221192 | tf_op jit(solution)/shard_map/ppermute | solution.py:537
  37.5 2.4 %collective-permute-start.4 = (s16[144,256]{1,0:T(8,128)(2,1)S(1)}, s16[144,256]{1,0:T(8,128)(2,1)S(1)}, u32[]{:S(2)}, u32[]{:S(2)}) collective-permute-start(s16[144,256]{1,0:T(8,128)(2,1)S(1)} %get-tuple-element.41), channel_id=1, source_target_pairs={{0,8},{1,9},{2,10},{3,11},{4,12},{5,13},{6,14},{7,15},{8,0},{9,1},... | collective-permute-start | bytes 221192 | tf_op jit(solution)/shard_map/ppermute | solution.py:537
  41.4 1.9 %place_rows.1.refs_4_.refs_9_ = bf16[2048,1152]{1,0:T(8,128)(2,1)S(1)} custom-call(s32[4]{0:T(128)S(1)} %pad_add_fusion.me_ref, s32[16,128]{1,0:T(8,128)S(1)} %bitcast.28, bf16[2048,1152]{1,0:T(8,128)(2,1)S(1)} %bitcast.24), custom_call_target="tpu_custom_call" | custom-call | flops 2415919104 | bytes 10000000 | tf_op jit(solution)/shard_map/place_rows/pallas_call | solution.py:189
  43.3 1.7 %collective-permute-done.4.refs_2_ = s16[144,256]{1,0:T(8,128)(2,1)S(1)} collective-permute-done((s16[144,256]{1,0:T(8,128)(2,1)S(1)}, s16[144,256]{1,0:T(8,128)(2,1)S(1)}, u32[]{:S(2)}, u32[]{:S(2)}) %collective-permute-start.4) | collective-permute-done | bytes 73760 | tf_op jit(solution)/shard_map/ppermute | solution.py:537
  45.0 4.0 %coarse_first.1 = (bf16[128,256]{1,0:T(8,128)(2,1)S(1)}, f32[128,256]{1,0:T(8,128)S(1)}, f32[8,256]{1,0:T(8,128)S(1)}) custom-call(bf16[128,80,256]{2,1,0:T(8,128)(2,1)S(1)} %bitcast.15, bf16[256,256]{1,0:T(8,128)(2,1)S(1)} %copy-done.6, f32[128,256]{1,0:T(8,128)S(1)} %get-tuple-element.39.refs_0_, s16[144,256]{1,0:T(8,128)(2,1)S(1)} %collective-permute-done.3.refs_1_, ...), custom_call_target="tpu_custom_call" | custom-call | flops 1342177280 | bytes 5000000 | tf_op jit(solution)/shard_map/coarse_first/pallas_call | solution.py:398
  49.0 1.7 %collective-permute-start.6 = (bf16[128,256]{1,0:T(8,128)(2,1)S(1)}, bf16[128,256]{1,0:T(8,128)(2,1)S(1)}, u32[]{:S(2)}, u32[]{:S(2)}) collective-permute-start(bf16[128,256]{1,0:T(8,128)(2,1)S(1)} %get-tuple-element.44.refs_0_), channel_id=1, source_target_pairs={{0,4},{1,5},{2,6},{3,7},{4,8},{5,9},{6,10},{7,11},{8,12},{9,13},{1... | collective-permute-start | bytes 196616 | tf_op jit(solution)/shard_map/ppermute | solution.py:537
  50.8 1.9 %collective-permute-start.7 = (bf16[128,256]{1,0:T(8,128)(2,1)S(1)}, bf16[128,256]{1,0:T(8,128)(2,1)S(1)}, u32[]{:S(2)}, u32[]{:S(2)}) collective-permute-start(bf16[128,256]{1,0:T(8,128)(2,1)S(1)} %get-tuple-element.44.refs_0_), channel_id=1, source_target_pairs={{0,8},{1,9},{2,10},{3,11},{4,12},{5,13},{6,14},{7,15},{8,0},{9,1},... | collective-permute-start | bytes 196616 | tf_op jit(solution)/shard_map/ppermute | solution.py:537
  53.2 2.3 %collective-permute-done.6 = bf16[128,256]{1,0:T(8,128)(2,1)S(1)} collective-permute-done((bf16[128,256]{1,0:T(8,128)(2,1)S(1)}, bf16[128,256]{1,0:T(8,128)(2,1)S(1)}, u32[]{:S(2)}, u32[]{:S(2)}) %collective-permute-start.6) | collective-permute-done | bytes 65568 | tf_op jit(solution)/shard_map/ppermute | solution.py:537
  55.5 2.0 %collective-permute-done.7 = bf16[128,256]{1,0:T(8,128)(2,1)S(1)} collective-permute-done((bf16[128,256]{1,0:T(8,128)(2,1)S(1)}, bf16[128,256]{1,0:T(8,128)(2,1)S(1)}, u32[]{:S(2)}, u32[]{:S(2)}) %collective-permute-start.7) | collective-permute-done | bytes 65568 | tf_op jit(solution)/shard_map/ppermute | solution.py:537
  60.8 3.5 %collective-permute-done.9.refs_2_ = bf16[128,256]{1,0:T(8,128)(2,1)S(1)} collective-permute-done((bf16[128,256]{1,0:T(8,128)(2,1)S(1)}, bf16[128,256]{1,0:T(8,128)(2,1)S(1)}, u32[]{:S(2)}, u32[]{:S(2)}) %collective-permute-start.9) | collective-permute-done | bytes 65568 | tf_op jit(solution)/shard_map/ppermute | solution.py:533
  64.8 8.3 %forward_matrix.1.refs_8_ = bf16[1152,2048]{1,0:T(8,128)(2,1)S(1)} custom-call(s32[4]{0:T(128)S(1)} %pad_add_fusion.me_ref, s32[1152,4]{1,0:T(8,128)S(1)} %bitcast.25, f32[1152,4]{1,0:T(8,128)S(1)} %bitcast.26, s32[16,128]{1,0:T(8,128)S(1)} %bitcast.29), custom_call_target="tpu_custom_call" | custom-call | flops 9663676416 | bytes 5000000 | tf_op jit(solution)/shard_map/forward_matrix/pallas_call | solution.py:157
  73.2 3.6 %image_first.1 = (f32[1152,256]{1,0:T(8,128)S(1)}, f32[8,256]{1,0:T(8,128)S(1)}, f32[512,256]{1,0:T(8,128)S(1)}, f32[512,256]{1,0:T(8,128)S(1)}, f32[512,256]{1,0:T(8,128)S(1)}, /*index=5*/f32[520,256]{1,0:T(8,128)S(1)}) custom-call(bf16[128,256]{1,0:T(8,128)(2,1)S(1)} %get-tuple-element.44.refs_0_, ...), custom_call_target="tpu_custom_call" | custom-call | flops 2415919104 | bytes 13000000 | tf_op jit(solution)/shard_map/image_first/pallas_call | solution.py:483
  80.2 7.3 %collective-permute-done.17.refs_2_ = s16[528,256]{1,0:T(8,128)(2,1)S(1)} collective-permute-done((s16[528,256]{1,0:T(8,128)(2,1)S(1)}, s16[528,256]{1,0:T(8,128)(2,1)S(1)}, u32[]{:S(2)}, u32[]{:S(2)}) %collective-permute-start.17) | collective-permute-done | bytes 270368 | tf_op jit(solution)/shard_map/ppermute | solution.py:533
  87.7 2.5 %collective-permute-start.18 = (s16[144,256]{1,0:T(8,128)(2,1)S(1)}, s16[144,256]{1,0:T(8,128)(2,1)S(1)}, u32[]{:S(2)}, u32[]{:S(2)}) collective-permute-start(s16[144,256]{1,0:T(8,128)(2,1)S(1)} %get-tuple-element.54), channel_id=1, source_target_pairs={{0,4},{1,5},{2,6},{3,7},{4,8},{5,9},{6,10},{7,11},{8,12},{9,13},{1... | collective-permute-start | bytes 221192 | tf_op jit(solution)/shard_map/ppermute | solution.py:537
  90.3 2.3 %collective-permute-start.20 = (s16[144,256]{1,0:T(8,128)(2,1)S(1)}, s16[144,256]{1,0:T(8,128)(2,1)S(1)}, u32[]{:S(2)}, u32[]{:S(2)}) collective-permute-start(s16[144,256]{1,0:T(8,128)(2,1)S(1)} %get-tuple-element.56), channel_id=1, source_target_pairs={{0,12},{1,13},{2,14},{3,15},{4,0},{5,1},{6,2},{7,3},{8,4},{9,5},{1... | collective-permute-start | bytes 221192 | tf_op jit(solution)/shard_map/ppermute | solution.py:537
  92.6 3.7 %project.2.refs_6_ = f32[80,8192]{1,0:T(8,128)S(1)} custom-call(bf16[128,80,256]{2,1,0:T(8,128)(2,1)S(1)} %bitcast.18, f32[128,256]{1,0:T(8,128)S(1)} %get-tuple-element.57.y_ref.refs_4_, bf16[2,256,128]{2,1,0:T(8,128)(2,1)S(1)} %copy-done.5), custom_call_target="tpu_custom_call" | custom-call | flops 1342177280 | bytes 8000000 | tf_op jit(solution)/shard_map/project/pallas_call | solution.py:431
  96.9 4.2 %coarse_second.1 = (bf16[128,256]{1,0:T(8,128)(2,1)S(1)}, f32[128,256]{1,0:T(8,128)S(1)}, f32[8,128]{1,0:T(8,128)S(1)}, f32[8,256]{1,0:T(8,128)S(1)}) custom-call(bf16[128,80,256]{2,1,0:T(8,128)(2,1)S(1)} %bitcast.19, bf16[256,256]{1,0:T(8,128)(2,1)S(1)} %copy-done.6, f32[128,256]{1,0:T(8,128)S(1)} %get-tuple-element.53.refs_0_, ...), custom_call_target="tpu_custom_call" | custom-call | flops 1342177280 | bytes 5000000 | tf_op jit(solution)/shard_map/coarse_second/pallas_call | solution.py:398
  101.1 1.7 %collective-permute-start.21 = (bf16[128,256]{1,0:T(8,128)(2,1)S(1)}, bf16[128,256]{1,0:T(8,128)(2,1)S(1)}, u32[]{:S(2)}, u32[]{:S(2)}) collective-permute-start(bf16[128,256]{1,0:T(8,128)(2,1)S(1)} %get-tuple-element.60.refs_0_), channel_id=1, source_target_pairs={{0,4},{1,5},{2,6},{3,7},{4,8},{5,9},{6,10},{7,11},{8,12},{9,13},{1... | collective-permute-start | bytes 196616 | tf_op jit(solution)/shard_map/ppermute | solution.py:537
  105.3 2.4 %collective-permute-done.21 = bf16[128,256]{1,0:T(8,128)(2,1)S(1)} collective-permute-done((bf16[128,256]{1,0:T(8,128)(2,1)S(1)}, bf16[128,256]{1,0:T(8,128)(2,1)S(1)}, u32[]{:S(2)}, u32[]{:S(2)}) %collective-permute-start.21) | collective-permute-done | bytes 65568 | tf_op jit(solution)/shard_map/ppermute | solution.py:537
  107.7 1.9 %collective-permute-done.22 = bf16[128,256]{1,0:T(8,128)(2,1)S(1)} collective-permute-done((bf16[128,256]{1,0:T(8,128)(2,1)S(1)}, bf16[128,256]{1,0:T(8,128)(2,1)S(1)}, u32[]{:S(2)}, u32[]{:S(2)}) %collective-permute-start.22) | collective-permute-done | bytes 65568 | tf_op jit(solution)/shard_map/ppermute | solution.py:537
  111.1 4.3 %collective-permute-done.25.refs_3_ = bf16[384,256]{1,0:T(8,128)(2,1)S(1)} collective-permute-done((bf16[384,256]{1,0:T(8,128)(2,1)S(1)}, bf16[384,256]{1,0:T(8,128)(2,1)S(1)}, u32[]{:S(2)}, u32[]{:S(2)}) %collective-permute-start.25) | collective-permute-done | bytes 196640 | tf_op jit(solution)/shard_map/ppermute | solution.py:533
  117.0 3.0 %collective-permute-done.24.refs_2_ = bf16[128,256]{1,0:T(8,128)(2,1)S(1)} collective-permute-done((bf16[128,256]{1,0:T(8,128)(2,1)S(1)}, bf16[128,256]{1,0:T(8,128)(2,1)S(1)}, u32[]{:S(2)}, u32[]{:S(2)}) %collective-permute-start.24) | collective-permute-done | bytes 65568 | tf_op jit(solution)/shard_map/ppermute | solution.py:533
  119.9 3.7 %project.3.refs_11_ = f32[80,8192]{1,0:T(8,128)S(1)} custom-call(bf16[128,80,256]{2,1,0:T(8,128)(2,1)S(1)} %bitcast.20, f32[128,256]{1,0:T(8,128)S(1)} %get-tuple-element.62.y_ref, bf16[2,256,128]{2,1,0:T(8,128)(2,1)S(1)} %copy-done.5), custom_call_target="tpu_custom_call" | custom-call | flops 1342177280 | bytes 8000000 | tf_op jit(solution)/shard_map/project/pallas_call | solution.py:431
  127.8 2.3 %collective-permute-done.31 = f32[8,256]{1,0:T(8,128)S(1)} collective-permute-done((f32[8,256]{1,0:T(8,128)S(1)}, f32[8,256]{1,0:T(8,128)S(1)}, u32[]{:S(2)}, u32[]{:S(2)}) %collective-permute-start.31) | collective-permute-done | bytes 8224 | tf_op jit(solution)/shard_map/ppermute | solution.py:533
  130.1 1.9 %collective-permute-start.32 = (f32[8,256]{1,0:T(8,128)S(1)}, f32[8,256]{1,0:T(8,128)S(1)}, u32[]{:S(2)}, u32[]{:S(2)}) collective-permute-start(f32[8,256]{1,0:T(8,128)S(1)} %add.36), channel_id=1, source_target_pairs={{0,4},{1,5},{2,6},{3,7},{4,8},{5,9},{6,10},{7,11},{8,12},{9,13},{1... | collective-permute-start | bytes 24584 | tf_op jit(solution)/shard_map/ppermute | solution.py:537
  139.3 2.5 %add_negate_fusion = f32[80,8192]{1,0:T(8,128)} fusion(f32[80,8192]{1,0:T(8,128)S(1)} %project.3.refs_11_, f32[80,8192]{1,0:T(8,128)S(1)} %project.2.refs_6_, f32[]{:T(128)} %bitcast.12, f32[]{:T(128)} %bitcast.9), kind=kLoop, calls=%fused_computation.1 | loop fusion | flops 2621440 | bytes 7864328 | tf_op jit(solution)/shard_map/neg | solution.py:635
  141.8 1.8 %add_negate_fusion.1 = f32[1152,256]{1,0:T(8,128)} fusion(f32[1152,256]{1,0:T(8,128)S(1)} %get-tuple-element.65, f32[1152,256]{1,0:T(8,128)S(1)} %get-tuple-element.64, f32[]{:T(128)} %bitcast.12, f32[]{:T(128)} %bitcast.9), kind=kLoop, calls=%fused_computation.2 | loop fusion | flops 1179648 | bytes 3538952 | tf_op jit(solution)/shard_map/neg | solution.py:635
  (110 shorter events, 33.6 us)
Async XLA Ops:
  0.6 22.8 %all-to-all-start = ((s32[1,16,128]{2,0,1:T(1,128)}), s32[1,16,128]{2,0,1:T(1,128)S(1)}, u32[]{:S(2)}, u32[]{:S(2)}) async-start(s32[1,16,128]{2,0,1:T(1,128)} %bitcast.30), calls=%async_computation | async-start | bytes 16384 | tf_op jit(solution)/shard_map/all_to_all | solution.py:591
  25.1 9.1 %collective-permute-start = (f32[512,256]{1,0:T(8,128)S(1)}, f32[512,256]{1,0:T(8,128)S(1)}, u32[]{:S(2)}, u32[]{:S(2)}) collective-permute-start(f32[512,256]{1,0:T(8,128)S(1)} %get-tuple-element.36), channel_id=1, source_target_pairs={{0,1},{1,0},{2,3},{3,2},{4,5},{5,4},{6,7},{7,6},{8,9},{9,8},{10,11... | collective-permute-start | bytes 1572872 | tf_op jit(solution)/shard_map/ppermute | solution.py:529
  26.8 8.8 %collective-permute-start.2 = (s16[528,256]{1,0:T(8,128)(2,1)S(1)}, s16[528,256]{1,0:T(8,128)(2,1)S(1)}, u32[]{:S(2)}, u32[]{:S(2)}) collective-permute-start(s16[528,256]{1,0:T(8,128)(2,1)S(1)} %merge_y.2), channel_id=1, source_target_pairs={{0,2},{1,3},{2,0},{3,1},{4,6},{5,7},{6,4},{7,5},{8,10},{9,11},{10,... | collective-permute-start | bytes 811016 | tf_op jit(solution)/shard_map/ppermute | solution.py:533
  35.8 7.5 %collective-permute-start.3 = (s16[144,256]{1,0:T(8,128)(2,1)S(1)}, s16[144,256]{1,0:T(8,128)(2,1)S(1)}, u32[]{:S(2)}, u32[]{:S(2)}) collective-permute-start(s16[144,256]{1,0:T(8,128)(2,1)S(1)} %get-tuple-element.40), channel_id=1, source_target_pairs={{0,4},{1,5},{2,6},{3,7},{4,8},{5,9},{6,10},{7,11},{8,12},{9,13},{1... | collective-permute-start | bytes 221192 | tf_op jit(solution)/shard_map/ppermute | solution.py:537
  37.5 7.4 %collective-permute-start.4 = (s16[144,256]{1,0:T(8,128)(2,1)S(1)}, s16[144,256]{1,0:T(8,128)(2,1)S(1)}, u32[]{:S(2)}, u32[]{:S(2)}) collective-permute-start(s16[144,256]{1,0:T(8,128)(2,1)S(1)} %get-tuple-element.41), channel_id=1, source_target_pairs={{0,8},{1,9},{2,10},{3,11},{4,12},{5,13},{6,14},{7,15},{8,0},{9,1},... | collective-permute-start | bytes 221192 | tf_op jit(solution)/shard_map/ppermute | solution.py:537
  39.9 5.1 %collective-permute-start.5 = (s16[144,256]{1,0:T(8,128)(2,1)S(1)}, s16[144,256]{1,0:T(8,128)(2,1)S(1)}, u32[]{:S(2)}, u32[]{:S(2)}) collective-permute-start(s16[144,256]{1,0:T(8,128)(2,1)S(1)} %get-tuple-element.42), channel_id=1, source_target_pairs={{0,12},{1,13},{2,14},{3,15},{4,0},{5,1},{6,2},{7,3},{8,4},{9,5},{1... | collective-permute-start | bytes 221192 | tf_op jit(solution)/shard_map/ppermute | solution.py:537
  49.0 6.5 %collective-permute-start.6 = (bf16[128,256]{1,0:T(8,128)(2,1)S(1)}, bf16[128,256]{1,0:T(8,128)(2,1)S(1)}, u32[]{:S(2)}, u32[]{:S(2)}) collective-permute-start(bf16[128,256]{1,0:T(8,128)(2,1)S(1)} %get-tuple-element.44.refs_0_), channel_id=1, source_target_pairs={{0,4},{1,5},{2,6},{3,7},{4,8},{5,9},{6,10},{7,11},{8,12},{9,13},{1... | collective-permute-start | bytes 196616 | tf_op jit(solution)/shard_map/ppermute | solution.py:537
  50.8 6.8 %collective-permute-start.7 = (bf16[128,256]{1,0:T(8,128)(2,1)S(1)}, bf16[128,256]{1,0:T(8,128)(2,1)S(1)}, u32[]{:S(2)}, u32[]{:S(2)}) collective-permute-start(bf16[128,256]{1,0:T(8,128)(2,1)S(1)} %get-tuple-element.44.refs_0_), channel_id=1, source_target_pairs={{0,8},{1,9},{2,10},{3,11},{4,12},{5,13},{6,14},{7,15},{8,0},{9,1},... | collective-permute-start | bytes 196616 | tf_op jit(solution)/shard_map/ppermute | solution.py:537
  52.6 4.9 %collective-permute-start.8 = (bf16[128,256]{1,0:T(8,128)(2,1)S(1)}, bf16[128,256]{1,0:T(8,128)(2,1)S(1)}, u32[]{:S(2)}, u32[]{:S(2)}) collective-permute-start(bf16[128,256]{1,0:T(8,128)(2,1)S(1)} %get-tuple-element.44.refs_0_), channel_id=1, source_target_pairs={{0,12},{1,13},{2,14},{3,15},{4,0},{5,1},{6,2},{7,3},{8,4},{9,5},{1... | collective-permute-start | bytes 196616 | tf_op jit(solution)/shard_map/ppermute | solution.py:537
  57.6 6.7 %collective-permute-start.10 = (bf16[384,256]{1,0:T(8,128)(2,1)S(1)}, bf16[384,256]{1,0:T(8,128)(2,1)S(1)}, u32[]{:S(2)}, u32[]{:S(2)}) collective-permute-start(bf16[384,256]{1,0:T(8,128)(2,1)S(1)} %constant_dynamic-update-slice_fusion.refs_1_), channel_id=1, source_target_pairs={{0,2},{1,3},{2,0},{3,1},{4,6},{5,7},{6,4},{7,5},{8,10},{9,11},{10,... | collective-permute-start | bytes 589832 | tf_op jit(solution)/shard_map/ppermute | solution.py:533
  59.1 5.1 %collective-permute-start.9 = (bf16[128,256]{1,0:T(8,128)(2,1)S(1)}, bf16[128,256]{1,0:T(8,128)(2,1)S(1)}, u32[]{:S(2)}, u32[]{:S(2)}) collective-permute-start(bf16[128,256]{1,0:T(8,128)(2,1)S(1)} %get-tuple-element.44.refs_0_), channel_id=1, source_target_pairs={{0,2},{1,3},{2,0},{3,1},{4,6},{5,7},{6,4},{7,5},{8,10},{9,11},{10,... | collective-permute-start | bytes 196616 | tf_op jit(solution)/shard_map/ppermute | solution.py:533
  60.2 12.9 %collective-permute-start.11 = (bf16[128,256]{1,0:T(8,128)(2,1)S(1)}, bf16[128,256]{1,0:T(8,128)(2,1)S(1)}, u32[]{:S(2)}, u32[]{:S(2)}) collective-permute-start(bf16[128,256]{1,0:T(8,128)(2,1)S(1)} %get-tuple-element.44.refs_0_), channel_id=1, source_target_pairs={{0,1},{1,0},{2,3},{3,2},{4,5},{5,4},{6,7},{7,6},{8,9},{9,8},{10,11... | collective-permute-start | bytes 196616 | tf_op jit(solution)/shard_map/ppermute | solution.py:529
  60.3 12.8 %collective-permute-start.12 = (bf16[384,256]{1,0:T(8,128)(2,1)S(1)}, bf16[384,256]{1,0:T(8,128)(2,1)S(1)}, u32[]{:S(2)}, u32[]{:S(2)}) collective-permute-start(bf16[384,256]{1,0:T(8,128)(2,1)S(1)} %constant_dynamic-update-slice_fusion.refs_1_), channel_id=1, source_target_pairs={{0,1},{1,0},{2,3},{3,2},{4,5},{5,4},{6,7},{7,6},{8,9},{9,8},{10,11... | collective-permute-start | bytes 589832 | tf_op jit(solution)/shard_map/ppermute | solution.py:529
  64.2 8.9 %collective-permute-start.13 = (bf16[128,256]{1,0:T(8,128)(2,1)S(1)}, bf16[128,256]{1,0:T(8,128)(2,1)S(1)}, u32[]{:S(2)}, u32[]{:S(2)}) collective-permute-start(bf16[128,256]{1,0:T(8,128)(2,1)S(1)} %collective-permute-done.9.refs_2_), channel_id=1, source_target_pairs={{0,1},{1,0},{2,3},{3,2},{4,5},{5,4},{6,7},{7,6},{8,9},{9,8},{10,11... | collective-permute-start | bytes 196616 | tf_op jit(solution)/shard_map/ppermute | solution.py:529
  64.2 8.9 %collective-permute-start.14 = (bf16[384,256]{1,0:T(8,128)(2,1)S(1)}, bf16[384,256]{1,0:T(8,128)(2,1)S(1)}, u32[]{:S(2)}, u32[]{:S(2)}) collective-permute-start(bf16[384,256]{1,0:T(8,128)(2,1)S(1)} %collective-permute-done.10.refs_3_), channel_id=1, source_target_pairs={{0,1},{1,0},{2,3},{3,2},{4,5},{5,4},{6,7},{7,6},{8,9},{9,8},{10,11... | collective-permute-start | bytes 589832 | tf_op jit(solution)/shard_map/ppermute | solution.py:529
  78.9 8.6 %collective-permute-start.17 = (s16[528,256]{1,0:T(8,128)(2,1)S(1)}, s16[528,256]{1,0:T(8,128)(2,1)S(1)}, u32[]{:S(2)}, u32[]{:S(2)}) collective-permute-start(s16[528,256]{1,0:T(8,128)(2,1)S(1)} %get-tuple-element.51), channel_id=1, source_target_pairs={{0,2},{1,3},{2,0},{3,1},{4,6},{5,7},{6,4},{7,5},{8,10},{9,11},{10,... | collective-permute-start | bytes 811016 | tf_op jit(solution)/shard_map/ppermute | solution.py:533
  87.7 8.6 %collective-permute-start.18 = (s16[144,256]{1,0:T(8,128)(2,1)S(1)}, s16[144,256]{1,0:T(8,128)(2,1)S(1)}, u32[]{:S(2)}, u32[]{:S(2)}) collective-permute-start(s16[144,256]{1,0:T(8,128)(2,1)S(1)} %get-tuple-element.54), channel_id=1, source_target_pairs={{0,4},{1,5},{2,6},{3,7},{4,8},{5,9},{6,10},{7,11},{8,12},{9,13},{1... | collective-permute-start | bytes 221192 | tf_op jit(solution)/shard_map/ppermute | solution.py:537
  90.2 6.7 %collective-permute-start.19 = (s16[144,256]{1,0:T(8,128)(2,1)S(1)}, s16[144,256]{1,0:T(8,128)(2,1)S(1)}, u32[]{:S(2)}, u32[]{:S(2)}) collective-permute-start(s16[144,256]{1,0:T(8,128)(2,1)S(1)} %get-tuple-element.55), channel_id=1, source_target_pairs={{0,8},{1,9},{2,10},{3,11},{4,12},{5,13},{6,14},{7,15},{8,0},{9,1},... | collective-permute-start | bytes 221192 | tf_op jit(solution)/shard_map/ppermute | solution.py:537
  90.3 6.6 %collective-permute-start.20 = (s16[144,256]{1,0:T(8,128)(2,1)S(1)}, s16[144,256]{1,0:T(8,128)(2,1)S(1)}, u32[]{:S(2)}, u32[]{:S(2)}) collective-permute-start(s16[144,256]{1,0:T(8,128)(2,1)S(1)} %get-tuple-element.56), channel_id=1, source_target_pairs={{0,12},{1,13},{2,14},{3,15},{4,0},{5,1},{6,2},{7,3},{8,4},{9,5},{1... | collective-permute-start | bytes 221192 | tf_op jit(solution)/shard_map/ppermute | solution.py:537
  101.1 6.6 %collective-permute-start.21 = (bf16[128,256]{1,0:T(8,128)(2,1)S(1)}, bf16[128,256]{1,0:T(8,128)(2,1)S(1)}, u32[]{:S(2)}, u32[]{:S(2)}) collective-permute-start(bf16[128,256]{1,0:T(8,128)(2,1)S(1)} %get-tuple-element.60.refs_0_), channel_id=1, source_target_pairs={{0,4},{1,5},{2,6},{3,7},{4,8},{5,9},{6,10},{7,11},{8,12},{9,13},{1... | collective-permute-start | bytes 196616 | tf_op jit(solution)/shard_map/ppermute | solution.py:537
  102.9 6.8 %collective-permute-start.22 = (bf16[128,256]{1,0:T(8,128)(2,1)S(1)}, bf16[128,256]{1,0:T(8,128)(2,1)S(1)}, u32[]{:S(2)}, u32[]{:S(2)}) collective-permute-start(bf16[128,256]{1,0:T(8,128)(2,1)S(1)} %get-tuple-element.60.refs_0_), channel_id=1, source_target_pairs={{0,8},{1,9},{2,10},{3,11},{4,12},{5,13},{6,14},{7,15},{8,0},{9,1},... | collective-permute-start | bytes 196616 | tf_op jit(solution)/shard_map/ppermute | solution.py:537
  104.4 5.2 %collective-permute-start.23 = (bf16[128,256]{1,0:T(8,128)(2,1)S(1)}, bf16[128,256]{1,0:T(8,128)(2,1)S(1)}, u32[]{:S(2)}, u32[]{:S(2)}) collective-permute-start(bf16[128,256]{1,0:T(8,128)(2,1)S(1)} %get-tuple-element.60.refs_0_), channel_id=1, source_target_pairs={{0,12},{1,13},{2,14},{3,15},{4,0},{5,1},{6,2},{7,3},{8,4},{9,5},{1... | collective-permute-start | bytes 196616 | tf_op jit(solution)/shard_map/ppermute | solution.py:537
  109.7 5.7 %collective-permute-start.25 = (bf16[384,256]{1,0:T(8,128)(2,1)S(1)}, bf16[384,256]{1,0:T(8,128)(2,1)S(1)}, u32[]{:S(2)}, u32[]{:S(2)}) collective-permute-start(bf16[384,256]{1,0:T(8,128)(2,1)S(1)} %constant_dynamic-update-slice_fusion.3.refs_1_), channel_id=1, source_target_pairs={{0,2},{1,3},{2,0},{3,1},{4,6},{5,7},{6,4},{7,5},{8,10},{9,11},{10,... | collective-permute-start | bytes 589832 | tf_op jit(solution)/shard_map/ppermute | solution.py:533
  111.1 12.6 %collective-permute-start.27 = (bf16[384,256]{1,0:T(8,128)(2,1)S(1)}, bf16[384,256]{1,0:T(8,128)(2,1)S(1)}, u32[]{:S(2)}, u32[]{:S(2)}) collective-permute-start(bf16[384,256]{1,0:T(8,128)(2,1)S(1)} %constant_dynamic-update-slice_fusion.3.refs_1_), channel_id=1, source_target_pairs={{0,1},{1,0},{2,3},{3,2},{4,5},{5,4},{6,7},{7,6},{8,9},{9,8},{10,11... | collective-permute-start | bytes 589832 | tf_op jit(solution)/shard_map/ppermute | solution.py:529
  115.4 8.2 %collective-permute-start.29 = (bf16[384,256]{1,0:T(8,128)(2,1)S(1)}, bf16[384,256]{1,0:T(8,128)(2,1)S(1)}, u32[]{:S(2)}, u32[]{:S(2)}) collective-permute-start(bf16[384,256]{1,0:T(8,128)(2,1)S(1)} %collective-permute-done.25.refs_3_), channel_id=1, source_target_pairs={{0,1},{1,0},{2,3},{3,2},{4,5},{5,4},{6,7},{7,6},{8,9},{9,8},{10,11... | collective-permute-start | bytes 589832 | tf_op jit(solution)/shard_map/ppermute | solution.py:529
  115.4 4.5 %collective-permute-start.24 = (bf16[128,256]{1,0:T(8,128)(2,1)S(1)}, bf16[128,256]{1,0:T(8,128)(2,1)S(1)}, u32[]{:S(2)}, u32[]{:S(2)}) collective-permute-start(bf16[128,256]{1,0:T(8,128)(2,1)S(1)} %get-tuple-element.60.refs_0_), channel_id=1, source_target_pairs={{0,2},{1,3},{2,0},{3,1},{4,6},{5,7},{6,4},{7,5},{8,10},{9,11},{10,... | collective-permute-start | bytes 196616 | tf_op jit(solution)/shard_map/ppermute | solution.py:533
  116.8 6.9 %collective-permute-start.26 = (bf16[128,256]{1,0:T(8,128)(2,1)S(1)}, bf16[128,256]{1,0:T(8,128)(2,1)S(1)}, u32[]{:S(2)}, u32[]{:S(2)}) collective-permute-start(bf16[128,256]{1,0:T(8,128)(2,1)S(1)} %get-tuple-element.60.refs_0_), channel_id=1, source_target_pairs={{0,1},{1,0},{2,3},{3,2},{4,5},{5,4},{6,7},{7,6},{8,9},{9,8},{10,11... | collective-permute-start | bytes 196616 | tf_op jit(solution)/shard_map/ppermute | solution.py:529
  119.9 3.7 %collective-permute-start.28 = (bf16[128,256]{1,0:T(8,128)(2,1)S(1)}, bf16[128,256]{1,0:T(8,128)(2,1)S(1)}, u32[]{:S(2)}, u32[]{:S(2)}) collective-permute-start(bf16[128,256]{1,0:T(8,128)(2,1)S(1)} %collective-permute-done.24.refs_2_), channel_id=1, source_target_pairs={{0,1},{1,0},{2,3},{3,2},{4,5},{5,4},{6,7},{7,6},{8,9},{9,8},{10,11... | collective-permute-start | bytes 196616 | tf_op jit(solution)/shard_map/ppermute | solution.py:529
  126.5 3.7 %collective-permute-start.31 = (f32[8,256]{1,0:T(8,128)S(1)}, f32[8,256]{1,0:T(8,128)S(1)}, u32[]{:S(2)}, u32[]{:S(2)}) collective-permute-start(f32[8,256]{1,0:T(8,128)S(1)} %add.35), channel_id=1, source_target_pairs={{0,2},{1,3},{2,0},{3,1},{4,6},{5,7},{6,4},{7,5},{8,10},{9,11},{10,... | collective-permute-start | bytes 24584 | tf_op jit(solution)/shard_map/ppermute | solution.py:533
  130.1 5.4 %collective-permute-start.32 = (f32[8,256]{1,0:T(8,128)S(1)}, f32[8,256]{1,0:T(8,128)S(1)}, u32[]{:S(2)}, u32[]{:S(2)}) collective-permute-start(f32[8,256]{1,0:T(8,128)S(1)} %add.36), channel_id=1, source_target_pairs={{0,4},{1,5},{2,6},{3,7},{4,8},{5,9},{6,10},{7,11},{8,12},{9,13},{1... | collective-permute-start | bytes 24584 | tf_op jit(solution)/shard_map/ppermute | solution.py:537
  132.1 4.5 %collective-permute-start.33 = (f32[8,256]{1,0:T(8,128)S(1)}, f32[8,256]{1,0:T(8,128)S(1)}, u32[]{:S(2)}, u32[]{:S(2)}) collective-permute-start(f32[8,256]{1,0:T(8,128)S(1)} %add.36), channel_id=1, source_target_pairs={{0,8},{1,9},{2,10},{3,11},{4,12},{5,13},{6,14},{7,15},{8,0},{9,1},... | collective-permute-start | bytes 24584 | tf_op jit(solution)/shard_map/ppermute | solution.py:537
  133.1 3.7 %collective-permute-start.34 = (f32[8,256]{1,0:T(8,128)S(1)}, f32[8,256]{1,0:T(8,128)S(1)}, u32[]{:S(2)}, u32[]{:S(2)}) collective-permute-start(f32[8,256]{1,0:T(8,128)S(1)} %add.36), channel_id=1, source_target_pairs={{0,12},{1,13},{2,14},{3,15},{4,0},{5,1},{6,2},{7,3},{8,4},{9,5},{1... | collective-permute-start | bytes 24584 | tf_op jit(solution)/shard_map/ppermute | solution.py:537
  (22 other events, 181.8 us)

commit v2 on v1

--- a/solution.py
+++ b/solution.py
@@ -18,6 +18,7 @@
 VMEM = pl.BlockSpec(memory_space=pltpu.VMEM)
 SMEM = pl.BlockSpec(memory_space=pltpu.SMEM)
 ANY = pl.BlockSpec(memory_space=pl.ANY)
+HBM = pl.BlockSpec(memory_space=pltpu.HBM)
 
 
 def vertical_taper(levels):
@@ -52,68 +53,86 @@
     return jax.ShapeDtypeStruct(dims, dtype)
 
 
-def adjoint_kernel(slot_ref, weight_ref, target_ref, obs_ref, at_ref, y_ref, wh_s, wl_s, lo_s):
-    step = pl.program_id(0)
-    rows, fine = at_ref.shape
-
-    @pl.when(step == 0)
-    def _():
-        w = -(obs_ref[...].astype(F32) * target_ref[...].astype(F32))
-        wh_s[...], wl_s[...] = halves(w)
-
+def adjoint_kernel(*refs):
+    slot_hbm, weight_hbm, obs_hbm, target_hbm, at_ref, y_ref = refs[:6]
+    slot_s, weight_s, obs_s, target_s, wh_s, wl_s, lo_s, sem = refs[6:]
+    copies = [
+        pltpu.make_async_copy(src, dst, sem.at[i])
+        for i, (src, dst) in enumerate(
+            [
+                (slot_hbm, slot_s),
+                (weight_hbm, weight_s),
+                (obs_hbm, obs_s),
+                (target_hbm, target_s),
+            ]
+        )
+    ]
+    for copy in copies:
+        copy.start()
+    slots, fine = at_ref.shape
+    rows = slots // BLOCKS
     row = lax.broadcasted_iota(jnp.int32, (rows, LANES), 0)
-    for j in range(fine // LANES):
-        lanes = pl.ds(j * LANES, LANES)
-        total = None
-        for b in range(slot_ref.shape[0]):
-            slots = slot_ref[b : b + 1, lanes] - step * rows
-            term = jnp.where(row == slots, weight_ref[b : b + 1, lanes], 0.0)
-            total = term if total is None else total + term
-        at_ref[:, lanes], lo_s[:, lanes] = halves(total)
-    y_ref[...] = dot(at_ref[...], wh_s[...]) + dot(at_ref[...], wl_s[...]) + dot(lo_s[...], wh_s[...])
+
+    def build(i):
+        for j in range(fine // LANES):
+            lanes = pl.ds(j * LANES, LANES)
+            total = None
+            for b in range(slot_s.shape[0]):
+                ids = slot_s[b : b + 1, lanes] - i * rows
+                term = jnp.where(row == ids, weight_s[b : b + 1, lanes], 0.0)
+                total = term if total is None else total + term
+            at_ref[pl.ds(i * rows, rows), lanes], lo_s[i % 2, :, lanes] = halves(total)
+
+    copies[0].wait()
+    copies[1].wait()
+    build(0)
+    copies[2].wait()
+    copies[3].wait()
+    w = -(obs_s[...].astype(F32) * target_s[...].astype(F32))
+    wh_s[...], wl_s[...] = halves(w)
+    for i in range(BLOCKS):
+        some = pl.ds(i * rows, rows)
+        y_ref[some, :] = (
+            dot(at_ref[some, :], wh_s[...])
+            + dot(at_ref[some, :], wl_s[...])
+            + dot(lo_s[i % 2], wh_s[...])
+        )
+        if i + 1 < BLOCKS:
+            build(i + 1)
+
+
+BLOCKS = 8
 
 
 def adjoint_first(slot_of, weight, target, obs, slots):
     sources, fine = slot_of.shape
     width = target.shape[1]
-    rows = slots // 8
-    full = lambda i: (0, 0)
+    rows = slots // BLOCKS
     return pl.pallas_call(
         adjoint_kernel,
-        grid=(8,),
-        in_specs=[
-            pl.BlockSpec((sources, fine), full),
-            pl.BlockSpec((sources, fine), full),
-            pl.BlockSpec((fine, width), full),
-            pl.BlockSpec((fine, width), full),
-        ],
-        out_specs=[
-            pl.BlockSpec((rows, fine), lambda i: (i, 0)),
-            pl.BlockSpec((rows, width), lambda i: (i, 0)),
-        ],
+        in_specs=[HBM] * 4,
+        out_specs=[VMEM] * 2,
         out_shape=[shape((slots, fine), BF), shape((slots, width), F32)],
-        scratch_shapes=[pltpu.VMEM((fine, width), BF)] * 2 + [pltpu.VMEM((rows, fine), BF)],
-        compiler_params=params(24),
-        cost_estimate=cost(2 * slots * fine * width, 8e6),
+        scratch_shapes=[
+            pltpu.VMEM((sources, fine), jnp.int32),
+            pltpu.VMEM((sources, fine), F32),
+        ]
+        + [pltpu.VMEM((fine, width), BF)] * 4
+        + [pltpu.VMEM((2, rows, fine), BF), pltpu.SemaphoreType.DMA((4,))],
+        compiler_params=params(20),
+        cost_estimate=cost(6 * slots * fine * width, 8e6),
         name="adjoint_first",
-    )(slot_of, weight, target, obs)
-
-
-PARTS = ((0, 0), (1, 0), (0, 1), (1, 1))
-STEPS = 4
+    )(slot_of, weight, obs, target)
+
+
+CHIPS = GROUP // 2
 HEAD = 16
 TOP = 32512.0
 
 
-def owner(me_ref, k, dy, dc):
-    z, y, c = me_ref[0], me_ref[1], me_ref[2]
-    y = y if dy == 0 else 1 - y
-    c = c if dc == 0 else 1 - c
-    return (lax.rem(z + k, STEPS) * 2 + y) * 2 + c
-
-
-def sources_of(me_ref):
-    return [owner(me_ref, (STEPS - k) % STEPS, dy, dc) for dy, dc in PARTS for k in range(STEPS)]
+def owners(me_ref):
+    c = me_ref[0]
+    return [2 * i + c for i in range(CHIPS)] + [2 * i + 1 - c for i in range(CHIPS)]
 
 
 def hits(lists_ref, o):
@@ -127,7 +146,7 @@
 
         @pl.when(pl.program_id(0) == 0)
         def _():
-            for i, o in enumerate(sources_of(me_ref)):
+            for i, o in enumerate(owners(me_ref)):
                 p_s[i] = hits(lists_ref, o).T.astype(BF)
 
     out = raw_s if grouped else a_ref
@@ -146,7 +165,7 @@
                 total = term if total is None else total + term
             out[some, pl.ds(j * LANES, LANES)] = total.astype(BF)
     if grouped:
-        for i, o in enumerate(sources_of(me_ref)):
+        for i, o in enumerate(owners(me_ref)):
             held = raw_s[:, pl.ds(pl.multiple_of(o * LANES, LANES), LANES)]
             a_ref[:, pl.ds(i * LANES, LANES)] = dot(held, p_s[i]).astype(BF)
 
@@ -176,12 +195,10 @@
 
 
 def place_kernel(me_ref, lists_ref, at_ref, out_ref):
-    for i, (dy, dc) in enumerate(PARTS):
-        for k in range(STEPS):
-            o = owner(me_ref, k, dy, dc)
-            held = at_ref[pl.ds(pl.multiple_of(o * LANES, LANES), LANES), :]
-            out = pl.ds((i * STEPS + k) * LANES, LANES)
-            out_ref[out, :] = dot(hits(lists_ref, o).astype(BF), held).astype(BF)
+    for i, o in enumerate(owners(me_ref)):
+        held = at_ref[pl.ds(pl.multiple_of(o * LANES, LANES), LANES), :]
+        hit = hits(lists_ref, o).astype(BF)
+        out_ref[pl.ds(i * LANES, LANES), :] = dot(hit, held).astype(BF)
 
 
 def place_rows(me, lists, at):
@@ -198,12 +215,11 @@
 
 
 def split_kernel(me_ref, lists_ref, y_ref, *outs):
-    for out, (dy, dc) in zip(outs, PARTS):
-        for k in range(STEPS):
-            o = owner(me_ref, k, dy, dc)
-            hit = hits(lists_ref, o).astype(BF)
-            high, low = halves(y_ref[pl.ds(pl.multiple_of(o * LANES, LANES), LANES), :])
-            out[pl.ds(k * LANES, LANES), :] = dot(hit, high) + dot(hit, low)
+    for i, o in enumerate(owners(me_ref)):
+        hit = hits(lists_ref, o).astype(BF)
+        high, low = halves(y_ref[pl.ds(pl.multiple_of(o * LANES, LANES), LANES), :])
+        rows = pl.ds(i % CHIPS * LANES, LANES)
+        outs[i // CHIPS][rows, :] = dot(hit, high) + dot(hit, low)
 
 
 def split_first(me, lists, y):
@@ -211,8 +227,8 @@
     return pl.pallas_call(
         split_kernel,
         in_specs=[SMEM, VMEM, VMEM],
-        out_specs=[VMEM] * 4,
-        out_shape=[shape((STEPS * LANES, width), F32)] * 4,
+        out_specs=[VMEM] * 2,
+        out_shape=[shape((CHIPS * LANES, width), F32)] * 2,
         compiler_params=params(16),
         cost_estimate=cost(2 * y.shape[0] * LANES * width, 2e6),
         name="split_first",
@@ -267,66 +283,41 @@
     return total
 
 
-def merge_y_kernel(with_sums, *refs):
-    if with_sums:
-        a_ref, b_ref, mine_ref, out_ref, s_ref = refs
-        sums = mine_ref[...] + b_ref[pl.ds(a_ref.shape[0], 8), :]
-        s_ref[...] = sums
-    else:
-        a_ref, b_ref, out_ref = refs
-        sums = None
-    pack(out_ref, a_ref[...] + b_ref[pl.ds(0, a_ref.shape[0]), :], sums)
-
-
-def merge_y(a, b, sums):
+def merge_kernel(with_sums, a_ref, b_ref, *refs):
+    out_ref = refs[-1]
+    sums = refs[0][...] + b_ref[pl.ds(a_ref.shape[0], 8), :] if with_sums else None
+    for i in range(CHIPS):
+        rows = pl.ds(i * LANES, LANES)
+        pack(out_ref.at[i], a_ref[rows, :] + b_ref[rows, :], sums)
+
+
+def merge(a, b, sums):
     rows, width = a.shape
-    out = [shape((rows + HEAD, width), jnp.int16)]
-    args = [a, b]
-    if sums is not None:
-        out.append(shape((8, width), F32))
-        args.append(sums)
-    return pl.pallas_call(
-        functools.partial(merge_y_kernel, sums is not None),
+    args = [a, b] + ([] if sums is None else [sums])
+    return pl.pallas_call(
+        functools.partial(merge_kernel, sums is not None),
         in_specs=[VMEM] * len(args),
-        out_specs=[VMEM] * len(out),
-        out_shape=out,
+        out_specs=VMEM,
+        out_shape=shape((CHIPS, LANES + HEAD, width), jnp.int16),
         compiler_params=params(8),
-        cost_estimate=cost(5 * rows * width, 1e6),
-        name="merge_y",
+        cost_estimate=cost(5 * rows * width, 2e6),
+        name="merge",
     )(*args)
 
 
-def merge_z_kernel(with_sums, *refs):
-    if with_sums:
-        a_ref, b_ref, p_ref, mine_ref, own_ref, *outs, s_ref = refs
-        sums = mine_ref[...] + unpack_sums(p_ref)
-        s_ref[...] = sums
-    else:
-        a_ref, b_ref, p_ref, own_ref, *outs = refs
-        sums = None
-    t = a_ref[...] + b_ref[...] + unpack(p_ref)
-    own_ref[...] = t[:LANES]
-    for k in range(1, STEPS):
-        pack(outs[k - 1], t[k * LANES : (k + 1) * LANES], sums)
-
-
-def merge_z(a, b, p, sums):
-    width = a.shape[1]
-    out = [shape((LANES, width), F32)]
-    out += [shape((LANES + HEAD, width), jnp.int16)] * (STEPS - 1)
-    args = [a, b, p]
-    if sums is not None:
-        out.append(shape((8, width), F32))
-        args.append(sums)
-    return pl.pallas_call(
-        functools.partial(merge_z_kernel, sums is not None),
-        in_specs=[VMEM] * len(args),
-        out_specs=[VMEM] * len(out),
-        out_shape=out,
-        compiler_params=params(8),
-        cost_estimate=cost(5 * STEPS * LANES * width, 1e6),
-        name="merge_z",
-    )(*args)
+def tie_kernel(x_ref, after_ref, out_ref):
+    del x_ref, after_ref, out_ref
+
+
+def tie(x, after):
+    return pl.pallas_call(
+        tie_kernel,
+        in_specs=[ANY, ANY],
+        out_specs=ANY,
+        out_shape=shape(x.shape, x.dtype),
+        input_output_aliases={0: 0},
+        name="tie",
+    )(x, after)
 
 
 def fold(a):
@@ -351,17 +342,19 @@
 BATCH = 16
 
 
-def coarse_kernel(packed, second, e_ref, k_ref, *refs):
+def coarse_kernel(packed, second, e_ref, k_ref, own_ref, *refs):
     refs = list(refs)
-    y = refs.pop(0)[...]
-    got = [refs.pop(0) for _ in range(packed)]
-    for r in got:
-        y = y + unpack(r)
+    if packed:
+        got = [own_ref.at[i] for i in range(own_ref.shape[0])]
+        y = sum(unpack(r) for r in got)
+    else:
+        y = own_ref[...]
     if second:
-        y0_ref, s_ref = refs.pop(0), refs.pop(0)
-        sums = s_ref[...]
-        for r in got:
-            sums = sums + unpack_sums(r)
+        y0_ref = refs.pop(0)
+        if packed:
+            sums = sum(unpack_sums(r) for r in got)
+        else:
+            sums = refs.pop(0)[...]
         l0, keep = length_of(sums)
         y = keep * y0_ref[...] - l0 * y
         refs.pop(0)
@@ -384,19 +377,22 @@
         for c in range(BATCH):
             parts.append(fold(t[c * members : (c + 1) * members] * e_ref[base + c].astype(F32)))
         x = jnp.concatenate(parts, axis=0)
-        x_ref[pl.ds(base, BATCH), :] = x.astype(BF)
+        for copy in range(x_ref.shape[0]):
+            x_ref[copy, pl.ds(base, BATCH), :] = x.astype(BF)
         sum_ref[0:1, :] += fold(x * yb)
 
 
-def coarse_image(ens, kern, own, got, after, y0=None, sums=None):
+def coarse_image(ens, kern, own, after, copies, y0=None, sums=None):
     columns, members, width = ens.shape
     second = y0 is not None
-    args = [ens, kern, own, *got] + ([y0, sums] if second else []) + [after]
-    out = [shape((columns, width), BF), shape((columns, width), F32)]
+    packed = own.ndim == 3
+    extra = ([y0] if packed else [y0, sums]) if second else []
+    args = [ens, kern, own, *extra, after]
+    out = [shape((copies, columns, width), BF), shape((columns, width), F32)]
     out += [shape((8, LANES), F32)] if second else []
     out += [shape((8, width), F32)]
     return pl.pallas_call(
-        functools.partial(coarse_kernel, len(got), second),
+        functools.partial(coarse_kernel, packed, second),
         in_specs=[VMEM] * (len(args) - 1) + [ANY],
         out_specs=[VMEM] * len(out),
         out_shape=out,
@@ -443,8 +439,9 @@
 def lay_out(x_refs, xs):
     at = 0
     for x in x_refs:
-        xs[pl.ds(at, x.shape[0]), :] = x[...]
-        at += x.shape[0]
+        for part in [x] if len(x.shape) == 2 else [x.at[i] for i in range(x.shape[0])]:
+            xs[pl.ds(at, part.shape[0]), :] = part[...]
+            at += part.shape[0]
 
 
 CUTS = 3
@@ -529,40 +526,29 @@
     return lax.ppermute(x, "space", [(i, i ^ 1) for i in range(GROUP)])
 
 
-def over_y(x):
-    return lax.ppermute(x, "space", [(i, i ^ 2) for i in range(GROUP)])
-
-
-def over_z(x, k):
-    return lax.ppermute(x, "space", [(i, (i + 4 * k) % GROUP) for i in range(GROUP)])
-
-
-def scatter_sums(parts, sums=None):
-    near, far_y, near_c, far_yc = parts
-    got_yc = over_core(far_yc)
-    got_c = over_core(near_c)
-    out, *s = merge_y(far_y, got_yc, sums)
-    got_y = over_y(out)
-    own, *out = merge_z(near, got_c, got_y, s[0] if s else None)
-    s = out[STEPS - 1 :]
-    got = [over_z(out[k - 1], k) for k in range(1, STEPS)]
-    return own, got, (s[0] if s else None)
-
-
-def gather_columns(x):
-    zs = [over_z(x, k) for k in range(1, STEPS)]
-    y_own = over_y(x)
-    c_own = over_core(x)
-    rest = jnp.concatenate(zs, axis=0)
-    y_rest = over_y(rest)
-    c_rest = over_core(rest)
-    return [x, rest, y_own, y_rest, c_own, c_rest, over_core(y_own), over_core(y_rest)]
+def over_chips(x):
+    groups = [list(range(c, GROUP, 2)) for c in range(2)]
+    return lax.all_to_all(
+        x, "space", split_axis=0, concat_axis=0, axis_index_groups=groups, tiled=True
+    )
+
+
+def scatter_sums(parts, after, sums=None):
+    near, far = parts
+    return tie(over_chips(merge(near, over_core(far), sums)), after), None
+
+
+def gather_columns(x, after):
+    got = over_chips(x)
+    if after is not None:
+        got = tie(got, after)
+    return [got, over_core(got)]
 
 
 def sum_all(x):
-    x = x + over_core(x)
-    x = x + over_y(x)
-    return x + over_z(x, 1) + over_z(x, 2) + over_z(x, 3)
+    x = jnp.broadcast_to(x[None], (GROUP,) + x.shape)
+    x = lax.all_to_all(x, "space", split_axis=0, concat_axis=0, tiled=True)
+    return jnp.sum(x, axis=0)
 
 
 def on_device(ensemble, innovation, obs_weight, interp_weight, slot_of, intersection_list):
@@ -586,15 +572,14 @@
     ens = jnp.transpose(ensemble, (1, 0, 2))
     at, y_slots = adjoint_first(slot_of, interp_weight, innovation, obs_weight, slots)
     index = lax.axis_index("space").astype(jnp.int32)
-    me = jnp.stack([index // 4, index // 2 % 2, index % 2, index])
+    me = jnp.stack([index % 2, index])
     if grouped:
-        lists = lax.all_to_all(
-            intersection_list, "space", split_axis=1, concat_axis=0, tiled=True
-        ).reshape(devices, capacity)
+        lists = lax.all_gather(intersection_list, "space", axis=0, tiled=True)
+        lists = lax.dynamic_index_in_dim(lists, index, axis=1, keepdims=False)
         scatter, gather, add_up = scatter_sums, gather_columns, sum_all
         first = split_first(me, lists, y_slots)
         at = place_rows(me, lists, at)
-        n = 4
+        n, copies = 2, CHIPS
     else:
         lists = intersection_list[0]
         hit = (lists.reshape(-1, 1) == jnp.arange(columns, dtype=jnp.int32)).astype(BF)
@@ -604,32 +589,32 @@
             x = lax.all_to_all(x, "space", split_axis=0, concat_axis=0, tiled=True)
             return x.reshape(slots, width)
 
-        def scatter(parts, sums=None):
+        def scatter(parts, after, sums=None):
             got = swap(parts[0])
             high = lax.reduce_precision(got, 8, 7)
             high, low = high.astype(BF), (got - high).astype(BF)
             if sums is not None:
                 sums = lax.psum(sums, "space")
-            return dot(hit.T, high) + dot(hit.T, low), [], sums
-
-        def gather(x):
-            return [swap(dot(hit, x).astype(BF))]
+            return dot(hit.T, high) + dot(hit.T, low), sums
+
+        def gather(x, after):
+            return [swap(dot(hit, x[0]).astype(BF))]
 
         def add_up(x):
             return lax.psum(x, "space")
 
         first = [y_slots]
-        n = 1
+        n, copies = 1, 1
 
     a = forward_matrix(me, slot_of.T, interp_weight.T, lists, slots, grouped)
-    own, got, _ = scatter(first)
-    x0, y0, g_sums = coarse_image(ens, kern, own, got, at)
-    im0, sums, *second = image_first(gather(x0), a, at, obs_weight, g_sums, n)
+    own, _ = scatter(first, ens)
+    x0, y0, g_sums = coarse_image(ens, kern, own, at, copies)
+    im0, sums, *second = image_first(gather(x0, a), a, at, obs_weight, g_sums, n)
     g0 = project(ens, y0, taps)
-    own, got, sums = scatter(second, sums)
-    x1, y1, l0, g_sums = coarse_image(ens, kern, own, got, g0, y0, sums)
+    own, sums = scatter(second, g0, sums)
+    x1, y1, l0, g_sums = coarse_image(ens, kern, own, g0, copies, y0, sums)
     g1 = project(ens, y1, taps)
-    im1, sums = image_second(gather(x1), a, obs_weight, g_sums, g1)
+    im1, sums = image_second(gather(x1, g1), a, obs_weight, g_sums, g1)
     l0 = l0[:1, :1]
     l1, _ = length_of(add_up(sums))
     return (-(l0 * g0 + l1 * g1), -(l0 * im0 + l1 * im1))

time: 144 us -> 196 us (1.36)
  local copies, waits for them, and re-layouts: 12.4 us -> 60.8 us
  starting transfers between devices: 43 us -> 19 us
  blocking collectives: 0 us -> 23.7 us
    unnamed x43 -> x83, local copies, waits for them, and re-layouts: 11.8 us -> 59.7 us
    ppermute x22 -> x0, waiting for transfers between devices: 34.4 us -> none  [the longest x7 21.8 us: over_y(): return lax.ppermute(x, 'space', [(i, i ^ 2) for i in range(GROUP)])]
    ppermute x22 -> x0, starting transfers between devices: 32.5 us -> none  [the longest x15 23.2 us: over_z(): lax.ppermute(x, 'space', [(i, (i + 4 * k) % GROUP) for i in range(GROUP)])]
    all_to_all x1 -> x5, waiting for transfers between devices: 0.01 us -> 28.9 us  [the longest x4 21.4 us: over_chips(): lax.all_to_all(x, 'space', split_axis=0, concat_axis=0, axis_index_groups...]
    all_gather x0 -> x1, blocking collectives: none -> 23.7 us  [on_device(): lists = lax.all_gather(intersection_list, 'space', axis=0, tiled=True)]
    all_to_all x1 -> x5, starting transfers between devices: 7.4 us -> 18.4 us  [the longest x4 14.7 us: over_chips(): lax.all_to_all(x, 'space', split_axis=0, concat_axis=0, axis_index_groups...]
    ppermute x13 -> x4, waiting for transfers between devices: 3.67 us -> 9.09 us  [over_core(): return lax.ppermute(x, 'space', [(i, i ^ 1) for i in range(GROUP)])]
    pallas_call x7 -> x9, Pallas kernels: 18.3 us -> 20.9 us  [the longest x1 9.78 us: adjoint_first(): pl.pallas_call(adjoint_kernel, in_specs=[HBM] * 4, out_specs=[VMEM] * 2,...]
  transfers between devices with their start and end apart: 36 -> 9, of which waited for: 18 -> 9; matrix products, arithmetic and copies ran while one was open for 5% -> 5% of each run, Pallas kernels for 19% -> 9%
where the time goes in v2:
time: 196 us; the launch traced here: 195 us
  local copies, waits for them, and re-layouts  60.8 us (31%)
  Pallas kernels  43.9 us (22%)
  waiting for transfers between devices  38 us (19%)
  blocking collectives  23.7 us (12%)
  starting transfers between devices  19 us (10%)
  other arithmetic  6.74 us (3%)
  between operations  2.67 us (1%)
    unnamed x83, local copies, waits for them, and re-layouts  59.7 us
    all_gather x1, blocking collectives, on_device(): lists = lax.all_gather(intersection_list, 'space', axis=0, tiled=True)  23.7 us
    all_to_all x4, waiting for transfers between devices, over_chips(): lax.all_to_all(x, 'space', split_axis=0, concat_axis=0, axis_index_groups...  21.4 us
    all_to_all x4, starting transfers between devices, over_chips(): lax.all_to_all(x, 'space', split_axis=0, concat_axis=0, axis_index_groups...  14.7 us
    pallas_call x1, Pallas kernels, adjoint_first(): pl.pallas_call(adjoint_kernel, in_specs=[HBM] * 4, out_specs=[VMEM] * 2,...  9.78 us
    ppermute x4, waiting for transfers between devices, over_core(): return lax.ppermute(x, 'space', [(i, i ^ 1) for i in range(GROUP)])  9.09 us
    pallas_call x2, Pallas kernels, coarse_image(): pl.pallas_call(functools.partial(coarse_kernel, packed, second), in_specs...  8.99 us
    pallas_call x1, Pallas kernels, forward_matrix(): pl.pallas_call(functools.partial(forward_matrix_kernel, grouped), grid=(f...  8.34 us
  transfers between devices with their start and end apart: 9, of which 9 were waited for; matrix products, arithmetic and copies ran while one was open for 5% of the time, Pallas kernels for 9%

profile of v2, /device:TPU:0, one launch (start us, length us, event | category | flops | bytes accessed | tf_op | source)
XLA Modules:
  0.0 194.7 jit_solution(16197667246755334714)
XLA Ops:
  0.6 23.7 %all_gather.3 = s32[16,16,128]{2,1,0:T(8,128)S(1)} all-gather(s32[1,16,128]{2,1,0:T(8,128)} %param.13), channel_id=1, replica_groups=mesh['case'=2,'space'=16] {'space'}, dimensions={0}, use_global_device_ids=true | all-gather | bytes 139264 | tf_op jit(solution)/shard_map/all_gather | solution.py:577
  28.0 9.8 %adjoint_first.1 = (bf16[2048,1152]{1,0:T(8,128)(2,1)S(1)}, f32[2048,256]{1,0:T(8,128)S(1)}) custom-call(s32[4,1152]{1,0:T(4,128)S(1)} %copy-done.35, f32[4,1152]{1,0:T(4,128)S(1)} %copy-done.37, bf16[1152,256]{1,0:T(8,128)(2,1)S(1)} %copy-done.24, bf16[1152,256]{1,0:T(8,128)(2,1)S(1)} %copy-done.39), custom_call_target="tpu_custom_call" | custom-call | flops 3623878656 | bytes 8000000 | tf_op jit(solution)/shard_map/adjoint_first/pallas_call | solution.py:111
  37.8 2.2 %copy-done.20 = bf16[2048,1152]{1,0:T(8,128)(2,1)} copy-done((bf16[2048,1152]{1,0:T(8,128)(2,1)}, bf16[2048,1152]{1,0:T(8,128)(2,1)S(1)}, u32[]{:S(2)}) %copy-start.20) | copy-done | bytes 4718616
  41.6 2.3 %collective-permute-done.b_ref = f32[1024,256]{1,0:T(8,128)S(1)} collective-permute-done((f32[1024,256]{1,0:T(8,128)S(1)}, f32[1024,256]{1,0:T(8,128)S(1)}, u32[]{:S(2)}, u32[]{:S(2)}) %collective-permute-start) | collective-permute-done | bytes 1048608 | tf_op jit(solution)/shard_map/ppermute | solution.py:526
  45.0 3.7 %all-to-all-start = ((s16[8,144,256]{2,1,0:T(8,128)(2,1)}), s16[8,144,256]{2,1,0:T(8,128)(2,1)S(1)}, u32[]{:S(2)}, u32[]{:S(2)}) async-start(s16[8,144,256]{2,1,0:T(8,128)(2,1)} %merge.2), calls=%async_computation | async-start | bytes 1179648 | tf_op jit(solution)/shard_map/all_to_all | solution.py:531
  48.7 7.8 %copy.24 = bf16[80,128,256]{2,0,1:T(8,128)(2,1)} copy(bf16[80,128,256]{2,1,0:T(8,128)(2,1)} %param.8) | data formatting | bytes 10485760 | tf_op args[0]
  56.5 2.3 %copy-done.21 = bf16[2048,1152]{1,0:T(8,128)(2,1)S(1)} copy-done((bf16[2048,1152]{1,0:T(8,128)(2,1)S(1)}, bf16[2048,1152]{1,0:T(8,128)(2,1)}, u32[]{:S(2)}) %copy-start.21) | copy-done | bytes 4718616
  60.8 2.2 %copy-done.7 = bf16[2048,1152]{1,0:T(8,128)(2,1)} copy-done((bf16[2048,1152]{1,0:T(8,128)(2,1)}, bf16[2048,1152]{1,0:T(8,128)(2,1)S(1)}, u32[]{:S(2)}) %copy-start.7) | copy-done | bytes 4718616
  66.9 2.5 %copy-done = bf16[80,128,256]{2,0,1:T(8,128)(2,1)S(1)} copy-done((bf16[80,128,256]{2,0,1:T(8,128)(2,1)S(1)}, bf16[80,128,256]{2,0,1:T(8,128)(2,1)}, u32[]{:S(2)}) %copy-start) | copy-done | bytes 5242904
  69.4 2.3 %copy-done.8 = bf16[2048,1152]{1,0:T(8,128)(2,1)S(1)} copy-done((bf16[2048,1152]{1,0:T(8,128)(2,1)S(1)}, bf16[2048,1152]{1,0:T(8,128)(2,1)}, u32[]{:S(2)}) %copy-start.8) | copy-done | bytes 4718616
  72.8 4.9 %coarse_first.1 = (bf16[8,128,256]{2,1,0:T(8,128)(2,1)}, f32[128,256]{1,0:T(8,128)S(1)}, f32[8,256]{1,0:T(8,128)S(1)}) custom-call(bf16[128,80,256]{2,1,0:T(8,128)(2,1)S(1)} %bitcast.13, bf16[256,256]{1,0:T(8,128)(2,1)S(1)} %copy-done.32, s16[8,144,256]{2,1,0:T(8,128)(2,1)S(1)} %copy-done.17, bf16[2048,1152]{1,0:T(8,128)(2,1)S(1)} %copy-done.8), custom_call_target="tpu_custom_call" | custom-call | flops 1342177280 | bytes 5000000 | tf_op jit(solution)/shard_map/coarse_first/pallas_call | solution.py:394
  77.7 3.6 %all-to-all-start.1 = ((bf16[8,128,256]{2,1,0:T(8,128)(2,1)}), bf16[8,128,256]{2,1,0:T(8,128)(2,1)S(1)}, u32[]{:S(2)}, u32[]{:S(2)}) async-start(bf16[8,128,256]{2,1,0:T(8,128)(2,1)} %get-tuple-element.23), calls=%async_computation.1 | async-start | bytes 1048576 | tf_op jit(solution)/shard_map/all_to_all | solution.py:531
  81.8 8.3 %forward_matrix.1.after_ref.refs_2_ = bf16[1152,2048]{1,0:T(8,128)(2,1)S(1)} custom-call(s32[2]{0:T(128)S(1)} %pad_add_fusion.me_ref, s32[1152,4]{1,0:T(8,128)S(1)} %bitcast.17, f32[1152,4]{1,0:T(8,128)S(1)} %bitcast.18, s32[16,128]{1,0:T(8,128)S(1)} %bitcast.21), custom_call_target="tpu_custom_call" | custom-call | flops 9663676416 | bytes 5000000 | tf_op jit(solution)/shard_map/forward_matrix/pallas_call | solution.py:176
  92.3 3.6 %all-to-all-done.1.x_ref = bf16[8,128,256]{2,1,0:T(8,128)(2,1)S(1)} async-done(((bf16[8,128,256]{2,1,0:T(8,128)(2,1)}), bf16[8,128,256]{2,1,0:T(8,128)(2,1)S(1)}, u32[]{:S(2)}, u32[]{:S(2)}) %all-to-all-start.1) | async-done | bytes 524320 | tf_op jit(solution)/shard_map/all_to_all | solution.py:531
  98.9 2.3 %copy-done.5 = bf16[1152,2048]{1,0:T(8,128)(2,1)S(1)} copy-done((bf16[1152,2048]{1,0:T(8,128)(2,1)S(1)}, bf16[1152,2048]{1,0:T(8,128)(2,1)}, u32[]{:S(2)}) %copy-start.5) | copy-done | bytes 4718616
  101.2 2.3 %copy-done.9 = bf16[2048,1152]{1,0:T(8,128)(2,1)S(1)} copy-done((bf16[2048,1152]{1,0:T(8,128)(2,1)S(1)}, bf16[2048,1152]{1,0:T(8,128)(2,1)}, u32[]{:S(2)}) %copy-start.9) | copy-done | bytes 4718616
  104.6 2.8 %image_first.1 = (f32[1152,256]{1,0:T(8,128)S(1)}, f32[8,256]{1,0:T(8,128)S(1)}, f32[1024,256]{1,0:T(8,128)S(1)}, f32[1032,256]{1,0:T(8,128)S(1)}) custom-call(bf16[8,128,256]{2,1,0:T(8,128)(2,1)S(1)} %copy-done.23, bf16[8,128,256]{2,1,0:T(8,128)(2,1)S(1)} %collective-permute-done.1.refs_1_, bf16[1152,2048]{1,0:T(8,128)(2,1)S(1)} %copy-done.5, ...), custom_call_target="tpu_custom_call" | custom-call | flops 2415919104 | bytes 13000000 | tf_op jit(solution)/shard_map/image_first/pallas_call | solution.py:480
  108.6 2.5 %collective-permute-done.2.b_ref = f32[1032,256]{1,0:T(8,128)S(1)} collective-permute-done((f32[1032,256]{1,0:T(8,128)S(1)}, f32[1032,256]{1,0:T(8,128)S(1)}, u32[]{:S(2)}, u32[]{:S(2)}) %collective-permute-start.2) | collective-permute-done | bytes 1056800 | tf_op jit(solution)/shard_map/ppermute | solution.py:526
  112.2 3.6 %all-to-all-start.2 = ((s16[8,144,256]{2,1,0:T(8,128)(2,1)}), s16[8,144,256]{2,1,0:T(8,128)(2,1)S(1)}, u32[]{:S(2)}, u32[]{:S(2)}) async-start(s16[8,144,256]{2,1,0:T(8,128)(2,1)} %merge.3), calls=%async_computation.2 | async-start | bytes 1179648 | tf_op jit(solution)/shard_map/all_to_all | solution.py:531
  115.9 2.5 %copy-done.1 = bf16[80,128,256]{2,0,1:T(8,128)(2,1)S(1)} copy-done((bf16[80,128,256]{2,0,1:T(8,128)(2,1)S(1)}, bf16[80,128,256]{2,0,1:T(8,128)(2,1)}, u32[]{:S(2)}) %copy-start.1) | copy-done | bytes 5242904
  118.3 3.6 %project.2.after_ref.refs_1_ = f32[80,8192]{1,0:T(8,128)S(1)} custom-call(bf16[128,80,256]{2,1,0:T(8,128)(2,1)S(1)} %bitcast.14, f32[128,256]{1,0:T(8,128)S(1)} %get-tuple-element.28.y_ref.refs_0_, bf16[2,256,128]{2,1,0:T(8,128)(2,1)S(1)} %copy-done.31), custom_call_target="tpu_custom_call" | custom-call | flops 1342177280 | bytes 8000000 | tf_op jit(solution)/shard_map/project/pallas_call | solution.py:427
  123.5 8.7 %all-to-all-done.2.x_ref = s16[8,144,256]{2,1,0:T(8,128)(2,1)S(1)} async-done(((s16[8,144,256]{2,1,0:T(8,128)(2,1)}), s16[8,144,256]{2,1,0:T(8,128)(2,1)S(1)}, u32[]{:S(2)}, u32[]{:S(2)}) %all-to-all-start.2) | async-done | bytes 589856 | tf_op jit(solution)/shard_map/all_to_all | solution.py:531
  134.7 2.5 %copy-done.2 = bf16[80,128,256]{2,0,1:T(8,128)(2,1)S(1)} copy-done((bf16[80,128,256]{2,0,1:T(8,128)(2,1)S(1)}, bf16[80,128,256]{2,0,1:T(8,128)(2,1)}, u32[]{:S(2)}) %copy-start.2) | copy-done | bytes 5242904
  139.2 4.1 %coarse_second.1 = (bf16[8,128,256]{2,1,0:T(8,128)(2,1)S(1)}, f32[128,256]{1,0:T(8,128)S(1)}, f32[8,128]{1,0:T(8,128)S(1)}, f32[8,256]{1,0:T(8,128)S(1)}) custom-call(bf16[128,80,256]{2,1,0:T(8,128)(2,1)S(1)} %bitcast.15, bf16[256,256]{1,0:T(8,128)(2,1)S(1)} %copy-done.33, s16[8,144,256]{2,1,0:T(8,128)(2,1)S(1)} %copy-done.15, ...), custom_call_target="tpu_custom_call" | custom-call | flops 1342177280 | bytes 5000000 | tf_op jit(solution)/shard_map/coarse_second/pallas_call | solution.py:394
  144.1 3.7 %all-to-all-start.3 = ((bf16[8,128,256]{2,1,0:T(8,128)(2,1)}), bf16[8,128,256]{2,1,0:T(8,128)(2,1)S(1)}, u32[]{:S(2)}, u32[]{:S(2)}) async-start(bf16[8,128,256]{2,1,0:T(8,128)(2,1)} %copy-done.34), calls=%async_computation.3 | async-start | bytes 1048576 | tf_op jit(solution)/shard_map/all_to_all | solution.py:531
  147.8 2.5 %copy-done.3 = bf16[80,128,256]{2,0,1:T(8,128)(2,1)S(1)} copy-done((bf16[80,128,256]{2,0,1:T(8,128)(2,1)S(1)}, bf16[80,128,256]{2,0,1:T(8,128)(2,1)}, u32[]{:S(2)}) %copy-start.3) | copy-done | bytes 5242904
  150.3 3.6 %project.3.after_ref.refs_5_ = f32[80,8192]{1,0:T(8,128)S(1)} custom-call(bf16[128,80,256]{2,1,0:T(8,128)(2,1)S(1)} %bitcast.16, f32[128,256]{1,0:T(8,128)S(1)} %get-tuple-element.31.y_ref, bf16[2,256,128]{2,1,0:T(8,128)(2,1)S(1)} %copy-done.31), custom_call_target="tpu_custom_call" | custom-call | flops 1342177280 | bytes 8000000 | tf_op jit(solution)/shard_map/project/pallas_call | solution.py:427
  155.4 6.9 %all-to-all-done.3.x_ref = bf16[8,128,256]{2,1,0:T(8,128)(2,1)S(1)} async-done(((bf16[8,128,256]{2,1,0:T(8,128)(2,1)}), bf16[8,128,256]{2,1,0:T(8,128)(2,1)S(1)}, u32[]{:S(2)}, u32[]{:S(2)}) %all-to-all-start.3) | async-done | bytes 524320 | tf_op jit(solution)/shard_map/all_to_all | solution.py:531
  165.3 2.3 %copy-done.6 = bf16[1152,2048]{1,0:T(8,128)(2,1)S(1)} copy-done((bf16[1152,2048]{1,0:T(8,128)(2,1)S(1)}, bf16[1152,2048]{1,0:T(8,128)(2,1)}, u32[]{:S(2)}) %copy-start.6) | copy-done | bytes 4718616
  174.6 3.7 %all-to-all-start.4 = ((f32[16,8,256]{2,1,0:T(8,128)}), f32[16,8,256]{2,1,0:T(8,128)S(1)}, u32[]{:S(2)}, u32[]{:S(2)}) async-start(f32[16,8,256]{2,1,0:T(8,128)} %broadcast_in_dim.12), calls=%async_computation.4 | async-start | bytes 262144 | tf_op jit(solution)/shard_map/all_to_all | solution.py:550
  178.8 7.5 %all-to-all-done.4 = f32[16,8,256]{2,1,0:T(8,128)S(1)} async-done(((f32[16,8,256]{2,1,0:T(8,128)}), f32[16,8,256]{2,1,0:T(8,128)S(1)}, u32[]{:S(2)}, u32[]{:S(2)}) %all-to-all-start.4) | async-done | bytes 131104 | tf_op jit(solution)/shard_map/all_to_all | solution.py:550
  188.7 4.3 %add_negate_fusion = f32[80,8192]{1,0:T(8,128)} fusion(f32[80,8192]{1,0:T(8,128)} %copy-done.12, f32[80,8192]{1,0:T(8,128)S(1)} %copy-done.11, f32[]{:T(128)} %bitcast.9, f32[]{:T(128)} %bitcast.6), kind=kLoop, calls=%fused_computation.1 | loop fusion | flops 2621440 | bytes 7864328 | tf_op jit(solution)/shard_map/neg | solution.py:620
  (94 shorter events, 43.1 us)
Async XLA Ops:
  24.4 1.1 copy-start.24
  37.8 2.2 %copy-start.20 = (bf16[2048,1152]{1,0:T(8,128)(2,1)}, bf16[2048,1152]{1,0:T(8,128)(2,1)S(1)}, u32[]{:S(2)}) copy-start(bf16[2048,1152]{1,0:T(8,128)(2,1)S(1)} %get-tuple-element.22.at_ref) | copy-start | bytes 14155780
  41.2 2.7 %collective-permute-start = (f32[1024,256]{1,0:T(8,128)S(1)}, f32[1024,256]{1,0:T(8,128)S(1)}, u32[]{:S(2)}, u32[]{:S(2)}) collective-permute-start(f32[1024,256]{1,0:T(8,128)S(1)} %get-tuple-element.21), channel_id=1, source_target_pairs={{0,1},{1,0},{2,3},{3,2},{4,5},{5,4},{6,7},{7,6},{8,9},{9,8},{10,11... | collective-permute-start | bytes 3145736 | tf_op jit(solution)/shard_map/ppermute | solution.py:526
  45.0 20.2 %all-to-all-start = ((s16[8,144,256]{2,1,0:T(8,128)(2,1)}), s16[8,144,256]{2,1,0:T(8,128)(2,1)S(1)}, u32[]{:S(2)}, u32[]{:S(2)}) async-start(s16[8,144,256]{2,1,0:T(8,128)(2,1)} %merge.2), calls=%async_computation | async-start | bytes 1179648 | tf_op jit(solution)/shard_map/all_to_all | solution.py:531
  56.5 2.3 %copy-start.21 = (bf16[2048,1152]{1,0:T(8,128)(2,1)S(1)}, bf16[2048,1152]{1,0:T(8,128)(2,1)}, u32[]{:S(2)}) copy-start(bf16[2048,1152]{1,0:T(8,128)(2,1)} %copy-done.20) | copy-start | bytes 14155780
  60.8 2.2 %copy-start.7 = (bf16[2048,1152]{1,0:T(8,128)(2,1)}, bf16[2048,1152]{1,0:T(8,128)(2,1)S(1)}, u32[]{:S(2)}) copy-start(bf16[2048,1152]{1,0:T(8,128)(2,1)S(1)} %place_rows.1.refs_0_.refs_3_) | copy-start | bytes 14155780
  66.9 2.5 %copy-start = (bf16[80,128,256]{2,0,1:T(8,128)(2,1)S(1)}, bf16[80,128,256]{2,0,1:T(8,128)(2,1)}, u32[]{:S(2)}) copy-start(bf16[80,128,256]{2,0,1:T(8,128)(2,1)} %copy.24) | copy-start | bytes 15728644
  69.4 2.3 %copy-start.8 = (bf16[2048,1152]{1,0:T(8,128)(2,1)S(1)}, bf16[2048,1152]{1,0:T(8,128)(2,1)}, u32[]{:S(2)}) copy-start(bf16[2048,1152]{1,0:T(8,128)(2,1)} %copy-done.7) | copy-start | bytes 14155780
  72.8 8.5 %copy-start.36 = (s32[4,1152]{1,0:T(4,128)S(1)}, s32[4,1152]{1,0:T(4,128)}, u32[]{:S(2)}) copy-start(s32[4,1152]{1,0:T(4,128)} %refs_0_.1) | copy-start | bytes 55300
  72.8 8.7 %copy-start.38 = (f32[4,1152]{1,0:T(4,128)S(1)}, f32[4,1152]{1,0:T(4,128)}, u32[]{:S(2)}) copy-start(f32[4,1152]{1,0:T(4,128)} %refs_1_.1) | copy-start | bytes 55300
  77.7 18.3 %all-to-all-start.1 = ((bf16[8,128,256]{2,1,0:T(8,128)(2,1)}), bf16[8,128,256]{2,1,0:T(8,128)(2,1)S(1)}, u32[]{:S(2)}, u32[]{:S(2)}) async-start(bf16[8,128,256]{2,1,0:T(8,128)(2,1)} %get-tuple-element.23), calls=%async_computation.1 | async-start | bytes 1048576 | tf_op jit(solution)/shard_map/all_to_all | solution.py:531
  90.1 2.2 %copy-start.4 = (bf16[1152,2048]{1,0:T(8,128)(2,1)}, bf16[1152,2048]{1,0:T(8,128)(2,1)S(1)}, u32[]{:S(2)}) copy-start(bf16[1152,2048]{1,0:T(8,128)(2,1)S(1)} %forward_matrix.1.after_ref.refs_2_) | copy-start | bytes 14155780
  92.3 6.6 %copy-start.25 = (bf16[1152,256]{1,0:T(8,128)(2,1)S(1)}, bf16[1152,256]{1,0:T(8,128)(2,1)}, u32[]{:S(2)}) copy-start(bf16[1152,256]{1,0:T(8,128)(2,1)} %refs_3_.3) | copy-start | bytes 1769476
  96.8 2.1 %collective-permute-start.1 = (bf16[8,128,256]{2,1,0:T(8,128)(2,1)}, bf16[8,128,256]{2,1,0:T(8,128)(2,1)S(1)}, u32[]{:S(2)}, u32[]{:S(2)}) collective-permute-start(bf16[8,128,256]{2,1,0:T(8,128)(2,1)} %tie.5.refs_0_), channel_id=1, source_target_pairs={{0,1},{1,0},{2,3},{3,2},{4,5},{5,4},{6,7},{7,6},{8,9},{9,8},{10,11... | collective-permute-start | bytes 1572872 | tf_op jit(solution)/shard_map/ppermute | solution.py:526
  98.9 2.3 %copy-start.5 = (bf16[1152,2048]{1,0:T(8,128)(2,1)S(1)}, bf16[1152,2048]{1,0:T(8,128)(2,1)}, u32[]{:S(2)}) copy-start(bf16[1152,2048]{1,0:T(8,128)(2,1)} %copy-done.4) | copy-start | bytes 14155780
  101.2 2.3 %copy-start.9 = (bf16[2048,1152]{1,0:T(8,128)(2,1)S(1)}, bf16[2048,1152]{1,0:T(8,128)(2,1)}, u32[]{:S(2)}) copy-start(bf16[2048,1152]{1,0:T(8,128)(2,1)} %copy-done.7) | copy-start | bytes 14155780
  108.5 7.4 %copy-start.31 = (bf16[2,256,128]{2,1,0:T(8,128)(2,1)S(1)}, bf16[2,256,128]{2,1,0:T(8,128)(2,1)}, u32[]{:S(2)}) copy-start(bf16[2,256,128]{2,1,0:T(8,128)(2,1)} %constant.29.clone.t_ref) | copy-start | bytes 393220
  108.5 2.7 %collective-permute-start.2 = (f32[1032,256]{1,0:T(8,128)S(1)}, f32[1032,256]{1,0:T(8,128)S(1)}, u32[]{:S(2)}, u32[]{:S(2)}) collective-permute-start(f32[1032,256]{1,0:T(8,128)S(1)} %get-tuple-element.26), channel_id=1, source_target_pairs={{0,1},{1,0},{2,3},{3,2},{4,5},{5,4},{6,7},{7,6},{8,9},{9,8},{10,11... | collective-permute-start | bytes 3170312 | tf_op jit(solution)/shard_map/ppermute | solution.py:526
  112.2 19.9 %all-to-all-start.2 = ((s16[8,144,256]{2,1,0:T(8,128)(2,1)}), s16[8,144,256]{2,1,0:T(8,128)(2,1)S(1)}, u32[]{:S(2)}, u32[]{:S(2)}) async-start(s16[8,144,256]{2,1,0:T(8,128)(2,1)} %merge.3), calls=%async_computation.2 | async-start | bytes 1179648 | tf_op jit(solution)/shard_map/all_to_all | solution.py:531
  115.9 2.5 %copy-start.1 = (bf16[80,128,256]{2,0,1:T(8,128)(2,1)S(1)}, bf16[80,128,256]{2,0,1:T(8,128)(2,1)}, u32[]{:S(2)}) copy-start(bf16[80,128,256]{2,0,1:T(8,128)(2,1)} %copy.24) | copy-start | bytes 15728644
  122.0 1.5 copy-start.10
  133.0 1.7 copy-start.11
  134.7 2.5 %copy-start.2 = (bf16[80,128,256]{2,0,1:T(8,128)(2,1)S(1)}, bf16[80,128,256]{2,0,1:T(8,128)(2,1)}, u32[]{:S(2)}) copy-start(bf16[80,128,256]{2,0,1:T(8,128)(2,1)} %copy.24) | copy-start | bytes 15728644
  144.1 18.3 %all-to-all-start.3 = ((bf16[8,128,256]{2,1,0:T(8,128)(2,1)}), bf16[8,128,256]{2,1,0:T(8,128)(2,1)S(1)}, u32[]{:S(2)}, u32[]{:S(2)}) async-start(bf16[8,128,256]{2,1,0:T(8,128)(2,1)} %copy-done.34), calls=%async_computation.3 | async-start | bytes 1048576 | tf_op jit(solution)/shard_map/all_to_all | solution.py:531
  147.8 2.5 %copy-start.3 = (bf16[80,128,256]{2,0,1:T(8,128)(2,1)S(1)}, bf16[80,128,256]{2,0,1:T(8,128)(2,1)}, u32[]{:S(2)}) copy-start(bf16[80,128,256]{2,0,1:T(8,128)(2,1)} %copy.24) | copy-start | bytes 15728644
  153.9 1.5 copy-start.12
  163.2 2.1 %collective-permute-start.3 = (bf16[8,128,256]{2,1,0:T(8,128)(2,1)}, bf16[8,128,256]{2,1,0:T(8,128)(2,1)S(1)}, u32[]{:S(2)}, u32[]{:S(2)}) collective-permute-start(bf16[8,128,256]{2,1,0:T(8,128)(2,1)} %tie.7.refs_0_), channel_id=1, source_target_pairs={{0,1},{1,0},{2,3},{3,2},{4,5},{5,4},{6,7},{7,6},{8,9},{9,8},{10,11... | collective-permute-start | bytes 1572872 | tf_op jit(solution)/shard_map/ppermute | solution.py:526
  165.3 2.3 %copy-start.6 = (bf16[1152,2048]{1,0:T(8,128)(2,1)S(1)}, bf16[1152,2048]{1,0:T(8,128)(2,1)}, u32[]{:S(2)}) copy-start(bf16[1152,2048]{1,0:T(8,128)(2,1)} %copy-done.4) | copy-start | bytes 14155780
  167.6 1.7 copy-start.13
  174.6 11.7 %all-to-all-start.4 = ((f32[16,8,256]{2,1,0:T(8,128)}), f32[16,8,256]{2,1,0:T(8,128)S(1)}, u32[]{:S(2)}, u32[]{:S(2)}) async-start(f32[16,8,256]{2,1,0:T(8,128)} %broadcast_in_dim.12), calls=%async_computation.4 | async-start | bytes 262144 | tf_op jit(solution)/shard_map/all_to_all | solution.py:550
  188.7 4.3 %copy-start.28 = (f32[1152,256]{1,0:T(8,128)S(1)}, f32[1152,256]{1,0:T(8,128)}, u32[]{:S(2)}) copy-start(f32[1152,256]{1,0:T(8,128)} %copy-done.27) | copy-start | bytes 3538948
  188.7 4.3 %copy-start.30 = (f32[1152,256]{1,0:T(8,128)S(1)}, f32[1152,256]{1,0:T(8,128)}, u32[]{:S(2)}) copy-start(f32[1152,256]{1,0:T(8,128)} %copy-done.29) | copy-start | bytes 3538948
  (17 other events, 15.6 us)

commit v3 on v1

v3 whole, which is shorter than its diff:
```python
import functools

import jax
import jax.numpy as jnp
import ml_dtypes
import numpy as np
from jax import lax
from jax.experimental import pallas as pl
from jax.experimental.pallas import tpu as pltpu
from jax.sharding import PartitionSpec as P

VAR = 4
LOC_SCALE = 3.0
BF = jnp.bfloat16
F32 = jnp.float32
LANES = 128
GROUP = 16
VMEM = pl.BlockSpec(memory_space=pltpu.VMEM)
SMEM = pl.BlockSpec(memory_space=pltpu.SMEM)
ANY = pl.BlockSpec(memory_space=pl.ANY)


def vertical_taper(levels):
    heights = np.arange(levels).astype(np.float32)
    spread = (heights[:, None] - heights[None, :]) / np.float32(LOC_SCALE)
    return np.exp(np.float32(-0.5) * spread * spread)


def host_halves(x):
    high = x.astype(ml_dtypes.bfloat16)
    return [high, (x - high.astype(x.dtype)).astype(ml_dtypes.bfloat16)]


def params(mib):
    return pltpu.CompilerParams(vmem_limit_bytes=mib << 20)


def cost(flops, nbytes):
    return pl.CostEstimate(flops=int(flops), bytes_accessed=int(nbytes), transcendentals=0)


def dot(a, b):
    return jnp.dot(a, b, preferred_element_type=F32)


def halves(x):
    high = x.astype(BF)
    return high, (x - high.astype(F32)).astype(BF)


def shape(dims, dtype):
    return jax.ShapeDtypeStruct(dims, dtype)


STEPS = 4
ORDER = (2, 1, 3, 0)
PARTS = ((0, 0), (1, 0), (0, 1), (1, 1))
HEAD = 16
TOP = 32512.0


def owner_at(me_ref, i):
    dy, dc = PARTS[i // STEPS]
    z, y, c = me_ref[0], me_ref[1], me_ref[2]
    y = y if dy == 0 else 1 - y
    c = c if dc == 0 else 1 - c
    return (lax.rem(z + ORDER[i % STEPS], STEPS) * 2 + y) * 2 + c


def places(me_ref, lists_ref, slots):
    slots = jnp.concatenate([slots, slots], axis=0)
    from_owner = jnp.right_shift(slots, 7)
    within = jnp.bitwise_and(slots, LANES - 1)
    rows = jnp.zeros(slots.shape, jnp.int32)
    for i in range(GROUP):
        o = owner_at(me_ref, i)
        row = jnp.broadcast_to(lists_ref[pl.ds(o, 1), :], slots.shape)
        column = jnp.take_along_axis(row, within, axis=1, mode="promise_in_bounds")
        rows = jnp.where(from_owner == o, column + i * LANES, rows)
    return rows[: slots.shape[0] // 2]


def build_rows(ids_ref, weight_ref, wh_ref, wl_ref, at_ref, y_refs, lo_s, base):
    sources, fine = ids_ref.shape
    rows = at_ref.shape[0] // len(y_refs)
    step = rows // 2
    row = lax.broadcasted_iota(jnp.int32, (step, LANES), 0)
    for n, y_ref in enumerate(y_refs):
        for m in range(2):
            start = n * rows + m * step
            for j in range(fine // LANES):
                lanes = pl.ds(j * LANES, LANES)
                total = None
                for b in range(sources):
                    ids = ids_ref[b : b + 1, lanes] - (base + start)
                    term = jnp.where(row == ids, weight_ref[b : b + 1, lanes], 0.0)
                    total = term if total is None else total + term
                high, low = halves(total)
                at_ref[pl.ds(start, step), lanes] = high
                lo_s[pl.ds(m * step, step), lanes] = low
        held = at_ref[pl.ds(n * rows, rows), :]
        y_ref[...] = dot(held, wh_ref[...]) + dot(held, wl_ref[...]) + dot(lo_s[...], wh_ref[...])


def far_kernel(grouped, me_ref, lists_ref, both_ref, wh_ref, wl_ref, *refs):
    ids_ref, weight_ref, at_ref, ya_ref, yb_ref, lo_s = refs
    sources = ids_ref.shape[0]
    for j in range(ids_ref.shape[1] // LANES):
        lanes = pl.ds(j * LANES, LANES)
        slots = both_ref[:sources, lanes].astype(jnp.int32)
        ids_ref[:, lanes] = places(me_ref, lists_ref, slots) if grouped else slots
        weight_ref[:, lanes] = both_ref[sources:, lanes]
    half = at_ref.shape[0]
    build_rows(ids_ref, weight_ref, wh_ref, wl_ref, at_ref, [ya_ref, yb_ref], lo_s, half)


def near_kernel(ids_ref, weight_ref, wh_ref, wl_ref, at_ref, ya_ref, yb_ref, lo_s):
    build_rows(ids_ref, weight_ref, wh_ref, wl_ref, at_ref, [ya_ref, yb_ref], lo_s, 0)


def adjoint_half(slots, args, head=None):
    fine, width = args[-1].shape
    half = slots // 2
    sources = args[0].shape[0] // (2 if head else 1)
    out = [shape((half, fine), BF)] + [shape((half // 2, width), F32)] * 2
    if head:
        grouped, me, lists = head
        kernel = functools.partial(far_kernel, grouped)
        args = [me, lists, *args]
        out = [shape((sources, fine), jnp.int32), shape((sources, fine), F32)] + out
    else:
        kernel = near_kernel
    return pl.pallas_call(
        kernel,
        in_specs=([SMEM] if head else []) + [VMEM] * (len(args) - (1 if head else 0)),
        out_specs=[VMEM] * len(out),
        out_shape=out,
        scratch_shapes=[pltpu.VMEM((half // 2, fine), BF)],
        compiler_params=params(16),
        cost_estimate=cost(3 * slots * fine * width, 4e6),
        name="adjoint_far" if head else "adjoint_near",
    )(*args)


def exponent(m):
    return jnp.clip(jnp.ceil(jnp.log2(jnp.maximum(m, 1e-30))), -100.0, 100.0)


def whole16(x):
    return x.astype(jnp.int32).astype(jnp.int16)


def wide(x):
    return x.astype(jnp.int32).astype(F32)


def pack(out_ref, t, sums=None):
    rows, width = t.shape
    e = exponent(jnp.max(jnp.abs(t), axis=0, keepdims=True))
    out_ref[pl.ds(0, rows), :] = whole16(jnp.round(t * (jnp.exp2(-e) * TOP)))
    head = [e]
    if sums is not None:
        for i in range(2):
            v = sums[i : i + 1, :]
            f = exponent(v)
            v = v * (jnp.exp2(-f) * 16384.0)
            first = jnp.floor(v)
            head += [f, first, jnp.floor((v - first) * 16384.0)]
    row = lax.broadcasted_iota(jnp.int32, (HEAD, width), 0)
    total = jnp.zeros((HEAD, width), F32)
    for i, h in enumerate(head):
        total = jnp.where(row == i, h, total)
    out_ref[pl.ds(rows, HEAD), :] = whole16(total)


def unpack(ref):
    rows = ref.shape[0] - HEAD
    head = wide(ref[pl.ds(rows, HEAD), :])
    return wide(ref[pl.ds(0, rows), :]) * (jnp.exp2(head[0:1, :]) * (1.0 / TOP))


def unpack_sums(ref):
    head = wide(ref[pl.ds(ref.shape[0] - HEAD, HEAD), :])
    row = lax.broadcasted_iota(jnp.int32, (8, head.shape[1]), 0)
    total = jnp.zeros(row.shape, F32)
    for i in range(2):
        f, first, second = [head[1 + 3 * i + j : 2 + 3 * i + j, :] for j in range(3)]
        v = (first + second * (1.0 / 16384.0)) * (jnp.exp2(f) * (1.0 / 16384.0))
        total = jnp.where(row == i, v, total)
    return total


def merge_y_kernel(with_sums, *refs):
    if with_sums:
        a_ref, b_ref, mine_ref, first_ref, second_ref, s_ref = refs
        sums = mine_ref[...] + b_ref[pl.ds(a_ref.shape[0], 8), :]
        s_ref[...] = sums
    else:
        a_ref, b_ref, first_ref, second_ref = refs
        sums = None
    half = a_ref.shape[0] // 2
    pack(first_ref, a_ref[pl.ds(0, half), :] + b_ref[pl.ds(0, half), :], sums)
    pack(second_ref, a_ref[pl.ds(half, half), :] + b_ref[pl.ds(half, half), :])


def merge_y(a, b, sums):
    rows, width = a.shape
    out = [shape((rows // 2 + HEAD, width), jnp.int16)] * 2
    args = [a, b]
    if sums is not None:
        out.append(shape((8, width), F32))
        args.append(sums)
    return pl.pallas_call(
        functools.partial(merge_y_kernel, sums is not None),
        in_specs=[VMEM] * len(args),
        out_specs=[VMEM] * len(out),
        out_shape=out,
        compiler_params=params(8),
        cost_estimate=cost(5 * rows * width, 1e6),
        name="merge_y",
    )(*args)


def merge_z_kernel(last, with_sums, a_ref, b_ref, p_ref, *refs):
    half = a_ref.shape[0] // 2
    rows = pl.ds(half if last else 0, half)
    t = a_ref[rows, :] + b_ref[rows, :] + unpack(p_ref)
    sums = None
    if with_sums:
        sums = refs[0][...]
        refs = refs[1:]
        if not last:
            sums = sums + unpack_sums(p_ref)
            refs[2][...] = sums
    pack(refs[0], t[:LANES], sums)
    if last:
        refs[1][...] = t[LANES:]
    else:
        pack(refs[1], t[LANES:], sums)


def merge_z(last, a, b, p, sums):
    width = a.shape[1]
    sent = shape((LANES + HEAD, width), jnp.int16)
    out = [sent, shape((LANES, width), F32) if last else sent]
    args = [a, b, p]
    if sums is not None:
        args.append(sums)
        if not last:
            out.append(shape((8, width), F32))
    return pl.pallas_call(
        functools.partial(merge_z_kernel, last, sums is not None),
        in_specs=[VMEM] * len(args),
        out_specs=[VMEM] * len(out),
        out_shape=out,
        compiler_params=params(8),
        cost_estimate=cost(5 * a.size, 1e6),
        name="merge_z_last" if last else "merge_z_first",
    )(*args)


def join_kernel(a_ref, b_ref, c_ref, after_ref, out_ref):
    for i, r in enumerate((a_ref, b_ref, c_ref)):
        out_ref[i] = r[...]


def join(blocks, after):
    return pl.pallas_call(
        join_kernel,
        in_specs=[VMEM] * 4,
        out_specs=VMEM,
        out_shape=shape((3,) + blocks[0].shape, BF),
        compiler_params=params(8),
        cost_estimate=cost(1e5, 4e5),
        name="join",
    )(*blocks, after)


def fold(a):
    return jnp.sum(a, axis=0, keepdims=True)


def length_of(sums):
    grad = jnp.sum(sums[0:1, :], axis=1, keepdims=True)
    image = jnp.sum(sums[1:2, :], axis=1, keepdims=True)
    return grad / (grad + image), image / (grad + image)


def products(e, y, held, rows):
    p = e.astype(F32) * y
    q = p[:, :LANES] + p[:, LANES:]
    q = q + pltpu.roll(q, LANES // 2, 1)
    high, low = halves(q)
    held[rows, :LANES] = high
    held[rows, LANES:] = low


BATCH = 16
SOME = 8


def coarse_kernel(packed, second, e_ref, k_ref, own_ref, *refs):
    refs = list(refs)
    got = [refs.pop(0) for _ in range(packed)]
    y = own_ref[...]
    for r in got:
        y = y + unpack(r)
    if second:
        y0_ref, s_ref = refs.pop(0), refs.pop(0)
        sums = s_ref[...]
        for r in got:
            sums = sums + unpack_sums(r)
        l0, keep = length_of(sums)
        y = keep * y0_ref[...] - l0 * y
        refs.pop(2)[...] = jnp.broadcast_to(l0, (8, LANES))
    x_ref, y_ref, sum_ref, p_s, x_s = refs
    members, columns, width = e_ref.shape
    y_ref[...] = y
    x_s[...] = jnp.zeros_like(x_s)

    @pl.loop(0, members // SOME)
    def _(i):
        for m in range(SOME):
            products(e_ref[i * SOME + m], y_ref[...], p_s, pl.ds(m * columns, columns))
        t = dot(p_s[...], k_ref[...])
        total = x_s[...]
        for m in range(SOME):
            total = total + t[m * columns : (m + 1) * columns] * e_ref[i * SOME + m].astype(F32)
        x_s[...] = total

    x = x_s[...]
    x_ref[...] = x.T.astype(BF)
    sum_ref[...] = jnp.zeros_like(sum_ref)
    sum_ref[0:1, :] = fold(x * y_ref[...])


def coarse_image(ensemble, kern, own, got, y0=None, sums=None):
    members, columns, width = ensemble.shape
    second = y0 is not None
    args = [ensemble, kern, own, *got] + ([y0, sums] if second else [])
    out = [shape((width, columns), BF), shape((columns, width), F32)]
    out += [shape((8, LANES), F32)] if second else []
    out += [shape((8, width), F32)]
    return pl.pallas_call(
        functools.partial(coarse_kernel, len(got), second),
        in_specs=[VMEM] * len(args),
        out_specs=[VMEM] * len(out),
        out_shape=out,
        scratch_shapes=[
            pltpu.VMEM((SOME * columns, width), BF),
            pltpu.VMEM((columns, width), F32),
        ],
        compiler_params=params(16),
        cost_estimate=cost(2 * columns * members * width * width, 5e6),
        name="coarse_second" if second else "coarse_first",
    )(*args)


def project_kernel(e_ref, y_ref, t_ref, g_ref, token_ref, even_s, odd_s):
    columns, members, width = e_ref.shape
    lanes = BATCH // 2 * LANES
    token_ref[...] = jnp.zeros_like(token_ref)

    @pl.loop(0, columns // BATCH)
    def _(i):
        base = pl.multiple_of(i * BATCH, BATCH)
        yb = y_ref[pl.ds(base, BATCH), :]
        for c in range(BATCH):
            held = odd_s if c % 2 else even_s
            rows = pl.ds((c // 2) * members, members)
            products(e_ref[base + c], yb[c : c + 1, :], held, rows)
        r = dot(even_s[...], t_ref[0]) + dot(odd_s[...], t_ref[1])
        for pair in range(BATCH // 2):
            at = pl.multiple_of(i * lanes + pair * LANES, LANES)
            g_ref[:, pl.ds(at, LANES)] = r[pair * members : (pair + 1) * members]


def project(ens, y, taps):
    columns, members, width = ens.shape
    levels = width // VAR
    return pl.pallas_call(
        project_kernel,
        in_specs=[VMEM] * 3,
        out_specs=[VMEM] * 2,
        out_shape=[shape((members, columns * levels), F32), shape((8, LANES), F32)],
        scratch_shapes=[pltpu.VMEM((BATCH // 2 * members, width), BF)] * 2,
        compiler_params=params(16),
        cost_estimate=cost(2 * columns * members * width * width, 8e6),
        name="project",
    )(ens, y, taps)


def lay_out(x_refs, xs):
    if len(x_refs) == 1:
        xs[...] = x_refs[0][...]
        return
    own, rest = x_refs[0::2], x_refs[1::2]
    for part in range(STEPS):
        at = part * STEPS * LANES
        for i in range(STEPS - 1):
            xs[:, pl.ds(at + i * LANES, LANES)] = rest[part][i]
        xs[:, pl.ds(at + (STEPS - 1) * LANES, LANES)] = own[part][...]


CUTS = 3


def images(x_refs, near_ref, far_ref, obs_ref, im_ref, xs):
    lay_out(x_refs, xs)
    half, fine = near_ref.shape
    rows = fine // CUTS
    for i in range(CUTS):
        some = pl.ds(i * rows, rows)
        turned = dot(xs[:, :half], near_ref[:, some]) + dot(xs[:, half:], far_ref[:, some])
        im = turned.T
        im_ref[some, :] = im
        yield some, im, obs_ref[some, :].astype(F32) * im


def image_kernel(count, *refs):
    x_refs, refs = refs[:count], refs[count:]
    near_ref, far_ref, obs_ref, g_ref, im_ref, sum_ref = refs[:6]
    outs, (xs, v_s) = refs[6:10], refs[10:]
    sums = g_ref[...]
    row = lax.broadcasted_iota(jnp.int32, sums.shape, 0)
    for some, im, v in images(x_refs, near_ref, far_ref, obs_ref, im_ref, xs):
        v_s[some, :] = v.astype(BF)
        sums = sums + jnp.where(row == 1, fold(v * im), 0.0)
    sum_ref[...] = sums
    rows = near_ref.shape[0] // 2
    for i, out in enumerate(outs):
        at_ref = far_ref if i > 1 else near_ref
        out[pl.ds(0, rows), :] = dot(at_ref[pl.ds(i % 2 * rows, rows), :], v_s[...])
    outs[3][pl.ds(rows, 8), :] = sums


def image_first(xs, near, far, obs, g_sums):
    half, fine = near.shape
    width = obs.shape[1]
    z_rows = [half // 2] * 3 + [half // 2 + 8]
    return pl.pallas_call(
        functools.partial(image_kernel, len(xs)),
        in_specs=[VMEM] * (len(xs) + 4),
        out_specs=[VMEM] * 6,
        out_shape=[shape((fine, width), F32), shape((8, width), F32)]
        + [shape((r, width), F32) for r in z_rows],
        scratch_shapes=[pltpu.VMEM((width, 2 * half), BF), pltpu.VMEM((fine, width), BF)],
        compiler_params=params(16),
        cost_estimate=cost(8 * half * fine * width, 13e6),
        name="image_first",
    )(*xs, near, far, obs, g_sums)


def second_kernel(count, *refs):
    x_refs, refs = refs[:count], refs[count:]
    near_ref, far_ref, obs_ref, g_ref, im_ref, sum_ref, xs = refs
    sums = g_ref[...]
    row = lax.broadcasted_iota(jnp.int32, sums.shape, 0)
    for _, im, v in images(x_refs, near_ref, far_ref, obs_ref, im_ref, xs):
        sums = sums + jnp.where(row == 1, fold(v * im), 0.0)
    sum_ref[...] = sums


def image_second(xs, near, far, obs, g_sums):
    half, fine = near.shape
    width = obs.shape[1]
    return pl.pallas_call(
        functools.partial(second_kernel, len(xs)),
        in_specs=[VMEM] * (len(xs) + 4),
        out_specs=[VMEM] * 2,
        out_shape=[shape((fine, width), F32), shape((8, width), F32)],
        scratch_shapes=[pltpu.VMEM((width, 2 * half), BF)],
        compiler_params=params(16),
        cost_estimate=cost(4 * half * fine * width, 8e6),
        name="image_second",
    )(*xs, near, far, obs, g_sums)


def result_kernel(count, l0_ref, *refs):
    sums = refs[0][...]
    for r in refs[1:count]:
        sums = sums + r[...]
    g0_ref, g1_ref, i0_ref, i1_ref, control_ref, increment_ref = refs[count:]
    l0 = -l0_ref[0:1, 0:1]
    l1, _ = length_of(sums)
    control_ref[...] = l0 * g0_ref[...] - l1 * g1_ref[...]
    increment_ref[...] = l0 * i0_ref[...] - l1 * i1_ref[...]


def result(l0, sums, g0, g1, im0, im1):
    cuts = 4
    whole = lambda i: (0, 0)
    g_spec = pl.BlockSpec((g0.shape[0], g0.shape[1] // cuts), lambda i: (0, i))
    i_spec = pl.BlockSpec((im0.shape[0] // cuts, im0.shape[1]), lambda i: (i, 0))
    return pl.pallas_call(
        functools.partial(result_kernel, len(sums)),
        grid=(cuts,),
        in_specs=[pl.BlockSpec(l0.shape, whole)]
        + [pl.BlockSpec(r.shape, whole) for r in sums]
        + [g_spec, g_spec, i_spec, i_spec],
        out_specs=[g_spec, i_spec],
        out_shape=[shape(g0.shape, F32), shape(im0.shape, F32)],
        compiler_params=params(24),
        cost_estimate=cost(3 * g0.size, 1e7),
        name="result",
    )(l0, *sums, g0, g1, im0, im1)


def over_core(x):
    return lax.ppermute(x, "space", [(i, i ^ 1) for i in range(GROUP)])


def over_y(x):
    return lax.ppermute(x, "space", [(i, i ^ 2) for i in range(GROUP)])


def over_z(x, k):
    return lax.ppermute(x, "space", [(i, (i + 4 * k) % GROUP) for i in range(GROUP)])


def scatter_sums(parts, sums=None):
    near, far_y, near_c, far_yc = parts
    got_yc = over_core(far_yc)
    got_c = over_core(near_c)
    first, second, *s = merge_y(far_y, got_yc, sums)
    first, second = over_y(first), over_y(second)
    two, one, *s = merge_z(False, near, got_c, first, s[0] if s else None)
    got = [over_z(two, 2), over_z(one, 1)]
    three, own = merge_z(True, near, got_c, second, s[0] if s else None)
    return own, got + [over_z(three, 3)], (s[0] if s else None)


def gather_columns(x, after):
    two, three, one = over_z(x, 2), over_z(x, 3), over_z(x, 1)
    y_own = over_y(x)
    c_own = over_core(x)
    rest = join([two, three, one], after)
    y_rest = over_y(rest)
    c_rest = over_core(rest)
    return [x, rest, y_own, y_rest, c_own, c_rest, over_core(y_own), over_core(y_rest)]


def sum_all(x):
    x = x + over_core(x)
    x = x + over_y(x)
    return [x] + [over_z(x, k) for k in range(1, STEPS)]


def on_device(ensemble, innovation, obs_weight, interp_weight, slot_of, intersection_list):
    members, columns, width = ensemble.shape
    levels = width // VAR
    devices = lax.axis_size("space")
    capacity = intersection_list.shape[2]
    slots = devices * capacity
    grouped = devices == GROUP and capacity == columns == LANES

    taper = vertical_taper(levels)
    both = taper.astype(np.float64) @ taper.T.astype(np.float64)
    kern = np.tile(np.concatenate(host_halves(both), axis=0), (2, VAR))
    tall = np.tile(np.concatenate(host_halves(taper), axis=0), (2, 1))
    none = np.zeros_like(tall)
    taps = np.stack(
        [np.concatenate([tall, none], axis=1), np.concatenate([none, tall], axis=1)]
    )
    kern, taps = jnp.asarray(kern), jnp.asarray(taps)

    index = lax.axis_index("space").astype(jnp.int32)
    me = jnp.stack([index // 4, index // 2 % 2, index % 2, index])
    w = -(obs_weight.astype(F32) * innovation.astype(F32))
    high = lax.reduce_precision(w, 8, 7)
    wh, wl = high.astype(BF), (w - high).astype(BF)
    named = jnp.concatenate([slot_of.astype(F32), interp_weight], axis=0)
    if grouped:
        lists = lax.all_to_all(
            intersection_list, "space", split_axis=1, concat_axis=0, tiled=True
        ).reshape(devices, capacity)
        scatter, gather, add_up = scatter_sums, gather_columns, sum_all
    else:
        lists = intersection_list[0]
        hit = (lists.reshape(-1, 1) == jnp.arange(columns, dtype=jnp.int32)).astype(BF)

        def swap(x):
            x = x.reshape(devices, capacity, width)
            x = lax.all_to_all(x, "space", split_axis=0, concat_axis=0, tiled=True)
            return x.reshape(slots, width)

        def scatter(parts, sums=None):
            got = swap(jnp.concatenate([p[: slots // 4] for p in parts], axis=0))
            high = lax.reduce_precision(got, 8, 7)
            high, low = high.astype(BF), (got - high).astype(BF)
            if sums is not None:
                sums = lax.psum(sums, "space")
            return dot(hit.T, high) + dot(hit.T, low), [], sums

        def gather(x, after):
            return [swap(dot(hit, x.T).astype(BF)).T]

        def add_up(x):
            return [lax.psum(x, "space")]

    ids, weight, far, c0, c1 = adjoint_half(slots, [named, wh, wl], (grouped, me, lists))
    near, n0, n1 = adjoint_half(slots, [ids, weight, wh, wl])
    own, got, _ = scatter([n0, n1, c0, c1])
    x0, y0, g_sums = coarse_image(ensemble, kern, own, got)
    ens = jnp.transpose(ensemble, (1, 0, 2))
    g0, token = project(ens, y0, taps)
    im0, sums, *second = image_first(gather(x0, token), near, far, obs_weight, g_sums)
    own, got, sums = scatter(second, sums)
    x1, y1, l0, g_sums = coarse_image(ensemble, kern, own, got, y0, sums)
    g1, token = project(ens, y1, taps)
    im1, sums = image_second(gather(x1, token), near, far, obs_weight, g_sums)
    return tuple(result(l0, add_up(sums), g0, g1, im0, im1))


def solution(mesh):
    placed = (
        P("case", "space", None),
        P(("case", "space"), None),
        P(("case", "space"), None),
        P("case", "space"),
        P("case", "space"),
        P(("case", "space"), None, None),
    )
    return jax.shard_map(
        on_device,
        mesh=mesh,
        in_specs=placed,
        out_specs=(P("case", "space"), P(("case", "space"), None)),
        check_vma=False,
    )
```

time: 144 us -> 129 us (0.90)
  waiting for transfers between devices: 38.1 us -> 50.9 us
  local copies, waits for them, and re-layouts: 12.4 us -> 2.99 us
  Pallas kernels: 42.1 us -> 34.5 us
  starting transfers between devices: 43 us -> 36.5 us
  between operations: 3.06 us -> 0.89 us
  other arithmetic: 4.96 us -> 3.07 us
    pallas_call x9 -> x12, Pallas kernels: 32.3 us -> 23.4 us  [the longest x2 9.63 us: adjoint_half(): pl.pallas_call(kernel, in_specs=([SMEM] if head else []) + [VMEM] * (len(...]
    unnamed x43 -> x11, local copies, waits for them, and re-layouts: 11.8 us -> 2.99 us
    ppermute x7 -> x9, waiting for transfers between devices: 21.8 us -> 29.5 us  [over_y(): return lax.ppermute(x, 'space', [(i, i ^ 2) for i in range(GROUP)])]
    ppermute x15, starting transfers between devices: 23.2 us -> 18.5 us  [over_z(): lax.ppermute(x, 'space', [(i, (i + 4 * k) % GROUP) for i in range(GROUP)])]
    neg x2 -> x0, other arithmetic: 4.26 us -> none  [on_device(): return (-(l0 * g0 + l1 * g1), -(l0 * im0 + l1 * im1))]
    all_to_all x1, waiting for transfers between devices: 0.01 us -> 3.23 us  [on_device(): lax.all_to_all(intersection_list, 'space', split_axis=1, concat_axis=0, t...]
    convert_element_type x0 -> x2, other arithmetic: none -> 2.25 us  [the longest x1 1.52 us: on_device(): wh, wl = (high.astype(BF), (w - high).astype(BF))]
    ppermute x7 -> x9, starting transfers between devices: 9.38 us -> 8.79 us  [over_y(): return lax.ppermute(x, 'space', [(i, i ^ 2) for i in range(GROUP)])]
  transfers between devices with their start and end apart: 36 -> 38, of which waited for: 18 -> 22; matrix products, arithmetic and copies ran while one was open for 5% -> 5% of each run, Pallas kernels for 19% -> 10%
where the time goes in v3:
time: 129 us
  waiting for transfers between devices  50.9 us (39%)
  starting transfers between devices  36.5 us (28%)
  Pallas kernels  34.5 us (27%)
  other arithmetic  3.07 us (2%)
  local copies, waits for them, and re-layouts  2.99 us (2%)
    ppermute x9, waiting for transfers between devices, over_y(): return lax.ppermute(x, 'space', [(i, i ^ 2) for i in range(GROUP)])  29.5 us
    ppermute x15, starting transfers between devices, over_z(): lax.ppermute(x, 'space', [(i, (i + 4 * k) % GROUP) for i in range(GROUP)])  18.5 us
    ppermute x15, waiting for transfers between devices, over_z(): lax.ppermute(x, 'space', [(i, (i + 4 * k) % GROUP) for i in range(GROUP)])  13.3 us
    pallas_call x2, Pallas kernels, adjoint_half(): pl.pallas_call(kernel, in_specs=([SMEM] if head else []) + [VMEM] * (len(...  9.63 us
    pallas_call x2, Pallas kernels, coarse_image(): pl.pallas_call(functools.partial(coarse_kernel, len(got), second), in_spe...  8.88 us
    ppermute x9, starting transfers between devices, over_y(): return lax.ppermute(x, 'space', [(i, i ^ 2) for i in range(GROUP)])  8.79 us
    all_to_all x1, starting transfers between devices, on_device(): lax.all_to_all(intersection_list, 'space', split_axis=1, concat_axis=0, t...  7.4 us
    pallas_call x2, Pallas kernels, project(): pl.pallas_call(project_kernel, in_specs=[VMEM] * 3, out_specs=[VMEM] * 2,...  7.29 us
  transfers between devices with their start and end apart: 38, of which 22 were waited for; matrix products, arithmetic and copies ran while one was open for 5% of the time, Pallas kernels for 10%

profile of v3, /device:TPU:0, one launch (start us, length us, event | category | flops | bytes accessed | tf_op | source)
XLA Modules:
  0.0 128.8 jit_solution(2981552833254188069)
XLA Ops:
  0.6 7.4 %all-to-all-start = ((s32[1,16,128]{2,0,1:T(1,128)}), s32[1,16,128]{2,0,1:T(1,128)S(1)}, u32[]{:S(2)}, u32[]{:S(2)}) async-start(s32[1,16,128]{2,0,1:T(1,128)} %bitcast.14), calls=%async_computation | async-start | bytes 16384 | tf_op jit(solution)/shard_map/all_to_all | solution.py:574
  9.5 1.5 %fusion = (bf16[1152,256]{1,0:T(8,128)(2,1)S(1)}, bf16[1152,256]{1,0:T(8,128)(2,1)S(1)}) fusion(bf16[1152,256]{1,0:T(8,128)(2,1)} %param.9, bf16[1152,256]{1,0:T(8,128)(2,1)} %refs_10_.3), kind=kLoop, calls=%fused_computation.3 | loop fusion | flops 2359296 | bytes 2359296 | tf_op jit(solution)/shard_map/convert_element_type | solution.py:571
  11.1 3.2 %all-to-all-done = s32[1,16,128]{2,0,1:T(1,128)S(1)} async-done(((s32[1,16,128]{2,0,1:T(1,128)}), s32[1,16,128]{2,0,1:T(1,128)S(1)}, u32[]{:S(2)}, u32[]{:S(2)}) %all-to-all-start) | async-done | bytes 8224 | tf_op jit(solution)/shard_map/all_to_all | solution.py:574
  14.4 5.2 %adjoint_far.1 = (s32[4,1152]{1,0:T(4,128)S(1)}, f32[4,1152]{1,0:T(4,128)S(1)}, bf16[1024,1152]{1,0:T(8,128)(2,1)S(1)}, f32[512,256]{1,0:T(8,128)S(1)}, f32[512,256]{1,0:T(8,128)S(1)}) custom-call(s32[4]{0:T(128)S(1)} %pad_add_fusion.me_ref, s32[16,128]{1,0:T(8,128)S(1)} %bitcast.13, f32[8,1152]{1,0:T(8,128)S(1)} %pad_maximum_fusion.both_ref, ...), custom_call_target="tpu_custom_call" | custom-call | flops 1811939328 | bytes 4000000 | tf_op jit(solution)/shard_map/adjoint_far/pallas_call | solution.py:133
  20.2 4.4 %adjoint_near.1 = (bf16[1024,1152]{1,0:T(8,128)(2,1)S(1)}, f32[512,256]{1,0:T(8,128)S(1)}, f32[512,256]{1,0:T(8,128)S(1)}) custom-call(s32[4,1152]{1,0:T(4,128)S(1)} %get-tuple-element.43.ids_ref, f32[4,1152]{1,0:T(4,128)S(1)} %get-tuple-element.44.weight_ref, bf16[1152,256]{1,0:T(8,128)(2,1)S(1)} %get-tuple-element.85.wh_ref, ...), custom_call_target="tpu_custom_call" | custom-call | flops 1811939328 | bytes 4000000 | tf_op jit(solution)/shard_map/adjoint_near/pallas_call | solution.py:133
  25.3 1.5 %collective-permute-start.3 = (s16[272,256]{1,0:T(8,128)(2,1)S(1)}, s16[272,256]{1,0:T(8,128)(2,1)S(1)}, u32[]{:S(2)}, u32[]{:S(2)}) collective-permute-start(s16[272,256]{1,0:T(8,128)(2,1)S(1)} %get-tuple-element.51), channel_id=1, source_target_pairs={{0,2},{1,3},{2,0},{3,1},{4,6},{5,7},{6,4},{7,5},{8,10},{9,11},{10,... | collective-permute-start | bytes 417800 | tf_op jit(solution)/shard_map/ppermute | solution.py:514
  26.8 4.5 %collective-permute-done.2.p_ref = s16[272,256]{1,0:T(8,128)(2,1)S(1)} collective-permute-done((s16[272,256]{1,0:T(8,128)(2,1)S(1)}, s16[272,256]{1,0:T(8,128)(2,1)S(1)}, u32[]{:S(2)}, u32[]{:S(2)}) %collective-permute-start.2) | collective-permute-done | bytes 139296 | tf_op jit(solution)/shard_map/ppermute | solution.py:514
  34.7 3.0 %copy.14 = bf16[80,128,256]{2,0,1:T(8,128)(2,1)S(1)} copy(bf16[80,128,256]{2,1,0:T(8,128)(2,1)S(1)} %bitcast.10) | data formatting | bytes 10485760 | tf_op args[0]
  37.7 3.3 %collective-permute-done.4.refs_0_ = s16[144,256]{1,0:T(8,128)(2,1)S(1)} collective-permute-done((s16[144,256]{1,0:T(8,128)(2,1)S(1)}, s16[144,256]{1,0:T(8,128)(2,1)S(1)}, u32[]{:S(2)}, u32[]{:S(2)}) %collective-permute-start.4) | collective-permute-done | bytes 73760 | tf_op jit(solution)/shard_map/ppermute | solution.py:518
  41.0 4.3 %coarse_first.1 = (bf16[256,128]{1,0:T(8,128)(2,1)S(1)}, f32[128,256]{1,0:T(8,128)S(1)}, f32[8,256]{1,0:T(8,128)S(1)}) custom-call(bf16[80,128,256]{2,1,0:T(8,128)(2,1)S(1)} %bitcast.10, bf16[256,256]{1,0:T(8,128)(2,1)S(1)} %copy-done.2, f32[128,256]{1,0:T(8,128)S(1)} %get-tuple-element.50.own_ref, s16[144,256]{1,0:T(8,128)(2,1)S(1)} %collective-permute-done.4.refs_0_, ...), custom_call_target="tpu_custom_call" | custom-call | flops 1342177280 | bytes 5000000 | tf_op jit(solution)/shard_map/coarse_first/pallas_call | solution.py:344
  45.4 3.8 %collective-permute-start.8 = (bf16[256,128]{1,0:T(8,128)(2,1)S(1)}, bf16[256,128]{1,0:T(8,128)(2,1)S(1)}, u32[]{:S(2)}, u32[]{:S(2)}) collective-permute-start(bf16[256,128]{1,0:T(8,128)(2,1)S(1)} %get-tuple-element.55.refs_0_), channel_id=1, source_target_pairs={{0,12},{1,13},{2,14},{3,15},{4,0},{5,1},{6,2},{7,3},{8,4},{9,5},{1... | collective-permute-start | bytes 196616 | tf_op jit(solution)/shard_map/ppermute | solution.py:518
  49.2 3.6 %project.2 = (f32[80,8192]{1,0:T(8,128)S(1)}, f32[8,128]{1,0:T(8,128)S(1)}) custom-call(bf16[128,80,256]{2,1,0:T(8,128)(2,1)S(1)} %bitcast.11, f32[128,256]{1,0:T(8,128)S(1)} %get-tuple-element.56.y_ref.refs_3_, bf16[2,256,128]{2,1,0:T(8,128)(2,1)S(1)} %copy-done.1), custom_call_target="tpu_custom_call" | custom-call | flops 1342177280 | bytes 8000000 | tf_op jit(solution)/shard_map/project/pallas_call | solution.py:381
  52.9 1.5 %collective-permute-done.7.a_ref = bf16[256,128]{1,0:T(8,128)(2,1)S(1)} collective-permute-done((bf16[256,128]{1,0:T(8,128)(2,1)S(1)}, bf16[256,128]{1,0:T(8,128)(2,1)S(1)}, u32[]{:S(2)}, u32[]{:S(2)}) %collective-permute-start.7) | collective-permute-done | bytes 65568 | tf_op jit(solution)/shard_map/ppermute | solution.py:518
  55.3 4.9 %collective-permute-done.11.refs_3_ = bf16[3,256,128]{2,1,0:T(8,128)(2,1)S(1)} collective-permute-done((bf16[3,256,128]{2,1,0:T(8,128)(2,1)S(1)}, bf16[3,256,128]{2,1,0:T(8,128)(2,1)S(1)}, u32[]{:S(2)}, u32[]{:S(2)}) %collective-permute-start.11) | collective-permute-done | bytes 196640 | tf_op jit(solution)/shard_map/ppermute | solution.py:514
  61.8 2.9 %collective-permute-done.10.refs_2_ = bf16[256,128]{1,0:T(8,128)(2,1)S(1)} collective-permute-done((bf16[256,128]{1,0:T(8,128)(2,1)S(1)}, bf16[256,128]{1,0:T(8,128)(2,1)S(1)}, u32[]{:S(2)}, u32[]{:S(2)}) %collective-permute-start.10) | collective-permute-done | bytes 65568 | tf_op jit(solution)/shard_map/ppermute | solution.py:514
  65.9 3.2 %image_first.1 = (f32[1152,256]{1,0:T(8,128)S(1)}, f32[8,256]{1,0:T(8,128)S(1)}, f32[512,256]{1,0:T(8,128)S(1)}, f32[512,256]{1,0:T(8,128)S(1)}, f32[512,256]{1,0:T(8,128)S(1)}, /*index=5*/f32[520,256]{1,0:T(8,128)S(1)}) custom-call(bf16[256,128]{1,0:T(8,128)(2,1)S(1)} %get-tuple-element.55.refs_0_, bf16[3,256,128]{2,1,0:T(8,128)(2,1)S(1)} %join.2.refs_1_, ...), custom_call_target="tpu_custom_call" | custom-call | flops 2415919104 | bytes 13000000 | tf_op jit(solution)/shard_map/image_first/pallas_call | solution.py:441
  69.7 1.4 %collective-permute-done.17.refs_1_ = f32[520,256]{1,0:T(8,128)S(1)} collective-permute-done((f32[520,256]{1,0:T(8,128)S(1)}, f32[520,256]{1,0:T(8,128)S(1)}, u32[]{:S(2)}, u32[]{:S(2)}) %collective-permute-start.17) | collective-permute-done | bytes 532512 | tf_op jit(solution)/shard_map/ppermute | solution.py:510
  71.2 1.4 %collective-permute-start.19 = (s16[272,256]{1,0:T(8,128)(2,1)S(1)}, s16[272,256]{1,0:T(8,128)(2,1)S(1)}, u32[]{:S(2)}, u32[]{:S(2)}) collective-permute-start(s16[272,256]{1,0:T(8,128)(2,1)S(1)} %get-tuple-element.67), channel_id=1, source_target_pairs={{0,2},{1,3},{2,0},{3,1},{4,6},{5,7},{6,4},{7,5},{8,10},{9,11},{10,... | collective-permute-start | bytes 417800 | tf_op jit(solution)/shard_map/ppermute | solution.py:514
  73.3 4.5 %collective-permute-done.19.p_ref = s16[272,256]{1,0:T(8,128)(2,1)S(1)} collective-permute-done((s16[272,256]{1,0:T(8,128)(2,1)S(1)}, s16[272,256]{1,0:T(8,128)(2,1)S(1)}, u32[]{:S(2)}, u32[]{:S(2)}) %collective-permute-start.19) | collective-permute-done | bytes 139296 | tf_op jit(solution)/shard_map/ppermute | solution.py:514
  77.9 1.5 %collective-permute-start.20 = (s16[144,256]{1,0:T(8,128)(2,1)S(1)}, s16[144,256]{1,0:T(8,128)(2,1)S(1)}, u32[]{:S(2)}, u32[]{:S(2)}) collective-permute-start(s16[144,256]{1,0:T(8,128)(2,1)S(1)} %get-tuple-element.71), channel_id=1, source_target_pairs={{0,8},{1,9},{2,10},{3,11},{4,12},{5,13},{6,14},{7,15},{8,0},{9,1},... | collective-permute-start | bytes 221192 | tf_op jit(solution)/shard_map/ppermute | solution.py:518
  80.8 2.7 %collective-permute-start.22 = (s16[144,256]{1,0:T(8,128)(2,1)S(1)}, s16[144,256]{1,0:T(8,128)(2,1)S(1)}, u32[]{:S(2)}, u32[]{:S(2)}) collective-permute-start(s16[144,256]{1,0:T(8,128)(2,1)S(1)} %get-tuple-element.73), channel_id=1, source_target_pairs={{0,12},{1,13},{2,14},{3,15},{4,0},{5,1},{6,2},{7,3},{8,4},{9,5},{1... | collective-permute-start | bytes 221192 | tf_op jit(solution)/shard_map/ppermute | solution.py:518
  83.4 1.4 %collective-permute-done.20.refs_0_ = s16[144,256]{1,0:T(8,128)(2,1)S(1)} collective-permute-done((s16[144,256]{1,0:T(8,128)(2,1)S(1)}, s16[144,256]{1,0:T(8,128)(2,1)S(1)}, u32[]{:S(2)}, u32[]{:S(2)}) %collective-permute-start.20) | collective-permute-done | bytes 73760 | tf_op jit(solution)/shard_map/ppermute | solution.py:518
  86.2 4.5 %coarse_second.1 = (bf16[256,128]{1,0:T(8,128)(2,1)S(1)}, f32[128,256]{1,0:T(8,128)S(1)}, f32[8,128]{1,0:T(8,128)S(1)}, f32[8,256]{1,0:T(8,128)S(1)}) custom-call(bf16[80,128,256]{2,1,0:T(8,128)(2,1)S(1)} %bitcast.10, bf16[256,256]{1,0:T(8,128)(2,1)S(1)} %copy-done.2, f32[128,256]{1,0:T(8,128)S(1)} %get-tuple-element.70.own_ref, ...), custom_call_target="tpu_custom_call" | custom-call | flops 1342177280 | bytes 5000000 | tf_op jit(solution)/shard_map/coarse_second/pallas_call | solution.py:344
  91.6 3.0 %collective-permute-start.24 = (bf16[256,128]{1,0:T(8,128)(2,1)S(1)}, bf16[256,128]{1,0:T(8,128)(2,1)S(1)}, u32[]{:S(2)}, u32[]{:S(2)}) collective-permute-start(bf16[256,128]{1,0:T(8,128)(2,1)S(1)} %get-tuple-element.75.refs_0_), channel_id=1, source_target_pairs={{0,12},{1,13},{2,14},{3,15},{4,0},{5,1},{6,2},{7,3},{8,4},{9,5},{1... | collective-permute-start | bytes 196616 | tf_op jit(solution)/shard_map/ppermute | solution.py:518
  94.8 3.7 %project.3 = (f32[80,8192]{1,0:T(8,128)S(1)}, f32[8,128]{1,0:T(8,128)S(1)}) custom-call(bf16[128,80,256]{2,1,0:T(8,128)(2,1)S(1)} %bitcast.12, f32[128,256]{1,0:T(8,128)S(1)} %get-tuple-element.76.y_ref, bf16[2,256,128]{2,1,0:T(8,128)(2,1)S(1)} %copy-done.1), custom_call_target="tpu_custom_call" | custom-call | flops 1342177280 | bytes 8000000 | tf_op jit(solution)/shard_map/project/pallas_call | solution.py:381
  100.7 4.9 %collective-permute-done.27.refs_3_ = bf16[3,256,128]{2,1,0:T(8,128)(2,1)S(1)} collective-permute-done((bf16[3,256,128]{2,1,0:T(8,128)(2,1)S(1)}, bf16[3,256,128]{2,1,0:T(8,128)(2,1)S(1)}, u32[]{:S(2)}, u32[]{:S(2)}) %collective-permute-start.27) | collective-permute-done | bytes 196640 | tf_op jit(solution)/shard_map/ppermute | solution.py:514
  106.6 3.5 %collective-permute-done.26.refs_2_ = bf16[256,128]{1,0:T(8,128)(2,1)S(1)} collective-permute-done((bf16[256,128]{1,0:T(8,128)(2,1)S(1)}, bf16[256,128]{1,0:T(8,128)(2,1)S(1)}, u32[]{:S(2)}, u32[]{:S(2)}) %collective-permute-start.26) | collective-permute-done | bytes 65568 | tf_op jit(solution)/shard_map/ppermute | solution.py:514
  111.4 1.9 %image_second.1 = (f32[1152,256]{1,0:T(8,128)S(1)}, f32[8,256]{1,0:T(8,128)S(1)}) custom-call(bf16[256,128]{1,0:T(8,128)(2,1)S(1)} %get-tuple-element.75.refs_0_, bf16[3,256,128]{2,1,0:T(8,128)(2,1)S(1)} %join.3.refs_1_, bf16[256,128]{1,0:T(8,128)(2,1)S(1)} %collective-permute-done.26.refs_2_, bf16[3,256,128]{2,1,0:T(8,128)(2,1)S(1)} %collective-permute-done.27.refs_3_, ...), custom_call_target="tpu_custom_call" | custom-call | flops 1207959552 | bytes 8000000 | tf_op jit(solution)/shard_map/image_second/pallas_call | solution.py:467
  115.3 2.9 %collective-permute-done.33 = f32[8,256]{1,0:T(8,128)S(1)} collective-permute-done((f32[8,256]{1,0:T(8,128)S(1)}, f32[8,256]{1,0:T(8,128)S(1)}, u32[]{:S(2)}, u32[]{:S(2)}) %collective-permute-start.33) | collective-permute-done | bytes 8224 | tf_op jit(solution)/shard_map/ppermute | solution.py:514
  118.2 2.3 %collective-permute-start.36 = (f32[8,256]{1,0:T(8,128)S(1)}, f32[8,256]{1,0:T(8,128)S(1)}, u32[]{:S(2)}, u32[]{:S(2)}) collective-permute-start(f32[8,256]{1,0:T(8,128)S(1)} %add.18.refs_0_), channel_id=1, source_target_pairs={{0,12},{1,13},{2,14},{3,15},{4,0},{5,1},{6,2},{7,3},{8,4},{9,5},{1... | collective-permute-start | bytes 24584 | tf_op jit(solution)/shard_map/ppermute | solution.py:518
  121.9 3.2 %collective-permute-done.35.refs_2_ = f32[8,256]{1,0:T(8,128)S(1)} collective-permute-done((f32[8,256]{1,0:T(8,128)S(1)}, f32[8,256]{1,0:T(8,128)S(1)}, u32[]{:S(2)}, u32[]{:S(2)}) %collective-permute-start.35) | collective-permute-done | bytes 8224 | tf_op jit(solution)/shard_map/ppermute | solution.py:518
  125.9 2.9 %result.1 = (f32[80,8192]{1,0:T(8,128)}, f32[1152,256]{1,0:T(8,128)}) custom-call(f32[8,128]{1,0:T(8,128)S(1)} %get-tuple-element.74.l0_ref, f32[8,256]{1,0:T(8,128)S(1)} %add.18.refs_0_, f32[8,256]{1,0:T(8,128)S(1)} %collective-permute-done.34.refs_1_, f32[8,256]{1,0:T(8,128)S(1)} %collective-permute-done.35.refs_2_, ...), custom_call_target="tpu_custom_call" | custom-call | flops 1966080 | bytes 10000000 | tf_op jit(solution)/shard_map/result/pallas_call | solution.py:495
  (79 shorter events, 23.9 us)
Async XLA Ops:
  0.6 13.7 %all-to-all-start = ((s32[1,16,128]{2,0,1:T(1,128)}), s32[1,16,128]{2,0,1:T(1,128)S(1)}, u32[]{:S(2)}, u32[]{:S(2)}) async-start(s32[1,16,128]{2,0,1:T(1,128)} %bitcast.14), calls=%async_computation | async-start | bytes 16384 | tf_op jit(solution)/shard_map/all_to_all | solution.py:574
  19.6 5.0 %collective-permute-start.1 = (f32[512,256]{1,0:T(8,128)S(1)}, f32[512,256]{1,0:T(8,128)S(1)}, u32[]{:S(2)}, u32[]{:S(2)}) collective-permute-start(f32[512,256]{1,0:T(8,128)S(1)} %get-tuple-element.48), channel_id=1, source_target_pairs={{0,1},{1,0},{2,3},{3,2},{4,5},{5,4},{6,7},{7,6},{8,9},{9,8},{10,11... | collective-permute-start | bytes 1572872 | tf_op jit(solution)/shard_map/ppermute | solution.py:510
  19.7 7.1 %collective-permute-start = (f32[512,256]{1,0:T(8,128)S(1)}, f32[512,256]{1,0:T(8,128)S(1)}, u32[]{:S(2)}, u32[]{:S(2)}) collective-permute-start(f32[512,256]{1,0:T(8,128)S(1)} %get-tuple-element.46), channel_id=1, source_target_pairs={{0,1},{1,0},{2,3},{3,2},{4,5},{5,4},{6,7},{7,6},{8,9},{9,8},{10,11... | collective-permute-start | bytes 1572872 | tf_op jit(solution)/shard_map/ppermute | solution.py:510
  24.7 6.6 %collective-permute-start.2 = (s16[272,256]{1,0:T(8,128)(2,1)S(1)}, s16[272,256]{1,0:T(8,128)(2,1)S(1)}, u32[]{:S(2)}, u32[]{:S(2)}) collective-permute-start(s16[272,256]{1,0:T(8,128)(2,1)S(1)} %get-tuple-element.49), channel_id=1, source_target_pairs={{0,2},{1,3},{2,0},{3,1},{4,6},{5,7},{6,4},{7,5},{8,10},{9,11},{10,... | collective-permute-start | bytes 417800 | tf_op jit(solution)/shard_map/ppermute | solution.py:514
  25.3 8.1 %collective-permute-start.3 = (s16[272,256]{1,0:T(8,128)(2,1)S(1)}, s16[272,256]{1,0:T(8,128)(2,1)S(1)}, u32[]{:S(2)}, u32[]{:S(2)}) collective-permute-start(s16[272,256]{1,0:T(8,128)(2,1)S(1)} %get-tuple-element.51), channel_id=1, source_target_pairs={{0,2},{1,3},{2,0},{3,1},{4,6},{5,7},{6,4},{7,5},{8,10},{9,11},{10,... | collective-permute-start | bytes 417800 | tf_op jit(solution)/shard_map/ppermute | solution.py:514
  31.4 6.3 %collective-permute-start.6 = (s16[144,256]{1,0:T(8,128)(2,1)S(1)}, s16[144,256]{1,0:T(8,128)(2,1)S(1)}, u32[]{:S(2)}, u32[]{:S(2)}) collective-permute-start(s16[144,256]{1,0:T(8,128)(2,1)S(1)} %get-tuple-element.54), channel_id=1, source_target_pairs={{0,12},{1,13},{2,14},{3,15},{4,0},{5,1},{6,2},{7,3},{8,4},{9,5},{1... | collective-permute-start | bytes 221192 | tf_op jit(solution)/shard_map/ppermute | solution.py:518
  33.5 7.5 %collective-permute-start.4 = (s16[144,256]{1,0:T(8,128)(2,1)S(1)}, s16[144,256]{1,0:T(8,128)(2,1)S(1)}, u32[]{:S(2)}, u32[]{:S(2)}) collective-permute-start(s16[144,256]{1,0:T(8,128)(2,1)S(1)} %get-tuple-element.52), channel_id=1, source_target_pairs={{0,8},{1,9},{2,10},{3,11},{4,12},{5,13},{6,14},{7,15},{8,0},{9,1},... | collective-permute-start | bytes 221192 | tf_op jit(solution)/shard_map/ppermute | solution.py:518
  34.1 6.9 %collective-permute-start.5 = (s16[144,256]{1,0:T(8,128)(2,1)S(1)}, s16[144,256]{1,0:T(8,128)(2,1)S(1)}, u32[]{:S(2)}, u32[]{:S(2)}) collective-permute-start(s16[144,256]{1,0:T(8,128)(2,1)S(1)} %get-tuple-element.53), channel_id=1, source_target_pairs={{0,4},{1,5},{2,6},{3,7},{4,8},{5,9},{6,10},{7,11},{8,12},{9,13},{1... | collective-permute-start | bytes 221192 | tf_op jit(solution)/shard_map/ppermute | solution.py:518
  45.4 7.5 %collective-permute-start.9 = (bf16[256,128]{1,0:T(8,128)(2,1)S(1)}, bf16[256,128]{1,0:T(8,128)(2,1)S(1)}, u32[]{:S(2)}, u32[]{:S(2)}) collective-permute-start(bf16[256,128]{1,0:T(8,128)(2,1)S(1)} %get-tuple-element.55.refs_0_), channel_id=1, source_target_pairs={{0,4},{1,5},{2,6},{3,7},{4,8},{5,9},{6,10},{7,11},{8,12},{9,13},{1... | collective-permute-start | bytes 196616 | tf_op jit(solution)/shard_map/ppermute | solution.py:518
  45.4 7.5 %collective-permute-start.8 = (bf16[256,128]{1,0:T(8,128)(2,1)S(1)}, bf16[256,128]{1,0:T(8,128)(2,1)S(1)}, u32[]{:S(2)}, u32[]{:S(2)}) collective-permute-start(bf16[256,128]{1,0:T(8,128)(2,1)S(1)} %get-tuple-element.55.refs_0_), channel_id=1, source_target_pairs={{0,12},{1,13},{2,14},{3,15},{4,0},{5,1},{6,2},{7,3},{8,4},{9,5},{1... | collective-permute-start | bytes 196616 | tf_op jit(solution)/shard_map/ppermute | solution.py:518
  49.2 5.2 %collective-permute-start.7 = (bf16[256,128]{1,0:T(8,128)(2,1)S(1)}, bf16[256,128]{1,0:T(8,128)(2,1)S(1)}, u32[]{:S(2)}, u32[]{:S(2)}) collective-permute-start(bf16[256,128]{1,0:T(8,128)(2,1)S(1)} %get-tuple-element.55.refs_0_), channel_id=1, source_target_pairs={{0,8},{1,9},{2,10},{3,11},{4,12},{5,13},{6,14},{7,15},{8,0},{9,1},... | collective-permute-start | bytes 196616 | tf_op jit(solution)/shard_map/ppermute | solution.py:518
  54.4 5.7 %collective-permute-start.11 = (bf16[3,256,128]{2,1,0:T(8,128)(2,1)S(1)}, bf16[3,256,128]{2,1,0:T(8,128)(2,1)S(1)}, u32[]{:S(2)}, u32[]{:S(2)}) collective-permute-start(bf16[3,256,128]{2,1,0:T(8,128)(2,1)S(1)} %join.2.refs_1_), channel_id=1, source_target_pairs={{0,2},{1,3},{2,0},{3,1},{4,6},{5,7},{6,4},{7,5},{8,10},{9,11},{10,... | collective-permute-start | bytes 589832 | tf_op jit(solution)/shard_map/ppermute | solution.py:514
  55.3 10.7 %collective-permute-start.13 = (bf16[3,256,128]{2,1,0:T(8,128)(2,1)S(1)}, bf16[3,256,128]{2,1,0:T(8,128)(2,1)S(1)}, u32[]{:S(2)}, u32[]{:S(2)}) collective-permute-start(bf16[3,256,128]{2,1,0:T(8,128)(2,1)S(1)} %join.2.refs_1_), channel_id=1, source_target_pairs={{0,1},{1,0},{2,3},{3,2},{4,5},{5,4},{6,7},{7,6},{8,9},{9,8},{10,11... | collective-permute-start | bytes 589832 | tf_op jit(solution)/shard_map/ppermute | solution.py:510
  60.2 5.8 %collective-permute-start.15 = (bf16[3,256,128]{2,1,0:T(8,128)(2,1)S(1)}, bf16[3,256,128]{2,1,0:T(8,128)(2,1)S(1)}, u32[]{:S(2)}, u32[]{:S(2)}) collective-permute-start(bf16[3,256,128]{2,1,0:T(8,128)(2,1)S(1)} %collective-permute-done.11.refs_3_), channel_id=1, source_target_pairs={{0,1},{1,0},{2,3},{3,2},{4,5},{5,4},{6,7},{7,6},{8,9},{9,8},{10,11... | collective-permute-start | bytes 589832 | tf_op jit(solution)/shard_map/ppermute | solution.py:510
  60.2 4.5 %collective-permute-start.10 = (bf16[256,128]{1,0:T(8,128)(2,1)S(1)}, bf16[256,128]{1,0:T(8,128)(2,1)S(1)}, u32[]{:S(2)}, u32[]{:S(2)}) collective-permute-start(bf16[256,128]{1,0:T(8,128)(2,1)S(1)} %get-tuple-element.55.refs_0_), channel_id=1, source_target_pairs={{0,2},{1,3},{2,0},{3,1},{4,6},{5,7},{6,4},{7,5},{8,10},{9,11},{10,... | collective-permute-start | bytes 196616 | tf_op jit(solution)/shard_map/ppermute | solution.py:514
  69.3 4.0 %collective-permute-start.16 = (f32[512,256]{1,0:T(8,128)S(1)}, f32[512,256]{1,0:T(8,128)S(1)}, u32[]{:S(2)}, u32[]{:S(2)}) collective-permute-start(f32[512,256]{1,0:T(8,128)S(1)} %get-tuple-element.62), channel_id=1, source_target_pairs={{0,1},{1,0},{2,3},{3,2},{4,5},{5,4},{6,7},{7,6},{8,9},{9,8},{10,11... | collective-permute-start | bytes 1572872 | tf_op jit(solution)/shard_map/ppermute | solution.py:510
  71.2 6.6 %collective-permute-start.19 = (s16[272,256]{1,0:T(8,128)(2,1)S(1)}, s16[272,256]{1,0:T(8,128)(2,1)S(1)}, u32[]{:S(2)}, u32[]{:S(2)}) collective-permute-start(s16[272,256]{1,0:T(8,128)(2,1)S(1)} %get-tuple-element.67), channel_id=1, source_target_pairs={{0,2},{1,3},{2,0},{3,1},{4,6},{5,7},{6,4},{7,5},{8,10},{9,11},{10,... | collective-permute-start | bytes 417800 | tf_op jit(solution)/shard_map/ppermute | solution.py:514
  72.7 8.0 %collective-permute-start.18 = (s16[272,256]{1,0:T(8,128)(2,1)S(1)}, s16[272,256]{1,0:T(8,128)(2,1)S(1)}, u32[]{:S(2)}, u32[]{:S(2)}) collective-permute-start(s16[272,256]{1,0:T(8,128)(2,1)S(1)} %get-tuple-element.66), channel_id=1, source_target_pairs={{0,2},{1,3},{2,0},{3,1},{4,6},{5,7},{6,4},{7,5},{8,10},{9,11},{10,... | collective-permute-start | bytes 417800 | tf_op jit(solution)/shard_map/ppermute | solution.py:514
  77.9 6.9 %collective-permute-start.20 = (s16[144,256]{1,0:T(8,128)(2,1)S(1)}, s16[144,256]{1,0:T(8,128)(2,1)S(1)}, u32[]{:S(2)}, u32[]{:S(2)}) collective-permute-start(s16[144,256]{1,0:T(8,128)(2,1)S(1)} %get-tuple-element.71), channel_id=1, source_target_pairs={{0,8},{1,9},{2,10},{3,11},{4,12},{5,13},{6,14},{7,15},{8,0},{9,1},... | collective-permute-start | bytes 221192 | tf_op jit(solution)/shard_map/ppermute | solution.py:518
  79.5 6.3 %collective-permute-start.21 = (s16[144,256]{1,0:T(8,128)(2,1)S(1)}, s16[144,256]{1,0:T(8,128)(2,1)S(1)}, u32[]{:S(2)}, u32[]{:S(2)}) collective-permute-start(s16[144,256]{1,0:T(8,128)(2,1)S(1)} %get-tuple-element.72), channel_id=1, source_target_pairs={{0,4},{1,5},{2,6},{3,7},{4,8},{5,9},{6,10},{7,11},{8,12},{9,13},{1... | collective-permute-start | bytes 221192 | tf_op jit(solution)/shard_map/ppermute | solution.py:518
  80.8 5.5 %collective-permute-start.22 = (s16[144,256]{1,0:T(8,128)(2,1)S(1)}, s16[144,256]{1,0:T(8,128)(2,1)S(1)}, u32[]{:S(2)}, u32[]{:S(2)}) collective-permute-start(s16[144,256]{1,0:T(8,128)(2,1)S(1)} %get-tuple-element.73), channel_id=1, source_target_pairs={{0,12},{1,13},{2,14},{3,15},{4,0},{5,1},{6,2},{7,3},{8,4},{9,5},{1... | collective-permute-start | bytes 221192 | tf_op jit(solution)/shard_map/ppermute | solution.py:518
  90.8 7.7 %collective-permute-start.25 = (bf16[256,128]{1,0:T(8,128)(2,1)S(1)}, bf16[256,128]{1,0:T(8,128)(2,1)S(1)}, u32[]{:S(2)}, u32[]{:S(2)}) collective-permute-start(bf16[256,128]{1,0:T(8,128)(2,1)S(1)} %get-tuple-element.75.refs_0_), channel_id=1, source_target_pairs={{0,4},{1,5},{2,6},{3,7},{4,8},{5,9},{6,10},{7,11},{8,12},{9,13},{1... | collective-permute-start | bytes 196616 | tf_op jit(solution)/shard_map/ppermute | solution.py:518
  91.6 6.8 %collective-permute-start.24 = (bf16[256,128]{1,0:T(8,128)(2,1)S(1)}, bf16[256,128]{1,0:T(8,128)(2,1)S(1)}, u32[]{:S(2)}, u32[]{:S(2)}) collective-permute-start(bf16[256,128]{1,0:T(8,128)(2,1)S(1)} %get-tuple-element.75.refs_0_), channel_id=1, source_target_pairs={{0,12},{1,13},{2,14},{3,15},{4,0},{5,1},{6,2},{7,3},{8,4},{9,5},{1... | collective-permute-start | bytes 196616 | tf_op jit(solution)/shard_map/ppermute | solution.py:518
  94.7 5.2 %collective-permute-start.23 = (bf16[256,128]{1,0:T(8,128)(2,1)S(1)}, bf16[256,128]{1,0:T(8,128)(2,1)S(1)}, u32[]{:S(2)}, u32[]{:S(2)}) collective-permute-start(bf16[256,128]{1,0:T(8,128)(2,1)S(1)} %get-tuple-element.75.refs_0_), channel_id=1, source_target_pairs={{0,8},{1,9},{2,10},{3,11},{4,12},{5,13},{6,14},{7,15},{8,0},{9,1},... | collective-permute-start | bytes 196616 | tf_op jit(solution)/shard_map/ppermute | solution.py:518
  99.9 5.7 %collective-permute-start.27 = (bf16[3,256,128]{2,1,0:T(8,128)(2,1)S(1)}, bf16[3,256,128]{2,1,0:T(8,128)(2,1)S(1)}, u32[]{:S(2)}, u32[]{:S(2)}) collective-permute-start(bf16[3,256,128]{2,1,0:T(8,128)(2,1)S(1)} %join.3.refs_1_), channel_id=1, source_target_pairs={{0,2},{1,3},{2,0},{3,1},{4,6},{5,7},{6,4},{7,5},{8,10},{9,11},{10,... | collective-permute-start | bytes 589832 | tf_op jit(solution)/shard_map/ppermute | solution.py:514
  100.7 10.7 %collective-permute-start.29 = (bf16[3,256,128]{2,1,0:T(8,128)(2,1)S(1)}, bf16[3,256,128]{2,1,0:T(8,128)(2,1)S(1)}, u32[]{:S(2)}, u32[]{:S(2)}) collective-permute-start(bf16[3,256,128]{2,1,0:T(8,128)(2,1)S(1)} %join.3.refs_1_), channel_id=1, source_target_pairs={{0,1},{1,0},{2,3},{3,2},{4,5},{5,4},{6,7},{7,6},{8,9},{9,8},{10,11... | collective-permute-start | bytes 589832 | tf_op jit(solution)/shard_map/ppermute | solution.py:510
  105.6 5.8 %collective-permute-start.31 = (bf16[3,256,128]{2,1,0:T(8,128)(2,1)S(1)}, bf16[3,256,128]{2,1,0:T(8,128)(2,1)S(1)}, u32[]{:S(2)}, u32[]{:S(2)}) collective-permute-start(bf16[3,256,128]{2,1,0:T(8,128)(2,1)S(1)} %collective-permute-done.27.refs_3_), channel_id=1, source_target_pairs={{0,1},{1,0},{2,3},{3,2},{4,5},{5,4},{6,7},{7,6},{8,9},{9,8},{10,11... | collective-permute-start | bytes 589832 | tf_op jit(solution)/shard_map/ppermute | solution.py:510
  105.6 4.5 %collective-permute-start.26 = (bf16[256,128]{1,0:T(8,128)(2,1)S(1)}, bf16[256,128]{1,0:T(8,128)(2,1)S(1)}, u32[]{:S(2)}, u32[]{:S(2)}) collective-permute-start(bf16[256,128]{1,0:T(8,128)(2,1)S(1)} %get-tuple-element.75.refs_0_), channel_id=1, source_target_pairs={{0,2},{1,3},{2,0},{3,1},{4,6},{5,7},{6,4},{7,5},{8,10},{9,11},{10,... | collective-permute-start | bytes 196616 | tf_op jit(solution)/shard_map/ppermute | solution.py:514
  106.4 3.7 %collective-permute-start.28 = (bf16[256,128]{1,0:T(8,128)(2,1)S(1)}, bf16[256,128]{1,0:T(8,128)(2,1)S(1)}, u32[]{:S(2)}, u32[]{:S(2)}) collective-permute-start(bf16[256,128]{1,0:T(8,128)(2,1)S(1)} %get-tuple-element.75.refs_0_), channel_id=1, source_target_pairs={{0,1},{1,0},{2,3},{3,2},{4,5},{5,4},{6,7},{7,6},{8,9},{9,8},{10,11... | collective-permute-start | bytes 196616 | tf_op jit(solution)/shard_map/ppermute | solution.py:510
  114.6 3.7 %collective-permute-start.33 = (f32[8,256]{1,0:T(8,128)S(1)}, f32[8,256]{1,0:T(8,128)S(1)}, u32[]{:S(2)}, u32[]{:S(2)}) collective-permute-start(f32[8,256]{1,0:T(8,128)S(1)} %add.17), channel_id=1, source_target_pairs={{0,2},{1,3},{2,0},{3,1},{4,6},{5,7},{6,4},{7,5},{8,10},{9,11},{10,... | collective-permute-start | bytes 24584 | tf_op jit(solution)/shard_map/ppermute | solution.py:514
  120.5 4.5 %collective-permute-start.35 = (f32[8,256]{1,0:T(8,128)S(1)}, f32[8,256]{1,0:T(8,128)S(1)}, u32[]{:S(2)}, u32[]{:S(2)}) collective-permute-start(f32[8,256]{1,0:T(8,128)S(1)} %add.18.refs_0_), channel_id=1, source_target_pairs={{0,8},{1,9},{2,10},{3,11},{4,12},{5,13},{6,14},{7,15},{8,0},{9,1},... | collective-permute-start | bytes 24584 | tf_op jit(solution)/shard_map/ppermute | solution.py:518
  120.5 5.4 %collective-permute-start.34 = (f32[8,256]{1,0:T(8,128)S(1)}, f32[8,256]{1,0:T(8,128)S(1)}, u32[]{:S(2)}, u32[]{:S(2)}) collective-permute-start(f32[8,256]{1,0:T(8,128)S(1)} %add.18.refs_0_), channel_id=1, source_target_pairs={{0,4},{1,5},{2,6},{3,7},{4,8},{5,9},{6,10},{7,11},{8,12},{9,13},{1... | collective-permute-start | bytes 24584 | tf_op jit(solution)/shard_map/ppermute | solution.py:518
  (11 other events, 79.3 us)

commit v4 on v3

--- a/solution.py
+++ b/solution.py
@@ -67,14 +67,16 @@
     return (lax.rem(z + ORDER[i % STEPS], STEPS) * 2 + y) * 2 + c
 
 
-def places(me_ref, lists_ref, slots):
+def places(me_ref, list_refs, slots):
     slots = jnp.concatenate([slots, slots], axis=0)
     from_owner = jnp.right_shift(slots, 7)
     within = jnp.bitwise_and(slots, LANES - 1)
     rows = jnp.zeros(slots.shape, jnp.int32)
     for i in range(GROUP):
         o = owner_at(me_ref, i)
-        row = jnp.broadcast_to(lists_ref[pl.ds(o, 1), :], slots.shape)
+        dy, dc = PARTS[i // STEPS]
+        held = list_refs[-ORDER[i % STEPS] % STEPS]
+        row = jnp.broadcast_to(held[2 * dy + dc : 2 * dy + dc + 1, :], slots.shape)
         column = jnp.take_along_axis(row, within, axis=1, mode="promise_in_bounds")
         rows = jnp.where(from_owner == o, column + i * LANES, rows)
     return rows[: slots.shape[0] // 2]
@@ -102,13 +104,15 @@
         y_ref[...] = dot(held, wh_ref[...]) + dot(held, wl_ref[...]) + dot(lo_s[...], wh_ref[...])
 
 
-def far_kernel(grouped, me_ref, lists_ref, both_ref, wh_ref, wl_ref, *refs):
+def far_kernel(grouped, me_ref, *refs):
+    list_refs, refs = refs[: 4 * grouped], refs[4 * grouped :]
+    both_ref, wh_ref, wl_ref, *refs = refs
     ids_ref, weight_ref, at_ref, ya_ref, yb_ref, lo_s = refs
     sources = ids_ref.shape[0]
     for j in range(ids_ref.shape[1] // LANES):
         lanes = pl.ds(j * LANES, LANES)
         slots = both_ref[:sources, lanes].astype(jnp.int32)
-        ids_ref[:, lanes] = places(me_ref, lists_ref, slots) if grouped else slots
+        ids_ref[:, lanes] = places(me_ref, list_refs, slots) if grouped else slots
         weight_ref[:, lanes] = both_ref[sources:, lanes]
     half = at_ref.shape[0]
     build_rows(ids_ref, weight_ref, wh_ref, wl_ref, at_ref, [ya_ref, yb_ref], lo_s, half)
@@ -126,7 +130,7 @@
     if head:
         grouped, me, lists = head
         kernel = functools.partial(far_kernel, grouped)
-        args = [me, lists, *args]
+        args = [me, *lists, *args]
         out = [shape((sources, fine), jnp.int32), shape((sources, fine), F32)] + out
     else:
         kernel = near_kernel
@@ -140,6 +144,51 @@
         cost_estimate=cost(3 * slots * fine * width, 4e6),
         name="adjoint_far" if head else "adjoint_near",
     )(*args)
+
+
+def pick_kernel(me_ref, lists_ref, near_ref, far_ref):
+    z, y, c = me_ref[0], me_ref[1], me_ref[2]
+    for dy in range(2):
+        for k in range(STEPS):
+            there = (lax.rem(z + k, STEPS) * 2 + (y if dy == 0 else 1 - y)) * 2
+            row = slice(dy * STEPS + k, dy * STEPS + k + 1)
+            near_ref[row, :] = lists_ref[pl.ds(there + c, 1), :]
+            far_ref[row, :] = lists_ref[pl.ds(there + 1 - c, 1), :]
+
+
+def mix_y_kernel(near_ref, got_ref, near_y_ref, far_y_ref):
+    for i, held in enumerate((near_ref, got_ref)):
+        rows = slice(i * STEPS, (i + 1) * STEPS)
+        near_y_ref[rows, :] = held[:STEPS, :]
+        far_y_ref[rows, :] = held[STEPS:, :]
+
+
+def mix_z_kernel(near_ref, got_ref, *outs):
+    for k, out in enumerate(outs):
+        out[...] = jnp.zeros_like(out)
+        for i, held in enumerate((near_ref, got_ref)):
+            for c in range(2):
+                row = c * STEPS + k
+                out[2 * i + c : 2 * i + c + 1, :] = held[row : row + 1, :]
+
+
+def small(kernel, n, name, *args, scalars=0):
+    return pl.pallas_call(
+        kernel,
+        in_specs=[SMEM] * scalars + [VMEM] * (len(args) - scalars),
+        out_specs=[VMEM] * n,
+        out_shape=[shape((8, LANES), jnp.int32)] * n,
+        compiler_params=params(8),
+        cost_estimate=cost(1e4, 3e4),
+        name=name,
+    )(*args)
+
+
+def exchange_lists(me, lists):
+    near, far = small(pick_kernel, 2, "pick", me, lists, scalars=1)
+    near, far = small(mix_y_kernel, 2, "mix_y", near, over_core(far))
+    own, *sent = small(mix_z_kernel, STEPS, "mix_z", near, over_y(far))
+    return [own] + [over_z(sent[k - 1], k) for k in range(1, STEPS)]
 
 
 def exponent(m):
@@ -259,21 +308,22 @@
     )(*args)
 
 
-def join_kernel(a_ref, b_ref, c_ref, after_ref, out_ref):
-    for i, r in enumerate((a_ref, b_ref, c_ref)):
+def join_kernel(*refs):
+    out_ref = refs[-1]
+    for i, r in enumerate(refs[:3]):
         out_ref[i] = r[...]
 
 
-def join(blocks, after):
+def join(blocks, *after):
     return pl.pallas_call(
         join_kernel,
-        in_specs=[VMEM] * 4,
+        in_specs=[VMEM] * (3 + len(after)),
         out_specs=VMEM,
         out_shape=shape((3,) + blocks[0].shape, BF),
         compiler_params=params(8),
         cost_estimate=cost(1e5, 4e5),
         name="join",
-    )(*blocks, after)
+    )(*blocks, *after)
 
 
 def fold(a):
@@ -313,20 +363,37 @@
         l0, keep = length_of(sums)
         y = keep * y0_ref[...] - l0 * y
         refs.pop(2)[...] = jnp.broadcast_to(l0, (8, LANES))
-    x_ref, y_ref, sum_ref, p_s, x_s = refs
+    x_ref, y_ref, sum_ref, even_s, odd_s, x_s = refs
     members, columns, width = e_ref.shape
     y_ref[...] = y
     x_s[...] = jnp.zeros_like(x_s)
 
-    @pl.loop(0, members // SOME)
-    def _(i):
+    def build(i, held):
         for m in range(SOME):
-            products(e_ref[i * SOME + m], y_ref[...], p_s, pl.ds(m * columns, columns))
-        t = dot(p_s[...], k_ref[...])
+            products(e_ref[i * SOME + m], y_ref[...], held, pl.ds(m * columns, columns))
+
+    def add_in(i, t):
         total = x_s[...]
         for m in range(SOME):
             total = total + t[m * columns : (m + 1) * columns] * e_ref[i * SOME + m].astype(F32)
         x_s[...] = total
+
+    pairs = members // SOME // 2
+    build(0, even_s)
+
+    @pl.loop(0, pairs - 1)
+    def _(i):
+        t = dot(even_s[...], k_ref[...])
+        build(2 * i + 1, odd_s)
+        add_in(2 * i, t)
+        t = dot(odd_s[...], k_ref[...])
+        build(2 * i + 2, even_s)
+        add_in(2 * i + 1, t)
+
+    t = dot(even_s[...], k_ref[...])
+    build(2 * pairs - 1, odd_s)
+    add_in(2 * pairs - 2, t)
+    add_in(2 * pairs - 1, dot(odd_s[...], k_ref[...]))
 
     x = x_s[...]
     x_ref[...] = x.T.astype(BF)
@@ -347,6 +414,7 @@
         out_specs=[VMEM] * len(out),
         out_shape=out,
         scratch_shapes=[
+            pltpu.VMEM((SOME * columns, width), BF),
             pltpu.VMEM((SOME * columns, width), BF),
             pltpu.VMEM((columns, width), F32),
         ],
@@ -476,31 +544,48 @@
     )(*xs, near, far, obs, g_sums)
 
 
+OUT_CUTS = 4
+
+
 def result_kernel(count, l0_ref, *refs):
     sums = refs[0][...]
     for r in refs[1:count]:
         sums = sums + r[...]
-    g0_ref, g1_ref, i0_ref, i1_ref, control_ref, increment_ref = refs[count:]
+    g0_ref, g1_ref, i0_ref, i1_ref, control_hbm, increment_hbm, c_s, i_s, sem = refs[count:]
     l0 = -l0_ref[0:1, 0:1]
     l1, _ = length_of(sums)
-    control_ref[...] = l0 * g0_ref[...] - l1 * g1_ref[...]
-    increment_ref[...] = l0 * i0_ref[...] - l1 * i1_ref[...]
+    lanes = c_s.shape[1] // OUT_CUTS
+    rows = i_s.shape[0] // OUT_CUTS
+    copies = []
+    for i in range(OUT_CUTS):
+        some = pl.ds(i * lanes, lanes)
+        c_s[:, some] = l0 * g0_ref[:, some] - l1 * g1_ref[:, some]
+        copies.append(
+            pltpu.make_async_copy(c_s.at[:, some], control_hbm.at[:, some], sem.at[2 * i])
+        )
+        copies[-1].start()
+        some = pl.ds(i * rows, rows)
+        i_s[some, :] = l0 * i0_ref[some, :] - l1 * i1_ref[some, :]
+        copies.append(
+            pltpu.make_async_copy(i_s.at[some, :], increment_hbm.at[some, :], sem.at[2 * i + 1])
+        )
+        copies[-1].start()
+    for copy in copies:
+        copy.wait()
 
 
 def result(l0, sums, g0, g1, im0, im1):
-    cuts = 4
-    whole = lambda i: (0, 0)
-    g_spec = pl.BlockSpec((g0.shape[0], g0.shape[1] // cuts), lambda i: (0, i))
-    i_spec = pl.BlockSpec((im0.shape[0] // cuts, im0.shape[1]), lambda i: (i, 0))
     return pl.pallas_call(
         functools.partial(result_kernel, len(sums)),
-        grid=(cuts,),
-        in_specs=[pl.BlockSpec(l0.shape, whole)]
-        + [pl.BlockSpec(r.shape, whole) for r in sums]
-        + [g_spec, g_spec, i_spec, i_spec],
-        out_specs=[g_spec, i_spec],
+        in_specs=[VMEM] * (5 + len(sums)),
+        out_specs=[ANY] * 2,
         out_shape=[shape(g0.shape, F32), shape(im0.shape, F32)],
-        compiler_params=params(24),
+        scratch_shapes=[
+            pltpu.VMEM(g0.shape, F32),
+            pltpu.VMEM(im0.shape, F32),
+            pltpu.SemaphoreType.DMA((2 * OUT_CUTS,)),
+        ],
+        compiler_params=params(16),
         cost_estimate=cost(3 * g0.size, 1e7),
         name="result",
     )(l0, *sums, g0, g1, im0, im1)
@@ -534,7 +619,7 @@
     two, three, one = over_z(x, 2), over_z(x, 3), over_z(x, 1)
     y_own = over_y(x)
     c_own = over_core(x)
-    rest = join([two, three, one], after)
+    rest = join([two, three, one], y_own, c_own, after)
     y_rest = over_y(rest)
     c_rest = over_core(rest)
     return [x, rest, y_own, y_rest, c_own, c_rest, over_core(y_own), over_core(y_rest)]
@@ -571,9 +656,7 @@
     wh, wl = high.astype(BF), (w - high).astype(BF)
     named = jnp.concatenate([slot_of.astype(F32), interp_weight], axis=0)
     if grouped:
-        lists = lax.all_to_all(
-            intersection_list, "space", split_axis=1, concat_axis=0, tiled=True
-        ).reshape(devices, capacity)
+        lists = exchange_lists(me, intersection_list[0])
         scatter, gather, add_up = scatter_sums, gather_columns, sum_all
     else:
         lists = intersection_list[0]
@@ -598,7 +681,7 @@
         def add_up(x):
             return [lax.psum(x, "space")]
 
-    ids, weight, far, c0, c1 = adjoint_half(slots, [named, wh, wl], (grouped, me, lists))
+    ids, weight, far, c0, c1 = adjoint_half(slots, [named, wh, wl], (grouped, me, lists if grouped else []))
     near, n0, n1 = adjoint_half(slots, [ids, weight, wh, wl])
     own, got, _ = scatter([n0, n1, c0, c1])
     x0, y0, g_sums = coarse_image(ensemble, kern, own, got)

time: 129 us -> 125 us (0.969)
  waiting for transfers between devices: 50.9 us -> 44.4 us
  starting transfers between devices: 36.5 us -> 41.6 us
  Pallas kernels: 34.5 us -> 32.6 us
  other arithmetic: 3.07 us -> 1.62 us
    all_to_all x1 -> x0, starting transfers between devices: 7.4 us -> none  [on_device(): lax.all_to_all(intersection_list, 'space', split_axis=1, concat_axis=0, t...]
    ppermute x15 -> x18, starting transfers between devices: 18.5 us -> 25.6 us  [over_z(): lax.ppermute(x, 'space', [(i, (i + 4 * k) % GROUP) for i in range(GROUP)])]
    ppermute x9 -> x10, waiting for transfers between devices: 29.5 us -> 23.1 us  [over_y(): return lax.ppermute(x, 'space', [(i, i ^ 2) for i in range(GROUP)])]
    ppermute x9 -> x10, starting transfers between devices: 8.79 us -> 12.9 us  [over_y(): return lax.ppermute(x, 'space', [(i, i ^ 2) for i in range(GROUP)])]
    all_to_all x1 -> x0, waiting for transfers between devices: 3.23 us -> none  [on_device(): lax.all_to_all(intersection_list, 'space', split_axis=1, concat_axis=0, t...]
    ppermute x15 -> x18, waiting for transfers between devices: 13.3 us -> 16.1 us  [over_z(): lax.ppermute(x, 'space', [(i, (i + 4 * k) % GROUP) for i in range(GROUP)])]
    pallas_call x2, Pallas kernels: 8.88 us -> 7.21 us  [coarse_image(): pl.pallas_call(functools.partial(coarse_kernel, len(got), second), in_spe...]
    ppermute x13 -> x14, starting transfers between devices: 1.84 us -> 3.12 us  [over_core(): return lax.ppermute(x, 'space', [(i, i ^ 1) for i in range(GROUP)])]
  transfers between devices with their start and end apart: 38 -> 42, of which waited for: 22 -> 21; matrix products, arithmetic and copies ran while one was open for 5% -> 4% of each run, Pallas kernels for 10% -> 10%
where the time goes in v4:
time: 125 us
  waiting for transfers between devices  44.4 us (36%)
  starting transfers between devices  41.6 us (33%)
  Pallas kernels  32.6 us (26%)
  local copies, waits for them, and re-layouts  3.7 us (3%)
  other arithmetic  1.62 us (1%)
    ppermute x18, starting transfers between devices, over_z(): lax.ppermute(x, 'space', [(i, (i + 4 * k) % GROUP) for i in range(GROUP)])  25.6 us
    ppermute x10, waiting for transfers between devices, over_y(): return lax.ppermute(x, 'space', [(i, i ^ 2) for i in range(GROUP)])  23.1 us
    ppermute x18, waiting for transfers between devices, over_z(): lax.ppermute(x, 'space', [(i, (i + 4 * k) % GROUP) for i in range(GROUP)])  16.1 us
    ppermute x10, starting transfers between devices, over_y(): return lax.ppermute(x, 'space', [(i, i ^ 2) for i in range(GROUP)])  12.9 us
    pallas_call x2, Pallas kernels, adjoint_half(): pl.pallas_call(kernel, in_specs=([SMEM] if head else []) + [VMEM] * (len(...  9.57 us
    pallas_call x2, Pallas kernels, project(): pl.pallas_call(project_kernel, in_specs=[VMEM] * 3, out_specs=[VMEM] * 2,...  7.27 us
    pallas_call x2, Pallas kernels, coarse_image(): pl.pallas_call(functools.partial(coarse_kernel, len(got), second), in_spe...  7.21 us
    ppermute x14, waiting for transfers between devices, over_core(): return lax.ppermute(x, 'space', [(i, i ^ 1) for i in range(GROUP)])  5.25 us
  transfers between devices with their start and end apart: 42, of which 21 were waited for; matrix products, arithmetic and copies ran while one was open for 4% of the time, Pallas kernels for 10%

profile of v4, /device:TPU:0, one launch (start us, length us, event | category | flops | bytes accessed | tf_op | source)
XLA Modules:
  0.0 125.1 jit_solution(7478806026028518157)
XLA Ops:
  3.4 2.9 %collective-permute-start.1 = (s32[8,128]{1,0:T(8,128)S(1)}, s32[8,128]{1,0:T(8,128)S(1)}, u32[]{:S(2)}, u32[]{:S(2)}) collective-permute-start(s32[8,128]{1,0:T(8,128)S(1)} %get-tuple-element.54), channel_id=1, source_target_pairs={{0,2},{1,3},{2,0},{3,1},{4,6},{5,7},{6,4},{7,5},{8,10},{9,11},{10,... | collective-permute-start | bytes 12296 | tf_op jit(solution)/shard_map/ppermute | solution.py:599
  7.8 2.1 %collective-permute-start.2 = (s32[8,128]{1,0:T(8,128)S(1)}, s32[8,128]{1,0:T(8,128)S(1)}, u32[]{:S(2)}, u32[]{:S(2)}) collective-permute-start(s32[8,128]{1,0:T(8,128)S(1)} %get-tuple-element.56), channel_id=1, source_target_pairs={{0,4},{1,5},{2,6},{3,7},{4,8},{5,9},{6,10},{7,11},{8,12},{9,13},{1... | collective-permute-start | bytes 12296 | tf_op jit(solution)/shard_map/ppermute | solution.py:603
  10.0 2.6 %collective-permute-start.3 = (s32[8,128]{1,0:T(8,128)S(1)}, s32[8,128]{1,0:T(8,128)S(1)}, u32[]{:S(2)}, u32[]{:S(2)}) collective-permute-start(s32[8,128]{1,0:T(8,128)S(1)} %get-tuple-element.57), channel_id=1, source_target_pairs={{0,8},{1,9},{2,10},{3,11},{4,12},{5,13},{6,14},{7,15},{8,0},{9,1},... | collective-permute-start | bytes 12296 | tf_op jit(solution)/shard_map/ppermute | solution.py:603
  14.5 1.7 %collective-permute-done.4.refs_3_ = s32[8,128]{1,0:T(8,128)S(1)} collective-permute-done((s32[8,128]{1,0:T(8,128)S(1)}, s32[8,128]{1,0:T(8,128)S(1)}, u32[]{:S(2)}, u32[]{:S(2)}) %collective-permute-start.4) | collective-permute-done | bytes 4128 | tf_op jit(solution)/shard_map/ppermute | solution.py:603
  16.2 5.2 %adjoint_far.1 = (s32[4,1152]{1,0:T(4,128)S(1)}, f32[4,1152]{1,0:T(4,128)S(1)}, bf16[1024,1152]{1,0:T(8,128)(2,1)S(1)}, f32[512,256]{1,0:T(8,128)S(1)}, f32[512,256]{1,0:T(8,128)S(1)}) custom-call(s32[4]{0:T(128)S(1)} %pad_add_fusion.me_ref, s32[8,128]{1,0:T(8,128)S(1)} %get-tuple-element.55.refs_0_, s32[8,128]{1,0:T(8,128)S(1)} %collective-permute-done.2.refs_1_, ...), custom_call_target="tpu_custom_call" | custom-call | flops 1811939328 | bytes 4000000 | tf_op jit(solution)/shard_map/adjoint_far/pallas_call | solution.py:137
  21.9 4.4 %adjoint_near.1 = (bf16[1024,1152]{1,0:T(8,128)(2,1)S(1)}, f32[512,256]{1,0:T(8,128)S(1)}, f32[512,256]{1,0:T(8,128)S(1)}) custom-call(s32[4,1152]{1,0:T(4,128)S(1)} %get-tuple-element.59.ids_ref, f32[4,1152]{1,0:T(4,128)S(1)} %get-tuple-element.60.weight_ref, bf16[1152,256]{1,0:T(8,128)(2,1)S(1)} %get-tuple-element.101.refs_5_.wh_ref, ...), custom_call_target="tpu_custom_call" | custom-call | flops 1811939328 | bytes 4000000 | tf_op jit(solution)/shard_map/adjoint_near/pallas_call | solution.py:137
  26.5 1.6 %collective-permute-start.7 = (s16[272,256]{1,0:T(8,128)(2,1)S(1)}, s16[272,256]{1,0:T(8,128)(2,1)S(1)}, u32[]{:S(2)}, u32[]{:S(2)}) collective-permute-start(s16[272,256]{1,0:T(8,128)(2,1)S(1)} %get-tuple-element.65), channel_id=1, source_target_pairs={{0,2},{1,3},{2,0},{3,1},{4,6},{5,7},{6,4},{7,5},{8,10},{9,11},{10,... | collective-permute-start | bytes 417800 | tf_op jit(solution)/shard_map/ppermute | solution.py:599
  28.6 4.5 %collective-permute-done.7.p_ref = s16[272,256]{1,0:T(8,128)(2,1)S(1)} collective-permute-done((s16[272,256]{1,0:T(8,128)(2,1)S(1)}, s16[272,256]{1,0:T(8,128)(2,1)S(1)}, u32[]{:S(2)}, u32[]{:S(2)}) %collective-permute-start.7) | collective-permute-done | bytes 139296 | tf_op jit(solution)/shard_map/ppermute | solution.py:599
  33.2 3.2 %collective-permute-start.11 = (s16[144,256]{1,0:T(8,128)(2,1)S(1)}, s16[144,256]{1,0:T(8,128)(2,1)S(1)}, u32[]{:S(2)}, u32[]{:S(2)}) collective-permute-start(s16[144,256]{1,0:T(8,128)(2,1)S(1)} %get-tuple-element.70), channel_id=1, source_target_pairs={{0,12},{1,13},{2,14},{3,15},{4,0},{5,1},{6,2},{7,3},{8,4},{9,5},{1... | collective-permute-start | bytes 221192 | tf_op jit(solution)/shard_map/ppermute | solution.py:603
  36.6 2.5 %collective-permute-start.10 = (s16[144,256]{1,0:T(8,128)(2,1)S(1)}, s16[144,256]{1,0:T(8,128)(2,1)S(1)}, u32[]{:S(2)}, u32[]{:S(2)}) collective-permute-start(s16[144,256]{1,0:T(8,128)(2,1)S(1)} %get-tuple-element.69), channel_id=1, source_target_pairs={{0,4},{1,5},{2,6},{3,7},{4,8},{5,9},{6,10},{7,11},{8,12},{9,13},{1... | collective-permute-start | bytes 221192 | tf_op jit(solution)/shard_map/ppermute | solution.py:603
  39.1 3.0 %copy.12 = bf16[80,128,256]{2,0,1:T(8,128)(2,1)S(1)} copy(bf16[80,128,256]{2,1,0:T(8,128)(2,1)S(1)} %bitcast.9) | data formatting | bytes 10485760 | tf_op args[0]
  42.9 3.6 %coarse_first.1 = (bf16[256,128]{1,0:T(8,128)(2,1)S(1)}, f32[128,256]{1,0:T(8,128)S(1)}, f32[8,256]{1,0:T(8,128)S(1)}) custom-call(bf16[80,128,256]{2,1,0:T(8,128)(2,1)S(1)} %bitcast.9, bf16[256,256]{1,0:T(8,128)(2,1)S(1)} %copy-done.2, f32[128,256]{1,0:T(8,128)S(1)} %get-tuple-element.66.own_ref, s16[144,256]{1,0:T(8,128)(2,1)S(1)} %collective-permute-done.9.refs_0_, ...), custom_call_target="tpu_custom_call" | custom-call | flops 1342177280 | bytes 5000000 | tf_op jit(solution)/shard_map/coarse_first/pallas_call | solution.py:411
  46.7 1.6 %collective-permute-start.15 = (bf16[256,128]{1,0:T(8,128)(2,1)S(1)}, bf16[256,128]{1,0:T(8,128)(2,1)S(1)}, u32[]{:S(2)}, u32[]{:S(2)}) collective-permute-start(bf16[256,128]{1,0:T(8,128)(2,1)S(1)} %get-tuple-element.71.refs_0_), channel_id=1, source_target_pairs={{0,2},{1,3},{2,0},{3,1},{4,6},{5,7},{6,4},{7,5},{8,10},{9,11},{10,... | collective-permute-start | bytes 196616 | tf_op jit(solution)/shard_map/ppermute | solution.py:599
  48.7 3.4 %collective-permute-start.13 = (bf16[256,128]{1,0:T(8,128)(2,1)S(1)}, bf16[256,128]{1,0:T(8,128)(2,1)S(1)}, u32[]{:S(2)}, u32[]{:S(2)}) collective-permute-start(bf16[256,128]{1,0:T(8,128)(2,1)S(1)} %get-tuple-element.71.refs_0_), channel_id=1, source_target_pairs={{0,12},{1,13},{2,14},{3,15},{4,0},{5,1},{6,2},{7,3},{8,4},{9,5},{1... | collective-permute-start | bytes 196616 | tf_op jit(solution)/shard_map/ppermute | solution.py:603
  52.4 3.6 %project.2 = (f32[80,8192]{1,0:T(8,128)S(1)}, f32[8,128]{1,0:T(8,128)S(1)}) custom-call(bf16[128,80,256]{2,1,0:T(8,128)(2,1)S(1)} %bitcast.10, f32[128,256]{1,0:T(8,128)S(1)} %get-tuple-element.72.y_ref.refs_3_, bf16[2,256,128]{2,1,0:T(8,128)(2,1)S(1)} %copy-done.1), custom_call_target="tpu_custom_call" | custom-call | flops 1342177280 | bytes 8000000 | tf_op jit(solution)/shard_map/project/pallas_call | solution.py:449
  56.1 2.3 %collective-permute-done.12.refs_0_ = bf16[256,128]{1,0:T(8,128)(2,1)S(1)} collective-permute-done((bf16[256,128]{1,0:T(8,128)(2,1)S(1)}, bf16[256,128]{1,0:T(8,128)(2,1)S(1)}, u32[]{:S(2)}, u32[]{:S(2)}) %collective-permute-start.12) | collective-permute-done | bytes 65568 | tf_op jit(solution)/shard_map/ppermute | solution.py:603
  59.0 6.1 %collective-permute-done.17.refs_3_ = bf16[3,256,128]{2,1,0:T(8,128)(2,1)S(1)} collective-permute-done((bf16[3,256,128]{2,1,0:T(8,128)(2,1)S(1)}, bf16[3,256,128]{2,1,0:T(8,128)(2,1)S(1)}, u32[]{:S(2)}, u32[]{:S(2)}) %collective-permute-start.17) | collective-permute-done | bytes 196640 | tf_op jit(solution)/shard_map/ppermute | solution.py:599
  66.7 3.2 %image_first.1 = (f32[1152,256]{1,0:T(8,128)S(1)}, f32[8,256]{1,0:T(8,128)S(1)}, f32[512,256]{1,0:T(8,128)S(1)}, f32[512,256]{1,0:T(8,128)S(1)}, f32[512,256]{1,0:T(8,128)S(1)}, /*index=5*/f32[520,256]{1,0:T(8,128)S(1)}) custom-call(bf16[256,128]{1,0:T(8,128)(2,1)S(1)} %get-tuple-element.71.refs_0_, bf16[3,256,128]{2,1,0:T(8,128)(2,1)S(1)} %join.2.refs_1_, ...), custom_call_target="tpu_custom_call" | custom-call | flops 2415919104 | bytes 13000000 | tf_op jit(solution)/shard_map/image_first/pallas_call | solution.py:509
  74.1 4.5 %collective-permute-done.24.p_ref = s16[272,256]{1,0:T(8,128)(2,1)S(1)} collective-permute-done((s16[272,256]{1,0:T(8,128)(2,1)S(1)}, s16[272,256]{1,0:T(8,128)(2,1)S(1)}, u32[]{:S(2)}, u32[]{:S(2)}) %collective-permute-start.24) | collective-permute-done | bytes 139296 | tf_op jit(solution)/shard_map/ppermute | solution.py:599
  81.0 1.8 %collective-permute-start.27 = (s16[144,256]{1,0:T(8,128)(2,1)S(1)}, s16[144,256]{1,0:T(8,128)(2,1)S(1)}, u32[]{:S(2)}, u32[]{:S(2)}) collective-permute-start(s16[144,256]{1,0:T(8,128)(2,1)S(1)} %get-tuple-element.89), channel_id=1, source_target_pairs={{0,12},{1,13},{2,14},{3,15},{4,0},{5,1},{6,2},{7,3},{8,4},{9,5},{1... | collective-permute-start | bytes 221192 | tf_op jit(solution)/shard_map/ppermute | solution.py:603
  82.9 2.8 %collective-permute-done.25.refs_0_ = s16[144,256]{1,0:T(8,128)(2,1)S(1)} collective-permute-done((s16[144,256]{1,0:T(8,128)(2,1)S(1)}, s16[144,256]{1,0:T(8,128)(2,1)S(1)}, u32[]{:S(2)}, u32[]{:S(2)}) %collective-permute-start.25) | collective-permute-done | bytes 73760 | tf_op jit(solution)/shard_map/ppermute | solution.py:603
  86.5 3.6 %coarse_second.1 = (bf16[256,128]{1,0:T(8,128)(2,1)S(1)}, f32[128,256]{1,0:T(8,128)S(1)}, f32[8,128]{1,0:T(8,128)S(1)}, f32[8,256]{1,0:T(8,128)S(1)}) custom-call(bf16[80,128,256]{2,1,0:T(8,128)(2,1)S(1)} %bitcast.9, bf16[256,256]{1,0:T(8,128)(2,1)S(1)} %copy-done.2, f32[128,256]{1,0:T(8,128)S(1)} %get-tuple-element.86.own_ref, ...), custom_call_target="tpu_custom_call" | custom-call | flops 1342177280 | bytes 5000000 | tf_op jit(solution)/shard_map/coarse_second/pallas_call | solution.py:411
  91.3 3.3 %collective-permute-start.29 = (bf16[256,128]{1,0:T(8,128)(2,1)S(1)}, bf16[256,128]{1,0:T(8,128)(2,1)S(1)}, u32[]{:S(2)}, u32[]{:S(2)}) collective-permute-start(bf16[256,128]{1,0:T(8,128)(2,1)S(1)} %get-tuple-element.91.refs_0_), channel_id=1, source_target_pairs={{0,12},{1,13},{2,14},{3,15},{4,0},{5,1},{6,2},{7,3},{8,4},{9,5},{1... | collective-permute-start | bytes 196616 | tf_op jit(solution)/shard_map/ppermute | solution.py:603
  94.6 3.6 %project.3 = (f32[80,8192]{1,0:T(8,128)S(1)}, f32[8,128]{1,0:T(8,128)S(1)}) custom-call(bf16[128,80,256]{2,1,0:T(8,128)(2,1)S(1)} %bitcast.11, f32[128,256]{1,0:T(8,128)S(1)} %get-tuple-element.92.y_ref, bf16[2,256,128]{2,1,0:T(8,128)(2,1)S(1)} %copy-done.1), custom_call_target="tpu_custom_call" | custom-call | flops 1342177280 | bytes 8000000 | tf_op jit(solution)/shard_map/project/pallas_call | solution.py:449
  98.3 2.1 %collective-permute-done.28.refs_0_ = bf16[256,128]{1,0:T(8,128)(2,1)S(1)} collective-permute-done((bf16[256,128]{1,0:T(8,128)(2,1)S(1)}, bf16[256,128]{1,0:T(8,128)(2,1)S(1)}, u32[]{:S(2)}, u32[]{:S(2)}) %collective-permute-start.28) | collective-permute-done | bytes 65568 | tf_op jit(solution)/shard_map/ppermute | solution.py:603
  100.4 1.6 %collective-permute-start.33 = (bf16[3,256,128]{2,1,0:T(8,128)(2,1)S(1)}, bf16[3,256,128]{2,1,0:T(8,128)(2,1)S(1)}, u32[]{:S(2)}, u32[]{:S(2)}) collective-permute-start(bf16[3,256,128]{2,1,0:T(8,128)(2,1)S(1)} %join.3.refs_1_), channel_id=1, source_target_pairs={{0,2},{1,3},{2,0},{3,1},{4,6},{5,7},{6,4},{7,5},{8,10},{9,11},{10,... | collective-permute-start | bytes 589832 | tf_op jit(solution)/shard_map/ppermute | solution.py:599
  101.9 4.7 %collective-permute-done.33.refs_3_ = bf16[3,256,128]{2,1,0:T(8,128)(2,1)S(1)} collective-permute-done((bf16[3,256,128]{2,1,0:T(8,128)(2,1)S(1)}, bf16[3,256,128]{2,1,0:T(8,128)(2,1)S(1)}, u32[]{:S(2)}, u32[]{:S(2)}) %collective-permute-start.33) | collective-permute-done | bytes 196640 | tf_op jit(solution)/shard_map/ppermute | solution.py:599
  108.2 1.9 %image_second.1 = (f32[1152,256]{1,0:T(8,128)S(1)}, f32[8,256]{1,0:T(8,128)S(1)}) custom-call(bf16[256,128]{1,0:T(8,128)(2,1)S(1)} %get-tuple-element.91.refs_0_, bf16[3,256,128]{2,1,0:T(8,128)(2,1)S(1)} %join.3.refs_1_, bf16[256,128]{1,0:T(8,128)(2,1)S(1)} %collective-permute-done.31.refs_3_.refs_2_, ...), custom_call_target="tpu_custom_call" | custom-call | flops 1207959552 | bytes 8000000 | tf_op jit(solution)/shard_map/image_second/pallas_call | solution.py:535
  112.9 2.1 %collective-permute-done.38 = f32[8,256]{1,0:T(8,128)S(1)} collective-permute-done((f32[8,256]{1,0:T(8,128)S(1)}, f32[8,256]{1,0:T(8,128)S(1)}, u32[]{:S(2)}, u32[]{:S(2)}) %collective-permute-start.38) | collective-permute-done | bytes 8224 | tf_op jit(solution)/shard_map/ppermute | solution.py:599
  115.1 2.2 %collective-permute-start.41 = (f32[8,256]{1,0:T(8,128)S(1)}, f32[8,256]{1,0:T(8,128)S(1)}, u32[]{:S(2)}, u32[]{:S(2)}) collective-permute-start(f32[8,256]{1,0:T(8,128)S(1)} %add.18.refs_0_), channel_id=1, source_target_pairs={{0,12},{1,13},{2,14},{3,15},{4,0},{5,1},{6,2},{7,3},{8,4},{9,5},{1... | collective-permute-start | bytes 24584 | tf_op jit(solution)/shard_map/ppermute | solution.py:603
  118.7 3.1 %collective-permute-done.40.refs_2_ = f32[8,256]{1,0:T(8,128)S(1)} collective-permute-done((f32[8,256]{1,0:T(8,128)S(1)}, f32[8,256]{1,0:T(8,128)S(1)}, u32[]{:S(2)}, u32[]{:S(2)}) %collective-permute-start.40) | collective-permute-done | bytes 8224 | tf_op jit(solution)/shard_map/ppermute | solution.py:603
  122.7 2.2 %result.1 = (f32[80,8192]{1,0:T(8,128)}, f32[1152,256]{1,0:T(8,128)}) custom-call(f32[8,128]{1,0:T(8,128)S(1)} %get-tuple-element.90.l0_ref, f32[8,256]{1,0:T(8,128)S(1)} %add.18.refs_0_, f32[8,256]{1,0:T(8,128)S(1)} %collective-permute-done.39.refs_1_, f32[8,256]{1,0:T(8,128)S(1)} %collective-permute-done.40.refs_2_, ...), custom_call_target="tpu_custom_call" | custom-call | flops 1966080 | bytes 10000000 | tf_op jit(solution)/shard_map/result/pallas_call | solution.py:578
  (96 shorter events, 26.9 us)
Async XLA Ops:
  3.4 4.4 %collective-permute-start.1 = (s32[8,128]{1,0:T(8,128)S(1)}, s32[8,128]{1,0:T(8,128)S(1)}, u32[]{:S(2)}, u32[]{:S(2)}) collective-permute-start(s32[8,128]{1,0:T(8,128)S(1)} %get-tuple-element.54), channel_id=1, source_target_pairs={{0,2},{1,3},{2,0},{3,1},{4,6},{5,7},{6,4},{7,5},{8,10},{9,11},{10,... | collective-permute-start | bytes 12296 | tf_op jit(solution)/shard_map/ppermute | solution.py:599
  7.8 6.1 %collective-permute-start.2 = (s32[8,128]{1,0:T(8,128)S(1)}, s32[8,128]{1,0:T(8,128)S(1)}, u32[]{:S(2)}, u32[]{:S(2)}) collective-permute-start(s32[8,128]{1,0:T(8,128)S(1)} %get-tuple-element.56), channel_id=1, source_target_pairs={{0,4},{1,5},{2,6},{3,7},{4,8},{5,9},{6,10},{7,11},{8,12},{9,13},{1... | collective-permute-start | bytes 12296 | tf_op jit(solution)/shard_map/ppermute | solution.py:603
  10.0 4.5 %collective-permute-start.3 = (s32[8,128]{1,0:T(8,128)S(1)}, s32[8,128]{1,0:T(8,128)S(1)}, u32[]{:S(2)}, u32[]{:S(2)}) collective-permute-start(s32[8,128]{1,0:T(8,128)S(1)} %get-tuple-element.57), channel_id=1, source_target_pairs={{0,8},{1,9},{2,10},{3,11},{4,12},{5,13},{6,14},{7,15},{8,0},{9,1},... | collective-permute-start | bytes 12296 | tf_op jit(solution)/shard_map/ppermute | solution.py:603
  21.3 5.0 %collective-permute-start.6 = (f32[512,256]{1,0:T(8,128)S(1)}, f32[512,256]{1,0:T(8,128)S(1)}, u32[]{:S(2)}, u32[]{:S(2)}) collective-permute-start(f32[512,256]{1,0:T(8,128)S(1)} %get-tuple-element.64), channel_id=1, source_target_pairs={{0,1},{1,0},{2,3},{3,2},{4,5},{5,4},{6,7},{7,6},{8,9},{9,8},{10,11... | collective-permute-start | bytes 1572872 | tf_op jit(solution)/shard_map/ppermute | solution.py:595
  21.4 7.1 %collective-permute-start.5 = (f32[512,256]{1,0:T(8,128)S(1)}, f32[512,256]{1,0:T(8,128)S(1)}, u32[]{:S(2)}, u32[]{:S(2)}) collective-permute-start(f32[512,256]{1,0:T(8,128)S(1)} %get-tuple-element.62), channel_id=1, source_target_pairs={{0,1},{1,0},{2,3},{3,2},{4,5},{5,4},{6,7},{7,6},{8,9},{9,8},{10,11... | collective-permute-start | bytes 1572872 | tf_op jit(solution)/shard_map/ppermute | solution.py:595
  26.5 6.6 %collective-permute-start.7 = (s16[272,256]{1,0:T(8,128)(2,1)S(1)}, s16[272,256]{1,0:T(8,128)(2,1)S(1)}, u32[]{:S(2)}, u32[]{:S(2)}) collective-permute-start(s16[272,256]{1,0:T(8,128)(2,1)S(1)} %get-tuple-element.65), channel_id=1, source_target_pairs={{0,2},{1,3},{2,0},{3,1},{4,6},{5,7},{6,4},{7,5},{8,10},{9,11},{10,... | collective-permute-start | bytes 417800 | tf_op jit(solution)/shard_map/ppermute | solution.py:599
  28.0 8.3 %collective-permute-start.8 = (s16[272,256]{1,0:T(8,128)(2,1)S(1)}, s16[272,256]{1,0:T(8,128)(2,1)S(1)}, u32[]{:S(2)}, u32[]{:S(2)}) collective-permute-start(s16[272,256]{1,0:T(8,128)(2,1)S(1)} %get-tuple-element.67), channel_id=1, source_target_pairs={{0,2},{1,3},{2,0},{3,1},{4,6},{5,7},{6,4},{7,5},{8,10},{9,11},{10,... | collective-permute-start | bytes 417800 | tf_op jit(solution)/shard_map/ppermute | solution.py:599
  33.2 8.9 %collective-permute-start.11 = (s16[144,256]{1,0:T(8,128)(2,1)S(1)}, s16[144,256]{1,0:T(8,128)(2,1)S(1)}, u32[]{:S(2)}, u32[]{:S(2)}) collective-permute-start(s16[144,256]{1,0:T(8,128)(2,1)S(1)} %get-tuple-element.70), channel_id=1, source_target_pairs={{0,12},{1,13},{2,14},{3,15},{4,0},{5,1},{6,2},{7,3},{8,4},{9,5},{1... | collective-permute-start | bytes 221192 | tf_op jit(solution)/shard_map/ppermute | solution.py:603
  36.5 5.6 %collective-permute-start.9 = (s16[144,256]{1,0:T(8,128)(2,1)S(1)}, s16[144,256]{1,0:T(8,128)(2,1)S(1)}, u32[]{:S(2)}, u32[]{:S(2)}) collective-permute-start(s16[144,256]{1,0:T(8,128)(2,1)S(1)} %get-tuple-element.68), channel_id=1, source_target_pairs={{0,8},{1,9},{2,10},{3,11},{4,12},{5,13},{6,14},{7,15},{8,0},{9,1},... | collective-permute-start | bytes 221192 | tf_op jit(solution)/shard_map/ppermute | solution.py:603
  36.6 6.4 %collective-permute-start.10 = (s16[144,256]{1,0:T(8,128)(2,1)S(1)}, s16[144,256]{1,0:T(8,128)(2,1)S(1)}, u32[]{:S(2)}, u32[]{:S(2)}) collective-permute-start(s16[144,256]{1,0:T(8,128)(2,1)S(1)} %get-tuple-element.69), channel_id=1, source_target_pairs={{0,4},{1,5},{2,6},{3,7},{4,8},{5,9},{6,10},{7,11},{8,12},{9,13},{1... | collective-permute-start | bytes 221192 | tf_op jit(solution)/shard_map/ppermute | solution.py:603
  46.6 9.5 %collective-permute-start.16 = (bf16[256,128]{1,0:T(8,128)(2,1)S(1)}, bf16[256,128]{1,0:T(8,128)(2,1)S(1)}, u32[]{:S(2)}, u32[]{:S(2)}) collective-permute-start(bf16[256,128]{1,0:T(8,128)(2,1)S(1)} %get-tuple-element.71.refs_0_), channel_id=1, source_target_pairs={{0,1},{1,0},{2,3},{3,2},{4,5},{5,4},{6,7},{7,6},{8,9},{9,8},{10,11... | collective-permute-start | bytes 196616 | tf_op jit(solution)/shard_map/ppermute | solution.py:595
  46.7 9.4 %collective-permute-start.15 = (bf16[256,128]{1,0:T(8,128)(2,1)S(1)}, bf16[256,128]{1,0:T(8,128)(2,1)S(1)}, u32[]{:S(2)}, u32[]{:S(2)}) collective-permute-start(bf16[256,128]{1,0:T(8,128)(2,1)S(1)} %get-tuple-element.71.refs_0_), channel_id=1, source_target_pairs={{0,2},{1,3},{2,0},{3,1},{4,6},{5,7},{6,4},{7,5},{8,10},{9,11},{10,... | collective-permute-start | bytes 196616 | tf_op jit(solution)/shard_map/ppermute | solution.py:599
  48.3 7.9 %collective-permute-start.14 = (bf16[256,128]{1,0:T(8,128)(2,1)S(1)}, bf16[256,128]{1,0:T(8,128)(2,1)S(1)}, u32[]{:S(2)}, u32[]{:S(2)}) collective-permute-start(bf16[256,128]{1,0:T(8,128)(2,1)S(1)} %get-tuple-element.71.refs_0_), channel_id=1, source_target_pairs={{0,4},{1,5},{2,6},{3,7},{4,8},{5,9},{6,10},{7,11},{8,12},{9,13},{1... | collective-permute-start | bytes 196616 | tf_op jit(solution)/shard_map/ppermute | solution.py:603
  48.7 7.4 %collective-permute-start.13 = (bf16[256,128]{1,0:T(8,128)(2,1)S(1)}, bf16[256,128]{1,0:T(8,128)(2,1)S(1)}, u32[]{:S(2)}, u32[]{:S(2)}) collective-permute-start(bf16[256,128]{1,0:T(8,128)(2,1)S(1)} %get-tuple-element.71.refs_0_), channel_id=1, source_target_pairs={{0,12},{1,13},{2,14},{3,15},{4,0},{5,1},{6,2},{7,3},{8,4},{9,5},{1... | collective-permute-start | bytes 196616 | tf_op jit(solution)/shard_map/ppermute | solution.py:603
  52.1 6.3 %collective-permute-start.12 = (bf16[256,128]{1,0:T(8,128)(2,1)S(1)}, bf16[256,128]{1,0:T(8,128)(2,1)S(1)}, u32[]{:S(2)}, u32[]{:S(2)}) collective-permute-start(bf16[256,128]{1,0:T(8,128)(2,1)S(1)} %get-tuple-element.71.refs_0_), channel_id=1, source_target_pairs={{0,8},{1,9},{2,10},{3,11},{4,12},{5,13},{6,14},{7,15},{8,0},{9,1},... | collective-permute-start | bytes 196616 | tf_op jit(solution)/shard_map/ppermute | solution.py:603
  58.4 6.7 %collective-permute-start.17 = (bf16[3,256,128]{2,1,0:T(8,128)(2,1)S(1)}, bf16[3,256,128]{2,1,0:T(8,128)(2,1)S(1)}, u32[]{:S(2)}, u32[]{:S(2)}) collective-permute-start(bf16[3,256,128]{2,1,0:T(8,128)(2,1)S(1)} %join.2.refs_1_), channel_id=1, source_target_pairs={{0,2},{1,3},{2,0},{3,1},{4,6},{5,7},{6,4},{7,5},{8,10},{9,11},{10,... | collective-permute-start | bytes 589832 | tf_op jit(solution)/shard_map/ppermute | solution.py:599
  59.0 7.7 %collective-permute-start.18 = (bf16[3,256,128]{2,1,0:T(8,128)(2,1)S(1)}, bf16[3,256,128]{2,1,0:T(8,128)(2,1)S(1)}, u32[]{:S(2)}, u32[]{:S(2)}) collective-permute-start(bf16[3,256,128]{2,1,0:T(8,128)(2,1)S(1)} %join.2.refs_1_), channel_id=1, source_target_pairs={{0,1},{1,0},{2,3},{3,2},{4,5},{5,4},{6,7},{7,6},{8,9},{9,8},{10,11... | collective-permute-start | bytes 589832 | tf_op jit(solution)/shard_map/ppermute | solution.py:595
  70.2 3.9 %collective-permute-start.21 = (f32[512,256]{1,0:T(8,128)S(1)}, f32[512,256]{1,0:T(8,128)S(1)}, u32[]{:S(2)}, u32[]{:S(2)}) collective-permute-start(f32[512,256]{1,0:T(8,128)S(1)} %get-tuple-element.78), channel_id=1, source_target_pairs={{0,1},{1,0},{2,3},{3,2},{4,5},{5,4},{6,7},{7,6},{8,9},{9,8},{10,11... | collective-permute-start | bytes 1572872 | tf_op jit(solution)/shard_map/ppermute | solution.py:595
  72.0 6.6 %collective-permute-start.24 = (s16[272,256]{1,0:T(8,128)(2,1)S(1)}, s16[272,256]{1,0:T(8,128)(2,1)S(1)}, u32[]{:S(2)}, u32[]{:S(2)}) collective-permute-start(s16[272,256]{1,0:T(8,128)(2,1)S(1)} %get-tuple-element.83), channel_id=1, source_target_pairs={{0,2},{1,3},{2,0},{3,1},{4,6},{5,7},{6,4},{7,5},{8,10},{9,11},{10,... | collective-permute-start | bytes 417800 | tf_op jit(solution)/shard_map/ppermute | solution.py:599
  72.6 8.3 %collective-permute-start.23 = (s16[272,256]{1,0:T(8,128)(2,1)S(1)}, s16[272,256]{1,0:T(8,128)(2,1)S(1)}, u32[]{:S(2)}, u32[]{:S(2)}) collective-permute-start(s16[272,256]{1,0:T(8,128)(2,1)S(1)} %get-tuple-element.82), channel_id=1, source_target_pairs={{0,2},{1,3},{2,0},{3,1},{4,6},{5,7},{6,4},{7,5},{8,10},{9,11},{10,... | collective-permute-start | bytes 417800 | tf_op jit(solution)/shard_map/ppermute | solution.py:599
  78.7 7.0 %collective-permute-start.25 = (s16[144,256]{1,0:T(8,128)(2,1)S(1)}, s16[144,256]{1,0:T(8,128)(2,1)S(1)}, u32[]{:S(2)}, u32[]{:S(2)}) collective-permute-start(s16[144,256]{1,0:T(8,128)(2,1)S(1)} %get-tuple-element.87), channel_id=1, source_target_pairs={{0,8},{1,9},{2,10},{3,11},{4,12},{5,13},{6,14},{7,15},{8,0},{9,1},... | collective-permute-start | bytes 221192 | tf_op jit(solution)/shard_map/ppermute | solution.py:603
  78.8 6.9 %collective-permute-start.26 = (s16[144,256]{1,0:T(8,128)(2,1)S(1)}, s16[144,256]{1,0:T(8,128)(2,1)S(1)}, u32[]{:S(2)}, u32[]{:S(2)}) collective-permute-start(s16[144,256]{1,0:T(8,128)(2,1)S(1)} %get-tuple-element.88), channel_id=1, source_target_pairs={{0,4},{1,5},{2,6},{3,7},{4,8},{5,9},{6,10},{7,11},{8,12},{9,13},{1... | collective-permute-start | bytes 221192 | tf_op jit(solution)/shard_map/ppermute | solution.py:603
  81.0 5.5 %collective-permute-start.27 = (s16[144,256]{1,0:T(8,128)(2,1)S(1)}, s16[144,256]{1,0:T(8,128)(2,1)S(1)}, u32[]{:S(2)}, u32[]{:S(2)}) collective-permute-start(s16[144,256]{1,0:T(8,128)(2,1)S(1)} %get-tuple-element.89), channel_id=1, source_target_pairs={{0,12},{1,13},{2,14},{3,15},{4,0},{5,1},{6,2},{7,3},{8,4},{9,5},{1... | collective-permute-start | bytes 221192 | tf_op jit(solution)/shard_map/ppermute | solution.py:603
  90.1 8.1 %collective-permute-start.32 = (bf16[256,128]{1,0:T(8,128)(2,1)S(1)}, bf16[256,128]{1,0:T(8,128)(2,1)S(1)}, u32[]{:S(2)}, u32[]{:S(2)}) collective-permute-start(bf16[256,128]{1,0:T(8,128)(2,1)S(1)} %get-tuple-element.91.refs_0_), channel_id=1, source_target_pairs={{0,1},{1,0},{2,3},{3,2},{4,5},{5,4},{6,7},{7,6},{8,9},{9,8},{10,11... | collective-permute-start | bytes 196616 | tf_op jit(solution)/shard_map/ppermute | solution.py:595
  90.2 8.1 %collective-permute-start.31 = (bf16[256,128]{1,0:T(8,128)(2,1)S(1)}, bf16[256,128]{1,0:T(8,128)(2,1)S(1)}, u32[]{:S(2)}, u32[]{:S(2)}) collective-permute-start(bf16[256,128]{1,0:T(8,128)(2,1)S(1)} %get-tuple-element.91.refs_0_), channel_id=1, source_target_pairs={{0,2},{1,3},{2,0},{3,1},{4,6},{5,7},{6,4},{7,5},{8,10},{9,11},{10,... | collective-permute-start | bytes 196616 | tf_op jit(solution)/shard_map/ppermute | solution.py:599
  90.8 7.5 %collective-permute-start.30 = (bf16[256,128]{1,0:T(8,128)(2,1)S(1)}, bf16[256,128]{1,0:T(8,128)(2,1)S(1)}, u32[]{:S(2)}, u32[]{:S(2)}) collective-permute-start(bf16[256,128]{1,0:T(8,128)(2,1)S(1)} %get-tuple-element.91.refs_0_), channel_id=1, source_target_pairs={{0,4},{1,5},{2,6},{3,7},{4,8},{5,9},{6,10},{7,11},{8,12},{9,13},{1... | collective-permute-start | bytes 196616 | tf_op jit(solution)/shard_map/ppermute | solution.py:603
  91.3 6.9 %collective-permute-start.29 = (bf16[256,128]{1,0:T(8,128)(2,1)S(1)}, bf16[256,128]{1,0:T(8,128)(2,1)S(1)}, u32[]{:S(2)}, u32[]{:S(2)}) collective-permute-start(bf16[256,128]{1,0:T(8,128)(2,1)S(1)} %get-tuple-element.91.refs_0_), channel_id=1, source_target_pairs={{0,12},{1,13},{2,14},{3,15},{4,0},{5,1},{6,2},{7,3},{8,4},{9,5},{1... | collective-permute-start | bytes 196616 | tf_op jit(solution)/shard_map/ppermute | solution.py:603
  94.6 5.7 %collective-permute-start.28 = (bf16[256,128]{1,0:T(8,128)(2,1)S(1)}, bf16[256,128]{1,0:T(8,128)(2,1)S(1)}, u32[]{:S(2)}, u32[]{:S(2)}) collective-permute-start(bf16[256,128]{1,0:T(8,128)(2,1)S(1)} %get-tuple-element.91.refs_0_), channel_id=1, source_target_pairs={{0,8},{1,9},{2,10},{3,11},{4,12},{5,13},{6,14},{7,15},{8,0},{9,1},... | collective-permute-start | bytes 196616 | tf_op jit(solution)/shard_map/ppermute | solution.py:603
  100.4 6.3 %collective-permute-start.33 = (bf16[3,256,128]{2,1,0:T(8,128)(2,1)S(1)}, bf16[3,256,128]{2,1,0:T(8,128)(2,1)S(1)}, u32[]{:S(2)}, u32[]{:S(2)}) collective-permute-start(bf16[3,256,128]{2,1,0:T(8,128)(2,1)S(1)} %join.3.refs_1_), channel_id=1, source_target_pairs={{0,2},{1,3},{2,0},{3,1},{4,6},{5,7},{6,4},{7,5},{8,10},{9,11},{10,... | collective-permute-start | bytes 589832 | tf_op jit(solution)/shard_map/ppermute | solution.py:599
  101.9 6.3 %collective-permute-start.34 = (bf16[3,256,128]{2,1,0:T(8,128)(2,1)S(1)}, bf16[3,256,128]{2,1,0:T(8,128)(2,1)S(1)}, u32[]{:S(2)}, u32[]{:S(2)}) collective-permute-start(bf16[3,256,128]{2,1,0:T(8,128)(2,1)S(1)} %join.3.refs_1_), channel_id=1, source_target_pairs={{0,1},{1,0},{2,3},{3,2},{4,5},{5,4},{6,7},{7,6},{8,9},{9,8},{10,11... | collective-permute-start | bytes 589832 | tf_op jit(solution)/shard_map/ppermute | solution.py:595
  117.3 4.5 %collective-permute-start.40 = (f32[8,256]{1,0:T(8,128)S(1)}, f32[8,256]{1,0:T(8,128)S(1)}, u32[]{:S(2)}, u32[]{:S(2)}) collective-permute-start(f32[8,256]{1,0:T(8,128)S(1)} %add.18.refs_0_), channel_id=1, source_target_pairs={{0,8},{1,9},{2,10},{3,11},{4,12},{5,13},{6,14},{7,15},{8,0},{9,1},... | collective-permute-start | bytes 24584 | tf_op jit(solution)/shard_map/ppermute | solution.py:603
  117.3 5.4 %collective-permute-start.39 = (f32[8,256]{1,0:T(8,128)S(1)}, f32[8,256]{1,0:T(8,128)S(1)}, u32[]{:S(2)}, u32[]{:S(2)}) collective-permute-start(f32[8,256]{1,0:T(8,128)S(1)} %add.18.refs_0_), channel_id=1, source_target_pairs={{0,4},{1,5},{2,6},{3,7},{4,8},{5,9},{6,10},{7,11},{8,12},{9,13},{1... | collective-permute-start | bytes 24584 | tf_op jit(solution)/shard_map/ppermute | solution.py:603
  (18 other events, 107.4 us)

commit v5 on v4

--- a/solution.py
+++ b/solution.py
@@ -53,6 +53,7 @@
 
 
 STEPS = 4
+CHIPS = GROUP // 2
 ORDER = (2, 1, 3, 0)
 PARTS = ((0, 0), (1, 0), (0, 1), (1, 1))
 HEAD = 16
@@ -67,16 +68,15 @@
     return (lax.rem(z + ORDER[i % STEPS], STEPS) * 2 + y) * 2 + c
 
 
-def places(me_ref, list_refs, slots):
+def places(me_ref, lists_ref, slots):
     slots = jnp.concatenate([slots, slots], axis=0)
     from_owner = jnp.right_shift(slots, 7)
     within = jnp.bitwise_and(slots, LANES - 1)
     rows = jnp.zeros(slots.shape, jnp.int32)
     for i in range(GROUP):
         o = owner_at(me_ref, i)
-        dy, dc = PARTS[i // STEPS]
-        held = list_refs[-ORDER[i % STEPS] % STEPS]
-        row = jnp.broadcast_to(held[2 * dy + dc : 2 * dy + dc + 1, :], slots.shape)
+        dc = PARTS[i // STEPS][1]
+        row = jnp.broadcast_to(lists_ref[jnp.right_shift(o, 1), dc : dc + 1, :], slots.shape)
         column = jnp.take_along_axis(row, within, axis=1, mode="promise_in_bounds")
         rows = jnp.where(from_owner == o, column + i * LANES, rows)
     return rows[: slots.shape[0] // 2]
@@ -105,14 +105,14 @@
 
 
 def far_kernel(grouped, me_ref, *refs):
-    list_refs, refs = refs[: 4 * grouped], refs[4 * grouped :]
+    lists_ref, refs = (refs[0], refs[1:]) if grouped else (None, refs)
     both_ref, wh_ref, wl_ref, *refs = refs
     ids_ref, weight_ref, at_ref, ya_ref, yb_ref, lo_s = refs
     sources = ids_ref.shape[0]
     for j in range(ids_ref.shape[1] // LANES):
         lanes = pl.ds(j * LANES, LANES)
         slots = both_ref[:sources, lanes].astype(jnp.int32)
-        ids_ref[:, lanes] = places(me_ref, list_refs, slots) if grouped else slots
+        ids_ref[:, lanes] = places(me_ref, lists_ref, slots) if grouped else slots
         weight_ref[:, lanes] = both_ref[sources:, lanes]
     half = at_ref.shape[0]
     build_rows(ids_ref, weight_ref, wh_ref, wl_ref, at_ref, [ya_ref, yb_ref], lo_s, half)
@@ -147,48 +147,51 @@
 
 
 def pick_kernel(me_ref, lists_ref, near_ref, far_ref):
-    z, y, c = me_ref[0], me_ref[1], me_ref[2]
-    for dy in range(2):
-        for k in range(STEPS):
-            there = (lax.rem(z + k, STEPS) * 2 + (y if dy == 0 else 1 - y)) * 2
-            row = slice(dy * STEPS + k, dy * STEPS + k + 1)
-            near_ref[row, :] = lists_ref[pl.ds(there + c, 1), :]
-            far_ref[row, :] = lists_ref[pl.ds(there + 1 - c, 1), :]
-
-
-def mix_y_kernel(near_ref, got_ref, near_y_ref, far_y_ref):
-    for i, held in enumerate((near_ref, got_ref)):
-        rows = slice(i * STEPS, (i + 1) * STEPS)
-        near_y_ref[rows, :] = held[:STEPS, :]
-        far_y_ref[rows, :] = held[STEPS:, :]
-
-
-def mix_z_kernel(near_ref, got_ref, *outs):
-    for k, out in enumerate(outs):
-        out[...] = jnp.zeros_like(out)
+    c = me_ref[2]
+    for chip in range(CHIPS):
+        row = slice(chip, chip + 1)
+        near_ref[row, :] = lists_ref[pl.ds(2 * chip + c, 1), :]
+        far_ref[row, :] = lists_ref[pl.ds(2 * chip + 1 - c, 1), :]
+
+
+def mix_kernel(near_ref, got_ref, out_ref):
+    out_ref[...] = jnp.zeros_like(out_ref)
+    for chip in range(CHIPS):
         for i, held in enumerate((near_ref, got_ref)):
-            for c in range(2):
-                row = c * STEPS + k
-                out[2 * i + c : 2 * i + c + 1, :] = held[row : row + 1, :]
-
-
-def small(kernel, n, name, *args, scalars=0):
+            out_ref[chip, i : i + 1, :] = held[chip : chip + 1, :]
+
+
+def spread_kernel(a_ref, b_ref, out_ref):
+    total = a_ref[...] + b_ref[...]
+    for chip in range(CHIPS):
+        out_ref[chip] = total
+
+
+def small(kernel, out, name, *args, scalars=0):
     return pl.pallas_call(
         kernel,
         in_specs=[SMEM] * scalars + [VMEM] * (len(args) - scalars),
-        out_specs=[VMEM] * n,
-        out_shape=[shape((8, LANES), jnp.int32)] * n,
+        out_specs=[VMEM] * len(out),
+        out_shape=out,
         compiler_params=params(8),
         cost_estimate=cost(1e4, 3e4),
         name=name,
     )(*args)
 
 
+def over_chips(x):
+    groups = [list(range(c, GROUP, 2)) for c in range(2)]
+    return lax.all_to_all(
+        x, "space", split_axis=0, concat_axis=0, axis_index_groups=groups, tiled=True
+    )
+
+
 def exchange_lists(me, lists):
-    near, far = small(pick_kernel, 2, "pick", me, lists, scalars=1)
-    near, far = small(mix_y_kernel, 2, "mix_y", near, over_core(far))
-    own, *sent = small(mix_z_kernel, STEPS, "mix_z", near, over_y(far))
-    return [own] + [over_z(sent[k - 1], k) for k in range(1, STEPS)]
+    one = shape((CHIPS, LANES), jnp.int32)
+    near, far = small(pick_kernel, [one, one], "pick", me, lists, scalars=1)
+    out = shape((CHIPS, 8, LANES), jnp.int32)
+    (both,) = small(mix_kernel, [out], "mix", near, over_core(far))
+    return [over_chips(both)]
 
 
 def exponent(m):
@@ -424,7 +427,7 @@
     )(*args)
 
 
-def project_kernel(e_ref, y_ref, t_ref, g_ref, token_ref, even_s, odd_s):
+def project_kernel(e_ref, y_ref, t_ref, after_ref, g_ref, token_ref, even_s, odd_s):
     columns, members, width = e_ref.shape
     lanes = BATCH // 2 * LANES
     token_ref[...] = jnp.zeros_like(token_ref)
@@ -443,19 +446,19 @@
             g_ref[:, pl.ds(at, LANES)] = r[pair * members : (pair + 1) * members]
 
 
-def project(ens, y, taps):
+def project(ens, y, taps, after):
     columns, members, width = ens.shape
     levels = width // VAR
     return pl.pallas_call(
         project_kernel,
-        in_specs=[VMEM] * 3,
+        in_specs=[VMEM] * 4,
         out_specs=[VMEM] * 2,
         out_shape=[shape((members, columns * levels), F32), shape((8, LANES), F32)],
         scratch_shapes=[pltpu.VMEM((BATCH // 2 * members, width), BF)] * 2,
         compiler_params=params(16),
         cost_estimate=cost(2 * columns * members * width * width, 8e6),
         name="project",
-    )(ens, y, taps)
+    )(ens, y, taps, after)
 
 
 def lay_out(x_refs, xs):
@@ -547,11 +550,11 @@
 OUT_CUTS = 4
 
 
-def result_kernel(count, l0_ref, *refs):
-    sums = refs[0][...]
-    for r in refs[1:count]:
-        sums = sums + r[...]
-    g0_ref, g1_ref, i0_ref, i1_ref, control_hbm, increment_hbm, c_s, i_s, sem = refs[count:]
+def result_kernel(l0_ref, sums_ref, *refs):
+    sums = sums_ref[0]
+    for i in range(1, sums_ref.shape[0]):
+        sums = sums + sums_ref[i]
+    g0_ref, g1_ref, i0_ref, i1_ref, control_hbm, increment_hbm, c_s, i_s, sem = refs
     l0 = -l0_ref[0:1, 0:1]
     l1, _ = length_of(sums)
     lanes = c_s.shape[1] // OUT_CUTS
@@ -576,8 +579,8 @@
 
 def result(l0, sums, g0, g1, im0, im1):
     return pl.pallas_call(
-        functools.partial(result_kernel, len(sums)),
-        in_specs=[VMEM] * (5 + len(sums)),
+        result_kernel,
+        in_specs=[VMEM] * 6,
         out_specs=[ANY] * 2,
         out_shape=[shape(g0.shape, F32), shape(im0.shape, F32)],
         scratch_shapes=[
@@ -588,7 +591,7 @@
         compiler_params=params(16),
         cost_estimate=cost(3 * g0.size, 1e7),
         name="result",
-    )(l0, *sums, g0, g1, im0, im1)
+    )(l0, sums, g0, g1, im0, im1)
 
 
 def over_core(x):
@@ -615,20 +618,27 @@
     return own, got + [over_z(three, 3)], (s[0] if s else None)
 
 
-def gather_columns(x, after):
+def relay_kernel(x_ref, after_ref, out_ref):
+    out_ref[...] = x_ref[...]
+
+
+def gather_columns(x, work):
     two, three, one = over_z(x, 2), over_z(x, 3), over_z(x, 1)
     y_own = over_y(x)
     c_own = over_core(x)
-    rest = join([two, three, one], y_own, c_own, after)
+    rest = join([two, three, one], y_own, c_own)
     y_rest = over_y(rest)
     c_rest = over_core(rest)
-    return [x, rest, y_own, y_rest, c_own, c_rest, over_core(y_own), over_core(y_rest)]
+    cy_own = over_core(y_own)
+    done, token = work(rest)
+    (y_rest,) = small(relay_kernel, [shape(rest.shape, BF)], "relay", y_rest, token)
+    return [x, rest, y_own, y_rest, c_own, c_rest, cy_own, over_core(y_rest)], done
 
 
 def sum_all(x):
-    x = x + over_core(x)
-    x = x + over_y(x)
-    return [x] + [over_z(x, k) for k in range(1, STEPS)]
+    out = shape((CHIPS,) + x.shape, F32)
+    (both,) = small(spread_kernel, [out], "spread", x, over_core(x))
+    return over_chips(both)
 
 
 def on_device(ensemble, innovation, obs_weight, interp_weight, slot_of, intersection_list):
@@ -675,23 +685,23 @@
                 sums = lax.psum(sums, "space")
             return dot(hit.T, high) + dot(hit.T, low), [], sums
 
-        def gather(x, after):
-            return [swap(dot(hit, x.T).astype(BF)).T]
+        def gather(x, work):
+            return [swap(dot(hit, x.T).astype(BF)).T], work(x)[0]
 
         def add_up(x):
-            return [lax.psum(x, "space")]
+            return lax.psum(x, "space")[None]
 
     ids, weight, far, c0, c1 = adjoint_half(slots, [named, wh, wl], (grouped, me, lists if grouped else []))
     near, n0, n1 = adjoint_half(slots, [ids, weight, wh, wl])
     own, got, _ = scatter([n0, n1, c0, c1])
     x0, y0, g_sums = coarse_image(ensemble, kern, own, got)
     ens = jnp.transpose(ensemble, (1, 0, 2))
-    g0, token = project(ens, y0, taps)
-    im0, sums, *second = image_first(gather(x0, token), near, far, obs_weight, g_sums)
+    xs, g0 = gather(x0, lambda after: project(ens, y0, taps, after))
+    im0, sums, *second = image_first(xs, near, far, obs_weight, g_sums)
     own, got, sums = scatter(second, sums)
     x1, y1, l0, g_sums = coarse_image(ensemble, kern, own, got, y0, sums)
-    g1, token = project(ens, y1, taps)
-    im1, sums = image_second(gather(x1, token), near, far, obs_weight, g_sums)
+    xs, g1 = gather(x1, lambda after: project(ens, y1, taps, after))
+    im1, sums = image_second(xs, near, far, obs_weight, g_sums)
     return tuple(result(l0, add_up(sums), g0, g1, im0, im1))
 
 

time: 125 us -> 128 us (1.024)
  blocking collectives: 0 us -> 11.4 us
  starting transfers between devices: 41.6 us -> 32.6 us
    ppermute x18 -> x12, starting transfers between devices: 25.6 us -> 13.9 us  [over_z(): lax.ppermute(x, 'space', [(i, (i + 4 * k) % GROUP) for i in range(GROUP)])]
    all_to_all x0 -> x1, blocking collectives: none -> 11.4 us  [over_chips(): lax.all_to_all(x, 'space', split_axis=0, concat_axis=0, axis_index_groups...]
    ppermute x10 -> x8, waiting for transfers between devices: 23.1 us -> 11.7 us  [over_y(): return lax.ppermute(x, 'space', [(i, i ^ 2) for i in range(GROUP)])]
    all_to_all x0 -> x1, starting transfers between devices: none -> 6.85 us  [over_chips(): lax.all_to_all(x, 'space', split_axis=0, concat_axis=0, axis_index_groups...]
    all_to_all x0 -> x1, waiting for transfers between devices: none -> 6.66 us  [over_chips(): lax.all_to_all(x, 'space', split_axis=0, concat_axis=0, axis_index_groups...]
    ppermute x18 -> x12, waiting for transfers between devices: 16.1 us -> 21.1 us  [over_z(): lax.ppermute(x, 'space', [(i, (i + 4 * k) % GROUP) for i in range(GROUP)])]
    ppermute x10 -> x8, starting transfers between devices: 12.9 us -> 8.49 us  [over_y(): return lax.ppermute(x, 'space', [(i, i ^ 2) for i in range(GROUP)])]
  transfers between devices with their start and end apart: 42 -> 35, of which waited for: 21 -> 17; matrix products, arithmetic and copies ran while one was open for 4% -> 4% of each run, Pallas kernels for 10% -> 10%
where the time goes in v5:
time: 128 us
  waiting for transfers between devices  44.1 us (34%)
  Pallas kernels  33.1 us (26%)
  starting transfers between devices  32.6 us (25%)
  blocking collectives  11.4 us (9%)
  local copies, waits for them, and re-layouts  3.71 us (3%)
  other arithmetic  1.61 us (1%)
    ppermute x12, waiting for transfers between devices, over_z(): lax.ppermute(x, 'space', [(i, (i + 4 * k) % GROUP) for i in range(GROUP)])  21.1 us
    ppermute x12, starting transfers between devices, over_z(): lax.ppermute(x, 'space', [(i, (i + 4 * k) % GROUP) for i in range(GROUP)])  13.9 us
    ppermute x8, waiting for transfers between devices, over_y(): return lax.ppermute(x, 'space', [(i, i ^ 2) for i in range(GROUP)])  11.7 us
    all_to_all x1, blocking collectives, over_chips(): lax.all_to_all(x, 'space', split_axis=0, concat_axis=0, axis_index_groups...  11.4 us
    pallas_call x2, Pallas kernels, adjoint_half(): pl.pallas_call(kernel, in_specs=([SMEM] if head else []) + [VMEM] * (len(...  9.61 us
    ppermute x8, starting transfers between devices, over_y(): return lax.ppermute(x, 'space', [(i, i ^ 2) for i in range(GROUP)])  8.49 us
    pallas_call x2, Pallas kernels, project(): pl.pallas_call(project_kernel, in_specs=[VMEM] * 4, out_specs=[VMEM] * 2,...  7.26 us
    pallas_call x2, Pallas kernels, coarse_image(): pl.pallas_call(functools.partial(coarse_kernel, len(got), second), in_spe...  7.03 us
  transfers between devices with their start and end apart: 35, of which 17 were waited for; matrix products, arithmetic and copies ran while one was open for 4% of the time, Pallas kernels for 10%

profile of v5, /device:TPU:0, one launch (start us, length us, event | category | flops | bytes accessed | tf_op | source)
XLA Modules:
  0.0 127.7 jit_solution(15937131900768048113)
XLA Ops:
  2.5 1.5 %fusion = (bf16[1152,256]{1,0:T(8,128)(2,1)S(1)}, bf16[1152,256]{1,0:T(8,128)(2,1)S(1)}) fusion(bf16[1152,256]{1,0:T(8,128)(2,1)} %param.9, bf16[1152,256]{1,0:T(8,128)(2,1)} %refs_10_.3), kind=kLoop, calls=%fused_computation.3 | loop fusion | flops 2359296 | bytes 2359296 | tf_op jit(solution)/shard_map/convert_element_type | solution.py:666
  4.7 6.8 %all-to-all-start = ((s32[8,8,128]{2,1,0:T(8,128)}), s32[8,8,128]{2,1,0:T(8,128)S(1)}, u32[]{:S(2)}, u32[]{:S(2)}) async-start(s32[8,8,128]{2,1,0:T(8,128)} %mix.1), calls=%async_computation | async-start | bytes 65536 | tf_op jit(solution)/shard_map/all_to_all | solution.py:184
  11.6 6.7 %all-to-all-done.refs_0_ = s32[8,8,128]{2,1,0:T(8,128)S(1)} async-done(((s32[8,8,128]{2,1,0:T(8,128)}), s32[8,8,128]{2,1,0:T(8,128)S(1)}, u32[]{:S(2)}, u32[]{:S(2)}) %all-to-all-start) | async-done | bytes 32800 | tf_op jit(solution)/shard_map/all_to_all | solution.py:184
  18.3 5.2 %adjoint_far.1 = (s32[4,1152]{1,0:T(4,128)S(1)}, f32[4,1152]{1,0:T(4,128)S(1)}, bf16[1024,1152]{1,0:T(8,128)(2,1)S(1)}, f32[512,256]{1,0:T(8,128)S(1)}, f32[512,256]{1,0:T(8,128)S(1)}) custom-call(s32[4]{0:T(128)S(1)} %pad_add_fusion.me_ref, s32[8,8,128]{2,1,0:T(8,128)S(1)} %all-to-all-done.refs_0_, f32[8,1152]{1,0:T(8,128)S(1)} %pad_maximum_fusion.refs_1_, ...), custom_call_target="tpu_custom_call" | custom-call | flops 1811939328 | bytes 4000000 | tf_op jit(solution)/shard_map/adjoint_far/pallas_call | solution.py:137
  24.1 4.4 %adjoint_near.1 = (bf16[1024,1152]{1,0:T(8,128)(2,1)S(1)}, f32[512,256]{1,0:T(8,128)S(1)}, f32[512,256]{1,0:T(8,128)S(1)}) custom-call(s32[4,1152]{1,0:T(4,128)S(1)} %get-tuple-element.47.ids_ref, f32[4,1152]{1,0:T(4,128)S(1)} %get-tuple-element.48.weight_ref, bf16[1152,256]{1,0:T(8,128)(2,1)S(1)} %get-tuple-element.89.refs_2_.wh_ref, ...), custom_call_target="tpu_custom_call" | custom-call | flops 1811939328 | bytes 4000000 | tf_op jit(solution)/shard_map/adjoint_near/pallas_call | solution.py:137
  29.1 1.6 %collective-permute-start.4 = (s16[272,256]{1,0:T(8,128)(2,1)S(1)}, s16[272,256]{1,0:T(8,128)(2,1)S(1)}, u32[]{:S(2)}, u32[]{:S(2)}) collective-permute-start(s16[272,256]{1,0:T(8,128)(2,1)S(1)} %get-tuple-element.55), channel_id=1, source_target_pairs={{0,2},{1,3},{2,0},{3,1},{4,6},{5,7},{6,4},{7,5},{8,10},{9,11},{10,... | collective-permute-start | bytes 417800 | tf_op jit(solution)/shard_map/ppermute | solution.py:602
  30.7 4.5 %collective-permute-done.3.p_ref = s16[272,256]{1,0:T(8,128)(2,1)S(1)} collective-permute-done((s16[272,256]{1,0:T(8,128)(2,1)S(1)}, s16[272,256]{1,0:T(8,128)(2,1)S(1)}, u32[]{:S(2)}, u32[]{:S(2)}) %collective-permute-start.3) | collective-permute-done | bytes 139296 | tf_op jit(solution)/shard_map/ppermute | solution.py:602
  35.9 1.4 %collective-permute-done.4.p_ref = s16[272,256]{1,0:T(8,128)(2,1)S(1)} collective-permute-done((s16[272,256]{1,0:T(8,128)(2,1)S(1)}, s16[272,256]{1,0:T(8,128)(2,1)S(1)}, u32[]{:S(2)}, u32[]{:S(2)}) %collective-permute-start.4) | collective-permute-done | bytes 139296 | tf_op jit(solution)/shard_map/ppermute | solution.py:602
  39.7 5.1 %collective-permute-done.5.refs_0_ = s16[144,256]{1,0:T(8,128)(2,1)S(1)} collective-permute-done((s16[144,256]{1,0:T(8,128)(2,1)S(1)}, s16[144,256]{1,0:T(8,128)(2,1)S(1)}, u32[]{:S(2)}, u32[]{:S(2)}) %collective-permute-start.5) | collective-permute-done | bytes 73760 | tf_op jit(solution)/shard_map/ppermute | solution.py:606
  44.8 3.5 %coarse_first.1 = (bf16[256,128]{1,0:T(8,128)(2,1)S(1)}, f32[128,256]{1,0:T(8,128)S(1)}, f32[8,256]{1,0:T(8,128)S(1)}) custom-call(bf16[80,128,256]{2,1,0:T(8,128)(2,1)S(1)} %bitcast.9, bf16[256,256]{1,0:T(8,128)(2,1)S(1)} %copy-done.2, f32[128,256]{1,0:T(8,128)S(1)} %get-tuple-element.54.own_ref, s16[144,256]{1,0:T(8,128)(2,1)S(1)} %collective-permute-done.5.refs_0_, ...), custom_call_target="tpu_custom_call" | custom-call | flops 1342177280 | bytes 5000000 | tf_op jit(solution)/shard_map/coarse_first/pallas_call | solution.py:414
  49.1 3.8 %collective-permute-start.9 = (bf16[256,128]{1,0:T(8,128)(2,1)S(1)}, bf16[256,128]{1,0:T(8,128)(2,1)S(1)}, u32[]{:S(2)}, u32[]{:S(2)}) collective-permute-start(bf16[256,128]{1,0:T(8,128)(2,1)S(1)} %get-tuple-element.59.refs_0_), channel_id=1, source_target_pairs={{0,12},{1,13},{2,14},{3,15},{4,0},{5,1},{6,2},{7,3},{8,4},{9,5},{1... | collective-permute-start | bytes 196616 | tf_op jit(solution)/shard_map/ppermute | solution.py:606
  52.9 2.9 %collective-permute-done.10.refs_2_ = bf16[256,128]{1,0:T(8,128)(2,1)S(1)} collective-permute-done((bf16[256,128]{1,0:T(8,128)(2,1)S(1)}, bf16[256,128]{1,0:T(8,128)(2,1)S(1)}, u32[]{:S(2)}, u32[]{:S(2)}) %collective-permute-start.10) | collective-permute-done | bytes 65568 | tf_op jit(solution)/shard_map/ppermute | solution.py:606
  55.8 2.8 %collective-permute-done.8.refs_0_ = bf16[256,128]{1,0:T(8,128)(2,1)S(1)} collective-permute-done((bf16[256,128]{1,0:T(8,128)(2,1)S(1)}, bf16[256,128]{1,0:T(8,128)(2,1)S(1)}, u32[]{:S(2)}, u32[]{:S(2)}) %collective-permute-start.8) | collective-permute-done | bytes 65568 | tf_op jit(solution)/shard_map/ppermute | solution.py:606
  58.7 1.4 %collective-permute-start.13 = (bf16[3,256,128]{2,1,0:T(8,128)(2,1)S(1)}, bf16[3,256,128]{2,1,0:T(8,128)(2,1)S(1)}, u32[]{:S(2)}, u32[]{:S(2)}) collective-permute-start(bf16[3,256,128]{2,1,0:T(8,128)(2,1)S(1)} %join.2.after_ref.refs_1_), channel_id=1, source_target_pairs={{0,2},{1,3},{2,0},{3,1},{4,6},{5,7},{6,4},{7,5},{8,10},{9,11},{10,... | collective-permute-start | bytes 589832 | tf_op jit(solution)/shard_map/ppermute | solution.py:602
  60.1 3.0 %copy.12 = bf16[80,128,256]{2,0,1:T(8,128)(2,1)S(1)} copy(bf16[80,128,256]{2,1,0:T(8,128)(2,1)S(1)} %bitcast.9) | data formatting | bytes 10485760 | tf_op args[0]
  63.2 3.6 %project.2 = (f32[80,8192]{1,0:T(8,128)S(1)}, f32[8,128]{1,0:T(8,128)S(1)}) custom-call(bf16[128,80,256]{2,1,0:T(8,128)(2,1)S(1)} %bitcast.10, f32[128,256]{1,0:T(8,128)S(1)} %get-tuple-element.60.y_ref.refs_3_, bf16[2,256,128]{2,1,0:T(8,128)(2,1)S(1)} %copy-done.1, bf16[3,256,128]{2,1,0:T(8,128)(2,1)S(1)} %join.2.after_ref.refs_1_), custom_call_target="tpu_custom_call" | custom-call | flops 1342177280 | bytes 8000000 | tf_op jit(solution)/shard_map/project/pallas_call | solution.py:452
  68.6 3.2 %image_first.1 = (f32[1152,256]{1,0:T(8,128)S(1)}, f32[8,256]{1,0:T(8,128)S(1)}, f32[512,256]{1,0:T(8,128)S(1)}, f32[512,256]{1,0:T(8,128)S(1)}, f32[512,256]{1,0:T(8,128)S(1)}, /*index=5*/f32[520,256]{1,0:T(8,128)S(1)}) custom-call(bf16[256,128]{1,0:T(8,128)(2,1)S(1)} %get-tuple-element.59.refs_0_, bf16[3,256,128]{2,1,0:T(8,128)(2,1)S(1)} %join.2.after_ref.refs_1_, ...), custom_call_target="tpu_custom_call" | custom-call | flops 2415919104 | bytes 13000000 | tf_op jit(solution)/shard_map/image_first/pallas_call | solution.py:512
  72.4 1.4 %collective-permute-done.18.refs_1_ = f32[520,256]{1,0:T(8,128)S(1)} collective-permute-done((f32[520,256]{1,0:T(8,128)S(1)}, f32[520,256]{1,0:T(8,128)S(1)}, u32[]{:S(2)}, u32[]{:S(2)}) %collective-permute-start.18) | collective-permute-done | bytes 532512 | tf_op jit(solution)/shard_map/ppermute | solution.py:598
  74.7 1.4 %collective-permute-start.19 = (s16[272,256]{1,0:T(8,128)(2,1)S(1)}, s16[272,256]{1,0:T(8,128)(2,1)S(1)}, u32[]{:S(2)}, u32[]{:S(2)}) collective-permute-start(s16[272,256]{1,0:T(8,128)(2,1)S(1)} %get-tuple-element.70), channel_id=1, source_target_pairs={{0,2},{1,3},{2,0},{3,1},{4,6},{5,7},{6,4},{7,5},{8,10},{9,11},{10,... | collective-permute-start | bytes 417800 | tf_op jit(solution)/shard_map/ppermute | solution.py:602
  76.1 4.5 %collective-permute-done.20.p_ref = s16[272,256]{1,0:T(8,128)(2,1)S(1)} collective-permute-done((s16[272,256]{1,0:T(8,128)(2,1)S(1)}, s16[272,256]{1,0:T(8,128)(2,1)S(1)}, u32[]{:S(2)}, u32[]{:S(2)}) %collective-permute-start.20) | collective-permute-done | bytes 139296 | tf_op jit(solution)/shard_map/ppermute | solution.py:602
  81.3 2.1 %collective-permute-start.22 = (s16[144,256]{1,0:T(8,128)(2,1)S(1)}, s16[144,256]{1,0:T(8,128)(2,1)S(1)}, u32[]{:S(2)}, u32[]{:S(2)}) collective-permute-start(s16[144,256]{1,0:T(8,128)(2,1)S(1)} %get-tuple-element.76), channel_id=1, source_target_pairs={{0,4},{1,5},{2,6},{3,7},{4,8},{5,9},{6,10},{7,11},{8,12},{9,13},{1... | collective-permute-start | bytes 221192 | tf_op jit(solution)/shard_map/ppermute | solution.py:606
  83.4 1.8 %collective-permute-start.23 = (s16[144,256]{1,0:T(8,128)(2,1)S(1)}, s16[144,256]{1,0:T(8,128)(2,1)S(1)}, u32[]{:S(2)}, u32[]{:S(2)}) collective-permute-start(s16[144,256]{1,0:T(8,128)(2,1)S(1)} %get-tuple-element.77), channel_id=1, source_target_pairs={{0,12},{1,13},{2,14},{3,15},{4,0},{5,1},{6,2},{7,3},{8,4},{9,5},{1... | collective-permute-start | bytes 221192 | tf_op jit(solution)/shard_map/ppermute | solution.py:606
  85.2 2.9 %collective-permute-done.21.refs_0_ = s16[144,256]{1,0:T(8,128)(2,1)S(1)} collective-permute-done((s16[144,256]{1,0:T(8,128)(2,1)S(1)}, s16[144,256]{1,0:T(8,128)(2,1)S(1)}, u32[]{:S(2)}, u32[]{:S(2)}) %collective-permute-start.21) | collective-permute-done | bytes 73760 | tf_op jit(solution)/shard_map/ppermute | solution.py:606
  88.6 3.6 %coarse_second.1 = (bf16[256,128]{1,0:T(8,128)(2,1)S(1)}, f32[128,256]{1,0:T(8,128)S(1)}, f32[8,128]{1,0:T(8,128)S(1)}, f32[8,256]{1,0:T(8,128)S(1)}) custom-call(bf16[80,128,256]{2,1,0:T(8,128)(2,1)S(1)} %bitcast.9, bf16[256,256]{1,0:T(8,128)(2,1)S(1)} %copy-done.2, f32[128,256]{1,0:T(8,128)S(1)} %get-tuple-element.74.own_ref, ...), custom_call_target="tpu_custom_call" | custom-call | flops 1342177280 | bytes 5000000 | tf_op jit(solution)/shard_map/coarse_second/pallas_call | solution.py:414
  93.9 3.0 %collective-permute-start.25 = (bf16[256,128]{1,0:T(8,128)(2,1)S(1)}, bf16[256,128]{1,0:T(8,128)(2,1)S(1)}, u32[]{:S(2)}, u32[]{:S(2)}) collective-permute-start(bf16[256,128]{1,0:T(8,128)(2,1)S(1)} %get-tuple-element.79.refs_0_), channel_id=1, source_target_pairs={{0,12},{1,13},{2,14},{3,15},{4,0},{5,1},{6,2},{7,3},{8,4},{9,5},{1... | collective-permute-start | bytes 196616 | tf_op jit(solution)/shard_map/ppermute | solution.py:606
  96.8 2.9 %collective-permute-done.26.refs_2_ = bf16[256,128]{1,0:T(8,128)(2,1)S(1)} collective-permute-done((bf16[256,128]{1,0:T(8,128)(2,1)S(1)}, bf16[256,128]{1,0:T(8,128)(2,1)S(1)}, u32[]{:S(2)}, u32[]{:S(2)}) %collective-permute-start.26) | collective-permute-done | bytes 65568 | tf_op jit(solution)/shard_map/ppermute | solution.py:606
  99.8 2.9 %collective-permute-done.24.refs_0_ = bf16[256,128]{1,0:T(8,128)(2,1)S(1)} collective-permute-done((bf16[256,128]{1,0:T(8,128)(2,1)S(1)}, bf16[256,128]{1,0:T(8,128)(2,1)S(1)}, u32[]{:S(2)}, u32[]{:S(2)}) %collective-permute-start.24) | collective-permute-done | bytes 65568 | tf_op jit(solution)/shard_map/ppermute | solution.py:606
  102.7 1.4 %collective-permute-start.29 = (bf16[3,256,128]{2,1,0:T(8,128)(2,1)S(1)}, bf16[3,256,128]{2,1,0:T(8,128)(2,1)S(1)}, u32[]{:S(2)}, u32[]{:S(2)}) collective-permute-start(bf16[3,256,128]{2,1,0:T(8,128)(2,1)S(1)} %join.3.after_ref.refs_1_), channel_id=1, source_target_pairs={{0,2},{1,3},{2,0},{3,1},{4,6},{5,7},{6,4},{7,5},{8,10},{9,11},{10,... | collective-permute-start | bytes 589832 | tf_op jit(solution)/shard_map/ppermute | solution.py:602
  104.1 3.6 %project.3 = (f32[80,8192]{1,0:T(8,128)S(1)}, f32[8,128]{1,0:T(8,128)S(1)}) custom-call(bf16[128,80,256]{2,1,0:T(8,128)(2,1)S(1)} %bitcast.11, f32[128,256]{1,0:T(8,128)S(1)} %get-tuple-element.80.y_ref, bf16[2,256,128]{2,1,0:T(8,128)(2,1)S(1)} %copy-done.1, bf16[3,256,128]{2,1,0:T(8,128)(2,1)S(1)} %join.3.after_ref.refs_1_), custom_call_target="tpu_custom_call" | custom-call | flops 1342177280 | bytes 8000000 | tf_op jit(solution)/shard_map/project/pallas_call | solution.py:452
  110.7 1.9 %image_second.1 = (f32[1152,256]{1,0:T(8,128)S(1)}, f32[8,256]{1,0:T(8,128)S(1)}) custom-call(bf16[256,128]{1,0:T(8,128)(2,1)S(1)} %get-tuple-element.79.refs_0_, bf16[3,256,128]{2,1,0:T(8,128)(2,1)S(1)} %join.3.after_ref.refs_1_, bf16[256,128]{1,0:T(8,128)(2,1)S(1)} %collective-permute-done.27.refs_3_.refs_2_, bf16[3,256,128]{2,1,0:T(8,128)(2,1)S(1)} %relay.3.refs_3_, ...), custom_call_target="tpu_custom_call" | custom-call | flops 1207959552 | bytes 8000000 | tf_op jit(solution)/shard_map/image_second/pallas_call | solution.py:538
  113.9 11.4 %all_to_all.10.sums_ref = f32[8,8,256]{2,1,0:T(8,128)S(1)} all-to-all(f32[8,8,256]{2,1,0:T(8,128)S(1)} %spread.1), channel_id=1, replica_groups={{0,2,4,6,8,10,12,14},{1,3,5,7,9,11,13,15},{16,18,20,22,24,26,28,30},{17..., dimensions={0} | all-to-all | bytes 131072 | tf_op jit(solution)/shard_map/all_to_all | solution.py:184
  125.4 2.2 %result.1 = (f32[80,8192]{1,0:T(8,128)}, f32[1152,256]{1,0:T(8,128)}) custom-call(f32[8,128]{1,0:T(8,128)S(1)} %get-tuple-element.78.l0_ref, f32[8,8,256]{2,1,0:T(8,128)S(1)} %all_to_all.10.sums_ref, f32[80,8192]{1,0:T(8,128)S(1)} %get-tuple-element.84.refs_0_, f32[80,8192]{1,0:T(8,128)S(1)} %get-tuple-element.85.refs_1_, ...), custom_call_target="tpu_custom_call" | custom-call | flops 1966080 | bytes 10000000 | tf_op jit(solution)/shard_map/result/pallas_call | solution.py:581
  (83 shorter events, 18.2 us)
Async XLA Ops:
  2.0 2.1 %collective-permute-start = (s32[8,128]{1,0:T(8,128)S(1)}, s32[8,128]{1,0:T(8,128)S(1)}, u32[]{:S(2)}, u32[]{:S(2)}) collective-permute-start(s32[8,128]{1,0:T(8,128)S(1)} %get-tuple-element.46), channel_id=1, source_target_pairs={{0,1},{1,0},{2,3},{3,2},{4,5},{5,4},{6,7},{7,6},{8,9},{9,8},{10,11... | collective-permute-start | bytes 12296 | tf_op jit(solution)/shard_map/ppermute | solution.py:598
  4.7 13.5 %all-to-all-start = ((s32[8,8,128]{2,1,0:T(8,128)}), s32[8,8,128]{2,1,0:T(8,128)S(1)}, u32[]{:S(2)}, u32[]{:S(2)}) async-start(s32[8,8,128]{2,1,0:T(8,128)} %mix.1), calls=%async_computation | async-start | bytes 65536 | tf_op jit(solution)/shard_map/all_to_all | solution.py:184
  23.5 5.0 %collective-permute-start.2 = (f32[512,256]{1,0:T(8,128)S(1)}, f32[512,256]{1,0:T(8,128)S(1)}, u32[]{:S(2)}, u32[]{:S(2)}) collective-permute-start(f32[512,256]{1,0:T(8,128)S(1)} %get-tuple-element.52), channel_id=1, source_target_pairs={{0,1},{1,0},{2,3},{3,2},{4,5},{5,4},{6,7},{7,6},{8,9},{9,8},{10,11... | collective-permute-start | bytes 1572872 | tf_op jit(solution)/shard_map/ppermute | solution.py:598
  23.6 7.1 %collective-permute-start.1 = (f32[512,256]{1,0:T(8,128)S(1)}, f32[512,256]{1,0:T(8,128)S(1)}, u32[]{:S(2)}, u32[]{:S(2)}) collective-permute-start(f32[512,256]{1,0:T(8,128)S(1)} %get-tuple-element.50), channel_id=1, source_target_pairs={{0,1},{1,0},{2,3},{3,2},{4,5},{5,4},{6,7},{7,6},{8,9},{9,8},{10,11... | collective-permute-start | bytes 1572872 | tf_op jit(solution)/shard_map/ppermute | solution.py:598
  28.6 6.6 %collective-permute-start.3 = (s16[272,256]{1,0:T(8,128)(2,1)S(1)}, s16[272,256]{1,0:T(8,128)(2,1)S(1)}, u32[]{:S(2)}, u32[]{:S(2)}) collective-permute-start(s16[272,256]{1,0:T(8,128)(2,1)S(1)} %get-tuple-element.53), channel_id=1, source_target_pairs={{0,2},{1,3},{2,0},{3,1},{4,6},{5,7},{6,4},{7,5},{8,10},{9,11},{10,... | collective-permute-start | bytes 417800 | tf_op jit(solution)/shard_map/ppermute | solution.py:602
  29.1 8.2 %collective-permute-start.4 = (s16[272,256]{1,0:T(8,128)(2,1)S(1)}, s16[272,256]{1,0:T(8,128)(2,1)S(1)}, u32[]{:S(2)}, u32[]{:S(2)}) collective-permute-start(s16[272,256]{1,0:T(8,128)(2,1)S(1)} %get-tuple-element.55), channel_id=1, source_target_pairs={{0,2},{1,3},{2,0},{3,1},{4,6},{5,7},{6,4},{7,5},{8,10},{9,11},{10,... | collective-permute-start | bytes 417800 | tf_op jit(solution)/shard_map/ppermute | solution.py:602
  35.3 4.4 %collective-permute-start.7 = (s16[144,256]{1,0:T(8,128)(2,1)S(1)}, s16[144,256]{1,0:T(8,128)(2,1)S(1)}, u32[]{:S(2)}, u32[]{:S(2)}) collective-permute-start(s16[144,256]{1,0:T(8,128)(2,1)S(1)} %get-tuple-element.58), channel_id=1, source_target_pairs={{0,12},{1,13},{2,14},{3,15},{4,0},{5,1},{6,2},{7,3},{8,4},{9,5},{1... | collective-permute-start | bytes 221192 | tf_op jit(solution)/shard_map/ppermute | solution.py:606
  37.4 7.4 %collective-permute-start.5 = (s16[144,256]{1,0:T(8,128)(2,1)S(1)}, s16[144,256]{1,0:T(8,128)(2,1)S(1)}, u32[]{:S(2)}, u32[]{:S(2)}) collective-permute-start(s16[144,256]{1,0:T(8,128)(2,1)S(1)} %get-tuple-element.56), channel_id=1, source_target_pairs={{0,8},{1,9},{2,10},{3,11},{4,12},{5,13},{6,14},{7,15},{8,0},{9,1},... | collective-permute-start | bytes 221192 | tf_op jit(solution)/shard_map/ppermute | solution.py:606
  38.0 6.8 %collective-permute-start.6 = (s16[144,256]{1,0:T(8,128)(2,1)S(1)}, s16[144,256]{1,0:T(8,128)(2,1)S(1)}, u32[]{:S(2)}, u32[]{:S(2)}) collective-permute-start(s16[144,256]{1,0:T(8,128)(2,1)S(1)} %get-tuple-element.57), channel_id=1, source_target_pairs={{0,4},{1,5},{2,6},{3,7},{4,8},{5,9},{6,10},{7,11},{8,12},{9,13},{1... | collective-permute-start | bytes 221192 | tf_op jit(solution)/shard_map/ppermute | solution.py:606
  48.3 4.6 %collective-permute-start.12 = (bf16[256,128]{1,0:T(8,128)(2,1)S(1)}, bf16[256,128]{1,0:T(8,128)(2,1)S(1)}, u32[]{:S(2)}, u32[]{:S(2)}) collective-permute-start(bf16[256,128]{1,0:T(8,128)(2,1)S(1)} %get-tuple-element.59.refs_0_), channel_id=1, source_target_pairs={{0,1},{1,0},{2,3},{3,2},{4,5},{5,4},{6,7},{7,6},{8,9},{9,8},{10,11... | collective-permute-start | bytes 196616 | tf_op jit(solution)/shard_map/ppermute | solution.py:598
  48.3 4.6 %collective-permute-start.11 = (bf16[256,128]{1,0:T(8,128)(2,1)S(1)}, bf16[256,128]{1,0:T(8,128)(2,1)S(1)}, u32[]{:S(2)}, u32[]{:S(2)}) collective-permute-start(bf16[256,128]{1,0:T(8,128)(2,1)S(1)} %get-tuple-element.59.refs_0_), channel_id=1, source_target_pairs={{0,2},{1,3},{2,0},{3,1},{4,6},{5,7},{6,4},{7,5},{8,10},{9,11},{10,... | collective-permute-start | bytes 196616 | tf_op jit(solution)/shard_map/ppermute | solution.py:602
  49.1 6.7 %collective-permute-start.10 = (bf16[256,128]{1,0:T(8,128)(2,1)S(1)}, bf16[256,128]{1,0:T(8,128)(2,1)S(1)}, u32[]{:S(2)}, u32[]{:S(2)}) collective-permute-start(bf16[256,128]{1,0:T(8,128)(2,1)S(1)} %get-tuple-element.59.refs_0_), channel_id=1, source_target_pairs={{0,4},{1,5},{2,6},{3,7},{4,8},{5,9},{6,10},{7,11},{8,12},{9,13},{1... | collective-permute-start | bytes 196616 | tf_op jit(solution)/shard_map/ppermute | solution.py:606
  49.1 6.7 %collective-permute-start.9 = (bf16[256,128]{1,0:T(8,128)(2,1)S(1)}, bf16[256,128]{1,0:T(8,128)(2,1)S(1)}, u32[]{:S(2)}, u32[]{:S(2)}) collective-permute-start(bf16[256,128]{1,0:T(8,128)(2,1)S(1)} %get-tuple-element.59.refs_0_), channel_id=1, source_target_pairs={{0,12},{1,13},{2,14},{3,15},{4,0},{5,1},{6,2},{7,3},{8,4},{9,5},{1... | collective-permute-start | bytes 196616 | tf_op jit(solution)/shard_map/ppermute | solution.py:606
  52.9 5.7 %collective-permute-start.8 = (bf16[256,128]{1,0:T(8,128)(2,1)S(1)}, bf16[256,128]{1,0:T(8,128)(2,1)S(1)}, u32[]{:S(2)}, u32[]{:S(2)}) collective-permute-start(bf16[256,128]{1,0:T(8,128)(2,1)S(1)} %get-tuple-element.59.refs_0_), channel_id=1, source_target_pairs={{0,8},{1,9},{2,10},{3,11},{4,12},{5,13},{6,14},{7,15},{8,0},{9,1},... | collective-permute-start | bytes 196616 | tf_op jit(solution)/shard_map/ppermute | solution.py:606
  58.7 8.2 %collective-permute-start.13 = (bf16[3,256,128]{2,1,0:T(8,128)(2,1)S(1)}, bf16[3,256,128]{2,1,0:T(8,128)(2,1)S(1)}, u32[]{:S(2)}, u32[]{:S(2)}) collective-permute-start(bf16[3,256,128]{2,1,0:T(8,128)(2,1)S(1)} %join.2.after_ref.refs_1_), channel_id=1, source_target_pairs={{0,2},{1,3},{2,0},{3,1},{4,6},{5,7},{6,4},{7,5},{8,10},{9,11},{10,... | collective-permute-start | bytes 589832 | tf_op jit(solution)/shard_map/ppermute | solution.py:602
  63.1 5.6 %collective-permute-start.14 = (bf16[3,256,128]{2,1,0:T(8,128)(2,1)S(1)}, bf16[3,256,128]{2,1,0:T(8,128)(2,1)S(1)}, u32[]{:S(2)}, u32[]{:S(2)}) collective-permute-start(bf16[3,256,128]{2,1,0:T(8,128)(2,1)S(1)} %join.2.after_ref.refs_1_), channel_id=1, source_target_pairs={{0,1},{1,0},{2,3},{3,2},{4,5},{5,4},{6,7},{7,6},{8,9},{9,8},{10,11... | collective-permute-start | bytes 589832 | tf_op jit(solution)/shard_map/ppermute | solution.py:598
  66.8 1.8 %collective-permute-start.16 = (bf16[3,256,128]{2,1,0:T(8,128)(2,1)S(1)}, bf16[3,256,128]{2,1,0:T(8,128)(2,1)S(1)}, u32[]{:S(2)}, u32[]{:S(2)}) collective-permute-start(bf16[3,256,128]{2,1,0:T(8,128)(2,1)S(1)} %relay.2.refs_3_), channel_id=1, source_target_pairs={{0,1},{1,0},{2,3},{3,2},{4,5},{5,4},{6,7},{7,6},{8,9},{9,8},{10,11... | collective-permute-start | bytes 589832 | tf_op jit(solution)/shard_map/ppermute | solution.py:598
  71.8 2.0 %collective-permute-start.18 = (f32[520,256]{1,0:T(8,128)S(1)}, f32[520,256]{1,0:T(8,128)S(1)}, u32[]{:S(2)}, u32[]{:S(2)}) collective-permute-start(f32[520,256]{1,0:T(8,128)S(1)} %get-tuple-element.68), channel_id=1, source_target_pairs={{0,1},{1,0},{2,3},{3,2},{4,5},{5,4},{6,7},{7,6},{8,9},{9,8},{10,11... | collective-permute-start | bytes 1597448 | tf_op jit(solution)/shard_map/ppermute | solution.py:598
  72.2 3.9 %collective-permute-start.17 = (f32[512,256]{1,0:T(8,128)S(1)}, f32[512,256]{1,0:T(8,128)S(1)}, u32[]{:S(2)}, u32[]{:S(2)}) collective-permute-start(f32[512,256]{1,0:T(8,128)S(1)} %get-tuple-element.66), channel_id=1, source_target_pairs={{0,1},{1,0},{2,3},{3,2},{4,5},{5,4},{6,7},{7,6},{8,9},{9,8},{10,11... | collective-permute-start | bytes 1572872 | tf_op jit(solution)/shard_map/ppermute | solution.py:598
  74.0 6.6 %collective-permute-start.20 = (s16[272,256]{1,0:T(8,128)(2,1)S(1)}, s16[272,256]{1,0:T(8,128)(2,1)S(1)}, u32[]{:S(2)}, u32[]{:S(2)}) collective-permute-start(s16[272,256]{1,0:T(8,128)(2,1)S(1)} %get-tuple-element.71), channel_id=1, source_target_pairs={{0,2},{1,3},{2,0},{3,1},{4,6},{5,7},{6,4},{7,5},{8,10},{9,11},{10,... | collective-permute-start | bytes 417800 | tf_op jit(solution)/shard_map/ppermute | solution.py:602
  74.7 8.6 %collective-permute-start.19 = (s16[272,256]{1,0:T(8,128)(2,1)S(1)}, s16[272,256]{1,0:T(8,128)(2,1)S(1)}, u32[]{:S(2)}, u32[]{:S(2)}) collective-permute-start(s16[272,256]{1,0:T(8,128)(2,1)S(1)} %get-tuple-element.70), channel_id=1, source_target_pairs={{0,2},{1,3},{2,0},{3,1},{4,6},{5,7},{6,4},{7,5},{8,10},{9,11},{10,... | collective-permute-start | bytes 417800 | tf_op jit(solution)/shard_map/ppermute | solution.py:602
  80.6 7.5 %collective-permute-start.21 = (s16[144,256]{1,0:T(8,128)(2,1)S(1)}, s16[144,256]{1,0:T(8,128)(2,1)S(1)}, u32[]{:S(2)}, u32[]{:S(2)}) collective-permute-start(s16[144,256]{1,0:T(8,128)(2,1)S(1)} %get-tuple-element.75), channel_id=1, source_target_pairs={{0,8},{1,9},{2,10},{3,11},{4,12},{5,13},{6,14},{7,15},{8,0},{9,1},... | collective-permute-start | bytes 221192 | tf_op jit(solution)/shard_map/ppermute | solution.py:606
  81.3 6.9 %collective-permute-start.22 = (s16[144,256]{1,0:T(8,128)(2,1)S(1)}, s16[144,256]{1,0:T(8,128)(2,1)S(1)}, u32[]{:S(2)}, u32[]{:S(2)}) collective-permute-start(s16[144,256]{1,0:T(8,128)(2,1)S(1)} %get-tuple-element.76), channel_id=1, source_target_pairs={{0,4},{1,5},{2,6},{3,7},{4,8},{5,9},{6,10},{7,11},{8,12},{9,13},{1... | collective-permute-start | bytes 221192 | tf_op jit(solution)/shard_map/ppermute | solution.py:606
  83.4 5.2 %collective-permute-start.23 = (s16[144,256]{1,0:T(8,128)(2,1)S(1)}, s16[144,256]{1,0:T(8,128)(2,1)S(1)}, u32[]{:S(2)}, u32[]{:S(2)}) collective-permute-start(s16[144,256]{1,0:T(8,128)(2,1)S(1)} %get-tuple-element.77), channel_id=1, source_target_pairs={{0,12},{1,13},{2,14},{3,15},{4,0},{5,1},{6,2},{7,3},{8,4},{9,5},{1... | collective-permute-start | bytes 221192 | tf_op jit(solution)/shard_map/ppermute | solution.py:606
  92.2 4.6 %collective-permute-start.28 = (bf16[256,128]{1,0:T(8,128)(2,1)S(1)}, bf16[256,128]{1,0:T(8,128)(2,1)S(1)}, u32[]{:S(2)}, u32[]{:S(2)}) collective-permute-start(bf16[256,128]{1,0:T(8,128)(2,1)S(1)} %get-tuple-element.79.refs_0_), channel_id=1, source_target_pairs={{0,1},{1,0},{2,3},{3,2},{4,5},{5,4},{6,7},{7,6},{8,9},{9,8},{10,11... | collective-permute-start | bytes 196616 | tf_op jit(solution)/shard_map/ppermute | solution.py:598
  92.3 4.6 %collective-permute-start.27 = (bf16[256,128]{1,0:T(8,128)(2,1)S(1)}, bf16[256,128]{1,0:T(8,128)(2,1)S(1)}, u32[]{:S(2)}, u32[]{:S(2)}) collective-permute-start(bf16[256,128]{1,0:T(8,128)(2,1)S(1)} %get-tuple-element.79.refs_0_), channel_id=1, source_target_pairs={{0,2},{1,3},{2,0},{3,1},{4,6},{5,7},{6,4},{7,5},{8,10},{9,11},{10,... | collective-permute-start | bytes 196616 | tf_op jit(solution)/shard_map/ppermute | solution.py:602
  93.0 6.7 %collective-permute-start.26 = (bf16[256,128]{1,0:T(8,128)(2,1)S(1)}, bf16[256,128]{1,0:T(8,128)(2,1)S(1)}, u32[]{:S(2)}, u32[]{:S(2)}) collective-permute-start(bf16[256,128]{1,0:T(8,128)(2,1)S(1)} %get-tuple-element.79.refs_0_), channel_id=1, source_target_pairs={{0,4},{1,5},{2,6},{3,7},{4,8},{5,9},{6,10},{7,11},{8,12},{9,13},{1... | collective-permute-start | bytes 196616 | tf_op jit(solution)/shard_map/ppermute | solution.py:606
  93.9 5.9 %collective-permute-start.25 = (bf16[256,128]{1,0:T(8,128)(2,1)S(1)}, bf16[256,128]{1,0:T(8,128)(2,1)S(1)}, u32[]{:S(2)}, u32[]{:S(2)}) collective-permute-start(bf16[256,128]{1,0:T(8,128)(2,1)S(1)} %get-tuple-element.79.refs_0_), channel_id=1, source_target_pairs={{0,12},{1,13},{2,14},{3,15},{4,0},{5,1},{6,2},{7,3},{8,4},{9,5},{1... | collective-permute-start | bytes 196616 | tf_op jit(solution)/shard_map/ppermute | solution.py:606
  96.8 5.8 %collective-permute-start.24 = (bf16[256,128]{1,0:T(8,128)(2,1)S(1)}, bf16[256,128]{1,0:T(8,128)(2,1)S(1)}, u32[]{:S(2)}, u32[]{:S(2)}) collective-permute-start(bf16[256,128]{1,0:T(8,128)(2,1)S(1)} %get-tuple-element.79.refs_0_), channel_id=1, source_target_pairs={{0,8},{1,9},{2,10},{3,11},{4,12},{5,13},{6,14},{7,15},{8,0},{9,1},... | collective-permute-start | bytes 196616 | tf_op jit(solution)/shard_map/ppermute | solution.py:606
  102.7 6.4 %collective-permute-start.29 = (bf16[3,256,128]{2,1,0:T(8,128)(2,1)S(1)}, bf16[3,256,128]{2,1,0:T(8,128)(2,1)S(1)}, u32[]{:S(2)}, u32[]{:S(2)}) collective-permute-start(bf16[3,256,128]{2,1,0:T(8,128)(2,1)S(1)} %join.3.after_ref.refs_1_), channel_id=1, source_target_pairs={{0,2},{1,3},{2,0},{3,1},{4,6},{5,7},{6,4},{7,5},{8,10},{9,11},{10,... | collective-permute-start | bytes 589832 | tf_op jit(solution)/shard_map/ppermute | solution.py:602
  104.1 6.6 %collective-permute-start.30 = (bf16[3,256,128]{2,1,0:T(8,128)(2,1)S(1)}, bf16[3,256,128]{2,1,0:T(8,128)(2,1)S(1)}, u32[]{:S(2)}, u32[]{:S(2)}) collective-permute-start(bf16[3,256,128]{2,1,0:T(8,128)(2,1)S(1)} %join.3.after_ref.refs_1_), channel_id=1, source_target_pairs={{0,1},{1,0},{2,3},{3,2},{4,5},{5,4},{6,7},{7,6},{8,9},{9,8},{10,11... | collective-permute-start | bytes 589832 | tf_op jit(solution)/shard_map/ppermute | solution.py:598
  109.1 1.6 %collective-permute-start.32 = (bf16[3,256,128]{2,1,0:T(8,128)(2,1)S(1)}, bf16[3,256,128]{2,1,0:T(8,128)(2,1)S(1)}, u32[]{:S(2)}, u32[]{:S(2)}) collective-permute-start(bf16[3,256,128]{2,1,0:T(8,128)(2,1)S(1)} %relay.3.refs_3_), channel_id=1, source_target_pairs={{0,1},{1,0},{2,3},{3,2},{4,5},{5,4},{6,7},{7,6},{8,9},{9,8},{10,11... | collective-permute-start | bytes 589832 | tf_op jit(solution)/shard_map/ppermute | solution.py:598
  (11 other events, 83.2 us)

commit v6 on v4

--- a/solution.py
+++ b/solution.py
@@ -53,7 +53,7 @@
 
 
 STEPS = 4
-ORDER = (2, 1, 3, 0)
+ORDER = (1, 3, 0, 2)
 PARTS = ((0, 0), (1, 0), (0, 1), (1, 1))
 HEAD = 16
 TOP = 32512.0
@@ -64,7 +64,7 @@
     z, y, c = me_ref[0], me_ref[1], me_ref[2]
     y = y if dy == 0 else 1 - y
     c = c if dc == 0 else 1 - c
-    return (lax.rem(z + ORDER[i % STEPS], STEPS) * 2 + y) * 2 + c
+    return (jnp.bitwise_xor(z, ORDER[i % STEPS]) * 2 + y) * 2 + c
 
 
 def places(me_ref, list_refs, slots):
@@ -75,39 +75,50 @@
     for i in range(GROUP):
         o = owner_at(me_ref, i)
         dy, dc = PARTS[i // STEPS]
-        held = list_refs[-ORDER[i % STEPS] % STEPS]
-        row = jnp.broadcast_to(held[2 * dy + dc : 2 * dy + dc + 1, :], slots.shape)
+        k = ORDER[i % STEPS]
+        row = k % 2 * STEPS + 2 * dy + dc
+        row = jnp.broadcast_to(list_refs[k // 2][row : row + 1, :], slots.shape)
         column = jnp.take_along_axis(row, within, axis=1, mode="promise_in_bounds")
         rows = jnp.where(from_owner == o, column + i * LANES, rows)
     return rows[: slots.shape[0] // 2]
 
 
-def build_rows(ids_ref, weight_ref, wh_ref, wl_ref, at_ref, y_refs, lo_s, base):
+PIECES = 4
+
+
+def build_rows(ids_ref, weight_ref, wh_ref, wl_ref, at_ref, y_refs, held, base):
     sources, fine = ids_ref.shape
-    rows = at_ref.shape[0] // len(y_refs)
-    step = rows // 2
-    row = lax.broadcasted_iota(jnp.int32, (step, LANES), 0)
-    for n, y_ref in enumerate(y_refs):
-        for m in range(2):
-            start = n * rows + m * step
-            for j in range(fine // LANES):
-                lanes = pl.ds(j * LANES, LANES)
-                total = None
-                for b in range(sources):
-                    ids = ids_ref[b : b + 1, lanes] - (base + start)
-                    term = jnp.where(row == ids, weight_ref[b : b + 1, lanes], 0.0)
-                    total = term if total is None else total + term
-                high, low = halves(total)
-                at_ref[pl.ds(start, step), lanes] = high
-                lo_s[pl.ds(m * step, step), lanes] = low
-        held = at_ref[pl.ds(n * rows, rows), :]
-        y_ref[...] = dot(held, wh_ref[...]) + dot(held, wl_ref[...]) + dot(lo_s[...], wh_ref[...])
+    rows = at_ref.shape[0] // PIECES
+    row = lax.broadcasted_iota(jnp.int32, (rows, LANES), 0)
+
+    def build(n):
+        high_s, low_s = held[2 * (n % 2) : 2 * (n % 2) + 2]
+        for j in range(fine // LANES):
+            lanes = pl.ds(j * LANES, LANES)
+            total = None
+            for b in range(sources):
+                ids = ids_ref[b : b + 1, lanes] - (base + n * rows)
+                term = jnp.where(row == ids, weight_ref[b : b + 1, lanes], 0.0)
+                total = term if total is None else total + term
+            high, low = halves(total)
+            at_ref[pl.ds(n * rows, rows), lanes] = high
+            high_s[:, lanes] = high
+            low_s[:, lanes] = low
+
+    build(0)
+    for n in range(PIECES):
+        high_s, low_s = held[2 * (n % 2) : 2 * (n % 2) + 2]
+        y = dot(high_s[...], wh_ref[...]) + dot(high_s[...], wl_ref[...])
+        y = y + dot(low_s[...], wh_ref[...])
+        if n + 1 < PIECES:
+            build(n + 1)
+        y_refs[n // 2][pl.ds(n % 2 * rows, rows), :] = y
 
 
 def far_kernel(grouped, me_ref, *refs):
-    list_refs, refs = refs[: 4 * grouped], refs[4 * grouped :]
+    list_refs, refs = refs[: 2 * grouped], refs[2 * grouped :]
     both_ref, wh_ref, wl_ref, *refs = refs
-    ids_ref, weight_ref, at_ref, ya_ref, yb_ref, lo_s = refs
+    ids_ref, weight_ref, at_ref, ya_ref, yb_ref, *held = refs
     sources = ids_ref.shape[0]
     for j in range(ids_ref.shape[1] // LANES):
         lanes = pl.ds(j * LANES, LANES)
@@ -115,11 +126,11 @@
         ids_ref[:, lanes] = places(me_ref, list_refs, slots) if grouped else slots
         weight_ref[:, lanes] = both_ref[sources:, lanes]
     half = at_ref.shape[0]
-    build_rows(ids_ref, weight_ref, wh_ref, wl_ref, at_ref, [ya_ref, yb_ref], lo_s, half)
-
-
-def near_kernel(ids_ref, weight_ref, wh_ref, wl_ref, at_ref, ya_ref, yb_ref, lo_s):
-    build_rows(ids_ref, weight_ref, wh_ref, wl_ref, at_ref, [ya_ref, yb_ref], lo_s, 0)
+    build_rows(ids_ref, weight_ref, wh_ref, wl_ref, at_ref, [ya_ref, yb_ref], held, half)
+
+
+def near_kernel(ids_ref, weight_ref, wh_ref, wl_ref, at_ref, ya_ref, yb_ref, *held):
+    build_rows(ids_ref, weight_ref, wh_ref, wl_ref, at_ref, [ya_ref, yb_ref], held, 0)
 
 
 def adjoint_half(slots, args, head=None):
@@ -139,7 +150,7 @@
         in_specs=([SMEM] if head else []) + [VMEM] * (len(args) - (1 if head else 0)),
         out_specs=[VMEM] * len(out),
         out_shape=out,
-        scratch_shapes=[pltpu.VMEM((half // 2, fine), BF)],
+        scratch_shapes=[pltpu.VMEM((half // PIECES, fine), BF)] * 4,
         compiler_params=params(16),
         cost_estimate=cost(3 * slots * fine * width, 4e6),
         name="adjoint_far" if head else "adjoint_near",
@@ -149,9 +160,9 @@
 def pick_kernel(me_ref, lists_ref, near_ref, far_ref):
     z, y, c = me_ref[0], me_ref[1], me_ref[2]
     for dy in range(2):
-        for k in range(STEPS):
-            there = (lax.rem(z + k, STEPS) * 2 + (y if dy == 0 else 1 - y)) * 2
-            row = slice(dy * STEPS + k, dy * STEPS + k + 1)
+        for p, k in enumerate(ORDER):
+            there = (jnp.bitwise_xor(z, k) * 2 + (y if dy == 0 else 1 - y)) * 2
+            row = slice(dy * STEPS + p, dy * STEPS + p + 1)
             near_ref[row, :] = lists_ref[pl.ds(there + c, 1), :]
             far_ref[row, :] = lists_ref[pl.ds(there + 1 - c, 1), :]
 
@@ -163,13 +174,20 @@
         far_y_ref[rows, :] = held[STEPS:, :]
 
 
-def mix_z_kernel(near_ref, got_ref, *outs):
-    for k, out in enumerate(outs):
-        out[...] = jnp.zeros_like(out)
-        for i, held in enumerate((near_ref, got_ref)):
-            for c in range(2):
-                row = c * STEPS + k
-                out[2 * i + c : 2 * i + c + 1, :] = held[row : row + 1, :]
+def mix_z_kernel(near_ref, got_ref, near_z_ref, far_z_ref):
+    for i, held in enumerate((near_ref, got_ref)):
+        for c in range(2):
+            rows = slice(4 * i + 2 * c, 4 * i + 2 * c + 2)
+            far_z_ref[rows, :] = held[c * STEPS : c * STEPS + 2, :]
+            near_z_ref[rows, :] = held[c * STEPS + 2 : c * STEPS + 4, :]
+
+
+def mix_end_kernel(near_ref, got_ref, own_ref, sent_ref):
+    for i, held in enumerate((near_ref, got_ref)):
+        for n in range(STEPS):
+            row = slice(i * STEPS + n, i * STEPS + n + 1)
+            own_ref[row, :] = held[2 * n : 2 * n + 1, :]
+            sent_ref[row, :] = held[2 * n + 1 : 2 * n + 2, :]
 
 
 def small(kernel, n, name, *args, scalars=0):
@@ -187,8 +205,9 @@
 def exchange_lists(me, lists):
     near, far = small(pick_kernel, 2, "pick", me, lists, scalars=1)
     near, far = small(mix_y_kernel, 2, "mix_y", near, over_core(far))
-    own, *sent = small(mix_z_kernel, STEPS, "mix_z", near, over_y(far))
-    return [own] + [over_z(sent[k - 1], k) for k in range(1, STEPS)]
+    near, far = small(mix_z_kernel, 2, "mix_z", near, over_y(far))
+    own, sent = small(mix_end_kernel, 2, "mix_end", near, over_z(far, 1))
+    return [own, over_z(sent, 2)]
 
 
 def exponent(m):
@@ -239,91 +258,77 @@
     return total
 
 
-def merge_y_kernel(with_sums, *refs):
+def half_of(ref, second):
+    half = ref.shape[0] // 2 // LANES * LANES
+    return ref[pl.ds(half if second else 0, half), :]
+
+
+def merge_a_kernel(with_sums, a_ref, b_ref, *refs):
+    sums = None
     if with_sums:
-        a_ref, b_ref, mine_ref, first_ref, second_ref, s_ref = refs
-        sums = mine_ref[...] + b_ref[pl.ds(a_ref.shape[0], 8), :]
-        s_ref[...] = sums
-    else:
-        a_ref, b_ref, first_ref, second_ref = refs
-        sums = None
-    half = a_ref.shape[0] // 2
-    pack(first_ref, a_ref[pl.ds(0, half), :] + b_ref[pl.ds(0, half), :], sums)
-    pack(second_ref, a_ref[pl.ds(half, half), :] + b_ref[pl.ds(half, half), :])
-
-
-def merge_y(a, b, sums):
-    rows, width = a.shape
-    out = [shape((rows // 2 + HEAD, width), jnp.int16)] * 2
-    args = [a, b]
+        sums = refs[0][...] + b_ref[pl.ds(a_ref.shape[0], 8), :]
+        refs[2][...] = sums
+    pack(refs[1 if with_sums else 0], half_of(a_ref, False) + half_of(b_ref, False), sums)
+
+
+def merge_b_kernel(a_ref, b_ref, after_ref, out_ref):
+    pack(out_ref, half_of(a_ref, True) + half_of(b_ref, True))
+
+
+def merge_c_kernel(with_sums, a_ref, b_ref, p_ref, *refs):
+    sums = None
+    if with_sums:
+        sums = refs[0][...] + unpack_sums(p_ref)
+        refs[2][...] = sums
+    t = half_of(a_ref, False) + half_of(b_ref, False) + unpack(p_ref)
+    pack(refs[1 if with_sums else 0], t, sums)
+
+
+def merge_d_kernel(with_sums, a_ref, b_ref, p_ref, q_ref, *refs):
+    sums = None
+    if with_sums:
+        sums = refs[0][...] + unpack_sums(q_ref)
+        refs[3][...] = sums
+        refs = refs[1:]
+    t = half_of(a_ref, True) + half_of(b_ref, True) + unpack(p_ref) + unpack(q_ref)
+    refs[0][...] = t[:LANES]
+    pack(refs[1], t[LANES:], sums)
+
+
+def merge(kernel, name, out, *args, sums=None):
     if sums is not None:
-        out.append(shape((8, width), F32))
-        args.append(sums)
-    return pl.pallas_call(
-        functools.partial(merge_y_kernel, sums is not None),
+        out = out + [shape(sums.shape, F32)]
+        args = args + (sums,)
+    return pl.pallas_call(
+        kernel if kernel is merge_b_kernel else functools.partial(kernel, sums is not None),
         in_specs=[VMEM] * len(args),
         out_specs=[VMEM] * len(out),
         out_shape=out,
         compiler_params=params(8),
-        cost_estimate=cost(5 * rows * width, 1e6),
-        name="merge_y",
+        cost_estimate=cost(5e5, 1e6),
+        name=name,
     )(*args)
 
 
-def merge_z_kernel(last, with_sums, a_ref, b_ref, p_ref, *refs):
-    half = a_ref.shape[0] // 2
-    rows = pl.ds(half if last else 0, half)
-    t = a_ref[rows, :] + b_ref[rows, :] + unpack(p_ref)
-    sums = None
-    if with_sums:
-        sums = refs[0][...]
-        refs = refs[1:]
-        if not last:
-            sums = sums + unpack_sums(p_ref)
-            refs[2][...] = sums
-    pack(refs[0], t[:LANES], sums)
-    if last:
-        refs[1][...] = t[LANES:]
-    else:
-        pack(refs[1], t[LANES:], sums)
-
-
-def merge_z(last, a, b, p, sums):
-    width = a.shape[1]
-    sent = shape((LANES + HEAD, width), jnp.int16)
-    out = [sent, shape((LANES, width), F32) if last else sent]
-    args = [a, b, p]
-    if sums is not None:
-        args.append(sums)
-        if not last:
-            out.append(shape((8, width), F32))
-    return pl.pallas_call(
-        functools.partial(merge_z_kernel, last, sums is not None),
+def join_kernel(a_ref, b_ref, out_ref):
+    out_ref[0] = a_ref[...]
+    out_ref[1] = b_ref[...]
+
+
+def relay_kernel(x_ref, after_ref, out_ref):
+    out_ref[...] = x_ref[...]
+
+
+def pair_of(kernel, name, out, *args):
+    return pl.pallas_call(
+        kernel,
         in_specs=[VMEM] * len(args),
-        out_specs=[VMEM] * len(out),
+        out_specs=VMEM,
         out_shape=out,
         compiler_params=params(8),
-        cost_estimate=cost(5 * a.size, 1e6),
-        name="merge_z_last" if last else "merge_z_first",
+        cost_estimate=cost(1e5, 4e5),
+        name=name,
     )(*args)
-
-
-def join_kernel(*refs):
-    out_ref = refs[-1]
-    for i, r in enumerate(refs[:3]):
-        out_ref[i] = r[...]
-
-
-def join(blocks, *after):
-    return pl.pallas_call(
-        join_kernel,
-        in_specs=[VMEM] * (3 + len(after)),
-        out_specs=VMEM,
-        out_shape=shape((3,) + blocks[0].shape, BF),
-        compiler_params=params(8),
-        cost_estimate=cost(1e5, 4e5),
-        name="join",
-    )(*blocks, *after)
 
 
 def fold(a):
@@ -349,7 +354,7 @@
 SOME = 8
 
 
-def coarse_kernel(packed, second, e_ref, k_ref, own_ref, *refs):
+def coarse_kernel(packed, second, after, e_ref, k_ref, own_ref, *refs):
     refs = list(refs)
     got = [refs.pop(0) for _ in range(packed)]
     y = own_ref[...]
@@ -362,8 +367,8 @@
             sums = sums + unpack_sums(r)
         l0, keep = length_of(sums)
         y = keep * y0_ref[...] - l0 * y
-        refs.pop(2)[...] = jnp.broadcast_to(l0, (8, LANES))
-    x_ref, y_ref, sum_ref, even_s, odd_s, x_s = refs
+        refs.pop(after + 2)[...] = jnp.broadcast_to(l0, (8, LANES))
+    x_ref, y_ref, sum_ref, even_s, odd_s, x_s = refs[after:]
     members, columns, width = e_ref.shape
     y_ref[...] = y
     x_s[...] = jnp.zeros_like(x_s)
@@ -401,16 +406,16 @@
     sum_ref[0:1, :] = fold(x * y_ref[...])
 
 
-def coarse_image(ensemble, kern, own, got, y0=None, sums=None):
+def coarse_image(ensemble, kern, own, got, y0=None, sums=None, after=()):
     members, columns, width = ensemble.shape
     second = y0 is not None
-    args = [ensemble, kern, own, *got] + ([y0, sums] if second else [])
+    args = [ensemble, kern, own, *got] + ([y0, sums] if second else []) + list(after)
     out = [shape((width, columns), BF), shape((columns, width), F32)]
     out += [shape((8, LANES), F32)] if second else []
     out += [shape((8, width), F32)]
     return pl.pallas_call(
-        functools.partial(coarse_kernel, len(got), second),
-        in_specs=[VMEM] * len(args),
+        functools.partial(coarse_kernel, len(got), second, len(after)),
+        in_specs=[VMEM] * (len(args) - len(after)) + [ANY] * len(after),
         out_specs=[VMEM] * len(out),
         out_shape=out,
         scratch_shapes=[
@@ -424,7 +429,7 @@
     )(*args)
 
 
-def project_kernel(e_ref, y_ref, t_ref, g_ref, token_ref, even_s, odd_s):
+def project_kernel(e_ref, y_ref, t_ref, after_ref, g_ref, token_ref, even_s, odd_s):
     columns, members, width = e_ref.shape
     lanes = BATCH // 2 * LANES
     token_ref[...] = jnp.zeros_like(token_ref)
@@ -443,31 +448,28 @@
             g_ref[:, pl.ds(at, LANES)] = r[pair * members : (pair + 1) * members]
 
 
-def project(ens, y, taps):
+def project(ens, y, taps, after):
     columns, members, width = ens.shape
     levels = width // VAR
     return pl.pallas_call(
         project_kernel,
-        in_specs=[VMEM] * 3,
+        in_specs=[VMEM] * 4,
         out_specs=[VMEM] * 2,
         out_shape=[shape((members, columns * levels), F32), shape((8, LANES), F32)],
         scratch_shapes=[pltpu.VMEM((BATCH // 2 * members, width), BF)] * 2,
         compiler_params=params(16),
         cost_estimate=cost(2 * columns * members * width * width, 8e6),
         name="project",
-    )(ens, y, taps)
+    )(ens, y, taps, after)
 
 
 def lay_out(x_refs, xs):
     if len(x_refs) == 1:
         xs[...] = x_refs[0][...]
         return
-    own, rest = x_refs[0::2], x_refs[1::2]
-    for part in range(STEPS):
-        at = part * STEPS * LANES
-        for i in range(STEPS - 1):
-            xs[:, pl.ds(at + i * LANES, LANES)] = rest[part][i]
-        xs[:, pl.ds(at + (STEPS - 1) * LANES, LANES)] = own[part][...]
+    for i, x in enumerate(x_refs):
+        for n in range(2):
+            xs[:, pl.ds((2 * i + n) * LANES, LANES)] = x[n]
 
 
 CUTS = 3
@@ -600,35 +602,42 @@
 
 
 def over_z(x, k):
-    return lax.ppermute(x, "space", [(i, (i + 4 * k) % GROUP) for i in range(GROUP)])
+    return lax.ppermute(x, "space", [(i, i ^ (4 * k)) for i in range(GROUP)])
 
 
 def scatter_sums(parts, sums=None):
     near, far_y, near_c, far_yc = parts
+    width = near.shape[1]
+    two = shape((2 * LANES + HEAD, width), jnp.int16)
+    one = shape((LANES + HEAD, width), jnp.int16)
     got_yc = over_core(far_yc)
     got_c = over_core(near_c)
-    first, second, *s = merge_y(far_y, got_yc, sums)
-    first, second = over_y(first), over_y(second)
-    two, one, *s = merge_z(False, near, got_c, first, s[0] if s else None)
-    got = [over_z(two, 2), over_z(one, 1)]
-    three, own = merge_z(True, near, got_c, second, s[0] if s else None)
-    return own, got + [over_z(three, 3)], (s[0] if s else None)
-
-
-def gather_columns(x, after):
-    two, three, one = over_z(x, 2), over_z(x, 3), over_z(x, 1)
-    y_own = over_y(x)
-    c_own = over_core(x)
-    rest = join([two, three, one], y_own, c_own, after)
-    y_rest = over_y(rest)
-    c_rest = over_core(rest)
-    return [x, rest, y_own, y_rest, c_own, c_rest, over_core(y_own), over_core(y_rest)]
+    p, *s = merge(merge_a_kernel, "merge_a", [two], far_y, got_yc, sums=sums)
+    p = over_y(p)
+    (q,) = merge(merge_b_kernel, "merge_b", [two], far_y, got_yc, p)
+    z, *s = merge(merge_c_kernel, "merge_c", [two], near, got_c, p, sums=s[0] if s else None)
+    z, q = over_z(z, 1), over_y(q)
+    out = [shape((LANES, width), F32), one]
+    own, z, *s = merge(merge_d_kernel, "merge_d", out, near, got_c, q, z, sums=s[0] if s else None)
+    return own, [over_z(z, 2)], (s[0] if s else None)
+
+
+def gather_columns(x, work):
+    two = shape((2,) + x.shape, BF)
+    a = pair_of(join_kernel, "join", two, x, over_z(x, 2))
+    b, ya, ca = over_z(a, 1), over_y(a), over_core(a)
+    cya = over_core(ya)
+    cb, yb = over_core(b), over_y(b)
+    done, token = work(b)
+    yb = pair_of(relay_kernel, "relay", two, yb, token)
+    return [b, a, yb, ya, cb, ca, over_core(yb), cya], done
 
 
 def sum_all(x):
     x = x + over_core(x)
     x = x + over_y(x)
-    return [x] + [over_z(x, k) for k in range(1, STEPS)]
+    x = x + over_z(x, 1)
+    return [x, over_z(x, 2)]
 
 
 def on_device(ensemble, innovation, obs_weight, interp_weight, slot_of, intersection_list):
@@ -675,8 +684,8 @@
                 sums = lax.psum(sums, "space")
             return dot(hit.T, high) + dot(hit.T, low), [], sums
 
-        def gather(x, after):
-            return [swap(dot(hit, x.T).astype(BF)).T]
+        def gather(x, work):
+            return [swap(dot(hit, x.T).astype(BF)).T], work(x)[0]
 
         def add_up(x):
             return [lax.psum(x, "space")]
@@ -684,14 +693,14 @@
     ids, weight, far, c0, c1 = adjoint_half(slots, [named, wh, wl], (grouped, me, lists if grouped else []))
     near, n0, n1 = adjoint_half(slots, [ids, weight, wh, wl])
     own, got, _ = scatter([n0, n1, c0, c1])
-    x0, y0, g_sums = coarse_image(ensemble, kern, own, got)
     ens = jnp.transpose(ensemble, (1, 0, 2))
-    g0, token = project(ens, y0, taps)
-    im0, sums, *second = image_first(gather(x0, token), near, far, obs_weight, g_sums)
+    x0, y0, g_sums = coarse_image(ensemble, kern, own, got, after=[ens])
+    xs, g0 = gather(x0, lambda after: project(ens, y0, taps, after))
+    im0, sums, *second = image_first(xs, near, far, obs_weight, g_sums)
     own, got, sums = scatter(second, sums)
     x1, y1, l0, g_sums = coarse_image(ensemble, kern, own, got, y0, sums)
-    g1, token = project(ens, y1, taps)
-    im1, sums = image_second(gather(x1, token), near, far, obs_weight, g_sums)
+    xs, g1 = gather(x1, lambda after: project(ens, y1, taps, after))
+    im1, sums = image_second(xs, near, far, obs_weight, g_sums)
     return tuple(result(l0, add_up(sums), g0, g1, im0, im1))
 
 

time: 125 us -> 130 us (1.040)
  waiting for transfers between devices: 44.4 us -> 48.1 us
    ppermute x18 -> x12, waiting for transfers between devices: 16.1 us -> 27.1 us  [over_z(): return lax.ppermute(x, 'space', [(i, i ^ 4 * k) for i in range(GROUP)])]
    ppermute x10, waiting for transfers between devices: 23.1 us -> 15.9 us  [over_y(): return lax.ppermute(x, 'space', [(i, i ^ 2) for i in range(GROUP)])]
    ppermute x18 -> x12, starting transfers between devices: 25.6 us -> 22.2 us  [over_z(): return lax.ppermute(x, 'space', [(i, i ^ 4 * k) for i in range(GROUP)])]
    ppermute x10, starting transfers between devices: 12.9 us -> 14.4 us  [over_y(): return lax.ppermute(x, 'space', [(i, i ^ 2) for i in range(GROUP)])]
    pallas_call x12 -> x16, Pallas kernels: 15.2 us -> 15.4 us  [the longest x2 7.3 us: project(): pl.pallas_call(project_kernel, in_specs=[VMEM] * 4, out_specs=[VMEM] * 2,...]
  transfers between devices with their start and end apart: 42 -> 36, of which waited for: 21 -> 22; matrix products, arithmetic and copies ran while one was open for 4% -> 4% of each run, Pallas kernels for 10% -> 10%
where the time goes in v6:
time: 130 us; the launch traced here: 129 us
  waiting for transfers between devices  48.1 us (37%)
  starting transfers between devices  40.9 us (31%)
  Pallas kernels  33.7 us (26%)
  local copies, waits for them, and re-layouts  3.88 us (3%)
  other arithmetic  1.62 us (1%)
    ppermute x12, waiting for transfers between devices, over_z(): return lax.ppermute(x, 'space', [(i, i ^ 4 * k) for i in range(GROUP)])  27.1 us
    ppermute x12, starting transfers between devices, over_z(): return lax.ppermute(x, 'space', [(i, i ^ 4 * k) for i in range(GROUP)])  22.2 us
    ppermute x10, waiting for transfers between devices, over_y(): return lax.ppermute(x, 'space', [(i, i ^ 2) for i in range(GROUP)])  15.9 us
    ppermute x10, starting transfers between devices, over_y(): return lax.ppermute(x, 'space', [(i, i ^ 2) for i in range(GROUP)])  14.4 us
    pallas_call x2, Pallas kernels, adjoint_half(): pl.pallas_call(kernel, in_specs=([SMEM] if head else []) + [VMEM] * (len(...  10.5 us
    pallas_call x2, Pallas kernels, project(): pl.pallas_call(project_kernel, in_specs=[VMEM] * 4, out_specs=[VMEM] * 2,...  7.3 us
    pallas_call x2, Pallas kernels, coarse_image(): pl.pallas_call(functools.partial(coarse_kernel, len(got), second, len(aft...  7.22 us
    ppermute x14, waiting for transfers between devices, over_core(): return lax.ppermute(x, 'space', [(i, i ^ 1) for i in range(GROUP)])  5.03 us
  transfers between devices with their start and end apart: 36, of which 22 were waited for; matrix products, arithmetic and copies ran while one was open for 4% of the time, Pallas kernels for 10%

profile of v6, /device:TPU:0, one launch (start us, length us, event | category | flops | bytes accessed | tf_op | source)
XLA Modules:
  0.0 129.3 jit_solution(17466097479254997456)
XLA Ops:
  3.4 2.9 %collective-permute-start.1 = (s32[8,128]{1,0:T(8,128)S(1)}, s32[8,128]{1,0:T(8,128)S(1)}, u32[]{:S(2)}, u32[]{:S(2)}) collective-permute-start(s32[8,128]{1,0:T(8,128)S(1)} %get-tuple-element.49), channel_id=1, source_target_pairs={{0,2},{1,3},{2,0},{3,1},{4,6},{5,7},{6,4},{7,5},{8,10},{9,11},{10,... | collective-permute-start | bytes 12296 | tf_op jit(solution)/shard_map/ppermute | solution.py:601
  7.8 2.1 %collective-permute-start.2 = (s32[8,128]{1,0:T(8,128)S(1)}, s32[8,128]{1,0:T(8,128)S(1)}, u32[]{:S(2)}, u32[]{:S(2)}) collective-permute-start(s32[8,128]{1,0:T(8,128)S(1)} %get-tuple-element.51), channel_id=1, source_target_pairs={{0,4},{1,5},{2,6},{3,7},{4,0},{5,1},{6,2},{7,3},{8,12},{9,13},{10,... | collective-permute-start | bytes 12296 | tf_op jit(solution)/shard_map/ppermute | solution.py:605
  11.6 3.0 %collective-permute-start.3 = (s32[8,128]{1,0:T(8,128)S(1)}, s32[8,128]{1,0:T(8,128)S(1)}, u32[]{:S(2)}, u32[]{:S(2)}) collective-permute-start(s32[8,128]{1,0:T(8,128)S(1)} %get-tuple-element.53), channel_id=1, source_target_pairs={{0,8},{1,9},{2,10},{3,11},{4,12},{5,13},{6,14},{7,15},{8,0},{9,1},... | collective-permute-start | bytes 12296 | tf_op jit(solution)/shard_map/ppermute | solution.py:605
  16.2 5.6 %adjoint_far.1 = (s32[4,1152]{1,0:T(4,128)S(1)}, f32[4,1152]{1,0:T(4,128)S(1)}, bf16[1024,1152]{1,0:T(8,128)(2,1)S(1)}, f32[512,256]{1,0:T(8,128)S(1)}, f32[512,256]{1,0:T(8,128)S(1)}) custom-call(s32[4]{0:T(128)S(1)} %pad_add_fusion.me_ref, s32[8,128]{1,0:T(8,128)S(1)} %get-tuple-element.52.refs_0_, s32[8,128]{1,0:T(8,128)S(1)} %collective-permute-done.3.refs_1_, ...), custom_call_target="tpu_custom_call" | custom-call | flops 1811939328 | bytes 4000000 | tf_op jit(solution)/shard_map/adjoint_far/pallas_call | solution.py:148
  22.3 5.0 %adjoint_near.1 = (bf16[1024,1152]{1,0:T(8,128)(2,1)S(1)}, f32[512,256]{1,0:T(8,128)S(1)}, f32[512,256]{1,0:T(8,128)S(1)}) custom-call(s32[4,1152]{1,0:T(4,128)S(1)} %get-tuple-element.54.ids_ref, f32[4,1152]{1,0:T(4,128)S(1)} %get-tuple-element.55.weight_ref, bf16[1152,256]{1,0:T(8,128)(2,1)S(1)} %get-tuple-element.91.refs_3_.wh_ref, ...), custom_call_target="tpu_custom_call" | custom-call | flops 1811939328 | bytes 4000000 | tf_op jit(solution)/shard_map/adjoint_near/pallas_call | solution.py:148
  27.4 1.9 %collective-permute-start.6 = (s16[272,256]{1,0:T(8,128)(2,1)S(1)}, s16[272,256]{1,0:T(8,128)(2,1)S(1)}, u32[]{:S(2)}, u32[]{:S(2)}) collective-permute-start(s16[272,256]{1,0:T(8,128)(2,1)S(1)} %merge_a.2), channel_id=1, source_target_pairs={{0,2},{1,3},{2,0},{3,1},{4,6},{5,7},{6,4},{7,5},{8,10},{9,11},{10,... | collective-permute-start | bytes 417800 | tf_op jit(solution)/shard_map/ppermute | solution.py:601
  29.3 3.9 %collective-permute-done.6.after_ref.p_ref = s16[272,256]{1,0:T(8,128)(2,1)S(1)} collective-permute-done((s16[272,256]{1,0:T(8,128)(2,1)S(1)}, s16[272,256]{1,0:T(8,128)(2,1)S(1)}, u32[]{:S(2)}, u32[]{:S(2)}) %collective-permute-start.6) | collective-permute-done | bytes 139296 | tf_op jit(solution)/shard_map/ppermute | solution.py:601
  38.4 1.9 %collective-permute-done.7.p_ref = s16[272,256]{1,0:T(8,128)(2,1)S(1)} collective-permute-done((s16[272,256]{1,0:T(8,128)(2,1)S(1)}, s16[272,256]{1,0:T(8,128)(2,1)S(1)}, u32[]{:S(2)}, u32[]{:S(2)}) %collective-permute-start.7) | collective-permute-done | bytes 139296 | tf_op jit(solution)/shard_map/ppermute | solution.py:601
  40.5 2.7 %collective-permute-start.9 = (s16[144,256]{1,0:T(8,128)(2,1)S(1)}, s16[144,256]{1,0:T(8,128)(2,1)S(1)}, u32[]{:S(2)}, u32[]{:S(2)}) collective-permute-start(s16[144,256]{1,0:T(8,128)(2,1)S(1)} %get-tuple-element.61), channel_id=1, source_target_pairs={{0,8},{1,9},{2,10},{3,11},{4,12},{5,13},{6,14},{7,15},{8,0},{9,1},... | collective-permute-start | bytes 221192 | tf_op jit(solution)/shard_map/ppermute | solution.py:605
  43.2 3.1 %copy.12 = bf16[80,128,256]{2,0,1:T(8,128)(2,1)S(1)} copy(bf16[80,128,256]{2,1,0:T(8,128)(2,1)S(1)} %bitcast.12) | data formatting | bytes 10485760 | tf_op args[0]
  46.4 3.6 %coarse_first.1 = (bf16[256,128]{1,0:T(8,128)(2,1)S(1)}, f32[128,256]{1,0:T(8,128)S(1)}, f32[8,256]{1,0:T(8,128)S(1)}) custom-call(bf16[80,128,256]{2,1,0:T(8,128)(2,1)S(1)} %bitcast.12, bf16[256,256]{1,0:T(8,128)(2,1)S(1)} %copy-done.1, f32[128,256]{1,0:T(8,128)S(1)} %get-tuple-element.60.own_ref, s16[144,256]{1,0:T(8,128)(2,1)S(1)} %collective-permute-done.9.refs_0_, ...), custom_call_target="tpu_custom_call" | custom-call | flops 1342177280 | bytes 5000000 | tf_op jit(solution)/shard_map/coarse_first/pallas_call | solution.py:416
  50.0 2.1 %collective-permute-start.10 = (bf16[256,128]{1,0:T(8,128)(2,1)S(1)}, bf16[256,128]{1,0:T(8,128)(2,1)S(1)}, u32[]{:S(2)}, u32[]{:S(2)}) collective-permute-start(bf16[256,128]{1,0:T(8,128)(2,1)S(1)} %get-tuple-element.62.a_ref), channel_id=1, source_target_pairs={{0,8},{1,9},{2,10},{3,11},{4,12},{5,13},{6,14},{7,15},{8,0},{9,1},... | collective-permute-start | bytes 196616 | tf_op jit(solution)/shard_map/ppermute | solution.py:605
  52.2 3.8 %collective-permute-done.10.b_ref = bf16[256,128]{1,0:T(8,128)(2,1)S(1)} collective-permute-done((bf16[256,128]{1,0:T(8,128)(2,1)S(1)}, bf16[256,128]{1,0:T(8,128)(2,1)S(1)}, u32[]{:S(2)}, u32[]{:S(2)}) %collective-permute-start.10) | collective-permute-done | bytes 65568 | tf_op jit(solution)/shard_map/ppermute | solution.py:605
  57.6 3.4 %collective-permute-done.11.after_ref.refs_0_ = bf16[2,256,128]{2,1,0:T(8,128)(2,1)S(1)} collective-permute-done((bf16[2,256,128]{2,1,0:T(8,128)(2,1)S(1)}, bf16[2,256,128]{2,1,0:T(8,128)(2,1)S(1)}, u32[]{:S(2)}, u32[]{:S(2)}) %collective-permute-start.11) | collective-permute-done | bytes 131104 | tf_op jit(solution)/shard_map/ppermute | solution.py:605
  63.0 3.7 %project.2 = (f32[80,8192]{1,0:T(8,128)S(1)}, f32[8,128]{1,0:T(8,128)S(1)}) custom-call(bf16[128,80,256]{2,1,0:T(8,128)(2,1)S(1)} %bitcast.9, f32[128,256]{1,0:T(8,128)S(1)} %get-tuple-element.63.y_ref.refs_1_, bf16[2,256,128]{2,1,0:T(8,128)(2,1)S(1)} %copy-done.2, bf16[2,256,128]{2,1,0:T(8,128)(2,1)S(1)} %collective-permute-done.11.after_ref.refs_0_), custom_call_target="tpu_custom_call" | custom-call | flops 1342177280 | bytes 8000000 | tf_op jit(solution)/shard_map/project/pallas_call | solution.py:454
  68.3 3.2 %image_first.1 = (f32[1152,256]{1,0:T(8,128)S(1)}, f32[8,256]{1,0:T(8,128)S(1)}, f32[512,256]{1,0:T(8,128)S(1)}, f32[512,256]{1,0:T(8,128)S(1)}, f32[512,256]{1,0:T(8,128)S(1)}, /*index=5*/f32[520,256]{1,0:T(8,128)S(1)}) custom-call(bf16[2,256,128]{2,1,0:T(8,128)(2,1)S(1)} %collective-permute-done.11.after_ref.refs_0_, ...), custom_call_target="tpu_custom_call" | custom-call | flops 2415919104 | bytes 13000000 | tf_op jit(solution)/shard_map/image_first/pallas_call | solution.py:511
  74.5 5.0 %collective-permute-done.20.after_ref.p_ref = s16[272,256]{1,0:T(8,128)(2,1)S(1)} collective-permute-done((s16[272,256]{1,0:T(8,128)(2,1)S(1)}, s16[272,256]{1,0:T(8,128)(2,1)S(1)}, u32[]{:S(2)}, u32[]{:S(2)}) %collective-permute-start.20) | collective-permute-done | bytes 139296 | tf_op jit(solution)/shard_map/ppermute | solution.py:601
  81.3 3.5 %collective-permute-done.22.q_ref = s16[272,256]{1,0:T(8,128)(2,1)S(1)} collective-permute-done((s16[272,256]{1,0:T(8,128)(2,1)S(1)}, s16[272,256]{1,0:T(8,128)(2,1)S(1)}, u32[]{:S(2)}, u32[]{:S(2)}) %collective-permute-start.22) | collective-permute-done | bytes 139296 | tf_op jit(solution)/shard_map/ppermute | solution.py:605
  85.1 2.2 %collective-permute-start.23 = (s16[144,256]{1,0:T(8,128)(2,1)S(1)}, s16[144,256]{1,0:T(8,128)(2,1)S(1)}, u32[]{:S(2)}, u32[]{:S(2)}) collective-permute-start(s16[144,256]{1,0:T(8,128)(2,1)S(1)} %get-tuple-element.78), channel_id=1, source_target_pairs={{0,8},{1,9},{2,10},{3,11},{4,12},{5,13},{6,14},{7,15},{8,0},{9,1},... | collective-permute-start | bytes 221192 | tf_op jit(solution)/shard_map/ppermute | solution.py:605
  87.3 3.1 %collective-permute-done.23.refs_0_ = s16[144,256]{1,0:T(8,128)(2,1)S(1)} collective-permute-done((s16[144,256]{1,0:T(8,128)(2,1)S(1)}, s16[144,256]{1,0:T(8,128)(2,1)S(1)}, u32[]{:S(2)}, u32[]{:S(2)}) %collective-permute-start.23) | collective-permute-done | bytes 73760 | tf_op jit(solution)/shard_map/ppermute | solution.py:605
  90.5 3.6 %coarse_second.1 = (bf16[256,128]{1,0:T(8,128)(2,1)S(1)}, f32[128,256]{1,0:T(8,128)S(1)}, f32[8,128]{1,0:T(8,128)S(1)}, f32[8,256]{1,0:T(8,128)S(1)}) custom-call(bf16[80,128,256]{2,1,0:T(8,128)(2,1)S(1)} %bitcast.12, bf16[256,256]{1,0:T(8,128)(2,1)S(1)} %copy-done.1, f32[128,256]{1,0:T(8,128)S(1)} %get-tuple-element.77.own_ref, ...), custom_call_target="tpu_custom_call" | custom-call | flops 1342177280 | bytes 5000000 | tf_op jit(solution)/shard_map/coarse_second/pallas_call | solution.py:416
  94.0 2.2 %collective-permute-start.24 = (bf16[256,128]{1,0:T(8,128)(2,1)S(1)}, bf16[256,128]{1,0:T(8,128)(2,1)S(1)}, u32[]{:S(2)}, u32[]{:S(2)}) collective-permute-start(bf16[256,128]{1,0:T(8,128)(2,1)S(1)} %get-tuple-element.81.a_ref), channel_id=1, source_target_pairs={{0,8},{1,9},{2,10},{3,11},{4,12},{5,13},{6,14},{7,15},{8,0},{9,1},... | collective-permute-start | bytes 196616 | tf_op jit(solution)/shard_map/ppermute | solution.py:605
  96.2 3.1 %collective-permute-done.24.b_ref = bf16[256,128]{1,0:T(8,128)(2,1)S(1)} collective-permute-done((bf16[256,128]{1,0:T(8,128)(2,1)S(1)}, bf16[256,128]{1,0:T(8,128)(2,1)S(1)}, u32[]{:S(2)}, u32[]{:S(2)}) %collective-permute-start.24) | collective-permute-done | bytes 65568 | tf_op jit(solution)/shard_map/ppermute | solution.py:605
  99.4 2.3 %collective-permute-start.25 = (bf16[2,256,128]{2,1,0:T(8,128)(2,1)S(1)}, bf16[2,256,128]{2,1,0:T(8,128)(2,1)S(1)}, u32[]{:S(2)}, u32[]{:S(2)}) collective-permute-start(bf16[2,256,128]{2,1,0:T(8,128)(2,1)S(1)} %join.3.refs_1_), channel_id=1, source_target_pairs={{0,4},{1,5},{2,6},{3,7},{4,0},{5,1},{6,2},{7,3},{8,12},{9,13},{10,... | collective-permute-start | bytes 393224 | tf_op jit(solution)/shard_map/ppermute | solution.py:605
  102.3 2.3 %collective-permute-done.25.after_ref.refs_0_ = bf16[2,256,128]{2,1,0:T(8,128)(2,1)S(1)} collective-permute-done((bf16[2,256,128]{2,1,0:T(8,128)(2,1)S(1)}, bf16[2,256,128]{2,1,0:T(8,128)(2,1)S(1)}, u32[]{:S(2)}, u32[]{:S(2)}) %collective-permute-start.25) | collective-permute-done | bytes 131104 | tf_op jit(solution)/shard_map/ppermute | solution.py:605
  106.7 3.6 %project.3 = (f32[80,8192]{1,0:T(8,128)S(1)}, f32[8,128]{1,0:T(8,128)S(1)}) custom-call(bf16[128,80,256]{2,1,0:T(8,128)(2,1)S(1)} %bitcast.10, f32[128,256]{1,0:T(8,128)S(1)} %get-tuple-element.82.y_ref, bf16[2,256,128]{2,1,0:T(8,128)(2,1)S(1)} %copy-done.2, bf16[2,256,128]{2,1,0:T(8,128)(2,1)S(1)} %collective-permute-done.25.after_ref.refs_0_), custom_call_target="tpu_custom_call" | custom-call | flops 1342177280 | bytes 8000000 | tf_op jit(solution)/shard_map/project/pallas_call | solution.py:454
  111.9 1.9 %image_second.1 = (f32[1152,256]{1,0:T(8,128)S(1)}, f32[8,256]{1,0:T(8,128)S(1)}) custom-call(bf16[2,256,128]{2,1,0:T(8,128)(2,1)S(1)} %collective-permute-done.25.after_ref.refs_0_, bf16[2,256,128]{2,1,0:T(8,128)(2,1)S(1)} %join.3.refs_1_, bf16[2,256,128]{2,1,0:T(8,128)(2,1)S(1)} %relay.3.refs_2_, bf16[2,256,128]{2,1,0:T(8,128)(2,1)S(1)} %collective-permute-done.27.refs_3_, ...), custom_call_target="tpu_custom_call" | custom-call | flops 1207959552 | bytes 8000000 | tf_op jit(solution)/shard_map/image_second/pallas_call | solution.py:537
  115.7 3.0 %collective-permute-done.33 = f32[8,256]{1,0:T(8,128)S(1)} collective-permute-done((f32[8,256]{1,0:T(8,128)S(1)}, f32[8,256]{1,0:T(8,128)S(1)}, u32[]{:S(2)}, u32[]{:S(2)}) %collective-permute-start.33) | collective-permute-done | bytes 8224 | tf_op jit(solution)/shard_map/ppermute | solution.py:601
  119.9 2.5 %collective-permute-done.34 = f32[8,256]{1,0:T(8,128)S(1)} collective-permute-done((f32[8,256]{1,0:T(8,128)S(1)}, f32[8,256]{1,0:T(8,128)S(1)}, u32[]{:S(2)}, u32[]{:S(2)}) %collective-permute-start.34) | collective-permute-done | bytes 8224 | tf_op jit(solution)/shard_map/ppermute | solution.py:605
  122.4 2.4 %collective-permute-start.35 = (f32[8,256]{1,0:T(8,128)S(1)}, f32[8,256]{1,0:T(8,128)S(1)}, u32[]{:S(2)}, u32[]{:S(2)}) collective-permute-start(f32[8,256]{1,0:T(8,128)S(1)} %add.22.refs_0_), channel_id=1, source_target_pairs={{0,8},{1,9},{2,10},{3,11},{4,12},{5,13},{6,14},{7,15},{8,0},{9,1},... | collective-permute-start | bytes 24584 | tf_op jit(solution)/shard_map/ppermute | solution.py:605
  124.8 2.1 %collective-permute-done.35.refs_1_ = f32[8,256]{1,0:T(8,128)S(1)} collective-permute-done((f32[8,256]{1,0:T(8,128)S(1)}, f32[8,256]{1,0:T(8,128)S(1)}, u32[]{:S(2)}, u32[]{:S(2)}) %collective-permute-start.35) | collective-permute-done | bytes 8224 | tf_op jit(solution)/shard_map/ppermute | solution.py:605
  127.0 2.2 %result.1 = (f32[80,8192]{1,0:T(8,128)}, f32[1152,256]{1,0:T(8,128)}) custom-call(f32[8,128]{1,0:T(8,128)S(1)} %get-tuple-element.80.l0_ref, f32[8,256]{1,0:T(8,128)S(1)} %add.22.refs_0_, f32[8,256]{1,0:T(8,128)S(1)} %collective-permute-done.35.refs_1_, f32[80,8192]{1,0:T(8,128)S(1)} %get-tuple-element.86.refs_2_, f32[80,8192]{1,0:T(8,128)S(1)} %get-tuple-element.87.refs_3_, ...), custom_call_target="tpu_custom_call" | custom-call | flops 1966080 | bytes 10000000 | tf_op jit(solution)/shard_map/result/pallas_call | solution.py:580
  (90 shorter events, 31.1 us)
Async XLA Ops:
  3.4 4.4 %collective-permute-start.1 = (s32[8,128]{1,0:T(8,128)S(1)}, s32[8,128]{1,0:T(8,128)S(1)}, u32[]{:S(2)}, u32[]{:S(2)}) collective-permute-start(s32[8,128]{1,0:T(8,128)S(1)} %get-tuple-element.49), channel_id=1, source_target_pairs={{0,2},{1,3},{2,0},{3,1},{4,6},{5,7},{6,4},{7,5},{8,10},{9,11},{10,... | collective-permute-start | bytes 12296 | tf_op jit(solution)/shard_map/ppermute | solution.py:601
  7.8 3.7 %collective-permute-start.2 = (s32[8,128]{1,0:T(8,128)S(1)}, s32[8,128]{1,0:T(8,128)S(1)}, u32[]{:S(2)}, u32[]{:S(2)}) collective-permute-start(s32[8,128]{1,0:T(8,128)S(1)} %get-tuple-element.51), channel_id=1, source_target_pairs={{0,4},{1,5},{2,6},{3,7},{4,0},{5,1},{6,2},{7,3},{8,12},{9,13},{10,... | collective-permute-start | bytes 12296 | tf_op jit(solution)/shard_map/ppermute | solution.py:605
  11.6 4.6 %collective-permute-start.3 = (s32[8,128]{1,0:T(8,128)S(1)}, s32[8,128]{1,0:T(8,128)S(1)}, u32[]{:S(2)}, u32[]{:S(2)}) collective-permute-start(s32[8,128]{1,0:T(8,128)S(1)} %get-tuple-element.53), channel_id=1, source_target_pairs={{0,8},{1,9},{2,10},{3,11},{4,12},{5,13},{6,14},{7,15},{8,0},{9,1},... | collective-permute-start | bytes 12296 | tf_op jit(solution)/shard_map/ppermute | solution.py:605
  21.7 5.6 %collective-permute-start.5 = (f32[512,256]{1,0:T(8,128)S(1)}, f32[512,256]{1,0:T(8,128)S(1)}, u32[]{:S(2)}, u32[]{:S(2)}) collective-permute-start(f32[512,256]{1,0:T(8,128)S(1)} %get-tuple-element.59), channel_id=1, source_target_pairs={{0,1},{1,0},{2,3},{3,2},{4,5},{5,4},{6,7},{7,6},{8,9},{9,8},{10,11... | collective-permute-start | bytes 1572872 | tf_op jit(solution)/shard_map/ppermute | solution.py:597
  21.8 7.5 %collective-permute-start.4 = (f32[512,256]{1,0:T(8,128)S(1)}, f32[512,256]{1,0:T(8,128)S(1)}, u32[]{:S(2)}, u32[]{:S(2)}) collective-permute-start(f32[512,256]{1,0:T(8,128)S(1)} %get-tuple-element.57), channel_id=1, source_target_pairs={{0,1},{1,0},{2,3},{3,2},{4,5},{5,4},{6,7},{7,6},{8,9},{9,8},{10,11... | collective-permute-start | bytes 1572872 | tf_op jit(solution)/shard_map/ppermute | solution.py:597
  27.4 5.8 %collective-permute-start.6 = (s16[272,256]{1,0:T(8,128)(2,1)S(1)}, s16[272,256]{1,0:T(8,128)(2,1)S(1)}, u32[]{:S(2)}, u32[]{:S(2)}) collective-permute-start(s16[272,256]{1,0:T(8,128)(2,1)S(1)} %merge_a.2), channel_id=1, source_target_pairs={{0,2},{1,3},{2,0},{3,1},{4,6},{5,7},{6,4},{7,5},{8,10},{9,11},{10,... | collective-permute-start | bytes 417800 | tf_op jit(solution)/shard_map/ppermute | solution.py:601
  33.3 5.1 %collective-permute-start.8 = (s16[272,256]{1,0:T(8,128)(2,1)S(1)}, s16[272,256]{1,0:T(8,128)(2,1)S(1)}, u32[]{:S(2)}, u32[]{:S(2)}) collective-permute-start(s16[272,256]{1,0:T(8,128)(2,1)S(1)} %merge_c.2), channel_id=1, source_target_pairs={{0,4},{1,5},{2,6},{3,7},{4,0},{5,1},{6,2},{7,3},{8,12},{9,13},{10,... | collective-permute-start | bytes 417800 | tf_op jit(solution)/shard_map/ppermute | solution.py:605
  35.3 5.1 %collective-permute-start.7 = (s16[272,256]{1,0:T(8,128)(2,1)S(1)}, s16[272,256]{1,0:T(8,128)(2,1)S(1)}, u32[]{:S(2)}, u32[]{:S(2)}) collective-permute-start(s16[272,256]{1,0:T(8,128)(2,1)S(1)} %merge_b.2), channel_id=1, source_target_pairs={{0,2},{1,3},{2,0},{3,1},{4,6},{5,7},{6,4},{7,5},{8,10},{9,11},{10,... | collective-permute-start | bytes 417800 | tf_op jit(solution)/shard_map/ppermute | solution.py:601
  40.5 5.8 %collective-permute-start.9 = (s16[144,256]{1,0:T(8,128)(2,1)S(1)}, s16[144,256]{1,0:T(8,128)(2,1)S(1)}, u32[]{:S(2)}, u32[]{:S(2)}) collective-permute-start(s16[144,256]{1,0:T(8,128)(2,1)S(1)} %get-tuple-element.61), channel_id=1, source_target_pairs={{0,8},{1,9},{2,10},{3,11},{4,12},{5,13},{6,14},{7,15},{8,0},{9,1},... | collective-permute-start | bytes 221192 | tf_op jit(solution)/shard_map/ppermute | solution.py:605
  50.0 5.9 %collective-permute-start.10 = (bf16[256,128]{1,0:T(8,128)(2,1)S(1)}, bf16[256,128]{1,0:T(8,128)(2,1)S(1)}, u32[]{:S(2)}, u32[]{:S(2)}) collective-permute-start(bf16[256,128]{1,0:T(8,128)(2,1)S(1)} %get-tuple-element.62.a_ref), channel_id=1, source_target_pairs={{0,8},{1,9},{2,10},{3,11},{4,12},{5,13},{6,14},{7,15},{8,0},{9,1},... | collective-permute-start | bytes 196616 | tf_op jit(solution)/shard_map/ppermute | solution.py:605
  56.0 5.0 %collective-permute-start.11 = (bf16[2,256,128]{2,1,0:T(8,128)(2,1)S(1)}, bf16[2,256,128]{2,1,0:T(8,128)(2,1)S(1)}, u32[]{:S(2)}, u32[]{:S(2)}) collective-permute-start(bf16[2,256,128]{2,1,0:T(8,128)(2,1)S(1)} %join.2.refs_1_), channel_id=1, source_target_pairs={{0,4},{1,5},{2,6},{3,7},{4,0},{5,1},{6,2},{7,3},{8,12},{9,13},{10,... | collective-permute-start | bytes 393224 | tf_op jit(solution)/shard_map/ppermute | solution.py:605
  56.0 6.9 %collective-permute-start.13 = (bf16[2,256,128]{2,1,0:T(8,128)(2,1)S(1)}, bf16[2,256,128]{2,1,0:T(8,128)(2,1)S(1)}, u32[]{:S(2)}, u32[]{:S(2)}) collective-permute-start(bf16[2,256,128]{2,1,0:T(8,128)(2,1)S(1)} %join.2.refs_1_), channel_id=1, source_target_pairs={{0,2},{1,3},{2,0},{3,1},{4,6},{5,7},{6,4},{7,5},{8,10},{9,11},{10,... | collective-permute-start | bytes 393224 | tf_op jit(solution)/shard_map/ppermute | solution.py:601
  61.0 5.7 %collective-permute-start.12 = (bf16[2,256,128]{2,1,0:T(8,128)(2,1)S(1)}, bf16[2,256,128]{2,1,0:T(8,128)(2,1)S(1)}, u32[]{:S(2)}, u32[]{:S(2)}) collective-permute-start(bf16[2,256,128]{2,1,0:T(8,128)(2,1)S(1)} %collective-permute-done.11.after_ref.refs_0_), channel_id=1, source_target_pairs={{0,2},{1,3},{2,0},{3,1},{4,6},{5,7},{6,4},{7,5},{8,10},{9,11},{10,... | collective-permute-start | bytes 393224 | tf_op jit(solution)/shard_map/ppermute | solution.py:601
  62.5 4.8 %collective-permute-start.15 = (bf16[2,256,128]{2,1,0:T(8,128)(2,1)S(1)}, bf16[2,256,128]{2,1,0:T(8,128)(2,1)S(1)}, u32[]{:S(2)}, u32[]{:S(2)}) collective-permute-start(bf16[2,256,128]{2,1,0:T(8,128)(2,1)S(1)} %join.2.refs_1_), channel_id=1, source_target_pairs={{0,1},{1,0},{2,3},{3,2},{4,5},{5,4},{6,7},{7,6},{8,9},{9,8},{10,11... | collective-permute-start | bytes 393224 | tf_op jit(solution)/shard_map/ppermute | solution.py:597
  62.5 4.8 %collective-permute-start.14 = (bf16[2,256,128]{2,1,0:T(8,128)(2,1)S(1)}, bf16[2,256,128]{2,1,0:T(8,128)(2,1)S(1)}, u32[]{:S(2)}, u32[]{:S(2)}) collective-permute-start(bf16[2,256,128]{2,1,0:T(8,128)(2,1)S(1)} %collective-permute-done.11.after_ref.refs_0_), channel_id=1, source_target_pairs={{0,1},{1,0},{2,3},{3,2},{4,5},{5,4},{6,7},{7,6},{8,9},{9,8},{10,11... | collective-permute-start | bytes 393224 | tf_op jit(solution)/shard_map/ppermute | solution.py:597
  63.0 4.3 %collective-permute-start.17 = (bf16[2,256,128]{2,1,0:T(8,128)(2,1)S(1)}, bf16[2,256,128]{2,1,0:T(8,128)(2,1)S(1)}, u32[]{:S(2)}, u32[]{:S(2)}) collective-permute-start(bf16[2,256,128]{2,1,0:T(8,128)(2,1)S(1)} %collective-permute-done.13.refs_3_), channel_id=1, source_target_pairs={{0,1},{1,0},{2,3},{3,2},{4,5},{5,4},{6,7},{7,6},{8,9},{9,8},{10,11... | collective-permute-start | bytes 393224 | tf_op jit(solution)/shard_map/ppermute | solution.py:597
  71.4 2.0 %collective-permute-start.19 = (f32[520,256]{1,0:T(8,128)S(1)}, f32[520,256]{1,0:T(8,128)S(1)}, u32[]{:S(2)}, u32[]{:S(2)}) collective-permute-start(f32[520,256]{1,0:T(8,128)S(1)} %get-tuple-element.71), channel_id=1, source_target_pairs={{0,1},{1,0},{2,3},{3,2},{4,5},{5,4},{6,7},{7,6},{8,9},{9,8},{10,11... | collective-permute-start | bytes 1597448 | tf_op jit(solution)/shard_map/ppermute | solution.py:597
  71.9 2.7 %collective-permute-start.18 = (f32[512,256]{1,0:T(8,128)S(1)}, f32[512,256]{1,0:T(8,128)S(1)}, u32[]{:S(2)}, u32[]{:S(2)}) collective-permute-start(f32[512,256]{1,0:T(8,128)S(1)} %get-tuple-element.69), channel_id=1, source_target_pairs={{0,1},{1,0},{2,3},{3,2},{4,5},{5,4},{6,7},{7,6},{8,9},{9,8},{10,11... | collective-permute-start | bytes 1572872 | tf_op jit(solution)/shard_map/ppermute | solution.py:597
  73.5 6.0 %collective-permute-start.20 = (s16[272,256]{1,0:T(8,128)(2,1)S(1)}, s16[272,256]{1,0:T(8,128)(2,1)S(1)}, u32[]{:S(2)}, u32[]{:S(2)}) collective-permute-start(s16[272,256]{1,0:T(8,128)(2,1)S(1)} %get-tuple-element.73), channel_id=1, source_target_pairs={{0,2},{1,3},{2,0},{3,1},{4,6},{5,7},{6,4},{7,5},{8,10},{9,11},{10,... | collective-permute-start | bytes 417800 | tf_op jit(solution)/shard_map/ppermute | solution.py:601
  79.6 5.2 %collective-permute-start.22 = (s16[272,256]{1,0:T(8,128)(2,1)S(1)}, s16[272,256]{1,0:T(8,128)(2,1)S(1)}, u32[]{:S(2)}, u32[]{:S(2)}) collective-permute-start(s16[272,256]{1,0:T(8,128)(2,1)S(1)} %get-tuple-element.75), channel_id=1, source_target_pairs={{0,4},{1,5},{2,6},{3,7},{4,0},{5,1},{6,2},{7,3},{8,12},{9,13},{10,... | collective-permute-start | bytes 417800 | tf_op jit(solution)/shard_map/ppermute | solution.py:605
  79.8 5.2 %collective-permute-start.21 = (s16[272,256]{1,0:T(8,128)(2,1)S(1)}, s16[272,256]{1,0:T(8,128)(2,1)S(1)}, u32[]{:S(2)}, u32[]{:S(2)}) collective-permute-start(s16[272,256]{1,0:T(8,128)(2,1)S(1)} %merge_b.3), channel_id=1, source_target_pairs={{0,2},{1,3},{2,0},{3,1},{4,6},{5,7},{6,4},{7,5},{8,10},{9,11},{10,... | collective-permute-start | bytes 417800 | tf_op jit(solution)/shard_map/ppermute | solution.py:601
  85.1 5.3 %collective-permute-start.23 = (s16[144,256]{1,0:T(8,128)(2,1)S(1)}, s16[144,256]{1,0:T(8,128)(2,1)S(1)}, u32[]{:S(2)}, u32[]{:S(2)}) collective-permute-start(s16[144,256]{1,0:T(8,128)(2,1)S(1)} %get-tuple-element.78), channel_id=1, source_target_pairs={{0,8},{1,9},{2,10},{3,11},{4,12},{5,13},{6,14},{7,15},{8,0},{9,1},... | collective-permute-start | bytes 221192 | tf_op jit(solution)/shard_map/ppermute | solution.py:605
  94.0 5.3 %collective-permute-start.24 = (bf16[256,128]{1,0:T(8,128)(2,1)S(1)}, bf16[256,128]{1,0:T(8,128)(2,1)S(1)}, u32[]{:S(2)}, u32[]{:S(2)}) collective-permute-start(bf16[256,128]{1,0:T(8,128)(2,1)S(1)} %get-tuple-element.81.a_ref), channel_id=1, source_target_pairs={{0,8},{1,9},{2,10},{3,11},{4,12},{5,13},{6,14},{7,15},{8,0},{9,1},... | collective-permute-start | bytes 196616 | tf_op jit(solution)/shard_map/ppermute | solution.py:605
  99.4 5.3 %collective-permute-start.25 = (bf16[2,256,128]{2,1,0:T(8,128)(2,1)S(1)}, bf16[2,256,128]{2,1,0:T(8,128)(2,1)S(1)}, u32[]{:S(2)}, u32[]{:S(2)}) collective-permute-start(bf16[2,256,128]{2,1,0:T(8,128)(2,1)S(1)} %join.3.refs_1_), channel_id=1, source_target_pairs={{0,4},{1,5},{2,6},{3,7},{4,0},{5,1},{6,2},{7,3},{8,12},{9,13},{10,... | collective-permute-start | bytes 393224 | tf_op jit(solution)/shard_map/ppermute | solution.py:605
  101.7 5.0 %collective-permute-start.27 = (bf16[2,256,128]{2,1,0:T(8,128)(2,1)S(1)}, bf16[2,256,128]{2,1,0:T(8,128)(2,1)S(1)}, u32[]{:S(2)}, u32[]{:S(2)}) collective-permute-start(bf16[2,256,128]{2,1,0:T(8,128)(2,1)S(1)} %join.3.refs_1_), channel_id=1, source_target_pairs={{0,2},{1,3},{2,0},{3,1},{4,6},{5,7},{6,4},{7,5},{8,10},{9,11},{10,... | collective-permute-start | bytes 393224 | tf_op jit(solution)/shard_map/ppermute | solution.py:601
  104.7 5.7 %collective-permute-start.26 = (bf16[2,256,128]{2,1,0:T(8,128)(2,1)S(1)}, bf16[2,256,128]{2,1,0:T(8,128)(2,1)S(1)}, u32[]{:S(2)}, u32[]{:S(2)}) collective-permute-start(bf16[2,256,128]{2,1,0:T(8,128)(2,1)S(1)} %collective-permute-done.25.after_ref.refs_0_), channel_id=1, source_target_pairs={{0,2},{1,3},{2,0},{3,1},{4,6},{5,7},{6,4},{7,5},{8,10},{9,11},{10,... | collective-permute-start | bytes 393224 | tf_op jit(solution)/shard_map/ppermute | solution.py:601
  105.9 5.1 %collective-permute-start.29 = (bf16[2,256,128]{2,1,0:T(8,128)(2,1)S(1)}, bf16[2,256,128]{2,1,0:T(8,128)(2,1)S(1)}, u32[]{:S(2)}, u32[]{:S(2)}) collective-permute-start(bf16[2,256,128]{2,1,0:T(8,128)(2,1)S(1)} %join.3.refs_1_), channel_id=1, source_target_pairs={{0,1},{1,0},{2,3},{3,2},{4,5},{5,4},{6,7},{7,6},{8,9},{9,8},{10,11... | collective-permute-start | bytes 393224 | tf_op jit(solution)/shard_map/ppermute | solution.py:597
  105.9 5.1 %collective-permute-start.28 = (bf16[2,256,128]{2,1,0:T(8,128)(2,1)S(1)}, bf16[2,256,128]{2,1,0:T(8,128)(2,1)S(1)}, u32[]{:S(2)}, u32[]{:S(2)}) collective-permute-start(bf16[2,256,128]{2,1,0:T(8,128)(2,1)S(1)} %collective-permute-done.25.after_ref.refs_0_), channel_id=1, source_target_pairs={{0,1},{1,0},{2,3},{3,2},{4,5},{5,4},{6,7},{7,6},{8,9},{9,8},{10,11... | collective-permute-start | bytes 393224 | tf_op jit(solution)/shard_map/ppermute | solution.py:597
  106.7 4.3 %collective-permute-start.31 = (bf16[2,256,128]{2,1,0:T(8,128)(2,1)S(1)}, bf16[2,256,128]{2,1,0:T(8,128)(2,1)S(1)}, u32[]{:S(2)}, u32[]{:S(2)}) collective-permute-start(bf16[2,256,128]{2,1,0:T(8,128)(2,1)S(1)} %collective-permute-done.27.refs_3_), channel_id=1, source_target_pairs={{0,1},{1,0},{2,3},{3,2},{4,5},{5,4},{6,7},{7,6},{8,9},{9,8},{10,11... | collective-permute-start | bytes 393224 | tf_op jit(solution)/shard_map/ppermute | solution.py:597
  115.1 3.7 %collective-permute-start.33 = (f32[8,256]{1,0:T(8,128)S(1)}, f32[8,256]{1,0:T(8,128)S(1)}, u32[]{:S(2)}, u32[]{:S(2)}) collective-permute-start(f32[8,256]{1,0:T(8,128)S(1)} %add.20), channel_id=1, source_target_pairs={{0,2},{1,3},{2,0},{3,1},{4,6},{5,7},{6,4},{7,5},{8,10},{9,11},{10,... | collective-permute-start | bytes 24584 | tf_op jit(solution)/shard_map/ppermute | solution.py:601
  118.8 3.7 %collective-permute-start.34 = (f32[8,256]{1,0:T(8,128)S(1)}, f32[8,256]{1,0:T(8,128)S(1)}, u32[]{:S(2)}, u32[]{:S(2)}) collective-permute-start(f32[8,256]{1,0:T(8,128)S(1)} %add.21), channel_id=1, source_target_pairs={{0,4},{1,5},{2,6},{3,7},{4,0},{5,1},{6,2},{7,3},{8,12},{9,13},{10,... | collective-permute-start | bytes 24584 | tf_op jit(solution)/shard_map/ppermute | solution.py:605
  122.4 4.5 %collective-permute-start.35 = (f32[8,256]{1,0:T(8,128)S(1)}, f32[8,256]{1,0:T(8,128)S(1)}, u32[]{:S(2)}, u32[]{:S(2)}) collective-permute-start(f32[8,256]{1,0:T(8,128)S(1)} %add.22.refs_0_), channel_id=1, source_target_pairs={{0,8},{1,9},{2,10},{3,11},{4,12},{5,13},{6,14},{7,15},{8,0},{9,1},... | collective-permute-start | bytes 24584 | tf_op jit(solution)/shard_map/ppermute | solution.py:605
  (12 other events, 92.5 us)

commit v7 on v4

--- a/solution.py
+++ b/solution.py
@@ -53,7 +53,7 @@
 
 
 STEPS = 4
-ORDER = (2, 1, 3, 0)
+ORDER = (2, 3, 1, 0)
 PARTS = ((0, 0), (1, 0), (0, 1), (1, 1))
 HEAD = 16
 TOP = 32512.0
@@ -64,7 +64,7 @@
     z, y, c = me_ref[0], me_ref[1], me_ref[2]
     y = y if dy == 0 else 1 - y
     c = c if dc == 0 else 1 - c
-    return (lax.rem(z + ORDER[i % STEPS], STEPS) * 2 + y) * 2 + c
+    return (jnp.bitwise_xor(z, ORDER[i % STEPS]) * 2 + y) * 2 + c
 
 
 def places(me_ref, list_refs, slots):
@@ -75,7 +75,7 @@
     for i in range(GROUP):
         o = owner_at(me_ref, i)
         dy, dc = PARTS[i // STEPS]
-        held = list_refs[-ORDER[i % STEPS] % STEPS]
+        held = list_refs[ORDER[i % STEPS]]
         row = jnp.broadcast_to(held[2 * dy + dc : 2 * dy + dc + 1, :], slots.shape)
         column = jnp.take_along_axis(row, within, axis=1, mode="promise_in_bounds")
         rows = jnp.where(from_owner == o, column + i * LANES, rows)
@@ -150,7 +150,7 @@
     z, y, c = me_ref[0], me_ref[1], me_ref[2]
     for dy in range(2):
         for k in range(STEPS):
-            there = (lax.rem(z + k, STEPS) * 2 + (y if dy == 0 else 1 - y)) * 2
+            there = (jnp.bitwise_xor(z, k) * 2 + (y if dy == 0 else 1 - y)) * 2
             row = slice(dy * STEPS + k, dy * STEPS + k + 1)
             near_ref[row, :] = lists_ref[pl.ds(there + c, 1), :]
             far_ref[row, :] = lists_ref[pl.ds(there + 1 - c, 1), :]
@@ -188,7 +188,7 @@
     near, far = small(pick_kernel, 2, "pick", me, lists, scalars=1)
     near, far = small(mix_y_kernel, 2, "mix_y", near, over_core(far))
     own, *sent = small(mix_z_kernel, STEPS, "mix_z", near, over_y(far))
-    return [own] + [over_z(sent[k - 1], k) for k in range(1, STEPS)]
+    return [own] + [over_z(sent[k - 1], k) for k in range(1, STEPS)], own
 
 
 def exponent(m):
@@ -309,21 +309,24 @@
 
 
 def join_kernel(*refs):
-    out_ref = refs[-1]
-    for i, r in enumerate(refs[:3]):
-        out_ref[i] = r[...]
-
-
-def join(blocks, *after):
-    return pl.pallas_call(
-        join_kernel,
-        in_specs=[VMEM] * (3 + len(after)),
+    for i, r in enumerate(refs[:-1]):
+        refs[-1][i] = r[...]
+
+
+def relay_kernel(x_ref, after_ref, out_ref):
+    out_ref[...] = x_ref[...]
+
+
+def copy_of(kernel, name, out, *args):
+    return pl.pallas_call(
+        kernel,
+        in_specs=[VMEM] * len(args),
         out_specs=VMEM,
-        out_shape=shape((3,) + blocks[0].shape, BF),
+        out_shape=out,
         compiler_params=params(8),
-        cost_estimate=cost(1e5, 4e5),
-        name="join",
-    )(*blocks, *after)
+        cost_estimate=cost(1e5, 5e5),
+        name=name,
+    )(*args)
 
 
 def fold(a):
@@ -349,7 +352,7 @@
 SOME = 8
 
 
-def coarse_kernel(packed, second, e_ref, k_ref, own_ref, *refs):
+def coarse_kernel(packed, second, after, e_ref, k_ref, own_ref, *refs):
     refs = list(refs)
     got = [refs.pop(0) for _ in range(packed)]
     y = own_ref[...]
@@ -362,8 +365,8 @@
             sums = sums + unpack_sums(r)
         l0, keep = length_of(sums)
         y = keep * y0_ref[...] - l0 * y
-        refs.pop(2)[...] = jnp.broadcast_to(l0, (8, LANES))
-    x_ref, y_ref, sum_ref, even_s, odd_s, x_s = refs
+        refs.pop(after + 2)[...] = jnp.broadcast_to(l0, (8, LANES))
+    x_ref, y_ref, sum_ref, even_s, odd_s, x_s = refs[after:]
     members, columns, width = e_ref.shape
     y_ref[...] = y
     x_s[...] = jnp.zeros_like(x_s)
@@ -401,16 +404,16 @@
     sum_ref[0:1, :] = fold(x * y_ref[...])
 
 
-def coarse_image(ensemble, kern, own, got, y0=None, sums=None):
+def coarse_image(ensemble, kern, own, got, y0=None, sums=None, after=()):
     members, columns, width = ensemble.shape
     second = y0 is not None
-    args = [ensemble, kern, own, *got] + ([y0, sums] if second else [])
+    args = [ensemble, kern, own, *got] + ([y0, sums] if second else []) + list(after)
     out = [shape((width, columns), BF), shape((columns, width), F32)]
     out += [shape((8, LANES), F32)] if second else []
     out += [shape((8, width), F32)]
     return pl.pallas_call(
-        functools.partial(coarse_kernel, len(got), second),
-        in_specs=[VMEM] * len(args),
+        functools.partial(coarse_kernel, len(got), second, len(after)),
+        in_specs=[VMEM] * (len(args) - len(after)) + [ANY] * len(after),
         out_specs=[VMEM] * len(out),
         out_shape=out,
         scratch_shapes=[
@@ -424,7 +427,7 @@
     )(*args)
 
 
-def project_kernel(e_ref, y_ref, t_ref, g_ref, token_ref, even_s, odd_s):
+def project_kernel(e_ref, y_ref, t_ref, after_ref, g_ref, token_ref, even_s, odd_s):
     columns, members, width = e_ref.shape
     lanes = BATCH // 2 * LANES
     token_ref[...] = jnp.zeros_like(token_ref)
@@ -443,31 +446,28 @@
             g_ref[:, pl.ds(at, LANES)] = r[pair * members : (pair + 1) * members]
 
 
-def project(ens, y, taps):
+def project(ens, y, taps, after):
     columns, members, width = ens.shape
     levels = width // VAR
     return pl.pallas_call(
         project_kernel,
-        in_specs=[VMEM] * 3,
+        in_specs=[VMEM] * 4,
         out_specs=[VMEM] * 2,
         out_shape=[shape((members, columns * levels), F32), shape((8, LANES), F32)],
         scratch_shapes=[pltpu.VMEM((BATCH // 2 * members, width), BF)] * 2,
         compiler_params=params(16),
         cost_estimate=cost(2 * columns * members * width * width, 8e6),
         name="project",
-    )(ens, y, taps)
+    )(ens, y, taps, after)
 
 
 def lay_out(x_refs, xs):
     if len(x_refs) == 1:
         xs[...] = x_refs[0][...]
         return
-    own, rest = x_refs[0::2], x_refs[1::2]
-    for part in range(STEPS):
-        at = part * STEPS * LANES
-        for i in range(STEPS - 1):
-            xs[:, pl.ds(at + i * LANES, LANES)] = rest[part][i]
-        xs[:, pl.ds(at + (STEPS - 1) * LANES, LANES)] = own[part][...]
+    for i, x in enumerate(x_refs):
+        for n in range(STEPS):
+            xs[:, pl.ds((i * STEPS + n) * LANES, LANES)] = x[n]
 
 
 CUTS = 3
@@ -600,7 +600,7 @@
 
 
 def over_z(x, k):
-    return lax.ppermute(x, "space", [(i, (i + 4 * k) % GROUP) for i in range(GROUP)])
+    return lax.ppermute(x, "space", [(i, i ^ (4 * k)) for i in range(GROUP)])
 
 
 def scatter_sums(parts, sums=None):
@@ -609,20 +609,19 @@
     got_c = over_core(near_c)
     first, second, *s = merge_y(far_y, got_yc, sums)
     first, second = over_y(first), over_y(second)
-    two, one, *s = merge_z(False, near, got_c, first, s[0] if s else None)
-    got = [over_z(two, 2), over_z(one, 1)]
-    three, own = merge_z(True, near, got_c, second, s[0] if s else None)
-    return own, got + [over_z(three, 3)], (s[0] if s else None)
-
-
-def gather_columns(x, after):
-    two, three, one = over_z(x, 2), over_z(x, 3), over_z(x, 1)
-    y_own = over_y(x)
-    c_own = over_core(x)
-    rest = join([two, three, one], y_own, c_own, after)
-    y_rest = over_y(rest)
-    c_rest = over_core(rest)
-    return [x, rest, y_own, y_rest, c_own, c_rest, over_core(y_own), over_core(y_rest)]
+    two, three, *s = merge_z(False, near, got_c, first, s[0] if s else None)
+    got = [over_z(two, 2), over_z(three, 3)]
+    one, own = merge_z(True, near, got_c, second, s[0] if s else None)
+    return own, got + [over_z(one, 1)], (s[0] if s else None)
+
+
+def gather_columns(x, work):
+    four = shape((STEPS,) + x.shape, BF)
+    a = copy_of(join_kernel, "join", four, *[over_z(x, k) for k in ORDER[:3]], x)
+    ya, ca = over_y(a), over_core(a)
+    done, token = work(a)
+    ya = copy_of(relay_kernel, "relay", four, ya, token)
+    return [a, ya, ca, over_core(ya)], done
 
 
 def sum_all(x):
@@ -651,15 +650,13 @@
 
     index = lax.axis_index("space").astype(jnp.int32)
     me = jnp.stack([index // 4, index // 2 % 2, index % 2, index])
-    w = -(obs_weight.astype(F32) * innovation.astype(F32))
-    high = lax.reduce_precision(w, 8, 7)
-    wh, wl = high.astype(BF), (w - high).astype(BF)
     named = jnp.concatenate([slot_of.astype(F32), interp_weight], axis=0)
     if grouped:
-        lists = exchange_lists(me, intersection_list[0])
+        lists, after = exchange_lists(me, intersection_list[0])
+        late = 0.0 * after[:1, :1].astype(F32)
         scatter, gather, add_up = scatter_sums, gather_columns, sum_all
     else:
-        lists = intersection_list[0]
+        lists, late = intersection_list[0], 0.0
         hit = (lists.reshape(-1, 1) == jnp.arange(columns, dtype=jnp.int32)).astype(BF)
 
         def swap(x):
@@ -675,23 +672,26 @@
                 sums = lax.psum(sums, "space")
             return dot(hit.T, high) + dot(hit.T, low), [], sums
 
-        def gather(x, after):
-            return [swap(dot(hit, x.T).astype(BF)).T]
+        def gather(x, work):
+            return [swap(dot(hit, x.T).astype(BF)).T], work(x)[0]
 
         def add_up(x):
             return [lax.psum(x, "space")]
 
+    w = late - obs_weight.astype(F32) * innovation.astype(F32)
+    high = lax.reduce_precision(w, 8, 7)
+    wh, wl = high.astype(BF), (w - high).astype(BF)
     ids, weight, far, c0, c1 = adjoint_half(slots, [named, wh, wl], (grouped, me, lists if grouped else []))
     near, n0, n1 = adjoint_half(slots, [ids, weight, wh, wl])
     own, got, _ = scatter([n0, n1, c0, c1])
-    x0, y0, g_sums = coarse_image(ensemble, kern, own, got)
     ens = jnp.transpose(ensemble, (1, 0, 2))
-    g0, token = project(ens, y0, taps)
-    im0, sums, *second = image_first(gather(x0, token), near, far, obs_weight, g_sums)
+    x0, y0, g_sums = coarse_image(ensemble, kern, own, got, after=[ens])
+    xs, g0 = gather(x0, lambda after: project(ens, y0, taps, after))
+    im0, sums, *second = image_first(xs, near, far, obs_weight, g_sums)
     own, got, sums = scatter(second, sums)
     x1, y1, l0, g_sums = coarse_image(ensemble, kern, own, got, y0, sums)
-    g1, token = project(ens, y1, taps)
-    im1, sums = image_second(gather(x1, token), near, far, obs_weight, g_sums)
+    xs, g1 = gather(x1, lambda after: project(ens, y1, taps, after))
+    im1, sums = image_second(xs, near, far, obs_weight, g_sums)
     return tuple(result(l0, add_up(sums), g0, g1, im0, im1))
 
 

time: 125 us -> 125 us (level)
  starting transfers between devices: 41.6 us -> 34.6 us
  waiting for transfers between devices: 44.4 us -> 47.9 us
  other arithmetic: 1.62 us -> 3.06 us
    ppermute x18, waiting for transfers between devices: 16.1 us -> 22.9 us  [over_z(): return lax.ppermute(x, 'space', [(i, i ^ 4 * k) for i in range(GROUP)])]
    ppermute x10 -> x8, waiting for transfers between devices: 23.1 us -> 19.3 us  [over_y(): return lax.ppermute(x, 'space', [(i, i ^ 2) for i in range(GROUP)])]
    ppermute x18, starting transfers between devices: 25.6 us -> 22.4 us  [over_z(): return lax.ppermute(x, 'space', [(i, i ^ 4 * k) for i in range(GROUP)])]
    ppermute x10 -> x8, starting transfers between devices: 12.9 us -> 10.2 us  [over_y(): return lax.ppermute(x, 'space', [(i, i ^ 2) for i in range(GROUP)])]
    ppermute x14 -> x10, starting transfers between devices: 3.12 us -> 2.01 us  [over_core(): return lax.ppermute(x, 'space', [(i, i ^ 1) for i in range(GROUP)])]
    ppermute x14 -> x10, waiting for transfers between devices: 5.25 us -> 5.58 us  [over_core(): return lax.ppermute(x, 'space', [(i, i ^ 1) for i in range(GROUP)])]
    unnamed x17 -> x13, local copies, waits for them, and re-layouts: 3.7 us -> 3.87 us
    pallas_call x6 -> x8, Pallas kernels: 14.5 us -> 14.6 us  [the longest x2 7.3 us: project(): pl.pallas_call(project_kernel, in_specs=[VMEM] * 4, out_specs=[VMEM] * 2,...]
  transfers between devices with their start and end apart: 42 -> 36, of which waited for: 21 -> 25; matrix products, arithmetic and copies ran while one was open for 4% -> 5% of each run, Pallas kernels for 10% -> 10%
where the time goes in v7:
time: 125 us; the launch traced here: 124 us
  waiting for transfers between devices  47.9 us (38%)
  starting transfers between devices  34.6 us (28%)
  Pallas kernels  32.8 us (26%)
  local copies, waits for them, and re-layouts  4.38 us (4%)
  other arithmetic  3.06 us (2%)
  between operations  1.73 us (1%)
    ppermute x18, waiting for transfers between devices, over_z(): return lax.ppermute(x, 'space', [(i, i ^ 4 * k) for i in range(GROUP)])  22.9 us
    ppermute x18, starting transfers between devices, over_z(): return lax.ppermute(x, 'space', [(i, i ^ 4 * k) for i in range(GROUP)])  22.4 us
    ppermute x8, waiting for transfers between devices, over_y(): return lax.ppermute(x, 'space', [(i, i ^ 2) for i in range(GROUP)])  19.3 us
    ppermute x8, starting transfers between devices, over_y(): return lax.ppermute(x, 'space', [(i, i ^ 2) for i in range(GROUP)])  10.2 us
    pallas_call x2, Pallas kernels, adjoint_half(): pl.pallas_call(kernel, in_specs=([SMEM] if head else []) + [VMEM] * (len(...  9.57 us
    pallas_call x2, Pallas kernels, project(): pl.pallas_call(project_kernel, in_specs=[VMEM] * 4, out_specs=[VMEM] * 2,...  7.3 us
    pallas_call x2, Pallas kernels, coarse_image(): pl.pallas_call(functools.partial(coarse_kernel, len(got), second, len(aft...  7.25 us
    ppermute x10, waiting for transfers between devices, over_core(): return lax.ppermute(x, 'space', [(i, i ^ 1) for i in range(GROUP)])  5.58 us
  transfers between devices with their start and end apart: 36, of which 25 were waited for; matrix products, arithmetic and copies ran while one was open for 5% of the time, Pallas kernels for 10%

profile of v7, /device:TPU:0, one launch (start us, length us, event | category | flops | bytes accessed | tf_op | source)
XLA Modules:
  0.0 124.4 jit_solution(12067238678811318688)
XLA Ops:
  3.4 2.9 %collective-permute-start.1 = (s32[8,128]{1,0:T(8,128)S(1)}, s32[8,128]{1,0:T(8,128)S(1)}, u32[]{:S(2)}, u32[]{:S(2)}) collective-permute-start(s32[8,128]{1,0:T(8,128)S(1)} %get-tuple-element.54), channel_id=1, source_target_pairs={{0,2},{1,3},{2,0},{3,1},{4,6},{5,7},{6,4},{7,5},{8,10},{9,11},{10,... | collective-permute-start | bytes 12296 | tf_op jit(solution)/shard_map/ppermute | solution.py:599
  9.0 2.1 %collective-permute-start.2 = (s32[8,128]{1,0:T(8,128)S(1)}, s32[8,128]{1,0:T(8,128)S(1)}, u32[]{:S(2)}, u32[]{:S(2)}) collective-permute-start(s32[8,128]{1,0:T(8,128)S(1)} %get-tuple-element.56), channel_id=1, source_target_pairs={{0,4},{1,5},{2,6},{3,7},{4,0},{5,1},{6,2},{7,3},{8,12},{9,13},{10,... | collective-permute-start | bytes 12296 | tf_op jit(solution)/shard_map/ppermute | solution.py:603
  11.1 2.6 %collective-permute-start.3 = (s32[8,128]{1,0:T(8,128)S(1)}, s32[8,128]{1,0:T(8,128)S(1)}, u32[]{:S(2)}, u32[]{:S(2)}) collective-permute-start(s32[8,128]{1,0:T(8,128)S(1)} %get-tuple-element.57), channel_id=1, source_target_pairs={{0,8},{1,9},{2,10},{3,11},{4,12},{5,13},{6,14},{7,15},{8,0},{9,1},... | collective-permute-start | bytes 12296 | tf_op jit(solution)/shard_map/ppermute | solution.py:603
  15.6 3.5 %collective-permute-done.4.refs_3_ = s32[8,128]{1,0:T(8,128)S(1)} collective-permute-done((s32[8,128]{1,0:T(8,128)S(1)}, s32[8,128]{1,0:T(8,128)S(1)}, u32[]{:S(2)}, u32[]{:S(2)}) %collective-permute-start.4) | collective-permute-done | bytes 4128 | tf_op jit(solution)/shard_map/ppermute | solution.py:603
  19.1 5.2 %adjoint_far.1 = (s32[4,1152]{1,0:T(4,128)S(1)}, f32[4,1152]{1,0:T(4,128)S(1)}, bf16[1024,1152]{1,0:T(8,128)(2,1)S(1)}, f32[512,256]{1,0:T(8,128)S(1)}, f32[512,256]{1,0:T(8,128)S(1)}) custom-call(s32[4]{0:T(128)S(1)} %pad_add_fusion.me_ref, s32[8,128]{1,0:T(8,128)S(1)} %get-tuple-element.55.refs_0_, s32[8,128]{1,0:T(8,128)S(1)} %collective-permute-done.2.refs_1_, ...), custom_call_target="tpu_custom_call" | custom-call | flops 1811939328 | bytes 4000000 | tf_op jit(solution)/shard_map/adjoint_far/pallas_call | solution.py:137
  24.9 4.4 %adjoint_near.1 = (bf16[1024,1152]{1,0:T(8,128)(2,1)S(1)}, f32[512,256]{1,0:T(8,128)S(1)}, f32[512,256]{1,0:T(8,128)S(1)}) custom-call(s32[4,1152]{1,0:T(4,128)S(1)} %get-tuple-element.59.ids_ref, f32[4,1152]{1,0:T(4,128)S(1)} %get-tuple-element.60.weight_ref, bf16[1152,256]{1,0:T(8,128)(2,1)S(1)} %get-tuple-element.101.refs_5_.wh_ref, ...), custom_call_target="tpu_custom_call" | custom-call | flops 1811939328 | bytes 4000000 | tf_op jit(solution)/shard_map/adjoint_near/pallas_call | solution.py:137
  31.5 4.5 %collective-permute-done.7.p_ref = s16[272,256]{1,0:T(8,128)(2,1)S(1)} collective-permute-done((s16[272,256]{1,0:T(8,128)(2,1)S(1)}, s16[272,256]{1,0:T(8,128)(2,1)S(1)}, u32[]{:S(2)}, u32[]{:S(2)}) %collective-permute-start.7) | collective-permute-done | bytes 139296 | tf_op jit(solution)/shard_map/ppermute | solution.py:599
  36.2 1.9 %collective-permute-done.8.p_ref = s16[272,256]{1,0:T(8,128)(2,1)S(1)} collective-permute-done((s16[272,256]{1,0:T(8,128)(2,1)S(1)}, s16[272,256]{1,0:T(8,128)(2,1)S(1)}, u32[]{:S(2)}, u32[]{:S(2)}) %collective-permute-start.8) | collective-permute-done | bytes 139296 | tf_op jit(solution)/shard_map/ppermute | solution.py:599
  38.3 2.4 %collective-permute-start.10 = (s16[144,256]{1,0:T(8,128)(2,1)S(1)}, s16[144,256]{1,0:T(8,128)(2,1)S(1)}, u32[]{:S(2)}, u32[]{:S(2)}) collective-permute-start(s16[144,256]{1,0:T(8,128)(2,1)S(1)} %get-tuple-element.69), channel_id=1, source_target_pairs={{0,12},{1,13},{2,14},{3,15},{4,8},{5,9},{6,10},{7,11},{8,4},{9,5},... | collective-permute-start | bytes 221192 | tf_op jit(solution)/shard_map/ppermute | solution.py:603
  40.8 3.1 %copy.12 = bf16[80,128,256]{2,0,1:T(8,128)(2,1)S(1)} copy(bf16[80,128,256]{2,1,0:T(8,128)(2,1)S(1)} %bitcast.13) | data formatting | bytes 10485760 | tf_op args[0]
  43.9 1.9 %collective-permute-done.9.refs_0_ = s16[144,256]{1,0:T(8,128)(2,1)S(1)} collective-permute-done((s16[144,256]{1,0:T(8,128)(2,1)S(1)}, s16[144,256]{1,0:T(8,128)(2,1)S(1)}, u32[]{:S(2)}, u32[]{:S(2)}) %collective-permute-start.9) | collective-permute-done | bytes 73760 | tf_op jit(solution)/shard_map/ppermute | solution.py:603
  45.8 3.7 %coarse_first.1 = (bf16[256,128]{1,0:T(8,128)(2,1)S(1)}, f32[128,256]{1,0:T(8,128)S(1)}, f32[8,256]{1,0:T(8,128)S(1)}) custom-call(bf16[80,128,256]{2,1,0:T(8,128)(2,1)S(1)} %bitcast.13, bf16[256,256]{1,0:T(8,128)(2,1)S(1)} %copy-done.1, f32[128,256]{1,0:T(8,128)S(1)} %get-tuple-element.66.own_ref, s16[144,256]{1,0:T(8,128)(2,1)S(1)} %collective-permute-done.9.refs_0_, ...), custom_call_target="tpu_custom_call" | custom-call | flops 1342177280 | bytes 5000000 | tf_op jit(solution)/shard_map/coarse_first/pallas_call | solution.py:414
  54.0 2.9 %collective-permute-done.13.refs_1_ = bf16[256,128]{1,0:T(8,128)(2,1)S(1)} collective-permute-done((bf16[256,128]{1,0:T(8,128)(2,1)S(1)}, bf16[256,128]{1,0:T(8,128)(2,1)S(1)}, u32[]{:S(2)}, u32[]{:S(2)}) %collective-permute-start.13) | collective-permute-done | bytes 65568 | tf_op jit(solution)/shard_map/ppermute | solution.py:603
  57.0 2.0 %collective-permute-done.12.refs_0_ = bf16[256,128]{1,0:T(8,128)(2,1)S(1)} collective-permute-done((bf16[256,128]{1,0:T(8,128)(2,1)S(1)}, bf16[256,128]{1,0:T(8,128)(2,1)S(1)}, u32[]{:S(2)}, u32[]{:S(2)}) %collective-permute-start.12) | collective-permute-done | bytes 65568 | tf_op jit(solution)/shard_map/ppermute | solution.py:603
  60.6 3.7 %project.2 = (f32[80,8192]{1,0:T(8,128)S(1)}, f32[8,128]{1,0:T(8,128)S(1)}) custom-call(bf16[128,80,256]{2,1,0:T(8,128)(2,1)S(1)} %bitcast.10, f32[128,256]{1,0:T(8,128)S(1)} %get-tuple-element.72.y_ref.refs_3_, bf16[2,256,128]{2,1,0:T(8,128)(2,1)S(1)} %copy-done.2, bf16[4,256,128]{2,1,0:T(8,128)(2,1)S(1)} %join.2.after_ref.refs_0_), custom_call_target="tpu_custom_call" | custom-call | flops 1342177280 | bytes 8000000 | tf_op jit(solution)/shard_map/project/pallas_call | solution.py:452
  64.3 2.1 %collective-permute-done.15.x_ref = bf16[4,256,128]{2,1,0:T(8,128)(2,1)S(1)} collective-permute-done((bf16[4,256,128]{2,1,0:T(8,128)(2,1)S(1)}, bf16[4,256,128]{2,1,0:T(8,128)(2,1)S(1)}, u32[]{:S(2)}, u32[]{:S(2)}) %collective-permute-start.15) | collective-permute-done | bytes 262176 | tf_op jit(solution)/shard_map/ppermute | solution.py:599
  68.0 3.2 %image_first.1 = (f32[1152,256]{1,0:T(8,128)S(1)}, f32[8,256]{1,0:T(8,128)S(1)}, f32[512,256]{1,0:T(8,128)S(1)}, f32[512,256]{1,0:T(8,128)S(1)}, f32[512,256]{1,0:T(8,128)S(1)}, /*index=5*/f32[520,256]{1,0:T(8,128)S(1)}) custom-call(bf16[4,256,128]{2,1,0:T(8,128)(2,1)S(1)} %join.2.after_ref.refs_0_, bf16[4,256,128]{2,1,0:T(8,128)(2,1)S(1)} %relay.2.refs_1_, ...), custom_call_target="tpu_custom_call" | custom-call | flops 2415919104 | bytes 13000000 | tf_op jit(solution)/shard_map/image_first/pallas_call | solution.py:509
  73.3 1.6 %collective-permute-start.21 = (s16[272,256]{1,0:T(8,128)(2,1)S(1)}, s16[272,256]{1,0:T(8,128)(2,1)S(1)}, u32[]{:S(2)}, u32[]{:S(2)}) collective-permute-start(s16[272,256]{1,0:T(8,128)(2,1)S(1)} %get-tuple-element.83), channel_id=1, source_target_pairs={{0,2},{1,3},{2,0},{3,1},{4,6},{5,7},{6,4},{7,5},{8,10},{9,11},{10,... | collective-permute-start | bytes 417800 | tf_op jit(solution)/shard_map/ppermute | solution.py:599
  75.4 4.5 %collective-permute-done.21.p_ref = s16[272,256]{1,0:T(8,128)(2,1)S(1)} collective-permute-done((s16[272,256]{1,0:T(8,128)(2,1)S(1)}, s16[272,256]{1,0:T(8,128)(2,1)S(1)}, u32[]{:S(2)}, u32[]{:S(2)}) %collective-permute-start.21) | collective-permute-done | bytes 139296 | tf_op jit(solution)/shard_map/ppermute | solution.py:599
  80.1 2.1 %collective-permute-start.23 = (s16[144,256]{1,0:T(8,128)(2,1)S(1)}, s16[144,256]{1,0:T(8,128)(2,1)S(1)}, u32[]{:S(2)}, u32[]{:S(2)}) collective-permute-start(s16[144,256]{1,0:T(8,128)(2,1)S(1)} %get-tuple-element.88), channel_id=1, source_target_pairs={{0,12},{1,13},{2,14},{3,15},{4,8},{5,9},{6,10},{7,11},{8,4},{9,5},... | collective-permute-start | bytes 221192 | tf_op jit(solution)/shard_map/ppermute | solution.py:603
  83.7 3.3 %collective-permute-done.22.refs_0_ = s16[144,256]{1,0:T(8,128)(2,1)S(1)} collective-permute-done((s16[144,256]{1,0:T(8,128)(2,1)S(1)}, s16[144,256]{1,0:T(8,128)(2,1)S(1)}, u32[]{:S(2)}, u32[]{:S(2)}) %collective-permute-start.22) | collective-permute-done | bytes 73760 | tf_op jit(solution)/shard_map/ppermute | solution.py:603
  87.6 3.6 %coarse_second.1 = (bf16[256,128]{1,0:T(8,128)(2,1)S(1)}, f32[128,256]{1,0:T(8,128)S(1)}, f32[8,128]{1,0:T(8,128)S(1)}, f32[8,256]{1,0:T(8,128)S(1)}) custom-call(bf16[80,128,256]{2,1,0:T(8,128)(2,1)S(1)} %bitcast.13, bf16[256,256]{1,0:T(8,128)(2,1)S(1)} %copy-done.1, f32[128,256]{1,0:T(8,128)S(1)} %get-tuple-element.86.own_ref, ...), custom_call_target="tpu_custom_call" | custom-call | flops 1342177280 | bytes 5000000 | tf_op jit(solution)/shard_map/coarse_second/pallas_call | solution.py:414
  92.0 1.8 %collective-permute-start.26 = (bf16[256,128]{1,0:T(8,128)(2,1)S(1)}, bf16[256,128]{1,0:T(8,128)(2,1)S(1)}, u32[]{:S(2)}, u32[]{:S(2)}) collective-permute-start(bf16[256,128]{1,0:T(8,128)(2,1)S(1)} %get-tuple-element.91.refs_3_), channel_id=1, source_target_pairs={{0,12},{1,13},{2,14},{3,15},{4,8},{5,9},{6,10},{7,11},{8,4},{9,5},... | collective-permute-start | bytes 196616 | tf_op jit(solution)/shard_map/ppermute | solution.py:603
  94.7 2.0 %collective-permute-done.27.refs_2_ = bf16[256,128]{1,0:T(8,128)(2,1)S(1)} collective-permute-done((bf16[256,128]{1,0:T(8,128)(2,1)S(1)}, bf16[256,128]{1,0:T(8,128)(2,1)S(1)}, u32[]{:S(2)}, u32[]{:S(2)}) %collective-permute-start.27) | collective-permute-done | bytes 65568 | tf_op jit(solution)/shard_map/ppermute | solution.py:603
  98.0 2.1 %collective-permute-done.25.refs_0_ = bf16[256,128]{1,0:T(8,128)(2,1)S(1)} collective-permute-done((bf16[256,128]{1,0:T(8,128)(2,1)S(1)}, bf16[256,128]{1,0:T(8,128)(2,1)S(1)}, u32[]{:S(2)}, u32[]{:S(2)}) %collective-permute-start.25) | collective-permute-done | bytes 65568 | tf_op jit(solution)/shard_map/ppermute | solution.py:603
  101.3 3.6 %project.3 = (f32[80,8192]{1,0:T(8,128)S(1)}, f32[8,128]{1,0:T(8,128)S(1)}) custom-call(bf16[128,80,256]{2,1,0:T(8,128)(2,1)S(1)} %bitcast.11, f32[128,256]{1,0:T(8,128)S(1)} %get-tuple-element.92.y_ref, bf16[2,256,128]{2,1,0:T(8,128)(2,1)S(1)} %copy-done.2, bf16[4,256,128]{2,1,0:T(8,128)(2,1)S(1)} %join.3.after_ref.refs_0_), custom_call_target="tpu_custom_call" | custom-call | flops 1342177280 | bytes 8000000 | tf_op jit(solution)/shard_map/project/pallas_call | solution.py:452
  104.9 2.3 %collective-permute-done.28.x_ref = bf16[4,256,128]{2,1,0:T(8,128)(2,1)S(1)} collective-permute-done((bf16[4,256,128]{2,1,0:T(8,128)(2,1)S(1)}, bf16[4,256,128]{2,1,0:T(8,128)(2,1)S(1)}, u32[]{:S(2)}, u32[]{:S(2)}) %collective-permute-start.28) | collective-permute-done | bytes 262176 | tf_op jit(solution)/shard_map/ppermute | solution.py:599
  108.8 1.9 %image_second.1 = (f32[1152,256]{1,0:T(8,128)S(1)}, f32[8,256]{1,0:T(8,128)S(1)}) custom-call(bf16[4,256,128]{2,1,0:T(8,128)(2,1)S(1)} %join.3.after_ref.refs_0_, bf16[4,256,128]{2,1,0:T(8,128)(2,1)S(1)} %relay.3.refs_1_, bf16[4,256,128]{2,1,0:T(8,128)(2,1)S(1)} %collective-permute-done.29.refs_2_, bf16[4,256,128]{2,1,0:T(8,128)(2,1)S(1)} %collective-permute-done.30.refs_3_, ...), custom_call_target="tpu_custom_call" | custom-call | flops 1207959552 | bytes 8000000 | tf_op jit(solution)/shard_map/image_second/pallas_call | solution.py:535
  112.4 3.2 %collective-permute-done.32 = f32[8,256]{1,0:T(8,128)S(1)} collective-permute-done((f32[8,256]{1,0:T(8,128)S(1)}, f32[8,256]{1,0:T(8,128)S(1)}, u32[]{:S(2)}, u32[]{:S(2)}) %collective-permute-start.32) | collective-permute-done | bytes 8224 | tf_op jit(solution)/shard_map/ppermute | solution.py:599
  115.6 1.8 %collective-permute-start.35 = (f32[8,256]{1,0:T(8,128)S(1)}, f32[8,256]{1,0:T(8,128)S(1)}, u32[]{:S(2)}, u32[]{:S(2)}) collective-permute-start(f32[8,256]{1,0:T(8,128)S(1)} %add.18.refs_0_), channel_id=1, source_target_pairs={{0,12},{1,13},{2,14},{3,15},{4,8},{5,9},{6,10},{7,11},{8,4},{9,5},... | collective-permute-start | bytes 24584 | tf_op jit(solution)/shard_map/ppermute | solution.py:603
  117.5 2.6 %collective-permute-start.33 = (f32[8,256]{1,0:T(8,128)S(1)}, f32[8,256]{1,0:T(8,128)S(1)}, u32[]{:S(2)}, u32[]{:S(2)}) collective-permute-start(f32[8,256]{1,0:T(8,128)S(1)} %add.18.refs_0_), channel_id=1, source_target_pairs={{0,4},{1,5},{2,6},{3,7},{4,0},{5,1},{6,2},{7,3},{8,12},{9,13},{10,... | collective-permute-start | bytes 24584 | tf_op jit(solution)/shard_map/ppermute | solution.py:603
  122.0 2.2 %result.1 = (f32[80,8192]{1,0:T(8,128)}, f32[1152,256]{1,0:T(8,128)}) custom-call(f32[8,128]{1,0:T(8,128)S(1)} %get-tuple-element.90.l0_ref, f32[8,256]{1,0:T(8,128)S(1)} %add.18.refs_0_, f32[8,256]{1,0:T(8,128)S(1)} %collective-permute-done.33.refs_1_, f32[8,256]{1,0:T(8,128)S(1)} %collective-permute-done.34.refs_2_, ...), custom_call_target="tpu_custom_call" | custom-call | flops 1966080 | bytes 10000000 | tf_op jit(solution)/shard_map/result/pallas_call | solution.py:578
  (83 shorter events, 32.0 us)
Async XLA Ops:
  3.4 4.4 %collective-permute-start.1 = (s32[8,128]{1,0:T(8,128)S(1)}, s32[8,128]{1,0:T(8,128)S(1)}, u32[]{:S(2)}, u32[]{:S(2)}) collective-permute-start(s32[8,128]{1,0:T(8,128)S(1)} %get-tuple-element.54), channel_id=1, source_target_pairs={{0,2},{1,3},{2,0},{3,1},{4,6},{5,7},{6,4},{7,5},{8,10},{9,11},{10,... | collective-permute-start | bytes 12296 | tf_op jit(solution)/shard_map/ppermute | solution.py:599
  9.0 6.3 %collective-permute-start.2 = (s32[8,128]{1,0:T(8,128)S(1)}, s32[8,128]{1,0:T(8,128)S(1)}, u32[]{:S(2)}, u32[]{:S(2)}) collective-permute-start(s32[8,128]{1,0:T(8,128)S(1)} %get-tuple-element.56), channel_id=1, source_target_pairs={{0,4},{1,5},{2,6},{3,7},{4,0},{5,1},{6,2},{7,3},{8,12},{9,13},{10,... | collective-permute-start | bytes 12296 | tf_op jit(solution)/shard_map/ppermute | solution.py:603
  11.1 4.5 %collective-permute-start.3 = (s32[8,128]{1,0:T(8,128)S(1)}, s32[8,128]{1,0:T(8,128)S(1)}, u32[]{:S(2)}, u32[]{:S(2)}) collective-permute-start(s32[8,128]{1,0:T(8,128)S(1)} %get-tuple-element.57), channel_id=1, source_target_pairs={{0,8},{1,9},{2,10},{3,11},{4,12},{5,13},{6,14},{7,15},{8,0},{9,1},... | collective-permute-start | bytes 12296 | tf_op jit(solution)/shard_map/ppermute | solution.py:603
  13.7 5.4 %collective-permute-start.4 = (s32[8,128]{1,0:T(8,128)S(1)}, s32[8,128]{1,0:T(8,128)S(1)}, u32[]{:S(2)}, u32[]{:S(2)}) collective-permute-start(s32[8,128]{1,0:T(8,128)S(1)} %get-tuple-element.58), channel_id=1, source_target_pairs={{0,12},{1,13},{2,14},{3,15},{4,8},{5,9},{6,10},{7,11},{8,4},{9,5},... | collective-permute-start | bytes 12296 | tf_op jit(solution)/shard_map/ppermute | solution.py:603
  24.3 5.0 %collective-permute-start.6 = (f32[512,256]{1,0:T(8,128)S(1)}, f32[512,256]{1,0:T(8,128)S(1)}, u32[]{:S(2)}, u32[]{:S(2)}) collective-permute-start(f32[512,256]{1,0:T(8,128)S(1)} %get-tuple-element.64), channel_id=1, source_target_pairs={{0,1},{1,0},{2,3},{3,2},{4,5},{5,4},{6,7},{7,6},{8,9},{9,8},{10,11... | collective-permute-start | bytes 1572872 | tf_op jit(solution)/shard_map/ppermute | solution.py:595
  24.4 7.2 %collective-permute-start.5 = (f32[512,256]{1,0:T(8,128)S(1)}, f32[512,256]{1,0:T(8,128)S(1)}, u32[]{:S(2)}, u32[]{:S(2)}) collective-permute-start(f32[512,256]{1,0:T(8,128)S(1)} %get-tuple-element.62), channel_id=1, source_target_pairs={{0,1},{1,0},{2,3},{3,2},{4,5},{5,4},{6,7},{7,6},{8,9},{9,8},{10,11... | collective-permute-start | bytes 1572872 | tf_op jit(solution)/shard_map/ppermute | solution.py:595
  29.4 6.6 %collective-permute-start.7 = (s16[272,256]{1,0:T(8,128)(2,1)S(1)}, s16[272,256]{1,0:T(8,128)(2,1)S(1)}, u32[]{:S(2)}, u32[]{:S(2)}) collective-permute-start(s16[272,256]{1,0:T(8,128)(2,1)S(1)} %get-tuple-element.65), channel_id=1, source_target_pairs={{0,2},{1,3},{2,0},{3,1},{4,6},{5,7},{6,4},{7,5},{8,10},{9,11},{10,... | collective-permute-start | bytes 417800 | tf_op jit(solution)/shard_map/ppermute | solution.py:599
  31.0 7.1 %collective-permute-start.8 = (s16[272,256]{1,0:T(8,128)(2,1)S(1)}, s16[272,256]{1,0:T(8,128)(2,1)S(1)}, u32[]{:S(2)}, u32[]{:S(2)}) collective-permute-start(s16[272,256]{1,0:T(8,128)(2,1)S(1)} %get-tuple-element.67), channel_id=1, source_target_pairs={{0,2},{1,3},{2,0},{3,1},{4,6},{5,7},{6,4},{7,5},{8,10},{9,11},{10,... | collective-permute-start | bytes 417800 | tf_op jit(solution)/shard_map/ppermute | solution.py:599
  36.1 7.8 %collective-permute-start.11 = (s16[144,256]{1,0:T(8,128)(2,1)S(1)}, s16[144,256]{1,0:T(8,128)(2,1)S(1)}, u32[]{:S(2)}, u32[]{:S(2)}) collective-permute-start(s16[144,256]{1,0:T(8,128)(2,1)S(1)} %get-tuple-element.70), channel_id=1, source_target_pairs={{0,4},{1,5},{2,6},{3,7},{4,0},{5,1},{6,2},{7,3},{8,12},{9,13},{10,... | collective-permute-start | bytes 221192 | tf_op jit(solution)/shard_map/ppermute | solution.py:603
  38.3 7.5 %collective-permute-start.9 = (s16[144,256]{1,0:T(8,128)(2,1)S(1)}, s16[144,256]{1,0:T(8,128)(2,1)S(1)}, u32[]{:S(2)}, u32[]{:S(2)}) collective-permute-start(s16[144,256]{1,0:T(8,128)(2,1)S(1)} %get-tuple-element.68), channel_id=1, source_target_pairs={{0,8},{1,9},{2,10},{3,11},{4,12},{5,13},{6,14},{7,15},{8,0},{9,1},... | collective-permute-start | bytes 221192 | tf_op jit(solution)/shard_map/ppermute | solution.py:603
  38.3 7.4 %collective-permute-start.10 = (s16[144,256]{1,0:T(8,128)(2,1)S(1)}, s16[144,256]{1,0:T(8,128)(2,1)S(1)}, u32[]{:S(2)}, u32[]{:S(2)}) collective-permute-start(s16[144,256]{1,0:T(8,128)(2,1)S(1)} %get-tuple-element.69), channel_id=1, source_target_pairs={{0,12},{1,13},{2,14},{3,15},{4,8},{5,9},{6,10},{7,11},{8,4},{9,5},... | collective-permute-start | bytes 221192 | tf_op jit(solution)/shard_map/ppermute | solution.py:603
  49.5 4.5 %collective-permute-start.14 = (bf16[256,128]{1,0:T(8,128)(2,1)S(1)}, bf16[256,128]{1,0:T(8,128)(2,1)S(1)}, u32[]{:S(2)}, u32[]{:S(2)}) collective-permute-start(bf16[256,128]{1,0:T(8,128)(2,1)S(1)} %get-tuple-element.71.refs_3_), channel_id=1, source_target_pairs={{0,4},{1,5},{2,6},{3,7},{4,0},{5,1},{6,2},{7,3},{8,12},{9,13},{10,... | collective-permute-start | bytes 196616 | tf_op jit(solution)/shard_map/ppermute | solution.py:603
  50.9 6.1 %collective-permute-start.13 = (bf16[256,128]{1,0:T(8,128)(2,1)S(1)}, bf16[256,128]{1,0:T(8,128)(2,1)S(1)}, u32[]{:S(2)}, u32[]{:S(2)}) collective-permute-start(bf16[256,128]{1,0:T(8,128)(2,1)S(1)} %get-tuple-element.71.refs_3_), channel_id=1, source_target_pairs={{0,12},{1,13},{2,14},{3,15},{4,8},{5,9},{6,10},{7,11},{8,4},{9,5},... | collective-permute-start | bytes 196616 | tf_op jit(solution)/shard_map/ppermute | solution.py:603
  52.2 6.8 %collective-permute-start.12 = (bf16[256,128]{1,0:T(8,128)(2,1)S(1)}, bf16[256,128]{1,0:T(8,128)(2,1)S(1)}, u32[]{:S(2)}, u32[]{:S(2)}) collective-permute-start(bf16[256,128]{1,0:T(8,128)(2,1)S(1)} %get-tuple-element.71.refs_3_), channel_id=1, source_target_pairs={{0,8},{1,9},{2,10},{3,11},{4,12},{5,13},{6,14},{7,15},{8,0},{9,1},... | collective-permute-start | bytes 196616 | tf_op jit(solution)/shard_map/ppermute | solution.py:603
  59.0 7.4 %collective-permute-start.15 = (bf16[4,256,128]{2,1,0:T(8,128)(2,1)S(1)}, bf16[4,256,128]{2,1,0:T(8,128)(2,1)S(1)}, u32[]{:S(2)}, u32[]{:S(2)}) collective-permute-start(bf16[4,256,128]{2,1,0:T(8,128)(2,1)S(1)} %join.2.after_ref.refs_0_), channel_id=1, source_target_pairs={{0,2},{1,3},{2,0},{3,1},{4,6},{5,7},{6,4},{7,5},{8,10},{9,11},{10,... | collective-permute-start | bytes 786440 | tf_op jit(solution)/shard_map/ppermute | solution.py:599
  60.6 5.9 %collective-permute-start.16 = (bf16[4,256,128]{2,1,0:T(8,128)(2,1)S(1)}, bf16[4,256,128]{2,1,0:T(8,128)(2,1)S(1)}, u32[]{:S(2)}, u32[]{:S(2)}) collective-permute-start(bf16[4,256,128]{2,1,0:T(8,128)(2,1)S(1)} %join.2.after_ref.refs_0_), channel_id=1, source_target_pairs={{0,1},{1,0},{2,3},{3,2},{4,5},{5,4},{6,7},{7,6},{8,9},{9,8},{10,11... | collective-permute-start | bytes 786440 | tf_op jit(solution)/shard_map/ppermute | solution.py:595
  71.2 2.0 %collective-permute-start.19 = (f32[520,256]{1,0:T(8,128)S(1)}, f32[520,256]{1,0:T(8,128)S(1)}, u32[]{:S(2)}, u32[]{:S(2)}) collective-permute-start(f32[520,256]{1,0:T(8,128)S(1)} %get-tuple-element.80), channel_id=1, source_target_pairs={{0,1},{1,0},{2,3},{3,2},{4,5},{5,4},{6,7},{7,6},{8,9},{9,8},{10,11... | collective-permute-start | bytes 1597448 | tf_op jit(solution)/shard_map/ppermute | solution.py:595
  71.4 4.0 %collective-permute-start.18 = (f32[512,256]{1,0:T(8,128)S(1)}, f32[512,256]{1,0:T(8,128)S(1)}, u32[]{:S(2)}, u32[]{:S(2)}) collective-permute-start(f32[512,256]{1,0:T(8,128)S(1)} %get-tuple-element.78), channel_id=1, source_target_pairs={{0,1},{1,0},{2,3},{3,2},{4,5},{5,4},{6,7},{7,6},{8,9},{9,8},{10,11... | collective-permute-start | bytes 1572872 | tf_op jit(solution)/shard_map/ppermute | solution.py:595
  73.3 6.6 %collective-permute-start.21 = (s16[272,256]{1,0:T(8,128)(2,1)S(1)}, s16[272,256]{1,0:T(8,128)(2,1)S(1)}, u32[]{:S(2)}, u32[]{:S(2)}) collective-permute-start(s16[272,256]{1,0:T(8,128)(2,1)S(1)} %get-tuple-element.83), channel_id=1, source_target_pairs={{0,2},{1,3},{2,0},{3,1},{4,6},{5,7},{6,4},{7,5},{8,10},{9,11},{10,... | collective-permute-start | bytes 417800 | tf_op jit(solution)/shard_map/ppermute | solution.py:599
  74.9 7.3 %collective-permute-start.20 = (s16[272,256]{1,0:T(8,128)(2,1)S(1)}, s16[272,256]{1,0:T(8,128)(2,1)S(1)}, u32[]{:S(2)}, u32[]{:S(2)}) collective-permute-start(s16[272,256]{1,0:T(8,128)(2,1)S(1)} %get-tuple-element.82), channel_id=1, source_target_pairs={{0,2},{1,3},{2,0},{3,1},{4,6},{5,7},{6,4},{7,5},{8,10},{9,11},{10,... | collective-permute-start | bytes 417800 | tf_op jit(solution)/shard_map/ppermute | solution.py:599
  80.0 7.0 %collective-permute-start.22 = (s16[144,256]{1,0:T(8,128)(2,1)S(1)}, s16[144,256]{1,0:T(8,128)(2,1)S(1)}, u32[]{:S(2)}, u32[]{:S(2)}) collective-permute-start(s16[144,256]{1,0:T(8,128)(2,1)S(1)} %get-tuple-element.87), channel_id=1, source_target_pairs={{0,8},{1,9},{2,10},{3,11},{4,12},{5,13},{6,14},{7,15},{8,0},{9,1},... | collective-permute-start | bytes 221192 | tf_op jit(solution)/shard_map/ppermute | solution.py:603
  80.1 6.9 %collective-permute-start.23 = (s16[144,256]{1,0:T(8,128)(2,1)S(1)}, s16[144,256]{1,0:T(8,128)(2,1)S(1)}, u32[]{:S(2)}, u32[]{:S(2)}) collective-permute-start(s16[144,256]{1,0:T(8,128)(2,1)S(1)} %get-tuple-element.88), channel_id=1, source_target_pairs={{0,12},{1,13},{2,14},{3,15},{4,8},{5,9},{6,10},{7,11},{8,4},{9,5},... | collective-permute-start | bytes 221192 | tf_op jit(solution)/shard_map/ppermute | solution.py:603
  82.3 5.3 %collective-permute-start.24 = (s16[144,256]{1,0:T(8,128)(2,1)S(1)}, s16[144,256]{1,0:T(8,128)(2,1)S(1)}, u32[]{:S(2)}, u32[]{:S(2)}) collective-permute-start(s16[144,256]{1,0:T(8,128)(2,1)S(1)} %get-tuple-element.89), channel_id=1, source_target_pairs={{0,4},{1,5},{2,6},{3,7},{4,0},{5,1},{6,2},{7,3},{8,12},{9,13},{10,... | collective-permute-start | bytes 221192 | tf_op jit(solution)/shard_map/ppermute | solution.py:603
  91.2 5.5 %collective-permute-start.27 = (bf16[256,128]{1,0:T(8,128)(2,1)S(1)}, bf16[256,128]{1,0:T(8,128)(2,1)S(1)}, u32[]{:S(2)}, u32[]{:S(2)}) collective-permute-start(bf16[256,128]{1,0:T(8,128)(2,1)S(1)} %get-tuple-element.91.refs_3_), channel_id=1, source_target_pairs={{0,4},{1,5},{2,6},{3,7},{4,0},{5,1},{6,2},{7,3},{8,12},{9,13},{10,... | collective-permute-start | bytes 196616 | tf_op jit(solution)/shard_map/ppermute | solution.py:603
  92.0 6.1 %collective-permute-start.26 = (bf16[256,128]{1,0:T(8,128)(2,1)S(1)}, bf16[256,128]{1,0:T(8,128)(2,1)S(1)}, u32[]{:S(2)}, u32[]{:S(2)}) collective-permute-start(bf16[256,128]{1,0:T(8,128)(2,1)S(1)} %get-tuple-element.91.refs_3_), channel_id=1, source_target_pairs={{0,12},{1,13},{2,14},{3,15},{4,8},{5,9},{6,10},{7,11},{8,4},{9,5},... | collective-permute-start | bytes 196616 | tf_op jit(solution)/shard_map/ppermute | solution.py:603
  93.8 6.3 %collective-permute-start.25 = (bf16[256,128]{1,0:T(8,128)(2,1)S(1)}, bf16[256,128]{1,0:T(8,128)(2,1)S(1)}, u32[]{:S(2)}, u32[]{:S(2)}) collective-permute-start(bf16[256,128]{1,0:T(8,128)(2,1)S(1)} %get-tuple-element.91.refs_3_), channel_id=1, source_target_pairs={{0,8},{1,9},{2,10},{3,11},{4,12},{5,13},{6,14},{7,15},{8,0},{9,1},... | collective-permute-start | bytes 196616 | tf_op jit(solution)/shard_map/ppermute | solution.py:603
  100.2 7.0 %collective-permute-start.28 = (bf16[4,256,128]{2,1,0:T(8,128)(2,1)S(1)}, bf16[4,256,128]{2,1,0:T(8,128)(2,1)S(1)}, u32[]{:S(2)}, u32[]{:S(2)}) collective-permute-start(bf16[4,256,128]{2,1,0:T(8,128)(2,1)S(1)} %join.3.after_ref.refs_0_), channel_id=1, source_target_pairs={{0,2},{1,3},{2,0},{3,1},{4,6},{5,7},{6,4},{7,5},{8,10},{9,11},{10,... | collective-permute-start | bytes 786440 | tf_op jit(solution)/shard_map/ppermute | solution.py:599
  101.3 6.0 %collective-permute-start.29 = (bf16[4,256,128]{2,1,0:T(8,128)(2,1)S(1)}, bf16[4,256,128]{2,1,0:T(8,128)(2,1)S(1)}, u32[]{:S(2)}, u32[]{:S(2)}) collective-permute-start(bf16[4,256,128]{2,1,0:T(8,128)(2,1)S(1)} %join.3.after_ref.refs_0_), channel_id=1, source_target_pairs={{0,1},{1,0},{2,3},{3,2},{4,5},{5,4},{6,7},{7,6},{8,9},{9,8},{10,11... | collective-permute-start | bytes 786440 | tf_op jit(solution)/shard_map/ppermute | solution.py:595
  112.0 3.7 %collective-permute-start.32 = (f32[8,256]{1,0:T(8,128)S(1)}, f32[8,256]{1,0:T(8,128)S(1)}, u32[]{:S(2)}, u32[]{:S(2)}) collective-permute-start(f32[8,256]{1,0:T(8,128)S(1)} %add.17), channel_id=1, source_target_pairs={{0,2},{1,3},{2,0},{3,1},{4,6},{5,7},{6,4},{7,5},{8,10},{9,11},{10,... | collective-permute-start | bytes 24584 | tf_op jit(solution)/shard_map/ppermute | solution.py:599
  115.6 5.4 %collective-permute-start.35 = (f32[8,256]{1,0:T(8,128)S(1)}, f32[8,256]{1,0:T(8,128)S(1)}, u32[]{:S(2)}, u32[]{:S(2)}) collective-permute-start(f32[8,256]{1,0:T(8,128)S(1)} %add.18.refs_0_), channel_id=1, source_target_pairs={{0,12},{1,13},{2,14},{3,15},{4,8},{5,9},{6,10},{7,11},{8,4},{9,5},... | collective-permute-start | bytes 24584 | tf_op jit(solution)/shard_map/ppermute | solution.py:603
  117.5 4.5 %collective-permute-start.34 = (f32[8,256]{1,0:T(8,128)S(1)}, f32[8,256]{1,0:T(8,128)S(1)}, u32[]{:S(2)}, u32[]{:S(2)}) collective-permute-start(f32[8,256]{1,0:T(8,128)S(1)} %add.18.refs_0_), channel_id=1, source_target_pairs={{0,8},{1,9},{2,10},{3,11},{4,12},{5,13},{6,14},{7,15},{8,0},{9,1},... | collective-permute-start | bytes 24584 | tf_op jit(solution)/shard_map/ppermute | solution.py:603
  117.5 4.5 %collective-permute-start.33 = (f32[8,256]{1,0:T(8,128)S(1)}, f32[8,256]{1,0:T(8,128)S(1)}, u32[]{:S(2)}, u32[]{:S(2)}) collective-permute-start(f32[8,256]{1,0:T(8,128)S(1)} %add.18.refs_0_), channel_id=1, source_target_pairs={{0,4},{1,5},{2,6},{3,7},{4,0},{5,1},{6,2},{7,3},{8,12},{9,13},{10,... | collective-permute-start | bytes 24584 | tf_op jit(solution)/shard_map/ppermute | solution.py:603
  (10 other events, 73.7 us)

commit v8 on v7

--- a/solution.py
+++ b/solution.py
@@ -188,7 +188,7 @@
     near, far = small(pick_kernel, 2, "pick", me, lists, scalars=1)
     near, far = small(mix_y_kernel, 2, "mix_y", near, over_core(far))
     own, *sent = small(mix_z_kernel, STEPS, "mix_z", near, over_y(far))
-    return [own] + [over_z(sent[k - 1], k) for k in range(1, STEPS)], own
+    return [own] + [over_z(sent[k - 1], k) for k in range(1, STEPS)]
 
 
 def exponent(m):
@@ -462,7 +462,7 @@
 
 
 def lay_out(x_refs, xs):
-    if len(x_refs) == 1:
+    if len(x_refs[0].shape) == 2:
         xs[...] = x_refs[0][...]
         return
     for i, x in enumerate(x_refs):
@@ -473,75 +473,108 @@
 CUTS = 3
 
 
-def images(x_refs, near_ref, far_ref, obs_ref, im_ref, xs):
+def part_kernel(*refs):
+    *x_refs, near_ref, far_ref, out_ref, xs = refs
     lay_out(x_refs, xs)
     half, fine = near_ref.shape
     rows = fine // CUTS
     for i in range(CUTS):
         some = pl.ds(i * rows, rows)
-        turned = dot(xs[:, :half], near_ref[:, some]) + dot(xs[:, half:], far_ref[:, some])
+        out_ref[:, some] = dot(xs[:, :half], near_ref[:, some]) + dot(
+            xs[:, half:], far_ref[pl.ds(0, xs.shape[1] - half), some]
+        )
+
+
+def image_part(xs, near, far, width):
+    half, fine = near.shape
+    return pl.pallas_call(
+        part_kernel,
+        in_specs=[VMEM] * (len(xs) + 2),
+        out_specs=VMEM,
+        out_shape=shape((width, fine), F32),
+        scratch_shapes=[pltpu.VMEM((width, len(xs) * STEPS * LANES), BF)],
+        compiler_params=params(16),
+        cost_estimate=cost(3 * half * fine * width, 4e6),
+        name="image_part",
+    )(*xs, near, far)
+
+
+def images(x_ref, part_ref, near_ref, far_ref, obs_ref, im_ref, xs):
+    lay_out([x_ref], xs)
+    half, fine = near_ref.shape
+    rows = fine // CUTS
+    for i in range(CUTS):
+        some = pl.ds(i * rows, rows)
+        if part_ref is None:
+            turned = dot(xs[:, :half], near_ref[:, some]) + dot(xs[:, half:], far_ref[:, some])
+        else:
+            last = xs.shape[1]
+            turned = dot(xs[...], far_ref[pl.ds(half - last, last), some]) + part_ref[:, some]
         im = turned.T
         im_ref[some, :] = im
         yield some, im, obs_ref[some, :].astype(F32) * im
 
 
-def image_kernel(count, *refs):
-    x_refs, refs = refs[:count], refs[count:]
-    near_ref, far_ref, obs_ref, g_ref, im_ref, sum_ref = refs[:6]
-    outs, (xs, v_s) = refs[6:10], refs[10:]
+def image_kernel(parts, first, x_ref, *refs):
+    part_ref, refs = (refs[0], refs[1:]) if parts else (None, refs)
+    near_ref, far_ref, obs_ref, g_ref, im_ref, sum_ref, *refs = refs
+    if first:
+        v_ref, *outs, xs = refs
+    else:
+        (xs,) = refs
     sums = g_ref[...]
     row = lax.broadcasted_iota(jnp.int32, sums.shape, 0)
-    for some, im, v in images(x_refs, near_ref, far_ref, obs_ref, im_ref, xs):
-        v_s[some, :] = v.astype(BF)
+    for some, im, v in images(x_ref, part_ref, near_ref, far_ref, obs_ref, im_ref, xs):
+        if first:
+            v_ref[some, :] = v.astype(BF)
         sums = sums + jnp.where(row == 1, fold(v * im), 0.0)
     sum_ref[...] = sums
+    if first:
+        rows = near_ref.shape[0] // 2
+        for i in (1, 0):
+            outs[i][pl.ds(0, rows), :] = dot(far_ref[pl.ds(i * rows, rows), :], v_ref[...])
+        outs[1][pl.ds(rows, 8), :] = sums
+
+
+def image_of(xs, near, far, obs, g_sums, first):
+    half, fine = near.shape
+    width = obs.shape[1]
+    part = [image_part(xs[:-1], near, far, width)] if len(xs) > 1 else []
+    out = [shape((fine, width), F32), shape((8, width), F32)]
+    if first:
+        out += [shape((fine, width), BF)]
+        out += [shape((half // 2, width), F32), shape((half // 2 + 8, width), F32)]
+    last = STEPS * LANES if part else 2 * half
+    return pl.pallas_call(
+        functools.partial(image_kernel, bool(part), first),
+        in_specs=[VMEM] * (5 + len(part)),
+        out_specs=[VMEM] * len(out),
+        out_shape=out,
+        scratch_shapes=[pltpu.VMEM((width, last), BF)],
+        compiler_params=params(16),
+        cost_estimate=cost(3 * half * fine * width, 8e6),
+        name="image_first" if first else "image_second",
+    )(xs[-1], *part, near, far, obs, g_sums)
+
+
+def back_kernel(near_ref, v_ref, *outs):
     rows = near_ref.shape[0] // 2
     for i, out in enumerate(outs):
-        at_ref = far_ref if i > 1 else near_ref
-        out[pl.ds(0, rows), :] = dot(at_ref[pl.ds(i % 2 * rows, rows), :], v_s[...])
-    outs[3][pl.ds(rows, 8), :] = sums
-
-
-def image_first(xs, near, far, obs, g_sums):
+        out[...] = dot(near_ref[pl.ds(i * rows, rows), :], v_ref[...])
+
+
+def back_near(near, v):
     half, fine = near.shape
-    width = obs.shape[1]
-    z_rows = [half // 2] * 3 + [half // 2 + 8]
-    return pl.pallas_call(
-        functools.partial(image_kernel, len(xs)),
-        in_specs=[VMEM] * (len(xs) + 4),
-        out_specs=[VMEM] * 6,
-        out_shape=[shape((fine, width), F32), shape((8, width), F32)]
-        + [shape((r, width), F32) for r in z_rows],
-        scratch_shapes=[pltpu.VMEM((width, 2 * half), BF), pltpu.VMEM((fine, width), BF)],
+    width = v.shape[1]
+    return pl.pallas_call(
+        back_kernel,
+        in_specs=[VMEM] * 2,
+        out_specs=[VMEM] * 2,
+        out_shape=[shape((half // 2, width), F32)] * 2,
         compiler_params=params(16),
-        cost_estimate=cost(8 * half * fine * width, 13e6),
-        name="image_first",
-    )(*xs, near, far, obs, g_sums)
-
-
-def second_kernel(count, *refs):
-    x_refs, refs = refs[:count], refs[count:]
-    near_ref, far_ref, obs_ref, g_ref, im_ref, sum_ref, xs = refs
-    sums = g_ref[...]
-    row = lax.broadcasted_iota(jnp.int32, sums.shape, 0)
-    for _, im, v in images(x_refs, near_ref, far_ref, obs_ref, im_ref, xs):
-        sums = sums + jnp.where(row == 1, fold(v * im), 0.0)
-    sum_ref[...] = sums
-
-
-def image_second(xs, near, far, obs, g_sums):
-    half, fine = near.shape
-    width = obs.shape[1]
-    return pl.pallas_call(
-        functools.partial(second_kernel, len(xs)),
-        in_specs=[VMEM] * (len(xs) + 4),
-        out_specs=[VMEM] * 2,
-        out_shape=[shape((fine, width), F32), shape((8, width), F32)],
-        scratch_shapes=[pltpu.VMEM((width, 2 * half), BF)],
-        compiler_params=params(16),
-        cost_estimate=cost(4 * half * fine * width, 8e6),
-        name="image_second",
-    )(*xs, near, far, obs, g_sums)
+        cost_estimate=cost(2 * half * fine * width, 4e6),
+        name="back_near",
+    )(near, v)
 
 
 OUT_CUTS = 4
@@ -650,13 +683,15 @@
 
     index = lax.axis_index("space").astype(jnp.int32)
     me = jnp.stack([index // 4, index // 2 % 2, index % 2, index])
+    w = -(obs_weight.astype(F32) * innovation.astype(F32))
+    high = lax.reduce_precision(w, 8, 7)
+    wh, wl = high.astype(BF), (w - high).astype(BF)
     named = jnp.concatenate([slot_of.astype(F32), interp_weight], axis=0)
     if grouped:
-        lists, after = exchange_lists(me, intersection_list[0])
-        late = 0.0 * after[:1, :1].astype(F32)
+        lists = exchange_lists(me, intersection_list[0])
         scatter, gather, add_up = scatter_sums, gather_columns, sum_all
     else:
-        lists, late = intersection_list[0], 0.0
+        lists = intersection_list[0]
         hit = (lists.reshape(-1, 1) == jnp.arange(columns, dtype=jnp.int32)).astype(BF)
 
         def swap(x):
@@ -678,20 +713,17 @@
         def add_up(x):
             return [lax.psum(x, "space")]
 
-    w = late - obs_weight.astype(F32) * innovation.astype(F32)
-    high = lax.reduce_precision(w, 8, 7)
-    wh, wl = high.astype(BF), (w - high).astype(BF)
     ids, weight, far, c0, c1 = adjoint_half(slots, [named, wh, wl], (grouped, me, lists if grouped else []))
     near, n0, n1 = adjoint_half(slots, [ids, weight, wh, wl])
     own, got, _ = scatter([n0, n1, c0, c1])
     ens = jnp.transpose(ensemble, (1, 0, 2))
     x0, y0, g_sums = coarse_image(ensemble, kern, own, got, after=[ens])
     xs, g0 = gather(x0, lambda after: project(ens, y0, taps, after))
-    im0, sums, *second = image_first(xs, near, far, obs_weight, g_sums)
-    own, got, sums = scatter(second, sums)
+    im0, sums, v, c0, c1 = image_of(xs, near, far, obs_weight, g_sums, True)
+    own, got, sums = scatter([*back_near(near, v), c0, c1], sums)
     x1, y1, l0, g_sums = coarse_image(ensemble, kern, own, got, y0, sums)
     xs, g1 = gather(x1, lambda after: project(ens, y1, taps, after))
-    im1, sums = image_second(xs, near, far, obs_weight, g_sums)
+    im1, sums = image_of(xs, near, far, obs_weight, g_sums, False)
     return tuple(result(l0, add_up(sums), g0, g1, im0, im1))
 
 

time: 125 us -> 121 us (0.968)
  waiting for transfers between devices: 47.9 us -> 45.2 us
  starting transfers between devices: 34.6 us -> 36.2 us
  other arithmetic: 3.06 us -> 1.62 us
    ppermute x10, waiting for transfers between devices: 5.58 us -> 2.48 us  [over_core(): return lax.ppermute(x, 'space', [(i, i ^ 1) for i in range(GROUP)])]
    ppermute x18, waiting for transfers between devices: 22.9 us -> 25.3 us  [over_z(): return lax.ppermute(x, 'space', [(i, i ^ 4 * k) for i in range(GROUP)])]
    ppermute x8, waiting for transfers between devices: 19.3 us -> 17.5 us  [over_y(): return lax.ppermute(x, 'space', [(i, i ^ 2) for i in range(GROUP)])]
    ppermute x8, starting transfers between devices: 10.2 us -> 11.7 us  [over_y(): return lax.ppermute(x, 'space', [(i, i ^ 2) for i in range(GROUP)])]
    pallas_call x2 -> x5, Pallas kernels: 5.11 us -> 5.55 us  [the longest x2 2.79 us: image_part(): pl.pallas_call(part_kernel, in_specs=[VMEM] * (len(xs) + 2), out_specs=VM...]
    unnamed x13 -> x17, local copies, waits for them, and re-layouts: 3.87 us -> 3.88 us
  transfers between devices with their start and end apart: 36 -> 36, of which waited for: 25 -> 25; matrix products, arithmetic and copies ran while one was open for 5% -> 4% of each run, Pallas kernels for 10% -> 13%
where the time goes in v8:
time: 121 us
  waiting for transfers between devices  45.2 us (37%)
  starting transfers between devices  36.2 us (30%)
  Pallas kernels  32.9 us (27%)
  local copies, waits for them, and re-layouts  3.88 us (3%)
  other arithmetic  1.62 us (1%)
    ppermute x18, waiting for transfers between devices, over_z(): return lax.ppermute(x, 'space', [(i, i ^ 4 * k) for i in range(GROUP)])  25.3 us
    ppermute x18, starting transfers between devices, over_z(): return lax.ppermute(x, 'space', [(i, i ^ 4 * k) for i in range(GROUP)])  22.3 us
    ppermute x8, waiting for transfers between devices, over_y(): return lax.ppermute(x, 'space', [(i, i ^ 2) for i in range(GROUP)])  17.5 us
    ppermute x8, starting transfers between devices, over_y(): return lax.ppermute(x, 'space', [(i, i ^ 2) for i in range(GROUP)])  11.7 us
    pallas_call x2, Pallas kernels, adjoint_half(): pl.pallas_call(kernel, in_specs=([SMEM] if head else []) + [VMEM] * (len(...  9.57 us
    pallas_call x2, Pallas kernels, project(): pl.pallas_call(project_kernel, in_specs=[VMEM] * 4, out_specs=[VMEM] * 2,...  7.26 us
    pallas_call x2, Pallas kernels, coarse_image(): pl.pallas_call(functools.partial(coarse_kernel, len(got), second, len(aft...  7.03 us
    unnamed x17, local copies, waits for them, and re-layouts  3.88 us
  transfers between devices with their start and end apart: 36, of which 25 were waited for; matrix products, arithmetic and copies ran while one was open for 4% of the time, Pallas kernels for 13%

profile of v8, /device:TPU:0, one launch (start us, length us, event | category | flops | bytes accessed | tf_op | source)
XLA Modules:
  0.0 121.0 jit_solution(234525796297672764)
XLA Ops:
  3.4 2.9 %collective-permute-start.1 = (s32[8,128]{1,0:T(8,128)S(1)}, s32[8,128]{1,0:T(8,128)S(1)}, u32[]{:S(2)}, u32[]{:S(2)}) collective-permute-start(s32[8,128]{1,0:T(8,128)S(1)} %get-tuple-element.55), channel_id=1, source_target_pairs={{0,2},{1,3},{2,0},{3,1},{4,6},{5,7},{6,4},{7,5},{8,10},{9,11},{10,... | collective-permute-start | bytes 12296 | tf_op jit(solution)/shard_map/ppermute | solution.py:632
  7.8 2.1 %collective-permute-start.2 = (s32[8,128]{1,0:T(8,128)S(1)}, s32[8,128]{1,0:T(8,128)S(1)}, u32[]{:S(2)}, u32[]{:S(2)}) collective-permute-start(s32[8,128]{1,0:T(8,128)S(1)} %get-tuple-element.57), channel_id=1, source_target_pairs={{0,4},{1,5},{2,6},{3,7},{4,0},{5,1},{6,2},{7,3},{8,12},{9,13},{10,... | collective-permute-start | bytes 12296 | tf_op jit(solution)/shard_map/ppermute | solution.py:636
  10.0 2.6 %collective-permute-start.3 = (s32[8,128]{1,0:T(8,128)S(1)}, s32[8,128]{1,0:T(8,128)S(1)}, u32[]{:S(2)}, u32[]{:S(2)}) collective-permute-start(s32[8,128]{1,0:T(8,128)S(1)} %get-tuple-element.58), channel_id=1, source_target_pairs={{0,8},{1,9},{2,10},{3,11},{4,12},{5,13},{6,14},{7,15},{8,0},{9,1},... | collective-permute-start | bytes 12296 | tf_op jit(solution)/shard_map/ppermute | solution.py:636
  12.6 1.9 %collective-permute-done.3.refs_2_ = s32[8,128]{1,0:T(8,128)S(1)} collective-permute-done((s32[8,128]{1,0:T(8,128)S(1)}, s32[8,128]{1,0:T(8,128)S(1)}, u32[]{:S(2)}, u32[]{:S(2)}) %collective-permute-start.3) | collective-permute-done | bytes 4128 | tf_op jit(solution)/shard_map/ppermute | solution.py:636
  14.5 3.5 %collective-permute-done.4.refs_3_ = s32[8,128]{1,0:T(8,128)S(1)} collective-permute-done((s32[8,128]{1,0:T(8,128)S(1)}, s32[8,128]{1,0:T(8,128)S(1)}, u32[]{:S(2)}, u32[]{:S(2)}) %collective-permute-start.4) | collective-permute-done | bytes 4128 | tf_op jit(solution)/shard_map/ppermute | solution.py:636
  18.0 5.2 %adjoint_far.1 = (s32[4,1152]{1,0:T(4,128)S(1)}, f32[4,1152]{1,0:T(4,128)S(1)}, bf16[1024,1152]{1,0:T(8,128)(2,1)S(1)}, f32[512,256]{1,0:T(8,128)S(1)}, f32[512,256]{1,0:T(8,128)S(1)}) custom-call(s32[4]{0:T(128)S(1)} %pad_add_fusion.me_ref, s32[8,128]{1,0:T(8,128)S(1)} %get-tuple-element.56.refs_0_, s32[8,128]{1,0:T(8,128)S(1)} %collective-permute-done.2.refs_1_, ...), custom_call_target="tpu_custom_call" | custom-call | flops 1811939328 | bytes 4000000 | tf_op jit(solution)/shard_map/adjoint_far/pallas_call | solution.py:137
  23.7 4.4 %adjoint_near.1 = (bf16[1024,1152]{1,0:T(8,128)(2,1)S(1)}, f32[512,256]{1,0:T(8,128)S(1)}, f32[512,256]{1,0:T(8,128)S(1)}) custom-call(s32[4,1152]{1,0:T(4,128)S(1)} %get-tuple-element.60.ids_ref, f32[4,1152]{1,0:T(4,128)S(1)} %get-tuple-element.61.weight_ref, bf16[1152,256]{1,0:T(8,128)(2,1)S(1)} %get-tuple-element.103.refs_5_.wh_ref, ...), custom_call_target="tpu_custom_call" | custom-call | flops 1811939328 | bytes 4000000 | tf_op jit(solution)/shard_map/adjoint_near/pallas_call | solution.py:137
  28.3 1.6 %collective-permute-start.7 = (s16[272,256]{1,0:T(8,128)(2,1)S(1)}, s16[272,256]{1,0:T(8,128)(2,1)S(1)}, u32[]{:S(2)}, u32[]{:S(2)}) collective-permute-start(s16[272,256]{1,0:T(8,128)(2,1)S(1)} %get-tuple-element.67), channel_id=1, source_target_pairs={{0,2},{1,3},{2,0},{3,1},{4,6},{5,7},{6,4},{7,5},{8,10},{9,11},{10,... | collective-permute-start | bytes 417800 | tf_op jit(solution)/shard_map/ppermute | solution.py:632
  30.4 4.5 %collective-permute-done.7.p_ref = s16[272,256]{1,0:T(8,128)(2,1)S(1)} collective-permute-done((s16[272,256]{1,0:T(8,128)(2,1)S(1)}, s16[272,256]{1,0:T(8,128)(2,1)S(1)}, u32[]{:S(2)}, u32[]{:S(2)}) %collective-permute-start.7) | collective-permute-done | bytes 139296 | tf_op jit(solution)/shard_map/ppermute | solution.py:632
  35.0 1.9 %collective-permute-done.8.p_ref = s16[272,256]{1,0:T(8,128)(2,1)S(1)} collective-permute-done((s16[272,256]{1,0:T(8,128)(2,1)S(1)}, s16[272,256]{1,0:T(8,128)(2,1)S(1)}, u32[]{:S(2)}, u32[]{:S(2)}) %collective-permute-start.8) | collective-permute-done | bytes 139296 | tf_op jit(solution)/shard_map/ppermute | solution.py:632
  37.2 2.4 %collective-permute-start.10 = (s16[144,256]{1,0:T(8,128)(2,1)S(1)}, s16[144,256]{1,0:T(8,128)(2,1)S(1)}, u32[]{:S(2)}, u32[]{:S(2)}) collective-permute-start(s16[144,256]{1,0:T(8,128)(2,1)S(1)} %get-tuple-element.71), channel_id=1, source_target_pairs={{0,12},{1,13},{2,14},{3,15},{4,8},{5,9},{6,10},{7,11},{8,4},{9,5},... | collective-permute-start | bytes 221192 | tf_op jit(solution)/shard_map/ppermute | solution.py:636
  39.6 3.1 %copy.12 = bf16[80,128,256]{2,0,1:T(8,128)(2,1)S(1)} copy(bf16[80,128,256]{2,1,0:T(8,128)(2,1)S(1)} %bitcast.12) | data formatting | bytes 10485760 | tf_op args[0]
  42.8 1.9 %collective-permute-done.9.refs_0_ = s16[144,256]{1,0:T(8,128)(2,1)S(1)} collective-permute-done((s16[144,256]{1,0:T(8,128)(2,1)S(1)}, s16[144,256]{1,0:T(8,128)(2,1)S(1)}, u32[]{:S(2)}, u32[]{:S(2)}) %collective-permute-start.9) | collective-permute-done | bytes 73760 | tf_op jit(solution)/shard_map/ppermute | solution.py:636
  44.6 3.5 %coarse_first.1 = (bf16[256,128]{1,0:T(8,128)(2,1)S(1)}, f32[128,256]{1,0:T(8,128)S(1)}, f32[8,256]{1,0:T(8,128)S(1)}) custom-call(bf16[80,128,256]{2,1,0:T(8,128)(2,1)S(1)} %bitcast.12, bf16[256,256]{1,0:T(8,128)(2,1)S(1)} %copy-done.1, f32[128,256]{1,0:T(8,128)S(1)} %get-tuple-element.68.own_ref, s16[144,256]{1,0:T(8,128)(2,1)S(1)} %collective-permute-done.9.refs_0_, ...), custom_call_target="tpu_custom_call" | custom-call | flops 1342177280 | bytes 5000000 | tf_op jit(solution)/shard_map/coarse_first/pallas_call | solution.py:414
  52.6 2.9 %collective-permute-done.13.refs_1_ = bf16[256,128]{1,0:T(8,128)(2,1)S(1)} collective-permute-done((bf16[256,128]{1,0:T(8,128)(2,1)S(1)}, bf16[256,128]{1,0:T(8,128)(2,1)S(1)}, u32[]{:S(2)}, u32[]{:S(2)}) %collective-permute-start.13) | collective-permute-done | bytes 65568 | tf_op jit(solution)/shard_map/ppermute | solution.py:636
  55.6 2.0 %collective-permute-done.12.refs_0_ = bf16[256,128]{1,0:T(8,128)(2,1)S(1)} collective-permute-done((bf16[256,128]{1,0:T(8,128)(2,1)S(1)}, bf16[256,128]{1,0:T(8,128)(2,1)S(1)}, u32[]{:S(2)}, u32[]{:S(2)}) %collective-permute-start.12) | collective-permute-done | bytes 65568 | tf_op jit(solution)/shard_map/ppermute | solution.py:636
  59.2 3.6 %project.2 = (f32[80,8192]{1,0:T(8,128)S(1)}, f32[8,128]{1,0:T(8,128)S(1)}) custom-call(bf16[128,80,256]{2,1,0:T(8,128)(2,1)S(1)} %bitcast.9, f32[128,256]{1,0:T(8,128)S(1)} %get-tuple-element.74.y_ref.refs_3_, bf16[2,256,128]{2,1,0:T(8,128)(2,1)S(1)} %copy-done.2, bf16[4,256,128]{2,1,0:T(8,128)(2,1)S(1)} %join.2.after_ref.refs_0_), custom_call_target="tpu_custom_call" | custom-call | flops 1342177280 | bytes 8000000 | tf_op jit(solution)/shard_map/project/pallas_call | solution.py:452
  62.8 2.2 %collective-permute-done.15.x_ref = bf16[4,256,128]{2,1,0:T(8,128)(2,1)S(1)} collective-permute-done((bf16[4,256,128]{2,1,0:T(8,128)(2,1)S(1)}, bf16[4,256,128]{2,1,0:T(8,128)(2,1)S(1)}, u32[]{:S(2)}, u32[]{:S(2)}) %collective-permute-start.15) | collective-permute-done | bytes 262176 | tf_op jit(solution)/shard_map/ppermute | solution.py:632
  70.0 1.6 %collective-permute-start.21 = (s16[272,256]{1,0:T(8,128)(2,1)S(1)}, s16[272,256]{1,0:T(8,128)(2,1)S(1)}, u32[]{:S(2)}, u32[]{:S(2)}) collective-permute-start(s16[272,256]{1,0:T(8,128)(2,1)S(1)} %get-tuple-element.85), channel_id=1, source_target_pairs={{0,2},{1,3},{2,0},{3,1},{4,6},{5,7},{6,4},{7,5},{8,10},{9,11},{10,... | collective-permute-start | bytes 417800 | tf_op jit(solution)/shard_map/ppermute | solution.py:632
  72.1 4.5 %collective-permute-done.21.p_ref = s16[272,256]{1,0:T(8,128)(2,1)S(1)} collective-permute-done((s16[272,256]{1,0:T(8,128)(2,1)S(1)}, s16[272,256]{1,0:T(8,128)(2,1)S(1)}, u32[]{:S(2)}, u32[]{:S(2)}) %collective-permute-start.21) | collective-permute-done | bytes 139296 | tf_op jit(solution)/shard_map/ppermute | solution.py:632
  76.8 2.1 %collective-permute-start.23 = (s16[144,256]{1,0:T(8,128)(2,1)S(1)}, s16[144,256]{1,0:T(8,128)(2,1)S(1)}, u32[]{:S(2)}, u32[]{:S(2)}) collective-permute-start(s16[144,256]{1,0:T(8,128)(2,1)S(1)} %get-tuple-element.90), channel_id=1, source_target_pairs={{0,12},{1,13},{2,14},{3,15},{4,8},{5,9},{6,10},{7,11},{8,4},{9,5},... | collective-permute-start | bytes 221192 | tf_op jit(solution)/shard_map/ppermute | solution.py:636
  80.4 3.8 %collective-permute-done.22.refs_0_ = s16[144,256]{1,0:T(8,128)(2,1)S(1)} collective-permute-done((s16[144,256]{1,0:T(8,128)(2,1)S(1)}, s16[144,256]{1,0:T(8,128)(2,1)S(1)}, u32[]{:S(2)}, u32[]{:S(2)}) %collective-permute-start.22) | collective-permute-done | bytes 73760 | tf_op jit(solution)/shard_map/ppermute | solution.py:636
  84.8 3.6 %coarse_second.1 = (bf16[256,128]{1,0:T(8,128)(2,1)S(1)}, f32[128,256]{1,0:T(8,128)S(1)}, f32[8,128]{1,0:T(8,128)S(1)}, f32[8,256]{1,0:T(8,128)S(1)}) custom-call(bf16[80,128,256]{2,1,0:T(8,128)(2,1)S(1)} %bitcast.12, bf16[256,256]{1,0:T(8,128)(2,1)S(1)} %copy-done.1, f32[128,256]{1,0:T(8,128)S(1)} %get-tuple-element.88.own_ref, ...), custom_call_target="tpu_custom_call" | custom-call | flops 1342177280 | bytes 5000000 | tf_op jit(solution)/shard_map/coarse_second/pallas_call | solution.py:414
  89.2 1.8 %collective-permute-start.26 = (bf16[256,128]{1,0:T(8,128)(2,1)S(1)}, bf16[256,128]{1,0:T(8,128)(2,1)S(1)}, u32[]{:S(2)}, u32[]{:S(2)}) collective-permute-start(bf16[256,128]{1,0:T(8,128)(2,1)S(1)} %get-tuple-element.93.refs_3_), channel_id=1, source_target_pairs={{0,12},{1,13},{2,14},{3,15},{4,8},{5,9},{6,10},{7,11},{8,4},{9,5},... | collective-permute-start | bytes 196616 | tf_op jit(solution)/shard_map/ppermute | solution.py:636
  93.0 2.3 %collective-permute-done.26.refs_1_ = bf16[256,128]{1,0:T(8,128)(2,1)S(1)} collective-permute-done((bf16[256,128]{1,0:T(8,128)(2,1)S(1)}, bf16[256,128]{1,0:T(8,128)(2,1)S(1)}, u32[]{:S(2)}, u32[]{:S(2)}) %collective-permute-start.26) | collective-permute-done | bytes 65568 | tf_op jit(solution)/shard_map/ppermute | solution.py:636
  95.3 2.3 %collective-permute-done.25.refs_0_ = bf16[256,128]{1,0:T(8,128)(2,1)S(1)} collective-permute-done((bf16[256,128]{1,0:T(8,128)(2,1)S(1)}, bf16[256,128]{1,0:T(8,128)(2,1)S(1)}, u32[]{:S(2)}, u32[]{:S(2)}) %collective-permute-start.25) | collective-permute-done | bytes 65568 | tf_op jit(solution)/shard_map/ppermute | solution.py:636
  99.3 3.6 %project.3 = (f32[80,8192]{1,0:T(8,128)S(1)}, f32[8,128]{1,0:T(8,128)S(1)}) custom-call(bf16[128,80,256]{2,1,0:T(8,128)(2,1)S(1)} %bitcast.10, f32[128,256]{1,0:T(8,128)S(1)} %get-tuple-element.94.y_ref, bf16[2,256,128]{2,1,0:T(8,128)(2,1)S(1)} %copy-done.2, bf16[4,256,128]{2,1,0:T(8,128)(2,1)S(1)} %join.3.after_ref.refs_0_), custom_call_target="tpu_custom_call" | custom-call | flops 1342177280 | bytes 8000000 | tf_op jit(solution)/shard_map/project/pallas_call | solution.py:452
  102.9 2.1 %collective-permute-done.28.x_ref = bf16[4,256,128]{2,1,0:T(8,128)(2,1)S(1)} collective-permute-done((bf16[4,256,128]{2,1,0:T(8,128)(2,1)S(1)}, bf16[4,256,128]{2,1,0:T(8,128)(2,1)S(1)}, u32[]{:S(2)}, u32[]{:S(2)}) %collective-permute-start.28) | collective-permute-done | bytes 262176 | tf_op jit(solution)/shard_map/ppermute | solution.py:632
  110.1 2.1 %collective-permute-done.32 = f32[8,256]{1,0:T(8,128)S(1)} collective-permute-done((f32[8,256]{1,0:T(8,128)S(1)}, f32[8,256]{1,0:T(8,128)S(1)}, u32[]{:S(2)}, u32[]{:S(2)}) %collective-permute-start.32) | collective-permute-done | bytes 8224 | tf_op jit(solution)/shard_map/ppermute | solution.py:632
  112.3 1.8 %collective-permute-start.35 = (f32[8,256]{1,0:T(8,128)S(1)}, f32[8,256]{1,0:T(8,128)S(1)}, u32[]{:S(2)}, u32[]{:S(2)}) collective-permute-start(f32[8,256]{1,0:T(8,128)S(1)} %add.18.refs_0_), channel_id=1, source_target_pairs={{0,12},{1,13},{2,14},{3,15},{4,8},{5,9},{6,10},{7,11},{8,4},{9,5},... | collective-permute-start | bytes 24584 | tf_op jit(solution)/shard_map/ppermute | solution.py:636
  114.1 2.6 %collective-permute-start.33 = (f32[8,256]{1,0:T(8,128)S(1)}, f32[8,256]{1,0:T(8,128)S(1)}, u32[]{:S(2)}, u32[]{:S(2)}) collective-permute-start(f32[8,256]{1,0:T(8,128)S(1)} %add.18.refs_0_), channel_id=1, source_target_pairs={{0,4},{1,5},{2,6},{3,7},{4,0},{5,1},{6,2},{7,3},{8,12},{9,13},{10,... | collective-permute-start | bytes 24584 | tf_op jit(solution)/shard_map/ppermute | solution.py:636
  118.6 2.2 %result.1 = (f32[80,8192]{1,0:T(8,128)}, f32[1152,256]{1,0:T(8,128)}) custom-call(f32[8,128]{1,0:T(8,128)S(1)} %get-tuple-element.92.l0_ref, f32[8,256]{1,0:T(8,128)S(1)} %add.18.refs_0_, f32[8,256]{1,0:T(8,128)S(1)} %collective-permute-done.33.refs_1_, f32[8,256]{1,0:T(8,128)S(1)} %collective-permute-done.34.refs_2_, ...), custom_call_target="tpu_custom_call" | custom-call | flops 1966080 | bytes 10000000 | tf_op jit(solution)/shard_map/result/pallas_call | solution.py:611
  (89 shorter events, 31.3 us)
Async XLA Ops:
  3.4 4.4 %collective-permute-start.1 = (s32[8,128]{1,0:T(8,128)S(1)}, s32[8,128]{1,0:T(8,128)S(1)}, u32[]{:S(2)}, u32[]{:S(2)}) collective-permute-start(s32[8,128]{1,0:T(8,128)S(1)} %get-tuple-element.55), channel_id=1, source_target_pairs={{0,2},{1,3},{2,0},{3,1},{4,6},{5,7},{6,4},{7,5},{8,10},{9,11},{10,... | collective-permute-start | bytes 12296 | tf_op jit(solution)/shard_map/ppermute | solution.py:632
  7.8 4.8 %collective-permute-start.2 = (s32[8,128]{1,0:T(8,128)S(1)}, s32[8,128]{1,0:T(8,128)S(1)}, u32[]{:S(2)}, u32[]{:S(2)}) collective-permute-start(s32[8,128]{1,0:T(8,128)S(1)} %get-tuple-element.57), channel_id=1, source_target_pairs={{0,4},{1,5},{2,6},{3,7},{4,0},{5,1},{6,2},{7,3},{8,12},{9,13},{10,... | collective-permute-start | bytes 12296 | tf_op jit(solution)/shard_map/ppermute | solution.py:636
  10.0 4.5 %collective-permute-start.3 = (s32[8,128]{1,0:T(8,128)S(1)}, s32[8,128]{1,0:T(8,128)S(1)}, u32[]{:S(2)}, u32[]{:S(2)}) collective-permute-start(s32[8,128]{1,0:T(8,128)S(1)} %get-tuple-element.58), channel_id=1, source_target_pairs={{0,8},{1,9},{2,10},{3,11},{4,12},{5,13},{6,14},{7,15},{8,0},{9,1},... | collective-permute-start | bytes 12296 | tf_op jit(solution)/shard_map/ppermute | solution.py:636
  12.6 5.4 %collective-permute-start.4 = (s32[8,128]{1,0:T(8,128)S(1)}, s32[8,128]{1,0:T(8,128)S(1)}, u32[]{:S(2)}, u32[]{:S(2)}) collective-permute-start(s32[8,128]{1,0:T(8,128)S(1)} %get-tuple-element.59), channel_id=1, source_target_pairs={{0,12},{1,13},{2,14},{3,15},{4,8},{5,9},{6,10},{7,11},{8,4},{9,5},... | collective-permute-start | bytes 12296 | tf_op jit(solution)/shard_map/ppermute | solution.py:636
  23.1 5.0 %collective-permute-start.6 = (f32[512,256]{1,0:T(8,128)S(1)}, f32[512,256]{1,0:T(8,128)S(1)}, u32[]{:S(2)}, u32[]{:S(2)}) collective-permute-start(f32[512,256]{1,0:T(8,128)S(1)} %get-tuple-element.66), channel_id=1, source_target_pairs={{0,1},{1,0},{2,3},{3,2},{4,5},{5,4},{6,7},{7,6},{8,9},{9,8},{10,11... | collective-permute-start | bytes 1572872 | tf_op jit(solution)/shard_map/ppermute | solution.py:628
  23.2 7.2 %collective-permute-start.5 = (f32[512,256]{1,0:T(8,128)S(1)}, f32[512,256]{1,0:T(8,128)S(1)}, u32[]{:S(2)}, u32[]{:S(2)}) collective-permute-start(f32[512,256]{1,0:T(8,128)S(1)} %get-tuple-element.64), channel_id=1, source_target_pairs={{0,1},{1,0},{2,3},{3,2},{4,5},{5,4},{6,7},{7,6},{8,9},{9,8},{10,11... | collective-permute-start | bytes 1572872 | tf_op jit(solution)/shard_map/ppermute | solution.py:628
  28.3 6.6 %collective-permute-start.7 = (s16[272,256]{1,0:T(8,128)(2,1)S(1)}, s16[272,256]{1,0:T(8,128)(2,1)S(1)}, u32[]{:S(2)}, u32[]{:S(2)}) collective-permute-start(s16[272,256]{1,0:T(8,128)(2,1)S(1)} %get-tuple-element.67), channel_id=1, source_target_pairs={{0,2},{1,3},{2,0},{3,1},{4,6},{5,7},{6,4},{7,5},{8,10},{9,11},{10,... | collective-permute-start | bytes 417800 | tf_op jit(solution)/shard_map/ppermute | solution.py:632
  29.9 7.1 %collective-permute-start.8 = (s16[272,256]{1,0:T(8,128)(2,1)S(1)}, s16[272,256]{1,0:T(8,128)(2,1)S(1)}, u32[]{:S(2)}, u32[]{:S(2)}) collective-permute-start(s16[272,256]{1,0:T(8,128)(2,1)S(1)} %get-tuple-element.69), channel_id=1, source_target_pairs={{0,2},{1,3},{2,0},{3,1},{4,6},{5,7},{6,4},{7,5},{8,10},{9,11},{10,... | collective-permute-start | bytes 417800 | tf_op jit(solution)/shard_map/ppermute | solution.py:632
  35.0 7.8 %collective-permute-start.11 = (s16[144,256]{1,0:T(8,128)(2,1)S(1)}, s16[144,256]{1,0:T(8,128)(2,1)S(1)}, u32[]{:S(2)}, u32[]{:S(2)}) collective-permute-start(s16[144,256]{1,0:T(8,128)(2,1)S(1)} %get-tuple-element.72), channel_id=1, source_target_pairs={{0,4},{1,5},{2,6},{3,7},{4,0},{5,1},{6,2},{7,3},{8,12},{9,13},{10,... | collective-permute-start | bytes 221192 | tf_op jit(solution)/shard_map/ppermute | solution.py:636
  37.1 7.5 %collective-permute-start.9 = (s16[144,256]{1,0:T(8,128)(2,1)S(1)}, s16[144,256]{1,0:T(8,128)(2,1)S(1)}, u32[]{:S(2)}, u32[]{:S(2)}) collective-permute-start(s16[144,256]{1,0:T(8,128)(2,1)S(1)} %get-tuple-element.70), channel_id=1, source_target_pairs={{0,8},{1,9},{2,10},{3,11},{4,12},{5,13},{6,14},{7,15},{8,0},{9,1},... | collective-permute-start | bytes 221192 | tf_op jit(solution)/shard_map/ppermute | solution.py:636
  37.2 7.4 %collective-permute-start.10 = (s16[144,256]{1,0:T(8,128)(2,1)S(1)}, s16[144,256]{1,0:T(8,128)(2,1)S(1)}, u32[]{:S(2)}, u32[]{:S(2)}) collective-permute-start(s16[144,256]{1,0:T(8,128)(2,1)S(1)} %get-tuple-element.71), channel_id=1, source_target_pairs={{0,12},{1,13},{2,14},{3,15},{4,8},{5,9},{6,10},{7,11},{8,4},{9,5},... | collective-permute-start | bytes 221192 | tf_op jit(solution)/shard_map/ppermute | solution.py:636
  48.1 4.5 %collective-permute-start.14 = (bf16[256,128]{1,0:T(8,128)(2,1)S(1)}, bf16[256,128]{1,0:T(8,128)(2,1)S(1)}, u32[]{:S(2)}, u32[]{:S(2)}) collective-permute-start(bf16[256,128]{1,0:T(8,128)(2,1)S(1)} %get-tuple-element.73.refs_3_), channel_id=1, source_target_pairs={{0,4},{1,5},{2,6},{3,7},{4,0},{5,1},{6,2},{7,3},{8,12},{9,13},{10,... | collective-permute-start | bytes 196616 | tf_op jit(solution)/shard_map/ppermute | solution.py:636
  49.5 6.1 %collective-permute-start.13 = (bf16[256,128]{1,0:T(8,128)(2,1)S(1)}, bf16[256,128]{1,0:T(8,128)(2,1)S(1)}, u32[]{:S(2)}, u32[]{:S(2)}) collective-permute-start(bf16[256,128]{1,0:T(8,128)(2,1)S(1)} %get-tuple-element.73.refs_3_), channel_id=1, source_target_pairs={{0,12},{1,13},{2,14},{3,15},{4,8},{5,9},{6,10},{7,11},{8,4},{9,5},... | collective-permute-start | bytes 196616 | tf_op jit(solution)/shard_map/ppermute | solution.py:636
  50.8 6.8 %collective-permute-start.12 = (bf16[256,128]{1,0:T(8,128)(2,1)S(1)}, bf16[256,128]{1,0:T(8,128)(2,1)S(1)}, u32[]{:S(2)}, u32[]{:S(2)}) collective-permute-start(bf16[256,128]{1,0:T(8,128)(2,1)S(1)} %get-tuple-element.73.refs_3_), channel_id=1, source_target_pairs={{0,8},{1,9},{2,10},{3,11},{4,12},{5,13},{6,14},{7,15},{8,0},{9,1},... | collective-permute-start | bytes 196616 | tf_op jit(solution)/shard_map/ppermute | solution.py:636
  57.6 7.4 %collective-permute-start.15 = (bf16[4,256,128]{2,1,0:T(8,128)(2,1)S(1)}, bf16[4,256,128]{2,1,0:T(8,128)(2,1)S(1)}, u32[]{:S(2)}, u32[]{:S(2)}) collective-permute-start(bf16[4,256,128]{2,1,0:T(8,128)(2,1)S(1)} %join.2.after_ref.refs_0_), channel_id=1, source_target_pairs={{0,2},{1,3},{2,0},{3,1},{4,6},{5,7},{6,4},{7,5},{8,10},{9,11},{10,... | collective-permute-start | bytes 786440 | tf_op jit(solution)/shard_map/ppermute | solution.py:632
  59.2 5.9 %collective-permute-start.17 = (bf16[4,256,128]{2,1,0:T(8,128)(2,1)S(1)}, bf16[4,256,128]{2,1,0:T(8,128)(2,1)S(1)}, u32[]{:S(2)}, u32[]{:S(2)}) collective-permute-start(bf16[4,256,128]{2,1,0:T(8,128)(2,1)S(1)} %join.2.after_ref.refs_0_), channel_id=1, source_target_pairs={{0,1},{1,0},{2,3},{3,2},{4,5},{5,4},{6,7},{7,6},{8,9},{9,8},{10,11... | collective-permute-start | bytes 786440 | tf_op jit(solution)/shard_map/ppermute | solution.py:628
  67.9 2.0 %collective-permute-start.19 = (f32[520,256]{1,0:T(8,128)S(1)}, f32[520,256]{1,0:T(8,128)S(1)}, u32[]{:S(2)}, u32[]{:S(2)}) collective-permute-start(f32[520,256]{1,0:T(8,128)S(1)} %get-tuple-element.82), channel_id=1, source_target_pairs={{0,1},{1,0},{2,3},{3,2},{4,5},{5,4},{6,7},{7,6},{8,9},{9,8},{10,11... | collective-permute-start | bytes 1597448 | tf_op jit(solution)/shard_map/ppermute | solution.py:628
  68.3 3.8 %collective-permute-start.18 = (f32[512,256]{1,0:T(8,128)S(1)}, f32[512,256]{1,0:T(8,128)S(1)}, u32[]{:S(2)}, u32[]{:S(2)}) collective-permute-start(f32[512,256]{1,0:T(8,128)S(1)} %get-tuple-element.80), channel_id=1, source_target_pairs={{0,1},{1,0},{2,3},{3,2},{4,5},{5,4},{6,7},{7,6},{8,9},{9,8},{10,11... | collective-permute-start | bytes 1572872 | tf_op jit(solution)/shard_map/ppermute | solution.py:628
  70.0 6.6 %collective-permute-start.21 = (s16[272,256]{1,0:T(8,128)(2,1)S(1)}, s16[272,256]{1,0:T(8,128)(2,1)S(1)}, u32[]{:S(2)}, u32[]{:S(2)}) collective-permute-start(s16[272,256]{1,0:T(8,128)(2,1)S(1)} %get-tuple-element.85), channel_id=1, source_target_pairs={{0,2},{1,3},{2,0},{3,1},{4,6},{5,7},{6,4},{7,5},{8,10},{9,11},{10,... | collective-permute-start | bytes 417800 | tf_op jit(solution)/shard_map/ppermute | solution.py:632
  71.6 7.4 %collective-permute-start.20 = (s16[272,256]{1,0:T(8,128)(2,1)S(1)}, s16[272,256]{1,0:T(8,128)(2,1)S(1)}, u32[]{:S(2)}, u32[]{:S(2)}) collective-permute-start(s16[272,256]{1,0:T(8,128)(2,1)S(1)} %get-tuple-element.84), channel_id=1, source_target_pairs={{0,2},{1,3},{2,0},{3,1},{4,6},{5,7},{6,4},{7,5},{8,10},{9,11},{10,... | collective-permute-start | bytes 417800 | tf_op jit(solution)/shard_map/ppermute | solution.py:632
  76.7 7.5 %collective-permute-start.22 = (s16[144,256]{1,0:T(8,128)(2,1)S(1)}, s16[144,256]{1,0:T(8,128)(2,1)S(1)}, u32[]{:S(2)}, u32[]{:S(2)}) collective-permute-start(s16[144,256]{1,0:T(8,128)(2,1)S(1)} %get-tuple-element.89), channel_id=1, source_target_pairs={{0,8},{1,9},{2,10},{3,11},{4,12},{5,13},{6,14},{7,15},{8,0},{9,1},... | collective-permute-start | bytes 221192 | tf_op jit(solution)/shard_map/ppermute | solution.py:636
  76.8 7.4 %collective-permute-start.23 = (s16[144,256]{1,0:T(8,128)(2,1)S(1)}, s16[144,256]{1,0:T(8,128)(2,1)S(1)}, u32[]{:S(2)}, u32[]{:S(2)}) collective-permute-start(s16[144,256]{1,0:T(8,128)(2,1)S(1)} %get-tuple-element.90), channel_id=1, source_target_pairs={{0,12},{1,13},{2,14},{3,15},{4,8},{5,9},{6,10},{7,11},{8,4},{9,5},... | collective-permute-start | bytes 221192 | tf_op jit(solution)/shard_map/ppermute | solution.py:636
  79.1 5.6 %collective-permute-start.24 = (s16[144,256]{1,0:T(8,128)(2,1)S(1)}, s16[144,256]{1,0:T(8,128)(2,1)S(1)}, u32[]{:S(2)}, u32[]{:S(2)}) collective-permute-start(s16[144,256]{1,0:T(8,128)(2,1)S(1)} %get-tuple-element.91), channel_id=1, source_target_pairs={{0,4},{1,5},{2,6},{3,7},{4,0},{5,1},{6,2},{7,3},{8,12},{9,13},{10,... | collective-permute-start | bytes 221192 | tf_op jit(solution)/shard_map/ppermute | solution.py:636
  88.3 4.7 %collective-permute-start.27 = (bf16[256,128]{1,0:T(8,128)(2,1)S(1)}, bf16[256,128]{1,0:T(8,128)(2,1)S(1)}, u32[]{:S(2)}, u32[]{:S(2)}) collective-permute-start(bf16[256,128]{1,0:T(8,128)(2,1)S(1)} %get-tuple-element.93.refs_3_), channel_id=1, source_target_pairs={{0,4},{1,5},{2,6},{3,7},{4,0},{5,1},{6,2},{7,3},{8,12},{9,13},{10,... | collective-permute-start | bytes 196616 | tf_op jit(solution)/shard_map/ppermute | solution.py:636
  89.2 6.2 %collective-permute-start.26 = (bf16[256,128]{1,0:T(8,128)(2,1)S(1)}, bf16[256,128]{1,0:T(8,128)(2,1)S(1)}, u32[]{:S(2)}, u32[]{:S(2)}) collective-permute-start(bf16[256,128]{1,0:T(8,128)(2,1)S(1)} %get-tuple-element.93.refs_3_), channel_id=1, source_target_pairs={{0,12},{1,13},{2,14},{3,15},{4,8},{5,9},{6,10},{7,11},{8,4},{9,5},... | collective-permute-start | bytes 196616 | tf_op jit(solution)/shard_map/ppermute | solution.py:636
  91.0 6.7 %collective-permute-start.25 = (bf16[256,128]{1,0:T(8,128)(2,1)S(1)}, bf16[256,128]{1,0:T(8,128)(2,1)S(1)}, u32[]{:S(2)}, u32[]{:S(2)}) collective-permute-start(bf16[256,128]{1,0:T(8,128)(2,1)S(1)} %get-tuple-element.93.refs_3_), channel_id=1, source_target_pairs={{0,8},{1,9},{2,10},{3,11},{4,12},{5,13},{6,14},{7,15},{8,0},{9,1},... | collective-permute-start | bytes 196616 | tf_op jit(solution)/shard_map/ppermute | solution.py:636
  97.7 7.3 %collective-permute-start.28 = (bf16[4,256,128]{2,1,0:T(8,128)(2,1)S(1)}, bf16[4,256,128]{2,1,0:T(8,128)(2,1)S(1)}, u32[]{:S(2)}, u32[]{:S(2)}) collective-permute-start(bf16[4,256,128]{2,1,0:T(8,128)(2,1)S(1)} %join.3.after_ref.refs_0_), channel_id=1, source_target_pairs={{0,2},{1,3},{2,0},{3,1},{4,6},{5,7},{6,4},{7,5},{8,10},{9,11},{10,... | collective-permute-start | bytes 786440 | tf_op jit(solution)/shard_map/ppermute | solution.py:632
  99.3 5.8 %collective-permute-start.30 = (bf16[4,256,128]{2,1,0:T(8,128)(2,1)S(1)}, bf16[4,256,128]{2,1,0:T(8,128)(2,1)S(1)}, u32[]{:S(2)}, u32[]{:S(2)}) collective-permute-start(bf16[4,256,128]{2,1,0:T(8,128)(2,1)S(1)} %join.3.after_ref.refs_0_), channel_id=1, source_target_pairs={{0,1},{1,0},{2,3},{3,2},{4,5},{5,4},{6,7},{7,6},{8,9},{9,8},{10,11... | collective-permute-start | bytes 786440 | tf_op jit(solution)/shard_map/ppermute | solution.py:628
  108.6 3.7 %collective-permute-start.32 = (f32[8,256]{1,0:T(8,128)S(1)}, f32[8,256]{1,0:T(8,128)S(1)}, u32[]{:S(2)}, u32[]{:S(2)}) collective-permute-start(f32[8,256]{1,0:T(8,128)S(1)} %add.17), channel_id=1, source_target_pairs={{0,2},{1,3},{2,0},{3,1},{4,6},{5,7},{6,4},{7,5},{8,10},{9,11},{10,... | collective-permute-start | bytes 24584 | tf_op jit(solution)/shard_map/ppermute | solution.py:632
  112.3 5.5 %collective-permute-start.35 = (f32[8,256]{1,0:T(8,128)S(1)}, f32[8,256]{1,0:T(8,128)S(1)}, u32[]{:S(2)}, u32[]{:S(2)}) collective-permute-start(f32[8,256]{1,0:T(8,128)S(1)} %add.18.refs_0_), channel_id=1, source_target_pairs={{0,12},{1,13},{2,14},{3,15},{4,8},{5,9},{6,10},{7,11},{8,4},{9,5},... | collective-permute-start | bytes 24584 | tf_op jit(solution)/shard_map/ppermute | solution.py:636
  114.1 4.5 %collective-permute-start.34 = (f32[8,256]{1,0:T(8,128)S(1)}, f32[8,256]{1,0:T(8,128)S(1)}, u32[]{:S(2)}, u32[]{:S(2)}) collective-permute-start(f32[8,256]{1,0:T(8,128)S(1)} %add.18.refs_0_), channel_id=1, source_target_pairs={{0,8},{1,9},{2,10},{3,11},{4,12},{5,13},{6,14},{7,15},{8,0},{9,1},... | collective-permute-start | bytes 24584 | tf_op jit(solution)/shard_map/ppermute | solution.py:636
  114.1 4.5 %collective-permute-start.33 = (f32[8,256]{1,0:T(8,128)S(1)}, f32[8,256]{1,0:T(8,128)S(1)}, u32[]{:S(2)}, u32[]{:S(2)}) collective-permute-start(f32[8,256]{1,0:T(8,128)S(1)} %add.18.refs_0_), channel_id=1, source_target_pairs={{0,4},{1,5},{2,6},{3,7},{4,0},{5,1},{6,2},{7,3},{8,12},{9,13},{10,... | collective-permute-start | bytes 24584 | tf_op jit(solution)/shard_map/ppermute | solution.py:636
  (12 other events, 81.2 us)

commit v9 on v8

--- a/solution.py
+++ b/solution.py
@@ -188,7 +188,8 @@
     near, far = small(pick_kernel, 2, "pick", me, lists, scalars=1)
     near, far = small(mix_y_kernel, 2, "mix_y", near, over_core(far))
     own, *sent = small(mix_z_kernel, STEPS, "mix_z", near, over_y(far))
-    return [own] + [over_z(sent[k - 1], k) for k in range(1, STEPS)]
+    three, two, one = [over_z(sent[k - 1], k) for k in (3, 2, 1)]
+    return [own, one, two, three]
 
 
 def exponent(m):
@@ -309,7 +310,7 @@
 
 
 def join_kernel(*refs):
-    for i, r in enumerate(refs[:-1]):
+    for i, r in enumerate(refs[:2]):
         refs[-1][i] = r[...]
 
 
@@ -466,22 +467,26 @@
         xs[...] = x_refs[0][...]
         return
     for i, x in enumerate(x_refs):
-        for n in range(STEPS):
-            xs[:, pl.ds((i * STEPS + n) * LANES, LANES)] = x[n]
+        for n in range(2):
+            xs[:, pl.ds((i * 2 + n) * LANES, LANES)] = x[n]
 
 
 CUTS = 3
+PAIR = 2 * LANES
 
 
 def part_kernel(*refs):
     *x_refs, near_ref, far_ref, out_ref, xs = refs
     lay_out(x_refs, xs)
     half, fine = near_ref.shape
+    split = half // 2
     rows = fine // CUTS
     for i in range(CUTS):
         some = pl.ds(i * rows, rows)
-        out_ref[:, some] = dot(xs[:, :half], near_ref[:, some]) + dot(
-            xs[:, half:], far_ref[pl.ds(0, xs.shape[1] - half), some]
+        out_ref[:, some] = (
+            dot(xs[:, :half], near_ref[:, some])
+            + dot(xs[:, half : half + split], far_ref[pl.ds(0, split), some])
+            + dot(xs[:, half + split :], far_ref[pl.ds(split + PAIR, half - split - PAIR), some])
         )
 
 
@@ -492,7 +497,7 @@
         in_specs=[VMEM] * (len(xs) + 2),
         out_specs=VMEM,
         out_shape=shape((width, fine), F32),
-        scratch_shapes=[pltpu.VMEM((width, len(xs) * STEPS * LANES), BF)],
+        scratch_shapes=[pltpu.VMEM((width, len(xs) * PAIR), BF)],
         compiler_params=params(16),
         cost_estimate=cost(3 * half * fine * width, 4e6),
         name="image_part",
@@ -508,8 +513,7 @@
         if part_ref is None:
             turned = dot(xs[:, :half], near_ref[:, some]) + dot(xs[:, half:], far_ref[:, some])
         else:
-            last = xs.shape[1]
-            turned = dot(xs[...], far_ref[pl.ds(half - last, last), some]) + part_ref[:, some]
+            turned = dot(xs[...], far_ref[pl.ds(half // 2, PAIR), some]) + part_ref[:, some]
         im = turned.T
         im_ref[some, :] = im
         yield some, im, obs_ref[some, :].astype(F32) * im
@@ -544,7 +548,7 @@
     if first:
         out += [shape((fine, width), BF)]
         out += [shape((half // 2, width), F32), shape((half // 2 + 8, width), F32)]
-    last = STEPS * LANES if part else 2 * half
+    last = PAIR if part else 2 * half
     return pl.pallas_call(
         functools.partial(image_kernel, bool(part), first),
         in_specs=[VMEM] * (5 + len(part)),
@@ -649,12 +653,14 @@
 
 
 def gather_columns(x, work):
-    four = shape((STEPS,) + x.shape, BF)
-    a = copy_of(join_kernel, "join", four, *[over_z(x, k) for k in ORDER[:3]], x)
+    two = shape((2,) + x.shape, BF)
+    a = copy_of(join_kernel, "join_first", two, over_z(x, 1), x)
     ya, ca = over_y(a), over_core(a)
-    done, token = work(a)
-    ya = copy_of(relay_kernel, "relay", four, ya, token)
-    return [a, ya, ca, over_core(ya)], done
+    b = copy_of(join_kernel, "join_second", two, over_z(x, 2), over_z(x, 3), ya)
+    yb, cb, cya = over_y(b), over_core(b), over_core(ya)
+    done, token = work(b)
+    yb = copy_of(relay_kernel, "relay", two, yb, token)
+    return [b, a, yb, ya, cb, ca, cya, over_core(yb)], done
 
 
 def sum_all(x):

time: 121 us -> 128 us (1.058)
  starting transfers between devices: 36.2 us -> 41.3 us
  waiting for transfers between devices: 45.2 us -> 46.6 us
    ppermute x18, waiting for transfers between devices: 25.3 us -> 28.1 us  [over_z(): return lax.ppermute(x, 'space', [(i, i ^ 4 * k) for i in range(GROUP)])]
    ppermute x18, starting transfers between devices: 22.3 us -> 25 us  [over_z(): return lax.ppermute(x, 'space', [(i, i ^ 4 * k) for i in range(GROUP)])]
    ppermute x8 -> x10, waiting for transfers between devices: 17.5 us -> 16 us  [over_y(): return lax.ppermute(x, 'space', [(i, i ^ 2) for i in range(GROUP)])]
    ppermute x10 -> x14, starting transfers between devices: 2.26 us -> 3.61 us  [over_core(): return lax.ppermute(x, 'space', [(i, i ^ 1) for i in range(GROUP)])]
    ppermute x8 -> x10, starting transfers between devices: 11.7 us -> 12.7 us  [over_y(): return lax.ppermute(x, 'space', [(i, i ^ 2) for i in range(GROUP)])]
    ppermute x10 -> x14, waiting for transfers between devices: 2.48 us -> 2.56 us  [over_core(): return lax.ppermute(x, 'space', [(i, i ^ 1) for i in range(GROUP)])]
  transfers between devices with their start and end apart: 36 -> 42, of which waited for: 25 -> 22; matrix products, arithmetic and copies ran while one was open for 4% -> 4% of each run, Pallas kernels for 13% -> 13%
where the time goes in v9:
time: 128 us
  waiting for transfers between devices  46.6 us (36%)
  starting transfers between devices  41.3 us (32%)
  Pallas kernels  33.5 us (26%)
  local copies, waits for them, and re-layouts  3.88 us (3%)
  other arithmetic  1.62 us (1%)
    ppermute x18, waiting for transfers between devices, over_z(): return lax.ppermute(x, 'space', [(i, i ^ 4 * k) for i in range(GROUP)])  28.1 us
    ppermute x18, starting transfers between devices, over_z(): return lax.ppermute(x, 'space', [(i, i ^ 4 * k) for i in range(GROUP)])  25 us
    ppermute x10, waiting for transfers between devices, over_y(): return lax.ppermute(x, 'space', [(i, i ^ 2) for i in range(GROUP)])  16 us
    ppermute x10, starting transfers between devices, over_y(): return lax.ppermute(x, 'space', [(i, i ^ 2) for i in range(GROUP)])  12.7 us
    pallas_call x2, Pallas kernels, adjoint_half(): pl.pallas_call(kernel, in_specs=([SMEM] if head else []) + [VMEM] * (len(...  9.57 us
    pallas_call x2, Pallas kernels, project(): pl.pallas_call(project_kernel, in_specs=[VMEM] * 4, out_specs=[VMEM] * 2,...  7.51 us
    pallas_call x2, Pallas kernels, coarse_image(): pl.pallas_call(functools.partial(coarse_kernel, len(got), second, len(aft...  7.22 us
    unnamed x17, local copies, waits for them, and re-layouts  3.88 us
  transfers between devices with their start and end apart: 42, of which 22 were waited for; matrix products, arithmetic and copies ran while one was open for 4% of the time, Pallas kernels for 13%

profile of v9, /device:TPU:0, one launch (start us, length us, event | category | flops | bytes accessed | tf_op | source)
XLA Modules:
  0.0 128.1 jit_solution(11830563484091153935)
XLA Ops:
  3.4 2.9 %collective-permute-start.1 = (s32[8,128]{1,0:T(8,128)S(1)}, s32[8,128]{1,0:T(8,128)S(1)}, u32[]{:S(2)}, u32[]{:S(2)}) collective-permute-start(s32[8,128]{1,0:T(8,128)S(1)} %get-tuple-element.55), channel_id=1, source_target_pairs={{0,2},{1,3},{2,0},{3,1},{4,6},{5,7},{6,4},{7,5},{8,10},{9,11},{10,... | collective-permute-start | bytes 12296 | tf_op jit(solution)/shard_map/ppermute | solution.py:636
  7.8 2.1 %collective-permute-start.2 = (s32[8,128]{1,0:T(8,128)S(1)}, s32[8,128]{1,0:T(8,128)S(1)}, u32[]{:S(2)}, u32[]{:S(2)}) collective-permute-start(s32[8,128]{1,0:T(8,128)S(1)} %get-tuple-element.57), channel_id=1, source_target_pairs={{0,4},{1,5},{2,6},{3,7},{4,0},{5,1},{6,2},{7,3},{8,12},{9,13},{10,... | collective-permute-start | bytes 12296 | tf_op jit(solution)/shard_map/ppermute | solution.py:640
  10.0 2.6 %collective-permute-start.3 = (s32[8,128]{1,0:T(8,128)S(1)}, s32[8,128]{1,0:T(8,128)S(1)}, u32[]{:S(2)}, u32[]{:S(2)}) collective-permute-start(s32[8,128]{1,0:T(8,128)S(1)} %get-tuple-element.58), channel_id=1, source_target_pairs={{0,8},{1,9},{2,10},{3,11},{4,12},{5,13},{6,14},{7,15},{8,0},{9,1},... | collective-permute-start | bytes 12296 | tf_op jit(solution)/shard_map/ppermute | solution.py:640
  12.6 1.9 %collective-permute-done.3.refs_2_ = s32[8,128]{1,0:T(8,128)S(1)} collective-permute-done((s32[8,128]{1,0:T(8,128)S(1)}, s32[8,128]{1,0:T(8,128)S(1)}, u32[]{:S(2)}, u32[]{:S(2)}) %collective-permute-start.3) | collective-permute-done | bytes 4128 | tf_op jit(solution)/shard_map/ppermute | solution.py:640
  14.5 3.5 %collective-permute-done.4.refs_3_ = s32[8,128]{1,0:T(8,128)S(1)} collective-permute-done((s32[8,128]{1,0:T(8,128)S(1)}, s32[8,128]{1,0:T(8,128)S(1)}, u32[]{:S(2)}, u32[]{:S(2)}) %collective-permute-start.4) | collective-permute-done | bytes 4128 | tf_op jit(solution)/shard_map/ppermute | solution.py:640
  18.0 5.2 %adjoint_far.1 = (s32[4,1152]{1,0:T(4,128)S(1)}, f32[4,1152]{1,0:T(4,128)S(1)}, bf16[1024,1152]{1,0:T(8,128)(2,1)S(1)}, f32[512,256]{1,0:T(8,128)S(1)}, f32[512,256]{1,0:T(8,128)S(1)}) custom-call(s32[4]{0:T(128)S(1)} %pad_add_fusion.me_ref, s32[8,128]{1,0:T(8,128)S(1)} %get-tuple-element.56.refs_0_, s32[8,128]{1,0:T(8,128)S(1)} %collective-permute-done.2.refs_1_, ...), custom_call_target="tpu_custom_call" | custom-call | flops 1811939328 | bytes 4000000 | tf_op jit(solution)/shard_map/adjoint_far/pallas_call | solution.py:137
  23.7 4.4 %adjoint_near.1 = (bf16[1024,1152]{1,0:T(8,128)(2,1)S(1)}, f32[512,256]{1,0:T(8,128)S(1)}, f32[512,256]{1,0:T(8,128)S(1)}) custom-call(s32[4,1152]{1,0:T(4,128)S(1)} %get-tuple-element.60.ids_ref, f32[4,1152]{1,0:T(4,128)S(1)} %get-tuple-element.61.weight_ref, bf16[1152,256]{1,0:T(8,128)(2,1)S(1)} %get-tuple-element.103.refs_5_.wh_ref, ...), custom_call_target="tpu_custom_call" | custom-call | flops 1811939328 | bytes 4000000 | tf_op jit(solution)/shard_map/adjoint_near/pallas_call | solution.py:137
  30.4 4.5 %collective-permute-done.8.p_ref = s16[272,256]{1,0:T(8,128)(2,1)S(1)} collective-permute-done((s16[272,256]{1,0:T(8,128)(2,1)S(1)}, s16[272,256]{1,0:T(8,128)(2,1)S(1)}, u32[]{:S(2)}, u32[]{:S(2)}) %collective-permute-start.8) | collective-permute-done | bytes 139296 | tf_op jit(solution)/shard_map/ppermute | solution.py:636
  35.2 1.8 %collective-permute-done.7.p_ref = s16[272,256]{1,0:T(8,128)(2,1)S(1)} collective-permute-done((s16[272,256]{1,0:T(8,128)(2,1)S(1)}, s16[272,256]{1,0:T(8,128)(2,1)S(1)}, u32[]{:S(2)}, u32[]{:S(2)}) %collective-permute-start.7) | collective-permute-done | bytes 139296 | tf_op jit(solution)/shard_map/ppermute | solution.py:636
  37.1 2.5 %collective-permute-start.11 = (s16[144,256]{1,0:T(8,128)(2,1)S(1)}, s16[144,256]{1,0:T(8,128)(2,1)S(1)}, u32[]{:S(2)}, u32[]{:S(2)}) collective-permute-start(s16[144,256]{1,0:T(8,128)(2,1)S(1)} %get-tuple-element.72), channel_id=1, source_target_pairs={{0,4},{1,5},{2,6},{3,7},{4,0},{5,1},{6,2},{7,3},{8,12},{9,13},{10,... | collective-permute-start | bytes 221192 | tf_op jit(solution)/shard_map/ppermute | solution.py:640
  39.6 3.1 %copy.12 = bf16[80,128,256]{2,0,1:T(8,128)(2,1)S(1)} copy(bf16[80,128,256]{2,1,0:T(8,128)(2,1)S(1)} %bitcast.12) | data formatting | bytes 10485760 | tf_op args[0]
  42.8 3.6 %coarse_first.1 = (bf16[256,128]{1,0:T(8,128)(2,1)S(1)}, f32[128,256]{1,0:T(8,128)S(1)}, f32[8,256]{1,0:T(8,128)S(1)}) custom-call(bf16[80,128,256]{2,1,0:T(8,128)(2,1)S(1)} %bitcast.12, bf16[256,256]{1,0:T(8,128)(2,1)S(1)} %copy-done.1, f32[128,256]{1,0:T(8,128)S(1)} %get-tuple-element.68.own_ref, s16[144,256]{1,0:T(8,128)(2,1)S(1)} %collective-permute-done.9.refs_0_, ...), custom_call_target="tpu_custom_call" | custom-call | flops 1342177280 | bytes 5000000 | tf_op jit(solution)/shard_map/coarse_first/pallas_call | solution.py:415
  47.7 3.1 %collective-permute-done.14.refs_0_ = bf16[256,128]{1,0:T(8,128)(2,1)S(1)} collective-permute-done((bf16[256,128]{1,0:T(8,128)(2,1)S(1)}, bf16[256,128]{1,0:T(8,128)(2,1)S(1)}, u32[]{:S(2)}, u32[]{:S(2)}) %collective-permute-start.14) | collective-permute-done | bytes 65568 | tf_op jit(solution)/shard_map/ppermute | solution.py:640
  53.0 3.1 %collective-permute-start.13 = (bf16[256,128]{1,0:T(8,128)(2,1)S(1)}, bf16[256,128]{1,0:T(8,128)(2,1)S(1)}, u32[]{:S(2)}, u32[]{:S(2)}) collective-permute-start(bf16[256,128]{1,0:T(8,128)(2,1)S(1)} %get-tuple-element.73.refs_1_), channel_id=1, source_target_pairs={{0,12},{1,13},{2,14},{3,15},{4,8},{5,9},{6,10},{7,11},{8,4},{9,5},... | collective-permute-start | bytes 196616 | tf_op jit(solution)/shard_map/ppermute | solution.py:640
  57.6 1.6 %collective-permute-done.13.refs_1_ = bf16[256,128]{1,0:T(8,128)(2,1)S(1)} collective-permute-done((bf16[256,128]{1,0:T(8,128)(2,1)S(1)}, bf16[256,128]{1,0:T(8,128)(2,1)S(1)}, u32[]{:S(2)}, u32[]{:S(2)}) %collective-permute-start.13) | collective-permute-done | bytes 65568 | tf_op jit(solution)/shard_map/ppermute | solution.py:640
  60.2 3.7 %project.2 = (f32[80,8192]{1,0:T(8,128)S(1)}, f32[8,128]{1,0:T(8,128)S(1)}) custom-call(bf16[128,80,256]{2,1,0:T(8,128)(2,1)S(1)} %bitcast.9, f32[128,256]{1,0:T(8,128)S(1)} %get-tuple-element.74.y_ref.refs_3_, bf16[2,256,128]{2,1,0:T(8,128)(2,1)S(1)} %copy-done.2, bf16[2,256,128]{2,1,0:T(8,128)(2,1)S(1)} %join_second.2.after_ref.refs_0_), custom_call_target="tpu_custom_call" | custom-call | flops 1342177280 | bytes 8000000 | tf_op jit(solution)/shard_map/project/pallas_call | solution.py:453
  64.5 1.6 %image_part.2.refs_0_ = f32[256,1152]{1,0:T(8,128)S(1)} custom-call(bf16[2,256,128]{2,1,0:T(8,128)(2,1)S(1)} %join_second.2.after_ref.refs_0_, bf16[2,256,128]{2,1,0:T(8,128)(2,1)S(1)} %join_first.2.refs_1_, bf16[2,256,128]{2,1,0:T(8,128)(2,1)S(1)} %relay.2.refs_2_, bf16[2,256,128]{2,1,0:T(8,128)(2,1)S(1)} %collective-permute-done.15.refs_2_.refs_3_, ...), custom_call_target="tpu_custom_call" | custom-call | flops 905969664 | bytes 4000000 | tf_op jit(solution)/shard_map/image_part/pallas_call | solution.py:495
  69.4 1.6 %collective-permute-start.24 = (s16[272,256]{1,0:T(8,128)(2,1)S(1)}, s16[272,256]{1,0:T(8,128)(2,1)S(1)}, u32[]{:S(2)}, u32[]{:S(2)}) collective-permute-start(s16[272,256]{1,0:T(8,128)(2,1)S(1)} %get-tuple-element.85), channel_id=1, source_target_pairs={{0,2},{1,3},{2,0},{3,1},{4,6},{5,7},{6,4},{7,5},{8,10},{9,11},{10,... | collective-permute-start | bytes 417800 | tf_op jit(solution)/shard_map/ppermute | solution.py:636
  71.5 4.5 %collective-permute-done.24.p_ref = s16[272,256]{1,0:T(8,128)(2,1)S(1)} collective-permute-done((s16[272,256]{1,0:T(8,128)(2,1)S(1)}, s16[272,256]{1,0:T(8,128)(2,1)S(1)}, u32[]{:S(2)}, u32[]{:S(2)}) %collective-permute-start.24) | collective-permute-done | bytes 139296 | tf_op jit(solution)/shard_map/ppermute | solution.py:636
  76.1 2.3 %collective-permute-done.23.p_ref = s16[272,256]{1,0:T(8,128)(2,1)S(1)} collective-permute-done((s16[272,256]{1,0:T(8,128)(2,1)S(1)}, s16[272,256]{1,0:T(8,128)(2,1)S(1)}, u32[]{:S(2)}, u32[]{:S(2)}) %collective-permute-start.23) | collective-permute-done | bytes 139296 | tf_op jit(solution)/shard_map/ppermute | solution.py:636
  79.6 2.5 %collective-permute-start.25 = (s16[144,256]{1,0:T(8,128)(2,1)S(1)}, s16[144,256]{1,0:T(8,128)(2,1)S(1)}, u32[]{:S(2)}, u32[]{:S(2)}) collective-permute-start(s16[144,256]{1,0:T(8,128)(2,1)S(1)} %get-tuple-element.89), channel_id=1, source_target_pairs={{0,8},{1,9},{2,10},{3,11},{4,12},{5,13},{6,14},{7,15},{8,0},{9,1},... | collective-permute-start | bytes 221192 | tf_op jit(solution)/shard_map/ppermute | solution.py:640
  83.7 3.3 %collective-permute-done.25.refs_0_ = s16[144,256]{1,0:T(8,128)(2,1)S(1)} collective-permute-done((s16[144,256]{1,0:T(8,128)(2,1)S(1)}, s16[144,256]{1,0:T(8,128)(2,1)S(1)}, u32[]{:S(2)}, u32[]{:S(2)}) %collective-permute-start.25) | collective-permute-done | bytes 73760 | tf_op jit(solution)/shard_map/ppermute | solution.py:640
  88.4 3.6 %coarse_second.1 = (bf16[256,128]{1,0:T(8,128)(2,1)S(1)}, f32[128,256]{1,0:T(8,128)S(1)}, f32[8,128]{1,0:T(8,128)S(1)}, f32[8,256]{1,0:T(8,128)S(1)}) custom-call(bf16[80,128,256]{2,1,0:T(8,128)(2,1)S(1)} %bitcast.12, bf16[256,256]{1,0:T(8,128)(2,1)S(1)} %copy-done.1, f32[128,256]{1,0:T(8,128)S(1)} %get-tuple-element.88.own_ref, ...), custom_call_target="tpu_custom_call" | custom-call | flops 1342177280 | bytes 5000000 | tf_op jit(solution)/shard_map/coarse_second/pallas_call | solution.py:415
  92.8 3.5 %collective-permute-done.30.refs_0_ = bf16[256,128]{1,0:T(8,128)(2,1)S(1)} collective-permute-done((bf16[256,128]{1,0:T(8,128)(2,1)S(1)}, bf16[256,128]{1,0:T(8,128)(2,1)S(1)}, u32[]{:S(2)}, u32[]{:S(2)}) %collective-permute-start.30) | collective-permute-done | bytes 65568 | tf_op jit(solution)/shard_map/ppermute | solution.py:640
  100.8 2.9 %collective-permute-done.28.refs_0_ = bf16[256,128]{1,0:T(8,128)(2,1)S(1)} collective-permute-done((bf16[256,128]{1,0:T(8,128)(2,1)S(1)}, bf16[256,128]{1,0:T(8,128)(2,1)S(1)}, u32[]{:S(2)}, u32[]{:S(2)}) %collective-permute-start.28) | collective-permute-done | bytes 65568 | tf_op jit(solution)/shard_map/ppermute | solution.py:640
  103.6 1.7 %collective-permute-done.29.refs_1_ = bf16[256,128]{1,0:T(8,128)(2,1)S(1)} collective-permute-done((bf16[256,128]{1,0:T(8,128)(2,1)S(1)}, bf16[256,128]{1,0:T(8,128)(2,1)S(1)}, u32[]{:S(2)}, u32[]{:S(2)}) %collective-permute-start.29) | collective-permute-done | bytes 65568 | tf_op jit(solution)/shard_map/ppermute | solution.py:640
  106.8 3.8 %project.3 = (f32[80,8192]{1,0:T(8,128)S(1)}, f32[8,128]{1,0:T(8,128)S(1)}) custom-call(bf16[128,80,256]{2,1,0:T(8,128)(2,1)S(1)} %bitcast.10, f32[128,256]{1,0:T(8,128)S(1)} %get-tuple-element.94.y_ref, bf16[2,256,128]{2,1,0:T(8,128)(2,1)S(1)} %copy-done.2, bf16[2,256,128]{2,1,0:T(8,128)(2,1)S(1)} %join_second.3.after_ref.refs_0_), custom_call_target="tpu_custom_call" | custom-call | flops 1342177280 | bytes 8000000 | tf_op jit(solution)/shard_map/project/pallas_call | solution.py:453
  115.8 2.5 %collective-permute-done.38 = f32[8,256]{1,0:T(8,128)S(1)} collective-permute-done((f32[8,256]{1,0:T(8,128)S(1)}, f32[8,256]{1,0:T(8,128)S(1)}, u32[]{:S(2)}, u32[]{:S(2)}) %collective-permute-start.38) | collective-permute-done | bytes 8224 | tf_op jit(solution)/shard_map/ppermute | solution.py:636
  118.3 2.0 %collective-permute-start.40 = (f32[8,256]{1,0:T(8,128)S(1)}, f32[8,256]{1,0:T(8,128)S(1)}, u32[]{:S(2)}, u32[]{:S(2)}) collective-permute-start(f32[8,256]{1,0:T(8,128)S(1)} %add.18.refs_0_), channel_id=1, source_target_pairs={{0,8},{1,9},{2,10},{3,11},{4,12},{5,13},{6,14},{7,15},{8,0},{9,1},... | collective-permute-start | bytes 24584 | tf_op jit(solution)/shard_map/ppermute | solution.py:640
  120.3 2.4 %collective-permute-start.41 = (f32[8,256]{1,0:T(8,128)S(1)}, f32[8,256]{1,0:T(8,128)S(1)}, u32[]{:S(2)}, u32[]{:S(2)}) collective-permute-start(f32[8,256]{1,0:T(8,128)S(1)} %add.18.refs_0_), channel_id=1, source_target_pairs={{0,12},{1,13},{2,14},{3,15},{4,8},{5,9},{6,10},{7,11},{8,4},{9,5},... | collective-permute-start | bytes 24584 | tf_op jit(solution)/shard_map/ppermute | solution.py:640
  122.9 2.9 %collective-permute-done.41.refs_3_ = f32[8,256]{1,0:T(8,128)S(1)} collective-permute-done((f32[8,256]{1,0:T(8,128)S(1)}, f32[8,256]{1,0:T(8,128)S(1)}, u32[]{:S(2)}, u32[]{:S(2)}) %collective-permute-start.41) | collective-permute-done | bytes 8224 | tf_op jit(solution)/shard_map/ppermute | solution.py:640
  125.7 2.2 %result.1 = (f32[80,8192]{1,0:T(8,128)}, f32[1152,256]{1,0:T(8,128)}) custom-call(f32[8,128]{1,0:T(8,128)S(1)} %get-tuple-element.92.l0_ref, f32[8,256]{1,0:T(8,128)S(1)} %add.18.refs_0_, f32[8,256]{1,0:T(8,128)S(1)} %collective-permute-done.39.refs_1_, f32[8,256]{1,0:T(8,128)S(1)} %collective-permute-done.40.refs_2_, ...), custom_call_target="tpu_custom_call" | custom-call | flops 1966080 | bytes 10000000 | tf_op jit(solution)/shard_map/result/pallas_call | solution.py:615
  (103 shorter events, 34.0 us)
Async XLA Ops:
  3.4 4.4 %collective-permute-start.1 = (s32[8,128]{1,0:T(8,128)S(1)}, s32[8,128]{1,0:T(8,128)S(1)}, u32[]{:S(2)}, u32[]{:S(2)}) collective-permute-start(s32[8,128]{1,0:T(8,128)S(1)} %get-tuple-element.55), channel_id=1, source_target_pairs={{0,2},{1,3},{2,0},{3,1},{4,6},{5,7},{6,4},{7,5},{8,10},{9,11},{10,... | collective-permute-start | bytes 12296 | tf_op jit(solution)/shard_map/ppermute | solution.py:636
  7.8 4.8 %collective-permute-start.2 = (s32[8,128]{1,0:T(8,128)S(1)}, s32[8,128]{1,0:T(8,128)S(1)}, u32[]{:S(2)}, u32[]{:S(2)}) collective-permute-start(s32[8,128]{1,0:T(8,128)S(1)} %get-tuple-element.57), channel_id=1, source_target_pairs={{0,4},{1,5},{2,6},{3,7},{4,0},{5,1},{6,2},{7,3},{8,12},{9,13},{10,... | collective-permute-start | bytes 12296 | tf_op jit(solution)/shard_map/ppermute | solution.py:640
  10.0 4.5 %collective-permute-start.3 = (s32[8,128]{1,0:T(8,128)S(1)}, s32[8,128]{1,0:T(8,128)S(1)}, u32[]{:S(2)}, u32[]{:S(2)}) collective-permute-start(s32[8,128]{1,0:T(8,128)S(1)} %get-tuple-element.58), channel_id=1, source_target_pairs={{0,8},{1,9},{2,10},{3,11},{4,12},{5,13},{6,14},{7,15},{8,0},{9,1},... | collective-permute-start | bytes 12296 | tf_op jit(solution)/shard_map/ppermute | solution.py:640
  12.6 5.4 %collective-permute-start.4 = (s32[8,128]{1,0:T(8,128)S(1)}, s32[8,128]{1,0:T(8,128)S(1)}, u32[]{:S(2)}, u32[]{:S(2)}) collective-permute-start(s32[8,128]{1,0:T(8,128)S(1)} %get-tuple-element.59), channel_id=1, source_target_pairs={{0,12},{1,13},{2,14},{3,15},{4,8},{5,9},{6,10},{7,11},{8,4},{9,5},... | collective-permute-start | bytes 12296 | tf_op jit(solution)/shard_map/ppermute | solution.py:640
  23.1 5.0 %collective-permute-start.6 = (f32[512,256]{1,0:T(8,128)S(1)}, f32[512,256]{1,0:T(8,128)S(1)}, u32[]{:S(2)}, u32[]{:S(2)}) collective-permute-start(f32[512,256]{1,0:T(8,128)S(1)} %get-tuple-element.66), channel_id=1, source_target_pairs={{0,1},{1,0},{2,3},{3,2},{4,5},{5,4},{6,7},{7,6},{8,9},{9,8},{10,11... | collective-permute-start | bytes 1572872 | tf_op jit(solution)/shard_map/ppermute | solution.py:632
  23.2 7.2 %collective-permute-start.5 = (f32[512,256]{1,0:T(8,128)S(1)}, f32[512,256]{1,0:T(8,128)S(1)}, u32[]{:S(2)}, u32[]{:S(2)}) collective-permute-start(f32[512,256]{1,0:T(8,128)S(1)} %get-tuple-element.64), channel_id=1, source_target_pairs={{0,1},{1,0},{2,3},{3,2},{4,5},{5,4},{6,7},{7,6},{8,9},{9,8},{10,11... | collective-permute-start | bytes 1572872 | tf_op jit(solution)/shard_map/ppermute | solution.py:632
  28.3 6.6 %collective-permute-start.8 = (s16[272,256]{1,0:T(8,128)(2,1)S(1)}, s16[272,256]{1,0:T(8,128)(2,1)S(1)}, u32[]{:S(2)}, u32[]{:S(2)}) collective-permute-start(s16[272,256]{1,0:T(8,128)(2,1)S(1)} %get-tuple-element.69), channel_id=1, source_target_pairs={{0,2},{1,3},{2,0},{3,1},{4,6},{5,7},{6,4},{7,5},{8,10},{9,11},{10,... | collective-permute-start | bytes 417800 | tf_op jit(solution)/shard_map/ppermute | solution.py:636
  29.9 7.1 %collective-permute-start.7 = (s16[272,256]{1,0:T(8,128)(2,1)S(1)}, s16[272,256]{1,0:T(8,128)(2,1)S(1)}, u32[]{:S(2)}, u32[]{:S(2)}) collective-permute-start(s16[272,256]{1,0:T(8,128)(2,1)S(1)} %get-tuple-element.67), channel_id=1, source_target_pairs={{0,2},{1,3},{2,0},{3,1},{4,6},{5,7},{6,4},{7,5},{8,10},{9,11},{10,... | collective-permute-start | bytes 417800 | tf_op jit(solution)/shard_map/ppermute | solution.py:636
  35.0 7.8 %collective-permute-start.10 = (s16[144,256]{1,0:T(8,128)(2,1)S(1)}, s16[144,256]{1,0:T(8,128)(2,1)S(1)}, u32[]{:S(2)}, u32[]{:S(2)}) collective-permute-start(s16[144,256]{1,0:T(8,128)(2,1)S(1)} %get-tuple-element.71), channel_id=1, source_target_pairs={{0,12},{1,13},{2,14},{3,15},{4,8},{5,9},{6,10},{7,11},{8,4},{9,5},... | collective-permute-start | bytes 221192 | tf_op jit(solution)/shard_map/ppermute | solution.py:640
  35.1 7.7 %collective-permute-start.9 = (s16[144,256]{1,0:T(8,128)(2,1)S(1)}, s16[144,256]{1,0:T(8,128)(2,1)S(1)}, u32[]{:S(2)}, u32[]{:S(2)}) collective-permute-start(s16[144,256]{1,0:T(8,128)(2,1)S(1)} %get-tuple-element.70), channel_id=1, source_target_pairs={{0,8},{1,9},{2,10},{3,11},{4,12},{5,13},{6,14},{7,15},{8,0},{9,1},... | collective-permute-start | bytes 221192 | tf_op jit(solution)/shard_map/ppermute | solution.py:640
  37.1 5.7 %collective-permute-start.11 = (s16[144,256]{1,0:T(8,128)(2,1)S(1)}, s16[144,256]{1,0:T(8,128)(2,1)S(1)}, u32[]{:S(2)}, u32[]{:S(2)}) collective-permute-start(s16[144,256]{1,0:T(8,128)(2,1)S(1)} %get-tuple-element.72), channel_id=1, source_target_pairs={{0,4},{1,5},{2,6},{3,7},{4,0},{5,1},{6,2},{7,3},{8,12},{9,13},{10,... | collective-permute-start | bytes 221192 | tf_op jit(solution)/shard_map/ppermute | solution.py:640
  50.8 8.4 %collective-permute-start.15 = (bf16[2,256,128]{2,1,0:T(8,128)(2,1)S(1)}, bf16[2,256,128]{2,1,0:T(8,128)(2,1)S(1)}, u32[]{:S(2)}, u32[]{:S(2)}) collective-permute-start(bf16[2,256,128]{2,1,0:T(8,128)(2,1)S(1)} %join_first.2.refs_1_), channel_id=1, source_target_pairs={{0,2},{1,3},{2,0},{3,1},{4,6},{5,7},{6,4},{7,5},{8,10},{9,11},{10,... | collective-permute-start | bytes 393224 | tf_op jit(solution)/shard_map/ppermute | solution.py:636
  52.4 5.2 %collective-permute-start.12 = (bf16[256,128]{1,0:T(8,128)(2,1)S(1)}, bf16[256,128]{1,0:T(8,128)(2,1)S(1)}, u32[]{:S(2)}, u32[]{:S(2)}) collective-permute-start(bf16[256,128]{1,0:T(8,128)(2,1)S(1)} %get-tuple-element.73.refs_1_), channel_id=1, source_target_pairs={{0,8},{1,9},{2,10},{3,11},{4,12},{5,13},{6,14},{7,15},{8,0},{9,1},... | collective-permute-start | bytes 196616 | tf_op jit(solution)/shard_map/ppermute | solution.py:640
  53.0 6.2 %collective-permute-start.13 = (bf16[256,128]{1,0:T(8,128)(2,1)S(1)}, bf16[256,128]{1,0:T(8,128)(2,1)S(1)}, u32[]{:S(2)}, u32[]{:S(2)}) collective-permute-start(bf16[256,128]{1,0:T(8,128)(2,1)S(1)} %get-tuple-element.73.refs_1_), channel_id=1, source_target_pairs={{0,12},{1,13},{2,14},{3,15},{4,8},{5,9},{6,10},{7,11},{8,4},{9,5},... | collective-permute-start | bytes 196616 | tf_op jit(solution)/shard_map/ppermute | solution.py:640
  59.2 5.0 %collective-permute-start.16 = (bf16[2,256,128]{2,1,0:T(8,128)(2,1)S(1)}, bf16[2,256,128]{2,1,0:T(8,128)(2,1)S(1)}, u32[]{:S(2)}, u32[]{:S(2)}) collective-permute-start(bf16[2,256,128]{2,1,0:T(8,128)(2,1)S(1)} %join_second.2.after_ref.refs_0_), channel_id=1, source_target_pairs={{0,2},{1,3},{2,0},{3,1},{4,6},{5,7},{6,4},{7,5},{8,10},{9,11},{10,... | collective-permute-start | bytes 393224 | tf_op jit(solution)/shard_map/ppermute | solution.py:636
  59.7 4.8 %collective-permute-start.19 = (bf16[2,256,128]{2,1,0:T(8,128)(2,1)S(1)}, bf16[2,256,128]{2,1,0:T(8,128)(2,1)S(1)}, u32[]{:S(2)}, u32[]{:S(2)}) collective-permute-start(bf16[2,256,128]{2,1,0:T(8,128)(2,1)S(1)} %join_first.2.refs_1_), channel_id=1, source_target_pairs={{0,1},{1,0},{2,3},{3,2},{4,5},{5,4},{6,7},{7,6},{8,9},{9,8},{10,11... | collective-permute-start | bytes 393224 | tf_op jit(solution)/shard_map/ppermute | solution.py:632
  59.7 4.8 %collective-permute-start.18 = (bf16[2,256,128]{2,1,0:T(8,128)(2,1)S(1)}, bf16[2,256,128]{2,1,0:T(8,128)(2,1)S(1)}, u32[]{:S(2)}, u32[]{:S(2)}) collective-permute-start(bf16[2,256,128]{2,1,0:T(8,128)(2,1)S(1)} %join_second.2.after_ref.refs_0_), channel_id=1, source_target_pairs={{0,1},{1,0},{2,3},{3,2},{4,5},{5,4},{6,7},{7,6},{8,9},{9,8},{10,11... | collective-permute-start | bytes 393224 | tf_op jit(solution)/shard_map/ppermute | solution.py:632
  69.4 6.6 %collective-permute-start.24 = (s16[272,256]{1,0:T(8,128)(2,1)S(1)}, s16[272,256]{1,0:T(8,128)(2,1)S(1)}, u32[]{:S(2)}, u32[]{:S(2)}) collective-permute-start(s16[272,256]{1,0:T(8,128)(2,1)S(1)} %get-tuple-element.85), channel_id=1, source_target_pairs={{0,2},{1,3},{2,0},{3,1},{4,6},{5,7},{6,4},{7,5},{8,10},{9,11},{10,... | collective-permute-start | bytes 417800 | tf_op jit(solution)/shard_map/ppermute | solution.py:636
  71.1 7.3 %collective-permute-start.23 = (s16[272,256]{1,0:T(8,128)(2,1)S(1)}, s16[272,256]{1,0:T(8,128)(2,1)S(1)}, u32[]{:S(2)}, u32[]{:S(2)}) collective-permute-start(s16[272,256]{1,0:T(8,128)(2,1)S(1)} %get-tuple-element.84), channel_id=1, source_target_pairs={{0,2},{1,3},{2,0},{3,1},{4,6},{5,7},{6,4},{7,5},{8,10},{9,11},{10,... | collective-permute-start | bytes 417800 | tf_op jit(solution)/shard_map/ppermute | solution.py:636
  78.5 5.2 %collective-permute-start.27 = (s16[144,256]{1,0:T(8,128)(2,1)S(1)}, s16[144,256]{1,0:T(8,128)(2,1)S(1)}, u32[]{:S(2)}, u32[]{:S(2)}) collective-permute-start(s16[144,256]{1,0:T(8,128)(2,1)S(1)} %get-tuple-element.91), channel_id=1, source_target_pairs={{0,4},{1,5},{2,6},{3,7},{4,0},{5,1},{6,2},{7,3},{8,12},{9,13},{10,... | collective-permute-start | bytes 221192 | tf_op jit(solution)/shard_map/ppermute | solution.py:640
  79.6 7.4 %collective-permute-start.25 = (s16[144,256]{1,0:T(8,128)(2,1)S(1)}, s16[144,256]{1,0:T(8,128)(2,1)S(1)}, u32[]{:S(2)}, u32[]{:S(2)}) collective-permute-start(s16[144,256]{1,0:T(8,128)(2,1)S(1)} %get-tuple-element.89), channel_id=1, source_target_pairs={{0,8},{1,9},{2,10},{3,11},{4,12},{5,13},{6,14},{7,15},{8,0},{9,1},... | collective-permute-start | bytes 221192 | tf_op jit(solution)/shard_map/ppermute | solution.py:640
  82.1 6.3 %collective-permute-start.26 = (s16[144,256]{1,0:T(8,128)(2,1)S(1)}, s16[144,256]{1,0:T(8,128)(2,1)S(1)}, u32[]{:S(2)}, u32[]{:S(2)}) collective-permute-start(s16[144,256]{1,0:T(8,128)(2,1)S(1)} %get-tuple-element.90), channel_id=1, source_target_pairs={{0,12},{1,13},{2,14},{3,15},{4,8},{5,9},{6,10},{7,11},{8,4},{9,5},... | collective-permute-start | bytes 221192 | tf_op jit(solution)/shard_map/ppermute | solution.py:640
  96.3 9.0 %collective-permute-start.31 = (bf16[2,256,128]{2,1,0:T(8,128)(2,1)S(1)}, bf16[2,256,128]{2,1,0:T(8,128)(2,1)S(1)}, u32[]{:S(2)}, u32[]{:S(2)}) collective-permute-start(bf16[2,256,128]{2,1,0:T(8,128)(2,1)S(1)} %join_first.3.refs_1_), channel_id=1, source_target_pairs={{0,2},{1,3},{2,0},{3,1},{4,6},{5,7},{6,4},{7,5},{8,10},{9,11},{10,... | collective-permute-start | bytes 393224 | tf_op jit(solution)/shard_map/ppermute | solution.py:636
  97.8 5.9 %collective-permute-start.28 = (bf16[256,128]{1,0:T(8,128)(2,1)S(1)}, bf16[256,128]{1,0:T(8,128)(2,1)S(1)}, u32[]{:S(2)}, u32[]{:S(2)}) collective-permute-start(bf16[256,128]{1,0:T(8,128)(2,1)S(1)} %get-tuple-element.93.refs_1_), channel_id=1, source_target_pairs={{0,8},{1,9},{2,10},{3,11},{4,12},{5,13},{6,14},{7,15},{8,0},{9,1},... | collective-permute-start | bytes 196616 | tf_op jit(solution)/shard_map/ppermute | solution.py:640
  99.2 6.1 %collective-permute-start.29 = (bf16[256,128]{1,0:T(8,128)(2,1)S(1)}, bf16[256,128]{1,0:T(8,128)(2,1)S(1)}, u32[]{:S(2)}, u32[]{:S(2)}) collective-permute-start(bf16[256,128]{1,0:T(8,128)(2,1)S(1)} %get-tuple-element.93.refs_1_), channel_id=1, source_target_pairs={{0,12},{1,13},{2,14},{3,15},{4,8},{5,9},{6,10},{7,11},{8,4},{9,5},... | collective-permute-start | bytes 196616 | tf_op jit(solution)/shard_map/ppermute | solution.py:640
  105.3 5.3 %collective-permute-start.32 = (bf16[2,256,128]{2,1,0:T(8,128)(2,1)S(1)}, bf16[2,256,128]{2,1,0:T(8,128)(2,1)S(1)}, u32[]{:S(2)}, u32[]{:S(2)}) collective-permute-start(bf16[2,256,128]{2,1,0:T(8,128)(2,1)S(1)} %join_second.3.after_ref.refs_0_), channel_id=1, source_target_pairs={{0,2},{1,3},{2,0},{3,1},{4,6},{5,7},{6,4},{7,5},{8,10},{9,11},{10,... | collective-permute-start | bytes 393224 | tf_op jit(solution)/shard_map/ppermute | solution.py:636
  106.3 5.0 %collective-permute-start.35 = (bf16[2,256,128]{2,1,0:T(8,128)(2,1)S(1)}, bf16[2,256,128]{2,1,0:T(8,128)(2,1)S(1)}, u32[]{:S(2)}, u32[]{:S(2)}) collective-permute-start(bf16[2,256,128]{2,1,0:T(8,128)(2,1)S(1)} %join_first.3.refs_1_), channel_id=1, source_target_pairs={{0,1},{1,0},{2,3},{3,2},{4,5},{5,4},{6,7},{7,6},{8,9},{9,8},{10,11... | collective-permute-start | bytes 393224 | tf_op jit(solution)/shard_map/ppermute | solution.py:632
  106.3 5.0 %collective-permute-start.34 = (bf16[2,256,128]{2,1,0:T(8,128)(2,1)S(1)}, bf16[2,256,128]{2,1,0:T(8,128)(2,1)S(1)}, u32[]{:S(2)}, u32[]{:S(2)}) collective-permute-start(bf16[2,256,128]{2,1,0:T(8,128)(2,1)S(1)} %join_second.3.after_ref.refs_0_), channel_id=1, source_target_pairs={{0,1},{1,0},{2,3},{3,2},{4,5},{5,4},{6,7},{7,6},{8,9},{9,8},{10,11... | collective-permute-start | bytes 393224 | tf_op jit(solution)/shard_map/ppermute | solution.py:632
  106.8 4.5 %collective-permute-start.36 = (bf16[2,256,128]{2,1,0:T(8,128)(2,1)S(1)}, bf16[2,256,128]{2,1,0:T(8,128)(2,1)S(1)}, u32[]{:S(2)}, u32[]{:S(2)}) collective-permute-start(bf16[2,256,128]{2,1,0:T(8,128)(2,1)S(1)} %collective-permute-done.31.refs_2_.refs_3_), channel_id=1, source_target_pairs={{0,1},{1,0},{2,3},{3,2},{4,5},{5,4},{6,7},{7,6},{8,9},{9,8},{10,11... | collective-permute-start | bytes 393224 | tf_op jit(solution)/shard_map/ppermute | solution.py:632
  118.3 4.4 %collective-permute-start.39 = (f32[8,256]{1,0:T(8,128)S(1)}, f32[8,256]{1,0:T(8,128)S(1)}, u32[]{:S(2)}, u32[]{:S(2)}) collective-permute-start(f32[8,256]{1,0:T(8,128)S(1)} %add.18.refs_0_), channel_id=1, source_target_pairs={{0,4},{1,5},{2,6},{3,7},{4,0},{5,1},{6,2},{7,3},{8,12},{9,13},{10,... | collective-permute-start | bytes 24584 | tf_op jit(solution)/shard_map/ppermute | solution.py:640
  118.3 4.6 %collective-permute-start.40 = (f32[8,256]{1,0:T(8,128)S(1)}, f32[8,256]{1,0:T(8,128)S(1)}, u32[]{:S(2)}, u32[]{:S(2)}) collective-permute-start(f32[8,256]{1,0:T(8,128)S(1)} %add.18.refs_0_), channel_id=1, source_target_pairs={{0,8},{1,9},{2,10},{3,11},{4,12},{5,13},{6,14},{7,15},{8,0},{9,1},... | collective-permute-start | bytes 24584 | tf_op jit(solution)/shard_map/ppermute | solution.py:640
  120.3 5.4 %collective-permute-start.41 = (f32[8,256]{1,0:T(8,128)S(1)}, f32[8,256]{1,0:T(8,128)S(1)}, u32[]{:S(2)}, u32[]{:S(2)}) collective-permute-start(f32[8,256]{1,0:T(8,128)S(1)} %add.18.refs_0_), channel_id=1, source_target_pairs={{0,12},{1,13},{2,14},{3,15},{4,8},{5,9},{6,10},{7,11},{8,4},{9,5},... | collective-permute-start | bytes 24584 | tf_op jit(solution)/shard_map/ppermute | solution.py:640
  (18 other events, 105.6 us)

commit v10 on v8

--- a/solution.py
+++ b/solution.py
@@ -54,6 +54,7 @@
 
 STEPS = 4
 ORDER = (2, 3, 1, 0)
+LIST_ORDER = (1, 3, 0, 2)
 PARTS = ((0, 0), (1, 0), (0, 1), (1, 1))
 HEAD = 16
 TOP = 32512.0
@@ -75,8 +76,9 @@
     for i in range(GROUP):
         o = owner_at(me_ref, i)
         dy, dc = PARTS[i // STEPS]
-        held = list_refs[ORDER[i % STEPS]]
-        row = jnp.broadcast_to(held[2 * dy + dc : 2 * dy + dc + 1, :], slots.shape)
+        k = ORDER[i % STEPS]
+        row = k % 2 * STEPS + 2 * dy + dc
+        row = jnp.broadcast_to(list_refs[k // 2][row : row + 1, :], slots.shape)
         column = jnp.take_along_axis(row, within, axis=1, mode="promise_in_bounds")
         rows = jnp.where(from_owner == o, column + i * LANES, rows)
     return rows[: slots.shape[0] // 2]
@@ -105,7 +107,7 @@
 
 
 def far_kernel(grouped, me_ref, *refs):
-    list_refs, refs = refs[: 4 * grouped], refs[4 * grouped :]
+    list_refs, refs = refs[: 2 * grouped], refs[2 * grouped :]
     both_ref, wh_ref, wl_ref, *refs = refs
     ids_ref, weight_ref, at_ref, ya_ref, yb_ref, lo_s = refs
     sources = ids_ref.shape[0]
@@ -118,40 +120,50 @@
     build_rows(ids_ref, weight_ref, wh_ref, wl_ref, at_ref, [ya_ref, yb_ref], lo_s, half)
 
 
-def near_kernel(ids_ref, weight_ref, wh_ref, wl_ref, at_ref, ya_ref, yb_ref, lo_s):
-    build_rows(ids_ref, weight_ref, wh_ref, wl_ref, at_ref, [ya_ref, yb_ref], lo_s, 0)
-
-
-def adjoint_half(slots, args, head=None):
+def near_kernel(base, ids_ref, weight_ref, wh_ref, wl_ref, at_ref, y_ref, lo_s):
+    build_rows(ids_ref, weight_ref, wh_ref, wl_ref, at_ref, [y_ref], lo_s, base)
+
+
+def adjoint_far(slots, args, grouped, me, lists):
     fine, width = args[-1].shape
     half = slots // 2
-    sources = args[0].shape[0] // (2 if head else 1)
-    out = [shape((half, fine), BF)] + [shape((half // 2, width), F32)] * 2
-    if head:
-        grouped, me, lists = head
-        kernel = functools.partial(far_kernel, grouped)
-        args = [me, *lists, *args]
-        out = [shape((sources, fine), jnp.int32), shape((sources, fine), F32)] + out
-    else:
-        kernel = near_kernel
-    return pl.pallas_call(
-        kernel,
-        in_specs=([SMEM] if head else []) + [VMEM] * (len(args) - (1 if head else 0)),
+    sources = args[0].shape[0] // 2
+    out = [shape((sources, fine), jnp.int32), shape((sources, fine), F32)]
+    out += [shape((half, fine), BF)] + [shape((half // 2, width), F32)] * 2
+    args = [me, *lists, *args]
+    return pl.pallas_call(
+        functools.partial(far_kernel, grouped),
+        in_specs=[SMEM] + [VMEM] * (len(args) - 1),
         out_specs=[VMEM] * len(out),
         out_shape=out,
         scratch_shapes=[pltpu.VMEM((half // 2, fine), BF)],
         compiler_params=params(16),
         cost_estimate=cost(3 * slots * fine * width, 4e6),
-        name="adjoint_far" if head else "adjoint_near",
+        name="adjoint_far",
+    )(*args)
+
+
+def adjoint_near(slots, args, base):
+    fine, width = args[-1].shape
+    rows = slots // 4
+    return pl.pallas_call(
+        functools.partial(near_kernel, base),
+        in_specs=[VMEM] * len(args),
+        out_specs=[VMEM] * 2,
+        out_shape=[shape((rows, fine), BF), shape((rows, width), F32)],
+        scratch_shapes=[pltpu.VMEM((rows, fine), BF)],
+        compiler_params=params(16),
+        cost_estimate=cost(1.5 * slots * fine * width, 2e6),
+        name="adjoint_near" if base else "adjoint_stay",
     )(*args)
 
 
 def pick_kernel(me_ref, lists_ref, near_ref, far_ref):
     z, y, c = me_ref[0], me_ref[1], me_ref[2]
     for dy in range(2):
-        for k in range(STEPS):
+        for p, k in enumerate(LIST_ORDER):
             there = (jnp.bitwise_xor(z, k) * 2 + (y if dy == 0 else 1 - y)) * 2
-            row = slice(dy * STEPS + k, dy * STEPS + k + 1)
+            row = slice(dy * STEPS + p, dy * STEPS + p + 1)
             near_ref[row, :] = lists_ref[pl.ds(there + c, 1), :]
             far_ref[row, :] = lists_ref[pl.ds(there + 1 - c, 1), :]
 
@@ -163,13 +175,20 @@
         far_y_ref[rows, :] = held[STEPS:, :]
 
 
-def mix_z_kernel(near_ref, got_ref, *outs):
-    for k, out in enumerate(outs):
-        out[...] = jnp.zeros_like(out)
-        for i, held in enumerate((near_ref, got_ref)):
-            for c in range(2):
-                row = c * STEPS + k
-                out[2 * i + c : 2 * i + c + 1, :] = held[row : row + 1, :]
+def mix_z_kernel(near_ref, got_ref, near_z_ref, far_z_ref):
+    for i, held in enumerate((near_ref, got_ref)):
+        for c in range(2):
+            rows = slice(4 * i + 2 * c, 4 * i + 2 * c + 2)
+            far_z_ref[rows, :] = held[c * STEPS : c * STEPS + 2, :]
+            near_z_ref[rows, :] = held[c * STEPS + 2 : c * STEPS + 4, :]
+
+
+def mix_end_kernel(near_ref, got_ref, own_ref, sent_ref):
+    for i, held in enumerate((near_ref, got_ref)):
+        for n in range(STEPS):
+            row = slice(i * STEPS + n, i * STEPS + n + 1)
+            own_ref[row, :] = held[2 * n : 2 * n + 1, :]
+            sent_ref[row, :] = held[2 * n + 1 : 2 * n + 2, :]
 
 
 def small(kernel, n, name, *args, scalars=0):
@@ -187,8 +206,9 @@
 def exchange_lists(me, lists):
     near, far = small(pick_kernel, 2, "pick", me, lists, scalars=1)
     near, far = small(mix_y_kernel, 2, "mix_y", near, over_core(far))
-    own, *sent = small(mix_z_kernel, STEPS, "mix_z", near, over_y(far))
-    return [own] + [over_z(sent[k - 1], k) for k in range(1, STEPS)]
+    near, far = small(mix_z_kernel, 2, "mix_z", near, over_y(far))
+    own, sent = small(mix_end_kernel, 2, "mix_end", near, over_z(far, 1))
+    return [own, over_z(sent, 2)]
 
 
 def exponent(m):
@@ -474,107 +494,114 @@
 
 
 def part_kernel(*refs):
-    *x_refs, near_ref, far_ref, out_ref, xs = refs
+    *x_refs, stay_ref, near_ref, far_ref, out_ref, xs = refs
     lay_out(x_refs, xs)
-    half, fine = near_ref.shape
+    half, fine = far_ref.shape
+    split = half // 2
     rows = fine // CUTS
     for i in range(CUTS):
         some = pl.ds(i * rows, rows)
-        out_ref[:, some] = dot(xs[:, :half], near_ref[:, some]) + dot(
-            xs[:, half:], far_ref[pl.ds(0, xs.shape[1] - half), some]
+        out_ref[:, some] = (
+            dot(xs[:, :split], stay_ref[:, some])
+            + dot(xs[:, split:half], near_ref[:, some])
+            + dot(xs[:, half:], far_ref[pl.ds(0, xs.shape[1] - half), some])
         )
 
 
-def image_part(xs, near, far, width):
-    half, fine = near.shape
+def image_part(xs, stay, near, far, width):
+    half, fine = far.shape
     return pl.pallas_call(
         part_kernel,
-        in_specs=[VMEM] * (len(xs) + 2),
+        in_specs=[VMEM] * (len(xs) + 3),
         out_specs=VMEM,
         out_shape=shape((width, fine), F32),
         scratch_shapes=[pltpu.VMEM((width, len(xs) * STEPS * LANES), BF)],
         compiler_params=params(16),
         cost_estimate=cost(3 * half * fine * width, 4e6),
         name="image_part",
-    )(*xs, near, far)
-
-
-def images(x_ref, part_ref, near_ref, far_ref, obs_ref, im_ref, xs):
+    )(*xs, stay, near, far)
+
+
+def images(x_ref, refs, far_ref, obs_ref, im_ref, xs):
     lay_out([x_ref], xs)
-    half, fine = near_ref.shape
+    half, fine = far_ref.shape
+    split = half // 2
     rows = fine // CUTS
     for i in range(CUTS):
         some = pl.ds(i * rows, rows)
-        if part_ref is None:
-            turned = dot(xs[:, :half], near_ref[:, some]) + dot(xs[:, half:], far_ref[:, some])
+        if len(refs) > 1:
+            turned = (
+                dot(xs[:, :split], refs[0][:, some])
+                + dot(xs[:, split:half], refs[1][:, some])
+                + dot(xs[:, half:], far_ref[:, some])
+            )
         else:
             last = xs.shape[1]
-            turned = dot(xs[...], far_ref[pl.ds(half - last, last), some]) + part_ref[:, some]
+            turned = dot(xs[...], far_ref[pl.ds(half - last, last), some]) + refs[0][:, some]
         im = turned.T
         im_ref[some, :] = im
         yield some, im, obs_ref[some, :].astype(F32) * im
 
 
 def image_kernel(parts, first, x_ref, *refs):
-    part_ref, refs = (refs[0], refs[1:]) if parts else (None, refs)
-    near_ref, far_ref, obs_ref, g_ref, im_ref, sum_ref, *refs = refs
+    part_refs, refs = refs[:parts], refs[parts:]
+    far_ref, obs_ref, g_ref, im_ref, sum_ref, *refs = refs
     if first:
         v_ref, *outs, xs = refs
     else:
         (xs,) = refs
     sums = g_ref[...]
     row = lax.broadcasted_iota(jnp.int32, sums.shape, 0)
-    for some, im, v in images(x_ref, part_ref, near_ref, far_ref, obs_ref, im_ref, xs):
+    for some, im, v in images(x_ref, part_refs, far_ref, obs_ref, im_ref, xs):
         if first:
             v_ref[some, :] = v.astype(BF)
         sums = sums + jnp.where(row == 1, fold(v * im), 0.0)
     sum_ref[...] = sums
     if first:
-        rows = near_ref.shape[0] // 2
+        rows = far_ref.shape[0] // 2
         for i in (1, 0):
             outs[i][pl.ds(0, rows), :] = dot(far_ref[pl.ds(i * rows, rows), :], v_ref[...])
         outs[1][pl.ds(rows, 8), :] = sums
 
 
-def image_of(xs, near, far, obs, g_sums, first):
-    half, fine = near.shape
+def image_of(xs, stay, near, far, obs, g_sums, first):
+    half, fine = far.shape
     width = obs.shape[1]
-    part = [image_part(xs[:-1], near, far, width)] if len(xs) > 1 else []
+    whole = len(xs) == 1
+    part = [stay, near] if whole else [image_part(xs[:-1], stay, near, far, width)]
     out = [shape((fine, width), F32), shape((8, width), F32)]
     if first:
         out += [shape((fine, width), BF)]
         out += [shape((half // 2, width), F32), shape((half // 2 + 8, width), F32)]
-    last = STEPS * LANES if part else 2 * half
-    return pl.pallas_call(
-        functools.partial(image_kernel, bool(part), first),
-        in_specs=[VMEM] * (5 + len(part)),
+    last = 2 * half if whole else STEPS * LANES
+    return pl.pallas_call(
+        functools.partial(image_kernel, len(part), first),
+        in_specs=[VMEM] * (4 + len(part)),
         out_specs=[VMEM] * len(out),
         out_shape=out,
         scratch_shapes=[pltpu.VMEM((width, last), BF)],
         compiler_params=params(16),
         cost_estimate=cost(3 * half * fine * width, 8e6),
         name="image_first" if first else "image_second",
-    )(xs[-1], *part, near, far, obs, g_sums)
-
-
-def back_kernel(near_ref, v_ref, *outs):
-    rows = near_ref.shape[0] // 2
-    for i, out in enumerate(outs):
-        out[...] = dot(near_ref[pl.ds(i * rows, rows), :], v_ref[...])
-
-
-def back_near(near, v):
-    half, fine = near.shape
+    )(xs[-1], *part, far, obs, g_sums)
+
+
+def back_kernel(at_ref, v_ref, out_ref):
+    out_ref[...] = dot(at_ref[...], v_ref[...])
+
+
+def back(at, v, name):
+    rows, fine = at.shape
     width = v.shape[1]
     return pl.pallas_call(
         back_kernel,
         in_specs=[VMEM] * 2,
-        out_specs=[VMEM] * 2,
-        out_shape=[shape((half // 2, width), F32)] * 2,
+        out_specs=VMEM,
+        out_shape=shape((rows, width), F32),
         compiler_params=params(16),
-        cost_estimate=cost(2 * half * fine * width, 4e6),
-        name="back_near",
-    )(near, v)
+        cost_estimate=cost(2 * rows * fine * width, 2e6),
+        name=name,
+    )(at, v)
 
 
 OUT_CUTS = 4
@@ -713,17 +740,21 @@
         def add_up(x):
             return [lax.psum(x, "space")]
 
-    ids, weight, far, c0, c1 = adjoint_half(slots, [named, wh, wl], (grouped, me, lists if grouped else []))
-    near, n0, n1 = adjoint_half(slots, [ids, weight, wh, wl])
+    ids, weight, far, c0, c1 = adjoint_far(
+        slots, [named, wh, wl], grouped, me, lists if grouped else []
+    )
+    near, n1 = adjoint_near(slots, [ids, weight, wh, wl], slots // 4)
+    stay, n0 = adjoint_near(slots, [ids, weight, wh, wl], 0)
     own, got, _ = scatter([n0, n1, c0, c1])
     ens = jnp.transpose(ensemble, (1, 0, 2))
     x0, y0, g_sums = coarse_image(ensemble, kern, own, got, after=[ens])
     xs, g0 = gather(x0, lambda after: project(ens, y0, taps, after))
-    im0, sums, v, c0, c1 = image_of(xs, near, far, obs_weight, g_sums, True)
-    own, got, sums = scatter([*back_near(near, v), c0, c1], sums)
+    im0, sums, v, c0, c1 = image_of(xs, stay, near, far, obs_weight, g_sums, True)
+    n1, n0 = back(near, v, "back_near"), back(stay, v, "back_stay")
+    own, got, sums = scatter([n0, n1, c0, c1], sums)
     x1, y1, l0, g_sums = coarse_image(ensemble, kern, own, got, y0, sums)
     xs, g1 = gather(x1, lambda after: project(ens, y1, taps, after))
-    im1, sums = image_of(xs, near, far, obs_weight, g_sums, False)
+    im1, sums = image_of(xs, stay, near, far, obs_weight, g_sums, False)
     return tuple(result(l0, add_up(sums), g0, g1, im0, im1))
 
 

time: 121 us -> 116 us (0.959)
  waiting for transfers between devices: 45.2 us -> 36.1 us
  starting transfers between devices: 36.2 us -> 39 us
    ppermute x8, waiting for transfers between devices: 17.5 us -> 12.8 us  [over_y(): return lax.ppermute(x, 'space', [(i, i ^ 2) for i in range(GROUP)])]
    ppermute x18 -> x17, waiting for transfers between devices: 25.3 us -> 20.6 us  [over_z(): return lax.ppermute(x, 'space', [(i, i ^ 4 * k) for i in range(GROUP)])]
    ppermute x18 -> x17, starting transfers between devices: 22.3 us -> 24.9 us  [over_z(): return lax.ppermute(x, 'space', [(i, i ^ 4 * k) for i in range(GROUP)])]
    pallas_call x7 -> x9, Pallas kernels: 15.1 us -> 15.4 us  [the longest x1 5.17 us: adjoint_far(): pl.pallas_call(functools.partial(far_kernel, grouped), in_specs=[SMEM] +...]
  transfers between devices with their start and end apart: 36 -> 35, of which waited for: 25 -> 24; matrix products, arithmetic and copies ran while one was open for 4% -> 4% of each run, Pallas kernels for 13% -> 14%
where the time goes in v10:
time: 116 us
  starting transfers between devices  39 us (34%)
  waiting for transfers between devices  36.1 us (31%)
  Pallas kernels  33.9 us (29%)
  local copies, waits for them, and re-layouts  3.88 us (3%)
  other arithmetic  1.62 us (1%)
    ppermute x17, starting transfers between devices, over_z(): return lax.ppermute(x, 'space', [(i, i ^ 4 * k) for i in range(GROUP)])  24.9 us
    ppermute x17, waiting for transfers between devices, over_z(): return lax.ppermute(x, 'space', [(i, i ^ 4 * k) for i in range(GROUP)])  20.6 us
    ppermute x8, waiting for transfers between devices, over_y(): return lax.ppermute(x, 'space', [(i, i ^ 2) for i in range(GROUP)])  12.8 us
    ppermute x8, starting transfers between devices, over_y(): return lax.ppermute(x, 'space', [(i, i ^ 2) for i in range(GROUP)])  11.8 us
    pallas_call x2, Pallas kernels, project(): pl.pallas_call(project_kernel, in_specs=[VMEM] * 4, out_specs=[VMEM] * 2,...  7.56 us
    pallas_call x2, Pallas kernels, coarse_image(): pl.pallas_call(functools.partial(coarse_kernel, len(got), second, len(aft...  7.44 us
    pallas_call x1, Pallas kernels, adjoint_far(): pl.pallas_call(functools.partial(far_kernel, grouped), in_specs=[SMEM] +...  5.17 us
    pallas_call x2, Pallas kernels, adjoint_near(): pl.pallas_call(functools.partial(near_kernel, base), in_specs=[VMEM] * le...  4.37 us
  transfers between devices with their start and end apart: 35, of which 24 were waited for; matrix products, arithmetic and copies ran while one was open for 4% of the time, Pallas kernels for 14%

profile of v10, /device:TPU:0, one launch (start us, length us, event | category | flops | bytes accessed | tf_op | source)
XLA Modules:
  0.0 115.6 jit_solution(13684043907661065707)
XLA Ops:
  3.4 2.9 %collective-permute-start.1 = (s32[8,128]{1,0:T(8,128)S(1)}, s32[8,128]{1,0:T(8,128)S(1)}, u32[]{:S(2)}, u32[]{:S(2)}) collective-permute-start(s32[8,128]{1,0:T(8,128)S(1)} %get-tuple-element.54), channel_id=1, source_target_pairs={{0,2},{1,3},{2,0},{3,1},{4,6},{5,7},{6,4},{7,5},{8,10},{9,11},{10,... | collective-permute-start | bytes 12296 | tf_op jit(solution)/shard_map/ppermute | solution.py:659
  6.2 1.6 %collective-permute-done.1.got_ref = s32[8,128]{1,0:T(8,128)S(1)} collective-permute-done((s32[8,128]{1,0:T(8,128)S(1)}, s32[8,128]{1,0:T(8,128)S(1)}, u32[]{:S(2)}, u32[]{:S(2)}) %collective-permute-start.1) | collective-permute-done | bytes 4128 | tf_op jit(solution)/shard_map/ppermute | solution.py:659
  7.8 2.1 %collective-permute-start.2 = (s32[8,128]{1,0:T(8,128)S(1)}, s32[8,128]{1,0:T(8,128)S(1)}, u32[]{:S(2)}, u32[]{:S(2)}) collective-permute-start(s32[8,128]{1,0:T(8,128)S(1)} %get-tuple-element.56), channel_id=1, source_target_pairs={{0,4},{1,5},{2,6},{3,7},{4,0},{5,1},{6,2},{7,3},{8,12},{9,13},{10,... | collective-permute-start | bytes 12296 | tf_op jit(solution)/shard_map/ppermute | solution.py:663
  11.6 3.0 %collective-permute-start.3 = (s32[8,128]{1,0:T(8,128)S(1)}, s32[8,128]{1,0:T(8,128)S(1)}, u32[]{:S(2)}, u32[]{:S(2)}) collective-permute-start(s32[8,128]{1,0:T(8,128)S(1)} %get-tuple-element.58), channel_id=1, source_target_pairs={{0,8},{1,9},{2,10},{3,11},{4,12},{5,13},{6,14},{7,15},{8,0},{9,1},... | collective-permute-start | bytes 12296 | tf_op jit(solution)/shard_map/ppermute | solution.py:663
  16.2 5.2 %adjoint_far.1 = (s32[4,1152]{1,0:T(4,128)S(1)}, f32[4,1152]{1,0:T(4,128)S(1)}, bf16[1024,1152]{1,0:T(8,128)(2,1)S(1)}, f32[512,256]{1,0:T(8,128)S(1)}, f32[512,256]{1,0:T(8,128)S(1)}) custom-call(s32[4]{0:T(128)S(1)} %pad_add_fusion.me_ref, s32[8,128]{1,0:T(8,128)S(1)} %get-tuple-element.57.refs_0_, s32[8,128]{1,0:T(8,128)S(1)} %collective-permute-done.3.refs_1_, ...), custom_call_target="tpu_custom_call" | custom-call | flops 1811939328 | bytes 4000000 | tf_op jit(solution)/shard_map/adjoint_far/pallas_call | solution.py:134
  21.9 2.2 %adjoint_near.1 = (bf16[512,1152]{1,0:T(8,128)(2,1)S(1)}, f32[512,256]{1,0:T(8,128)S(1)}) custom-call(s32[4,1152]{1,0:T(4,128)S(1)} %get-tuple-element.59.ids_ref, f32[4,1152]{1,0:T(4,128)S(1)} %get-tuple-element.60.weight_ref, bf16[1152,256]{1,0:T(8,128)(2,1)S(1)} %get-tuple-element.101.refs_3_.wh_ref, bf16[1152,256]{1,0:T(8,128)(2,1)S(1)} %get-tuple-element.100.refs_4_.wl_ref), custom_call_target="tpu_custom_call" | custom-call | flops 905969664 | bytes 2000000 | tf_op jit(solution)/shard_map/adjoint_near/pallas_call | solution.py:149
  24.3 1.9 %collective-permute-start.7 = (s16[272,256]{1,0:T(8,128)(2,1)S(1)}, s16[272,256]{1,0:T(8,128)(2,1)S(1)}, u32[]{:S(2)}, u32[]{:S(2)}) collective-permute-start(s16[272,256]{1,0:T(8,128)(2,1)S(1)} %get-tuple-element.68), channel_id=1, source_target_pairs={{0,2},{1,3},{2,0},{3,1},{4,6},{5,7},{6,4},{7,5},{8,10},{9,11},{10,... | collective-permute-start | bytes 417800 | tf_op jit(solution)/shard_map/ppermute | solution.py:659
  26.4 2.2 %adjoint_stay.1 = (bf16[512,1152]{1,0:T(8,128)(2,1)S(1)}, f32[512,256]{1,0:T(8,128)S(1)}) custom-call(s32[4,1152]{1,0:T(4,128)S(1)} %get-tuple-element.59.ids_ref, f32[4,1152]{1,0:T(4,128)S(1)} %get-tuple-element.60.weight_ref, bf16[1152,256]{1,0:T(8,128)(2,1)S(1)} %get-tuple-element.101.refs_3_.wh_ref, bf16[1152,256]{1,0:T(8,128)(2,1)S(1)} %get-tuple-element.100.refs_4_.wl_ref), custom_call_target="tpu_custom_call" | custom-call | flops 905969664 | bytes 2000000 | tf_op jit(solution)/shard_map/adjoint_stay/pallas_call | solution.py:149
  28.6 2.3 %collective-permute-done.7.p_ref = s16[272,256]{1,0:T(8,128)(2,1)S(1)} collective-permute-done((s16[272,256]{1,0:T(8,128)(2,1)S(1)}, s16[272,256]{1,0:T(8,128)(2,1)S(1)}, u32[]{:S(2)}, u32[]{:S(2)}) %collective-permute-start.7) | collective-permute-done | bytes 139296 | tf_op jit(solution)/shard_map/ppermute | solution.py:659
  31.0 3.0 %collective-permute-start.8 = (s16[144,256]{1,0:T(8,128)(2,1)S(1)}, s16[144,256]{1,0:T(8,128)(2,1)S(1)}, u32[]{:S(2)}, u32[]{:S(2)}) collective-permute-start(s16[144,256]{1,0:T(8,128)(2,1)S(1)} %get-tuple-element.69), channel_id=1, source_target_pairs={{0,8},{1,9},{2,10},{3,11},{4,12},{5,13},{6,14},{7,15},{8,0},{9,1},... | collective-permute-start | bytes 221192 | tf_op jit(solution)/shard_map/ppermute | solution.py:663
  35.8 3.1 %copy.12 = bf16[80,128,256]{2,0,1:T(8,128)(2,1)S(1)} copy(bf16[80,128,256]{2,1,0:T(8,128)(2,1)S(1)} %bitcast.12) | data formatting | bytes 10485760 | tf_op args[0]
  40.7 3.7 %coarse_first.1 = (bf16[256,128]{1,0:T(8,128)(2,1)S(1)}, f32[128,256]{1,0:T(8,128)S(1)}, f32[8,256]{1,0:T(8,128)S(1)}) custom-call(bf16[80,128,256]{2,1,0:T(8,128)(2,1)S(1)} %bitcast.12, bf16[256,256]{1,0:T(8,128)(2,1)S(1)} %copy-done.1, f32[128,256]{1,0:T(8,128)S(1)} %get-tuple-element.67.own_ref, s16[144,256]{1,0:T(8,128)(2,1)S(1)} %collective-permute-done.8.refs_0_, ...), custom_call_target="tpu_custom_call" | custom-call | flops 1342177280 | bytes 5000000 | tf_op jit(solution)/shard_map/coarse_first/pallas_call | solution.py:434
  44.6 2.8 %collective-permute-start.12 = (bf16[256,128]{1,0:T(8,128)(2,1)S(1)}, bf16[256,128]{1,0:T(8,128)(2,1)S(1)}, u32[]{:S(2)}, u32[]{:S(2)}) collective-permute-start(bf16[256,128]{1,0:T(8,128)(2,1)S(1)} %get-tuple-element.72.refs_3_), channel_id=1, source_target_pairs={{0,12},{1,13},{2,14},{3,15},{4,8},{5,9},{6,10},{7,11},{8,4},{9,5},... | collective-permute-start | bytes 196616 | tf_op jit(solution)/shard_map/ppermute | solution.py:663
  49.0 1.8 %collective-permute-done.12.refs_1_ = bf16[256,128]{1,0:T(8,128)(2,1)S(1)} collective-permute-done((bf16[256,128]{1,0:T(8,128)(2,1)S(1)}, bf16[256,128]{1,0:T(8,128)(2,1)S(1)}, u32[]{:S(2)}, u32[]{:S(2)}) %collective-permute-start.12) | collective-permute-done | bytes 65568 | tf_op jit(solution)/shard_map/ppermute | solution.py:663
  50.7 2.3 %collective-permute-done.11.refs_0_ = bf16[256,128]{1,0:T(8,128)(2,1)S(1)} collective-permute-done((bf16[256,128]{1,0:T(8,128)(2,1)S(1)}, bf16[256,128]{1,0:T(8,128)(2,1)S(1)}, u32[]{:S(2)}, u32[]{:S(2)}) %collective-permute-start.11) | collective-permute-done | bytes 65568 | tf_op jit(solution)/shard_map/ppermute | solution.py:663
  53.1 1.6 %collective-permute-start.14 = (bf16[4,256,128]{2,1,0:T(8,128)(2,1)S(1)}, bf16[4,256,128]{2,1,0:T(8,128)(2,1)S(1)}, u32[]{:S(2)}, u32[]{:S(2)}) collective-permute-start(bf16[4,256,128]{2,1,0:T(8,128)(2,1)S(1)} %join.2.after_ref.refs_0_), channel_id=1, source_target_pairs={{0,2},{1,3},{2,0},{3,1},{4,6},{5,7},{6,4},{7,5},{8,10},{9,11},{10,... | collective-permute-start | bytes 786440 | tf_op jit(solution)/shard_map/ppermute | solution.py:659
  54.7 3.7 %project.2 = (f32[80,8192]{1,0:T(8,128)S(1)}, f32[8,128]{1,0:T(8,128)S(1)}) custom-call(bf16[128,80,256]{2,1,0:T(8,128)(2,1)S(1)} %bitcast.9, f32[128,256]{1,0:T(8,128)S(1)} %get-tuple-element.73.y_ref.refs_3_, bf16[2,256,128]{2,1,0:T(8,128)(2,1)S(1)} %copy-done.2, bf16[4,256,128]{2,1,0:T(8,128)(2,1)S(1)} %join.2.after_ref.refs_0_), custom_call_target="tpu_custom_call" | custom-call | flops 1342177280 | bytes 8000000 | tf_op jit(solution)/shard_map/project/pallas_call | solution.py:472
  64.6 1.6 %collective-permute-start.20 = (s16[272,256]{1,0:T(8,128)(2,1)S(1)}, s16[272,256]{1,0:T(8,128)(2,1)S(1)}, u32[]{:S(2)}, u32[]{:S(2)}) collective-permute-start(s16[272,256]{1,0:T(8,128)(2,1)S(1)} %get-tuple-element.83), channel_id=1, source_target_pairs={{0,2},{1,3},{2,0},{3,1},{4,6},{5,7},{6,4},{7,5},{8,10},{9,11},{10,... | collective-permute-start | bytes 417800 | tf_op jit(solution)/shard_map/ppermute | solution.py:659
  67.3 3.9 %collective-permute-done.20.p_ref = s16[272,256]{1,0:T(8,128)(2,1)S(1)} collective-permute-done((s16[272,256]{1,0:T(8,128)(2,1)S(1)}, s16[272,256]{1,0:T(8,128)(2,1)S(1)}, u32[]{:S(2)}, u32[]{:S(2)}) %collective-permute-start.20) | collective-permute-done | bytes 139296 | tf_op jit(solution)/shard_map/ppermute | solution.py:659
  71.7 2.0 %collective-permute-start.22 = (s16[144,256]{1,0:T(8,128)(2,1)S(1)}, s16[144,256]{1,0:T(8,128)(2,1)S(1)}, u32[]{:S(2)}, u32[]{:S(2)}) collective-permute-start(s16[144,256]{1,0:T(8,128)(2,1)S(1)} %get-tuple-element.88), channel_id=1, source_target_pairs={{0,12},{1,13},{2,14},{3,15},{4,8},{5,9},{6,10},{7,11},{8,4},{9,5},... | collective-permute-start | bytes 221192 | tf_op jit(solution)/shard_map/ppermute | solution.py:663
  75.0 3.7 %collective-permute-done.21.refs_0_ = s16[144,256]{1,0:T(8,128)(2,1)S(1)} collective-permute-done((s16[144,256]{1,0:T(8,128)(2,1)S(1)}, s16[144,256]{1,0:T(8,128)(2,1)S(1)}, u32[]{:S(2)}, u32[]{:S(2)}) %collective-permute-start.21) | collective-permute-done | bytes 73760 | tf_op jit(solution)/shard_map/ppermute | solution.py:663
  79.3 3.8 %coarse_second.1 = (bf16[256,128]{1,0:T(8,128)(2,1)S(1)}, f32[128,256]{1,0:T(8,128)S(1)}, f32[8,128]{1,0:T(8,128)S(1)}, f32[8,256]{1,0:T(8,128)S(1)}) custom-call(bf16[80,128,256]{2,1,0:T(8,128)(2,1)S(1)} %bitcast.12, bf16[256,256]{1,0:T(8,128)(2,1)S(1)} %copy-done.1, f32[128,256]{1,0:T(8,128)S(1)} %get-tuple-element.86.own_ref, ...), custom_call_target="tpu_custom_call" | custom-call | flops 1342177280 | bytes 5000000 | tf_op jit(solution)/shard_map/coarse_second/pallas_call | solution.py:434
  84.0 1.8 %collective-permute-start.25 = (bf16[256,128]{1,0:T(8,128)(2,1)S(1)}, bf16[256,128]{1,0:T(8,128)(2,1)S(1)}, u32[]{:S(2)}, u32[]{:S(2)}) collective-permute-start(bf16[256,128]{1,0:T(8,128)(2,1)S(1)} %get-tuple-element.91.refs_3_), channel_id=1, source_target_pairs={{0,12},{1,13},{2,14},{3,15},{4,8},{5,9},{6,10},{7,11},{8,4},{9,5},... | collective-permute-start | bytes 196616 | tf_op jit(solution)/shard_map/ppermute | solution.py:663
  87.7 2.3 %collective-permute-done.25.refs_1_ = bf16[256,128]{1,0:T(8,128)(2,1)S(1)} collective-permute-done((bf16[256,128]{1,0:T(8,128)(2,1)S(1)}, bf16[256,128]{1,0:T(8,128)(2,1)S(1)}, u32[]{:S(2)}, u32[]{:S(2)}) %collective-permute-start.25) | collective-permute-done | bytes 65568 | tf_op jit(solution)/shard_map/ppermute | solution.py:663
  90.1 2.2 %collective-permute-done.24.refs_0_ = bf16[256,128]{1,0:T(8,128)(2,1)S(1)} collective-permute-done((bf16[256,128]{1,0:T(8,128)(2,1)S(1)}, bf16[256,128]{1,0:T(8,128)(2,1)S(1)}, u32[]{:S(2)}, u32[]{:S(2)}) %collective-permute-start.24) | collective-permute-done | bytes 65568 | tf_op jit(solution)/shard_map/ppermute | solution.py:663
  92.3 1.6 %collective-permute-start.27 = (bf16[4,256,128]{2,1,0:T(8,128)(2,1)S(1)}, bf16[4,256,128]{2,1,0:T(8,128)(2,1)S(1)}, u32[]{:S(2)}, u32[]{:S(2)}) collective-permute-start(bf16[4,256,128]{2,1,0:T(8,128)(2,1)S(1)} %join.3.after_ref.refs_0_), channel_id=1, source_target_pairs={{0,2},{1,3},{2,0},{3,1},{4,6},{5,7},{6,4},{7,5},{8,10},{9,11},{10,... | collective-permute-start | bytes 786440 | tf_op jit(solution)/shard_map/ppermute | solution.py:659
  93.9 3.9 %project.3 = (f32[80,8192]{1,0:T(8,128)S(1)}, f32[8,128]{1,0:T(8,128)S(1)}) custom-call(bf16[128,80,256]{2,1,0:T(8,128)(2,1)S(1)} %bitcast.10, f32[128,256]{1,0:T(8,128)S(1)} %get-tuple-element.92.y_ref, bf16[2,256,128]{2,1,0:T(8,128)(2,1)S(1)} %copy-done.2, bf16[4,256,128]{2,1,0:T(8,128)(2,1)S(1)} %join.3.after_ref.refs_0_), custom_call_target="tpu_custom_call" | custom-call | flops 1342177280 | bytes 8000000 | tf_op jit(solution)/shard_map/project/pallas_call | solution.py:472
  97.8 1.7 %collective-permute-done.27.x_ref = bf16[4,256,128]{2,1,0:T(8,128)(2,1)S(1)} collective-permute-done((bf16[4,256,128]{2,1,0:T(8,128)(2,1)S(1)}, bf16[4,256,128]{2,1,0:T(8,128)(2,1)S(1)}, u32[]{:S(2)}, u32[]{:S(2)}) %collective-permute-start.27) | collective-permute-done | bytes 262176 | tf_op jit(solution)/shard_map/ppermute | solution.py:659
  104.7 2.1 %collective-permute-done.31 = f32[8,256]{1,0:T(8,128)S(1)} collective-permute-done((f32[8,256]{1,0:T(8,128)S(1)}, f32[8,256]{1,0:T(8,128)S(1)}, u32[]{:S(2)}, u32[]{:S(2)}) %collective-permute-start.31) | collective-permute-done | bytes 8224 | tf_op jit(solution)/shard_map/ppermute | solution.py:659
  106.8 1.9 %collective-permute-start.34 = (f32[8,256]{1,0:T(8,128)S(1)}, f32[8,256]{1,0:T(8,128)S(1)}, u32[]{:S(2)}, u32[]{:S(2)}) collective-permute-start(f32[8,256]{1,0:T(8,128)S(1)} %add.18.refs_0_), channel_id=1, source_target_pairs={{0,12},{1,13},{2,14},{3,15},{4,8},{5,9},{6,10},{7,11},{8,4},{9,5},... | collective-permute-start | bytes 24584 | tf_op jit(solution)/shard_map/ppermute | solution.py:663
  108.7 2.5 %collective-permute-start.32 = (f32[8,256]{1,0:T(8,128)S(1)}, f32[8,256]{1,0:T(8,128)S(1)}, u32[]{:S(2)}, u32[]{:S(2)}) collective-permute-start(f32[8,256]{1,0:T(8,128)S(1)} %add.18.refs_0_), channel_id=1, source_target_pairs={{0,4},{1,5},{2,6},{3,7},{4,0},{5,1},{6,2},{7,3},{8,12},{9,13},{10,... | collective-permute-start | bytes 24584 | tf_op jit(solution)/shard_map/ppermute | solution.py:663
  113.3 2.2 %result.1 = (f32[80,8192]{1,0:T(8,128)}, f32[1152,256]{1,0:T(8,128)}) custom-call(f32[8,128]{1,0:T(8,128)S(1)} %get-tuple-element.90.l0_ref, f32[8,256]{1,0:T(8,128)S(1)} %add.18.refs_0_, f32[8,256]{1,0:T(8,128)S(1)} %collective-permute-done.32.refs_1_, f32[8,256]{1,0:T(8,128)S(1)} %collective-permute-done.33.refs_2_, ...), custom_call_target="tpu_custom_call" | custom-call | flops 1966080 | bytes 10000000 | tf_op jit(solution)/shard_map/result/pallas_call | solution.py:638
  (90 shorter events, 31.8 us)
Async XLA Ops:
  3.4 4.4 %collective-permute-start.1 = (s32[8,128]{1,0:T(8,128)S(1)}, s32[8,128]{1,0:T(8,128)S(1)}, u32[]{:S(2)}, u32[]{:S(2)}) collective-permute-start(s32[8,128]{1,0:T(8,128)S(1)} %get-tuple-element.54), channel_id=1, source_target_pairs={{0,2},{1,3},{2,0},{3,1},{4,6},{5,7},{6,4},{7,5},{8,10},{9,11},{10,... | collective-permute-start | bytes 12296 | tf_op jit(solution)/shard_map/ppermute | solution.py:659
  7.8 3.7 %collective-permute-start.2 = (s32[8,128]{1,0:T(8,128)S(1)}, s32[8,128]{1,0:T(8,128)S(1)}, u32[]{:S(2)}, u32[]{:S(2)}) collective-permute-start(s32[8,128]{1,0:T(8,128)S(1)} %get-tuple-element.56), channel_id=1, source_target_pairs={{0,4},{1,5},{2,6},{3,7},{4,0},{5,1},{6,2},{7,3},{8,12},{9,13},{10,... | collective-permute-start | bytes 12296 | tf_op jit(solution)/shard_map/ppermute | solution.py:663
  11.6 4.6 %collective-permute-start.3 = (s32[8,128]{1,0:T(8,128)S(1)}, s32[8,128]{1,0:T(8,128)S(1)}, u32[]{:S(2)}, u32[]{:S(2)}) collective-permute-start(s32[8,128]{1,0:T(8,128)S(1)} %get-tuple-element.58), channel_id=1, source_target_pairs={{0,8},{1,9},{2,10},{3,11},{4,12},{5,13},{6,14},{7,15},{8,0},{9,1},... | collective-permute-start | bytes 12296 | tf_op jit(solution)/shard_map/ppermute | solution.py:663
  21.4 2.8 %collective-permute-start.5 = (f32[512,256]{1,0:T(8,128)S(1)}, f32[512,256]{1,0:T(8,128)S(1)}, u32[]{:S(2)}, u32[]{:S(2)}) collective-permute-start(f32[512,256]{1,0:T(8,128)S(1)} %get-tuple-element.65), channel_id=1, source_target_pairs={{0,1},{1,0},{2,3},{3,2},{4,5},{5,4},{6,7},{7,6},{8,9},{9,8},{10,11... | collective-permute-start | bytes 1572872 | tf_op jit(solution)/shard_map/ppermute | solution.py:655
  21.4 7.1 %collective-permute-start.4 = (f32[512,256]{1,0:T(8,128)S(1)}, f32[512,256]{1,0:T(8,128)S(1)}, u32[]{:S(2)}, u32[]{:S(2)}) collective-permute-start(f32[512,256]{1,0:T(8,128)S(1)} %get-tuple-element.63), channel_id=1, source_target_pairs={{0,1},{1,0},{2,3},{3,2},{4,5},{5,4},{6,7},{7,6},{8,9},{9,8},{10,11... | collective-permute-start | bytes 1572872 | tf_op jit(solution)/shard_map/ppermute | solution.py:655
  24.3 6.6 %collective-permute-start.7 = (s16[272,256]{1,0:T(8,128)(2,1)S(1)}, s16[272,256]{1,0:T(8,128)(2,1)S(1)}, u32[]{:S(2)}, u32[]{:S(2)}) collective-permute-start(s16[272,256]{1,0:T(8,128)(2,1)S(1)} %get-tuple-element.68), channel_id=1, source_target_pairs={{0,2},{1,3},{2,0},{3,1},{4,6},{5,7},{6,4},{7,5},{8,10},{9,11},{10,... | collective-permute-start | bytes 417800 | tf_op jit(solution)/shard_map/ppermute | solution.py:659
  26.2 9.1 %collective-permute-start.6 = (s16[272,256]{1,0:T(8,128)(2,1)S(1)}, s16[272,256]{1,0:T(8,128)(2,1)S(1)}, u32[]{:S(2)}, u32[]{:S(2)}) collective-permute-start(s16[272,256]{1,0:T(8,128)(2,1)S(1)} %get-tuple-element.66), channel_id=1, source_target_pairs={{0,2},{1,3},{2,0},{3,1},{4,6},{5,7},{6,4},{7,5},{8,10},{9,11},{10,... | collective-permute-start | bytes 417800 | tf_op jit(solution)/shard_map/ppermute | solution.py:659
  31.0 7.9 %collective-permute-start.8 = (s16[144,256]{1,0:T(8,128)(2,1)S(1)}, s16[144,256]{1,0:T(8,128)(2,1)S(1)}, u32[]{:S(2)}, u32[]{:S(2)}) collective-permute-start(s16[144,256]{1,0:T(8,128)(2,1)S(1)} %get-tuple-element.69), channel_id=1, source_target_pairs={{0,8},{1,9},{2,10},{3,11},{4,12},{5,13},{6,14},{7,15},{8,0},{9,1},... | collective-permute-start | bytes 221192 | tf_op jit(solution)/shard_map/ppermute | solution.py:663
  34.0 6.3 %collective-permute-start.9 = (s16[144,256]{1,0:T(8,128)(2,1)S(1)}, s16[144,256]{1,0:T(8,128)(2,1)S(1)}, u32[]{:S(2)}, u32[]{:S(2)}) collective-permute-start(s16[144,256]{1,0:T(8,128)(2,1)S(1)} %get-tuple-element.70), channel_id=1, source_target_pairs={{0,12},{1,13},{2,14},{3,15},{4,8},{5,9},{6,10},{7,11},{8,4},{9,5},... | collective-permute-start | bytes 221192 | tf_op jit(solution)/shard_map/ppermute | solution.py:663
  35.5 5.2 %collective-permute-start.10 = (s16[144,256]{1,0:T(8,128)(2,1)S(1)}, s16[144,256]{1,0:T(8,128)(2,1)S(1)}, u32[]{:S(2)}, u32[]{:S(2)}) collective-permute-start(s16[144,256]{1,0:T(8,128)(2,1)S(1)} %get-tuple-element.71), channel_id=1, source_target_pairs={{0,4},{1,5},{2,6},{3,7},{4,0},{5,1},{6,2},{7,3},{8,12},{9,13},{10,... | collective-permute-start | bytes 221192 | tf_op jit(solution)/shard_map/ppermute | solution.py:663
  44.3 4.6 %collective-permute-start.13 = (bf16[256,128]{1,0:T(8,128)(2,1)S(1)}, bf16[256,128]{1,0:T(8,128)(2,1)S(1)}, u32[]{:S(2)}, u32[]{:S(2)}) collective-permute-start(bf16[256,128]{1,0:T(8,128)(2,1)S(1)} %get-tuple-element.72.refs_3_), channel_id=1, source_target_pairs={{0,4},{1,5},{2,6},{3,7},{4,0},{5,1},{6,2},{7,3},{8,12},{9,13},{10,... | collective-permute-start | bytes 196616 | tf_op jit(solution)/shard_map/ppermute | solution.py:663
  44.6 6.2 %collective-permute-start.12 = (bf16[256,128]{1,0:T(8,128)(2,1)S(1)}, bf16[256,128]{1,0:T(8,128)(2,1)S(1)}, u32[]{:S(2)}, u32[]{:S(2)}) collective-permute-start(bf16[256,128]{1,0:T(8,128)(2,1)S(1)} %get-tuple-element.72.refs_3_), channel_id=1, source_target_pairs={{0,12},{1,13},{2,14},{3,15},{4,8},{5,9},{6,10},{7,11},{8,4},{9,5},... | collective-permute-start | bytes 196616 | tf_op jit(solution)/shard_map/ppermute | solution.py:663
  47.4 5.7 %collective-permute-start.11 = (bf16[256,128]{1,0:T(8,128)(2,1)S(1)}, bf16[256,128]{1,0:T(8,128)(2,1)S(1)}, u32[]{:S(2)}, u32[]{:S(2)}) collective-permute-start(bf16[256,128]{1,0:T(8,128)(2,1)S(1)} %get-tuple-element.72.refs_3_), channel_id=1, source_target_pairs={{0,8},{1,9},{2,10},{3,11},{4,12},{5,13},{6,14},{7,15},{8,0},{9,1},... | collective-permute-start | bytes 196616 | tf_op jit(solution)/shard_map/ppermute | solution.py:663
  53.1 6.4 %collective-permute-start.14 = (bf16[4,256,128]{2,1,0:T(8,128)(2,1)S(1)}, bf16[4,256,128]{2,1,0:T(8,128)(2,1)S(1)}, u32[]{:S(2)}, u32[]{:S(2)}) collective-permute-start(bf16[4,256,128]{2,1,0:T(8,128)(2,1)S(1)} %join.2.after_ref.refs_0_), channel_id=1, source_target_pairs={{0,2},{1,3},{2,0},{3,1},{4,6},{5,7},{6,4},{7,5},{8,10},{9,11},{10,... | collective-permute-start | bytes 786440 | tf_op jit(solution)/shard_map/ppermute | solution.py:659
  54.7 5.0 %collective-permute-start.16 = (bf16[4,256,128]{2,1,0:T(8,128)(2,1)S(1)}, bf16[4,256,128]{2,1,0:T(8,128)(2,1)S(1)}, u32[]{:S(2)}, u32[]{:S(2)}) collective-permute-start(bf16[4,256,128]{2,1,0:T(8,128)(2,1)S(1)} %join.2.after_ref.refs_0_), channel_id=1, source_target_pairs={{0,1},{1,0},{2,3},{3,2},{4,5},{5,4},{6,7},{7,6},{8,9},{9,8},{10,11... | collective-permute-start | bytes 786440 | tf_op jit(solution)/shard_map/ppermute | solution.py:655
  59.6 1.6 %collective-permute-start.15 = (bf16[4,256,128]{2,1,0:T(8,128)(2,1)S(1)}, bf16[4,256,128]{2,1,0:T(8,128)(2,1)S(1)}, u32[]{:S(2)}, u32[]{:S(2)}) collective-permute-start(bf16[4,256,128]{2,1,0:T(8,128)(2,1)S(1)} %relay.2.refs_1_), channel_id=1, source_target_pairs={{0,1},{1,0},{2,3},{3,2},{4,5},{5,4},{6,7},{7,6},{8,9},{9,8},{10,11... | collective-permute-start | bytes 786440 | tf_op jit(solution)/shard_map/ppermute | solution.py:655
  62.5 2.0 %collective-permute-start.18 = (f32[520,256]{1,0:T(8,128)S(1)}, f32[520,256]{1,0:T(8,128)S(1)}, u32[]{:S(2)}, u32[]{:S(2)}) collective-permute-start(f32[520,256]{1,0:T(8,128)S(1)} %get-tuple-element.80), channel_id=1, source_target_pairs={{0,1},{1,0},{2,3},{3,2},{4,5},{5,4},{6,7},{7,6},{8,9},{9,8},{10,11... | collective-permute-start | bytes 1597448 | tf_op jit(solution)/shard_map/ppermute | solution.py:655
  62.9 4.3 %collective-permute-start.17 = (f32[512,256]{1,0:T(8,128)S(1)}, f32[512,256]{1,0:T(8,128)S(1)}, u32[]{:S(2)}, u32[]{:S(2)}) collective-permute-start(f32[512,256]{1,0:T(8,128)S(1)} %get-tuple-element.79), channel_id=1, source_target_pairs={{0,1},{1,0},{2,3},{3,2},{4,5},{5,4},{6,7},{7,6},{8,9},{9,8},{10,11... | collective-permute-start | bytes 1572872 | tf_op jit(solution)/shard_map/ppermute | solution.py:655
  64.6 6.6 %collective-permute-start.20 = (s16[272,256]{1,0:T(8,128)(2,1)S(1)}, s16[272,256]{1,0:T(8,128)(2,1)S(1)}, u32[]{:S(2)}, u32[]{:S(2)}) collective-permute-start(s16[272,256]{1,0:T(8,128)(2,1)S(1)} %get-tuple-element.83), channel_id=1, source_target_pairs={{0,2},{1,3},{2,0},{3,1},{4,6},{5,7},{6,4},{7,5},{8,10},{9,11},{10,... | collective-permute-start | bytes 417800 | tf_op jit(solution)/shard_map/ppermute | solution.py:659
  66.2 7.4 %collective-permute-start.19 = (s16[272,256]{1,0:T(8,128)(2,1)S(1)}, s16[272,256]{1,0:T(8,128)(2,1)S(1)}, u32[]{:S(2)}, u32[]{:S(2)}) collective-permute-start(s16[272,256]{1,0:T(8,128)(2,1)S(1)} %get-tuple-element.82), channel_id=1, source_target_pairs={{0,2},{1,3},{2,0},{3,1},{4,6},{5,7},{6,4},{7,5},{8,10},{9,11},{10,... | collective-permute-start | bytes 417800 | tf_op jit(solution)/shard_map/ppermute | solution.py:659
  71.3 7.5 %collective-permute-start.21 = (s16[144,256]{1,0:T(8,128)(2,1)S(1)}, s16[144,256]{1,0:T(8,128)(2,1)S(1)}, u32[]{:S(2)}, u32[]{:S(2)}) collective-permute-start(s16[144,256]{1,0:T(8,128)(2,1)S(1)} %get-tuple-element.87), channel_id=1, source_target_pairs={{0,8},{1,9},{2,10},{3,11},{4,12},{5,13},{6,14},{7,15},{8,0},{9,1},... | collective-permute-start | bytes 221192 | tf_op jit(solution)/shard_map/ppermute | solution.py:663
  71.7 7.1 %collective-permute-start.22 = (s16[144,256]{1,0:T(8,128)(2,1)S(1)}, s16[144,256]{1,0:T(8,128)(2,1)S(1)}, u32[]{:S(2)}, u32[]{:S(2)}) collective-permute-start(s16[144,256]{1,0:T(8,128)(2,1)S(1)} %get-tuple-element.88), channel_id=1, source_target_pairs={{0,12},{1,13},{2,14},{3,15},{4,8},{5,9},{6,10},{7,11},{8,4},{9,5},... | collective-permute-start | bytes 221192 | tf_op jit(solution)/shard_map/ppermute | solution.py:663
  73.8 5.5 %collective-permute-start.23 = (s16[144,256]{1,0:T(8,128)(2,1)S(1)}, s16[144,256]{1,0:T(8,128)(2,1)S(1)}, u32[]{:S(2)}, u32[]{:S(2)}) collective-permute-start(s16[144,256]{1,0:T(8,128)(2,1)S(1)} %get-tuple-element.89), channel_id=1, source_target_pairs={{0,4},{1,5},{2,6},{3,7},{4,0},{5,1},{6,2},{7,3},{8,12},{9,13},{10,... | collective-permute-start | bytes 221192 | tf_op jit(solution)/shard_map/ppermute | solution.py:663
  83.1 4.7 %collective-permute-start.26 = (bf16[256,128]{1,0:T(8,128)(2,1)S(1)}, bf16[256,128]{1,0:T(8,128)(2,1)S(1)}, u32[]{:S(2)}, u32[]{:S(2)}) collective-permute-start(bf16[256,128]{1,0:T(8,128)(2,1)S(1)} %get-tuple-element.91.refs_3_), channel_id=1, source_target_pairs={{0,4},{1,5},{2,6},{3,7},{4,0},{5,1},{6,2},{7,3},{8,12},{9,13},{10,... | collective-permute-start | bytes 196616 | tf_op jit(solution)/shard_map/ppermute | solution.py:663
  84.0 6.1 %collective-permute-start.25 = (bf16[256,128]{1,0:T(8,128)(2,1)S(1)}, bf16[256,128]{1,0:T(8,128)(2,1)S(1)}, u32[]{:S(2)}, u32[]{:S(2)}) collective-permute-start(bf16[256,128]{1,0:T(8,128)(2,1)S(1)} %get-tuple-element.91.refs_3_), channel_id=1, source_target_pairs={{0,12},{1,13},{2,14},{3,15},{4,8},{5,9},{6,10},{7,11},{8,4},{9,5},... | collective-permute-start | bytes 196616 | tf_op jit(solution)/shard_map/ppermute | solution.py:663
  85.8 6.5 %collective-permute-start.24 = (bf16[256,128]{1,0:T(8,128)(2,1)S(1)}, bf16[256,128]{1,0:T(8,128)(2,1)S(1)}, u32[]{:S(2)}, u32[]{:S(2)}) collective-permute-start(bf16[256,128]{1,0:T(8,128)(2,1)S(1)} %get-tuple-element.91.refs_3_), channel_id=1, source_target_pairs={{0,8},{1,9},{2,10},{3,11},{4,12},{5,13},{6,14},{7,15},{8,0},{9,1},... | collective-permute-start | bytes 196616 | tf_op jit(solution)/shard_map/ppermute | solution.py:663
  92.3 7.2 %collective-permute-start.27 = (bf16[4,256,128]{2,1,0:T(8,128)(2,1)S(1)}, bf16[4,256,128]{2,1,0:T(8,128)(2,1)S(1)}, u32[]{:S(2)}, u32[]{:S(2)}) collective-permute-start(bf16[4,256,128]{2,1,0:T(8,128)(2,1)S(1)} %join.3.after_ref.refs_0_), channel_id=1, source_target_pairs={{0,2},{1,3},{2,0},{3,1},{4,6},{5,7},{6,4},{7,5},{8,10},{9,11},{10,... | collective-permute-start | bytes 786440 | tf_op jit(solution)/shard_map/ppermute | solution.py:659
  93.9 5.7 %collective-permute-start.29 = (bf16[4,256,128]{2,1,0:T(8,128)(2,1)S(1)}, bf16[4,256,128]{2,1,0:T(8,128)(2,1)S(1)}, u32[]{:S(2)}, u32[]{:S(2)}) collective-permute-start(bf16[4,256,128]{2,1,0:T(8,128)(2,1)S(1)} %join.3.after_ref.refs_0_), channel_id=1, source_target_pairs={{0,1},{1,0},{2,3},{3,2},{4,5},{5,4},{6,7},{7,6},{8,9},{9,8},{10,11... | collective-permute-start | bytes 786440 | tf_op jit(solution)/shard_map/ppermute | solution.py:655
  103.1 3.7 %collective-permute-start.31 = (f32[8,256]{1,0:T(8,128)S(1)}, f32[8,256]{1,0:T(8,128)S(1)}, u32[]{:S(2)}, u32[]{:S(2)}) collective-permute-start(f32[8,256]{1,0:T(8,128)S(1)} %add.17), channel_id=1, source_target_pairs={{0,2},{1,3},{2,0},{3,1},{4,6},{5,7},{6,4},{7,5},{8,10},{9,11},{10,... | collective-permute-start | bytes 24584 | tf_op jit(solution)/shard_map/ppermute | solution.py:659
  106.8 5.4 %collective-permute-start.34 = (f32[8,256]{1,0:T(8,128)S(1)}, f32[8,256]{1,0:T(8,128)S(1)}, u32[]{:S(2)}, u32[]{:S(2)}) collective-permute-start(f32[8,256]{1,0:T(8,128)S(1)} %add.18.refs_0_), channel_id=1, source_target_pairs={{0,12},{1,13},{2,14},{3,15},{4,8},{5,9},{6,10},{7,11},{8,4},{9,5},... | collective-permute-start | bytes 24584 | tf_op jit(solution)/shard_map/ppermute | solution.py:663
  108.7 4.5 %collective-permute-start.33 = (f32[8,256]{1,0:T(8,128)S(1)}, f32[8,256]{1,0:T(8,128)S(1)}, u32[]{:S(2)}, u32[]{:S(2)}) collective-permute-start(f32[8,256]{1,0:T(8,128)S(1)} %add.18.refs_0_), channel_id=1, source_target_pairs={{0,8},{1,9},{2,10},{3,11},{4,12},{5,13},{6,14},{7,15},{8,0},{9,1},... | collective-permute-start | bytes 24584 | tf_op jit(solution)/shard_map/ppermute | solution.py:663
  108.7 4.5 %collective-permute-start.32 = (f32[8,256]{1,0:T(8,128)S(1)}, f32[8,256]{1,0:T(8,128)S(1)}, u32[]{:S(2)}, u32[]{:S(2)}) collective-permute-start(f32[8,256]{1,0:T(8,128)S(1)} %add.18.refs_0_), channel_id=1, source_target_pairs={{0,4},{1,5},{2,6},{3,7},{4,0},{5,1},{6,2},{7,3},{8,12},{9,13},{10,... | collective-permute-start | bytes 24584 | tf_op jit(solution)/shard_map/ppermute | solution.py:663
  (11 other events, 69.5 us)

commit v11 on v10

--- a/solution.py
+++ b/solution.py
@@ -109,15 +109,15 @@
 def far_kernel(grouped, me_ref, *refs):
     list_refs, refs = refs[: 2 * grouped], refs[2 * grouped :]
     both_ref, wh_ref, wl_ref, *refs = refs
-    ids_ref, weight_ref, at_ref, ya_ref, yb_ref, lo_s = refs
+    ids_ref, weight_ref, at_ref, y_ref, lo_s = refs
     sources = ids_ref.shape[0]
     for j in range(ids_ref.shape[1] // LANES):
         lanes = pl.ds(j * LANES, LANES)
         slots = both_ref[:sources, lanes].astype(jnp.int32)
         ids_ref[:, lanes] = places(me_ref, list_refs, slots) if grouped else slots
         weight_ref[:, lanes] = both_ref[sources:, lanes]
-    half = at_ref.shape[0]
-    build_rows(ids_ref, weight_ref, wh_ref, wl_ref, at_ref, [ya_ref, yb_ref], lo_s, half)
+    base = 3 * at_ref.shape[0]
+    build_rows(ids_ref, weight_ref, wh_ref, wl_ref, at_ref, [y_ref], lo_s, base)
 
 
 def near_kernel(base, ids_ref, weight_ref, wh_ref, wl_ref, at_ref, y_ref, lo_s):
@@ -126,19 +126,19 @@
 
 def adjoint_far(slots, args, grouped, me, lists):
     fine, width = args[-1].shape
-    half = slots // 2
+    rows = slots // 4
     sources = args[0].shape[0] // 2
     out = [shape((sources, fine), jnp.int32), shape((sources, fine), F32)]
-    out += [shape((half, fine), BF)] + [shape((half // 2, width), F32)] * 2
+    out += [shape((rows, fine), BF), shape((rows, width), F32)]
     args = [me, *lists, *args]
     return pl.pallas_call(
         functools.partial(far_kernel, grouped),
         in_specs=[SMEM] + [VMEM] * (len(args) - 1),
         out_specs=[VMEM] * len(out),
         out_shape=out,
-        scratch_shapes=[pltpu.VMEM((half // 2, fine), BF)],
+        scratch_shapes=[pltpu.VMEM((rows, fine), BF)],
         compiler_params=params(16),
-        cost_estimate=cost(3 * slots * fine * width, 4e6),
+        cost_estimate=cost(1.5 * slots * fine * width, 2e6),
         name="adjoint_far",
     )(*args)
 
@@ -154,7 +154,7 @@
         scratch_shapes=[pltpu.VMEM((rows, fine), BF)],
         compiler_params=params(16),
         cost_estimate=cost(1.5 * slots * fine * width, 2e6),
-        name="adjoint_near" if base else "adjoint_stay",
+        name=("adjoint_stay", "adjoint_near", "adjoint_side")[base // rows],
     )(*args)
 
 
@@ -494,50 +494,45 @@
 
 
 def part_kernel(*refs):
-    *x_refs, stay_ref, near_ref, far_ref, out_ref, xs = refs
+    *x_refs, a_ref, b_ref, c_ref, out_ref, xs = refs
     lay_out(x_refs, xs)
-    half, fine = far_ref.shape
-    split = half // 2
+    quarter, fine = a_ref.shape
     rows = fine // CUTS
     for i in range(CUTS):
         some = pl.ds(i * rows, rows)
-        out_ref[:, some] = (
-            dot(xs[:, :split], stay_ref[:, some])
-            + dot(xs[:, split:half], near_ref[:, some])
-            + dot(xs[:, half:], far_ref[pl.ds(0, xs.shape[1] - half), some])
-        )
-
-
-def image_part(xs, stay, near, far, width):
-    half, fine = far.shape
+        total = None
+        for n, m in enumerate((a_ref, b_ref, c_ref)):
+            term = dot(xs[:, n * quarter : (n + 1) * quarter], m[:, some])
+            total = term if total is None else total + term
+        out_ref[:, some] = total
+
+
+def image_part(xs, quarters, width):
+    quarter, fine = quarters[0].shape
     return pl.pallas_call(
         part_kernel,
-        in_specs=[VMEM] * (len(xs) + 3),
+        in_specs=[VMEM] * 6,
         out_specs=VMEM,
         out_shape=shape((width, fine), F32),
-        scratch_shapes=[pltpu.VMEM((width, len(xs) * STEPS * LANES), BF)],
+        scratch_shapes=[pltpu.VMEM((width, 3 * quarter), BF)],
         compiler_params=params(16),
-        cost_estimate=cost(3 * half * fine * width, 4e6),
+        cost_estimate=cost(6 * quarter * fine * width, 4e6),
         name="image_part",
-    )(*xs, stay, near, far)
-
-
-def images(x_ref, refs, far_ref, obs_ref, im_ref, xs):
+    )(*xs, *quarters)
+
+
+def images(x_ref, refs, last_ref, obs_ref, im_ref, xs):
     lay_out([x_ref], xs)
-    half, fine = far_ref.shape
-    split = half // 2
+    quarter, fine = last_ref.shape
     rows = fine // CUTS
     for i in range(CUTS):
         some = pl.ds(i * rows, rows)
         if len(refs) > 1:
-            turned = (
-                dot(xs[:, :split], refs[0][:, some])
-                + dot(xs[:, split:half], refs[1][:, some])
-                + dot(xs[:, half:], far_ref[:, some])
-            )
+            turned = dot(xs[:, 3 * quarter :], last_ref[:, some])
+            for n, m in enumerate(refs):
+                turned = turned + dot(xs[:, n * quarter : (n + 1) * quarter], m[:, some])
         else:
-            last = xs.shape[1]
-            turned = dot(xs[...], far_ref[pl.ds(half - last, last), some]) + refs[0][:, some]
+            turned = dot(xs[...], last_ref[:, some]) + refs[0][:, some]
         im = turned.T
         im_ref[some, :] = im
         yield some, im, obs_ref[some, :].astype(F32) * im
@@ -547,7 +542,7 @@
     part_refs, refs = refs[:parts], refs[parts:]
     far_ref, obs_ref, g_ref, im_ref, sum_ref, *refs = refs
     if first:
-        v_ref, *outs, xs = refs
+        v_ref, out_ref, xs = refs
     else:
         (xs,) = refs
     sums = g_ref[...]
@@ -558,22 +553,21 @@
         sums = sums + jnp.where(row == 1, fold(v * im), 0.0)
     sum_ref[...] = sums
     if first:
-        rows = far_ref.shape[0] // 2
-        for i in (1, 0):
-            outs[i][pl.ds(0, rows), :] = dot(far_ref[pl.ds(i * rows, rows), :], v_ref[...])
-        outs[1][pl.ds(rows, 8), :] = sums
-
-
-def image_of(xs, stay, near, far, obs, g_sums, first):
-    half, fine = far.shape
+        rows = far_ref.shape[0]
+        out_ref[pl.ds(0, rows), :] = dot(far_ref[...], v_ref[...])
+        out_ref[pl.ds(rows, 8), :] = sums
+
+
+def image_of(xs, quarters, far, obs, g_sums, first):
+    quarter, fine = far.shape
     width = obs.shape[1]
     whole = len(xs) == 1
-    part = [stay, near] if whole else [image_part(xs[:-1], stay, near, far, width)]
+    part = quarters if whole else [image_part(xs[:-1], quarters, width)]
     out = [shape((fine, width), F32), shape((8, width), F32)]
     if first:
         out += [shape((fine, width), BF)]
-        out += [shape((half // 2, width), F32), shape((half // 2 + 8, width), F32)]
-    last = 2 * half if whole else STEPS * LANES
+        out += [shape((quarter + 8, width), F32)]
+    last = 4 * quarter if whole else quarter
     return pl.pallas_call(
         functools.partial(image_kernel, len(part), first),
         in_specs=[VMEM] * (4 + len(part)),
@@ -581,7 +575,7 @@
         out_shape=out,
         scratch_shapes=[pltpu.VMEM((width, last), BF)],
         compiler_params=params(16),
-        cost_estimate=cost(3 * half * fine * width, 8e6),
+        cost_estimate=cost(4 * quarter * fine * width, 6e6),
         name="image_first" if first else "image_second",
     )(xs[-1], *part, far, obs, g_sums)
 
@@ -740,21 +734,25 @@
         def add_up(x):
             return [lax.psum(x, "space")]
 
-    ids, weight, far, c0, c1 = adjoint_far(
+    ids, weight, far, c1 = adjoint_far(
         slots, [named, wh, wl], grouped, me, lists if grouped else []
     )
-    near, n1 = adjoint_near(slots, [ids, weight, wh, wl], slots // 4)
-    stay, n0 = adjoint_near(slots, [ids, weight, wh, wl], 0)
+    built = [ids, weight, wh, wl]
+    near, n1 = adjoint_near(slots, built, slots // 4)
+    side, c0 = adjoint_near(slots, built, slots // 2)
+    stay, n0 = adjoint_near(slots, built, 0)
+    quarters = [stay, near, side]
     own, got, _ = scatter([n0, n1, c0, c1])
     ens = jnp.transpose(ensemble, (1, 0, 2))
     x0, y0, g_sums = coarse_image(ensemble, kern, own, got, after=[ens])
     xs, g0 = gather(x0, lambda after: project(ens, y0, taps, after))
-    im0, sums, v, c0, c1 = image_of(xs, stay, near, far, obs_weight, g_sums, True)
+    im0, sums, v, c1 = image_of(xs, quarters, far, obs_weight, g_sums, True)
+    c0 = back(side, v, "back_side")
     n1, n0 = back(near, v, "back_near"), back(stay, v, "back_stay")
     own, got, sums = scatter([n0, n1, c0, c1], sums)
     x1, y1, l0, g_sums = coarse_image(ensemble, kern, own, got, y0, sums)
     xs, g1 = gather(x1, lambda after: project(ens, y1, taps, after))
-    im1, sums = image_of(xs, stay, near, far, obs_weight, g_sums, False)
+    im1, sums = image_of(xs, quarters, far, obs_weight, g_sums, False)
     return tuple(result(l0, add_up(sums), g0, g1, im0, im1))
 
 

time: 116 us -> 115 us (level)
    pallas_call x1, Pallas kernels: 5.17 us -> 2.9 us  [adjoint_far(): pl.pallas_call(functools.partial(far_kernel, grouped), in_specs=[SMEM] +...]
    pallas_call x2 -> x3, Pallas kernels: 4.37 us -> 6.58 us  [adjoint_near(): pl.pallas_call(functools.partial(near_kernel, base), in_specs=[VMEM] * le...]
  transfers between devices with their start and end apart: 35 -> 35, of which waited for: 24 -> 24; matrix products, arithmetic and copies ran while one was open for 4% -> 4% of each run, Pallas kernels for 14% -> 17%
where the time goes in v11:
time: 115 us
  starting transfers between devices  39.1 us (34%)
  waiting for transfers between devices  35.7 us (31%)
  Pallas kernels  33.5 us (29%)
  local copies, waits for them, and re-layouts  3.88 us (3%)
  other arithmetic  1.62 us (1%)
  between operations  1.17 us (1%)
    ppermute x17, starting transfers between devices, over_z(): return lax.ppermute(x, 'space', [(i, i ^ 4 * k) for i in range(GROUP)])  24.9 us
    ppermute x17, waiting for transfers between devices, over_z(): return lax.ppermute(x, 'space', [(i, i ^ 4 * k) for i in range(GROUP)])  20.6 us
    ppermute x8, waiting for transfers between devices, over_y(): return lax.ppermute(x, 'space', [(i, i ^ 2) for i in range(GROUP)])  12.9 us
    ppermute x8, starting transfers between devices, over_y(): return lax.ppermute(x, 'space', [(i, i ^ 2) for i in range(GROUP)])  11.8 us
    pallas_call x2, Pallas kernels, project(): pl.pallas_call(project_kernel, in_specs=[VMEM] * 4, out_specs=[VMEM] * 2,...  7.47 us
    pallas_call x2, Pallas kernels, coarse_image(): pl.pallas_call(functools.partial(coarse_kernel, len(got), second, len(aft...  7.02 us
    pallas_call x3, Pallas kernels, adjoint_near(): pl.pallas_call(functools.partial(near_kernel, base), in_specs=[VMEM] * le...  6.58 us
    unnamed x17, local copies, waits for them, and re-layouts  3.88 us
  transfers between devices with their start and end apart: 35, of which 24 were waited for; matrix products, arithmetic and copies ran while one was open for 4% of the time, Pallas kernels for 17%

profile of v11, /device:TPU:0, one launch (start us, length us, event | category | flops | bytes accessed | tf_op | source)
XLA Modules:
  0.0 115.0 jit_solution(10766523808308687183)
XLA Ops:
  3.4 2.9 %collective-permute-start.1 = (s32[8,128]{1,0:T(8,128)S(1)}, s32[8,128]{1,0:T(8,128)S(1)}, u32[]{:S(2)}, u32[]{:S(2)}) collective-permute-start(s32[8,128]{1,0:T(8,128)S(1)} %get-tuple-element.54), channel_id=1, source_target_pairs={{0,2},{1,3},{2,0},{3,1},{4,6},{5,7},{6,4},{7,5},{8,10},{9,11},{10,... | collective-permute-start | bytes 12296 | tf_op jit(solution)/shard_map/ppermute | solution.py:653
  7.8 2.1 %collective-permute-start.2 = (s32[8,128]{1,0:T(8,128)S(1)}, s32[8,128]{1,0:T(8,128)S(1)}, u32[]{:S(2)}, u32[]{:S(2)}) collective-permute-start(s32[8,128]{1,0:T(8,128)S(1)} %get-tuple-element.56), channel_id=1, source_target_pairs={{0,4},{1,5},{2,6},{3,7},{4,0},{5,1},{6,2},{7,3},{8,12},{9,13},{10,... | collective-permute-start | bytes 12296 | tf_op jit(solution)/shard_map/ppermute | solution.py:657
  11.6 3.0 %collective-permute-start.3 = (s32[8,128]{1,0:T(8,128)S(1)}, s32[8,128]{1,0:T(8,128)S(1)}, u32[]{:S(2)}, u32[]{:S(2)}) collective-permute-start(s32[8,128]{1,0:T(8,128)S(1)} %get-tuple-element.58), channel_id=1, source_target_pairs={{0,8},{1,9},{2,10},{3,11},{4,12},{5,13},{6,14},{7,15},{8,0},{9,1},... | collective-permute-start | bytes 12296 | tf_op jit(solution)/shard_map/ppermute | solution.py:657
  16.2 2.9 %adjoint_far.1 = (s32[4,1152]{1,0:T(4,128)S(1)}, f32[4,1152]{1,0:T(4,128)S(1)}, bf16[512,1152]{1,0:T(8,128)(2,1)S(1)}, f32[512,256]{1,0:T(8,128)S(1)}) custom-call(s32[4]{0:T(128)S(1)} %pad_add_fusion.me_ref, s32[8,128]{1,0:T(8,128)S(1)} %get-tuple-element.57.refs_0_, s32[8,128]{1,0:T(8,128)S(1)} %collective-permute-done.3.refs_1_, ...), custom_call_target="tpu_custom_call" | custom-call | flops 905969664 | bytes 2000000 | tf_op jit(solution)/shard_map/adjoint_far/pallas_call | solution.py:134
  19.2 2.2 %adjoint_side.1 = (bf16[512,1152]{1,0:T(8,128)(2,1)S(1)}, f32[512,256]{1,0:T(8,128)S(1)}) custom-call(s32[4,1152]{1,0:T(4,128)S(1)} %get-tuple-element.59.ids_ref, f32[4,1152]{1,0:T(4,128)S(1)} %get-tuple-element.60.weight_ref, bf16[1152,256]{1,0:T(8,128)(2,1)S(1)} %get-tuple-element.101.refs_3_.wh_ref, bf16[1152,256]{1,0:T(8,128)(2,1)S(1)} %get-tuple-element.100.refs_4_.wl_ref), custom_call_target="tpu_custom_call" | custom-call | flops 905969664 | bytes 2000000 | tf_op jit(solution)/shard_map/adjoint_side/pallas_call | solution.py:149
  22.0 2.2 %adjoint_near.1 = (bf16[512,1152]{1,0:T(8,128)(2,1)S(1)}, f32[512,256]{1,0:T(8,128)S(1)}) custom-call(s32[4,1152]{1,0:T(4,128)S(1)} %get-tuple-element.59.ids_ref, f32[4,1152]{1,0:T(4,128)S(1)} %get-tuple-element.60.weight_ref, bf16[1152,256]{1,0:T(8,128)(2,1)S(1)} %get-tuple-element.101.refs_3_.wh_ref, bf16[1152,256]{1,0:T(8,128)(2,1)S(1)} %get-tuple-element.100.refs_4_.wl_ref), custom_call_target="tpu_custom_call" | custom-call | flops 905969664 | bytes 2000000 | tf_op jit(solution)/shard_map/adjoint_near/pallas_call | solution.py:149
  24.3 1.9 %collective-permute-start.7 = (s16[272,256]{1,0:T(8,128)(2,1)S(1)}, s16[272,256]{1,0:T(8,128)(2,1)S(1)}, u32[]{:S(2)}, u32[]{:S(2)}) collective-permute-start(s16[272,256]{1,0:T(8,128)(2,1)S(1)} %get-tuple-element.68), channel_id=1, source_target_pairs={{0,2},{1,3},{2,0},{3,1},{4,6},{5,7},{6,4},{7,5},{8,10},{9,11},{10,... | collective-permute-start | bytes 417800 | tf_op jit(solution)/shard_map/ppermute | solution.py:653
  26.4 2.2 %adjoint_stay.1 = (bf16[512,1152]{1,0:T(8,128)(2,1)S(1)}, f32[512,256]{1,0:T(8,128)S(1)}) custom-call(s32[4,1152]{1,0:T(4,128)S(1)} %get-tuple-element.59.ids_ref, f32[4,1152]{1,0:T(4,128)S(1)} %get-tuple-element.60.weight_ref, bf16[1152,256]{1,0:T(8,128)(2,1)S(1)} %get-tuple-element.101.refs_3_.wh_ref, bf16[1152,256]{1,0:T(8,128)(2,1)S(1)} %get-tuple-element.100.refs_4_.wl_ref), custom_call_target="tpu_custom_call" | custom-call | flops 905969664 | bytes 2000000 | tf_op jit(solution)/shard_map/adjoint_stay/pallas_call | solution.py:149
  28.6 2.3 %collective-permute-done.7.p_ref = s16[272,256]{1,0:T(8,128)(2,1)S(1)} collective-permute-done((s16[272,256]{1,0:T(8,128)(2,1)S(1)}, s16[272,256]{1,0:T(8,128)(2,1)S(1)}, u32[]{:S(2)}, u32[]{:S(2)}) %collective-permute-start.7) | collective-permute-done | bytes 139296 | tf_op jit(solution)/shard_map/ppermute | solution.py:653
  31.0 3.0 %collective-permute-start.8 = (s16[144,256]{1,0:T(8,128)(2,1)S(1)}, s16[144,256]{1,0:T(8,128)(2,1)S(1)}, u32[]{:S(2)}, u32[]{:S(2)}) collective-permute-start(s16[144,256]{1,0:T(8,128)(2,1)S(1)} %get-tuple-element.69), channel_id=1, source_target_pairs={{0,8},{1,9},{2,10},{3,11},{4,12},{5,13},{6,14},{7,15},{8,0},{9,1},... | collective-permute-start | bytes 221192 | tf_op jit(solution)/shard_map/ppermute | solution.py:657
  35.8 3.1 %copy.12 = bf16[80,128,256]{2,0,1:T(8,128)(2,1)S(1)} copy(bf16[80,128,256]{2,1,0:T(8,128)(2,1)S(1)} %bitcast.12) | data formatting | bytes 10485760 | tf_op args[0]
  40.7 3.5 %coarse_first.1 = (bf16[256,128]{1,0:T(8,128)(2,1)S(1)}, f32[128,256]{1,0:T(8,128)S(1)}, f32[8,256]{1,0:T(8,128)S(1)}) custom-call(bf16[80,128,256]{2,1,0:T(8,128)(2,1)S(1)} %bitcast.12, bf16[256,256]{1,0:T(8,128)(2,1)S(1)} %copy-done.1, f32[128,256]{1,0:T(8,128)S(1)} %get-tuple-element.67.own_ref, s16[144,256]{1,0:T(8,128)(2,1)S(1)} %collective-permute-done.8.refs_0_, ...), custom_call_target="tpu_custom_call" | custom-call | flops 1342177280 | bytes 5000000 | tf_op jit(solution)/shard_map/coarse_first/pallas_call | solution.py:434
  44.4 2.6 %collective-permute-start.12 = (bf16[256,128]{1,0:T(8,128)(2,1)S(1)}, bf16[256,128]{1,0:T(8,128)(2,1)S(1)}, u32[]{:S(2)}, u32[]{:S(2)}) collective-permute-start(bf16[256,128]{1,0:T(8,128)(2,1)S(1)} %get-tuple-element.72.refs_3_), channel_id=1, source_target_pairs={{0,12},{1,13},{2,14},{3,15},{4,8},{5,9},{6,10},{7,11},{8,4},{9,5},... | collective-permute-start | bytes 196616 | tf_op jit(solution)/shard_map/ppermute | solution.py:657
  48.5 2.1 %collective-permute-done.12.refs_1_ = bf16[256,128]{1,0:T(8,128)(2,1)S(1)} collective-permute-done((bf16[256,128]{1,0:T(8,128)(2,1)S(1)}, bf16[256,128]{1,0:T(8,128)(2,1)S(1)}, u32[]{:S(2)}, u32[]{:S(2)}) %collective-permute-start.12) | collective-permute-done | bytes 65568 | tf_op jit(solution)/shard_map/ppermute | solution.py:657
  50.5 2.3 %collective-permute-done.11.refs_0_ = bf16[256,128]{1,0:T(8,128)(2,1)S(1)} collective-permute-done((bf16[256,128]{1,0:T(8,128)(2,1)S(1)}, bf16[256,128]{1,0:T(8,128)(2,1)S(1)}, u32[]{:S(2)}, u32[]{:S(2)}) %collective-permute-start.11) | collective-permute-done | bytes 65568 | tf_op jit(solution)/shard_map/ppermute | solution.py:657
  52.9 1.6 %collective-permute-start.14 = (bf16[4,256,128]{2,1,0:T(8,128)(2,1)S(1)}, bf16[4,256,128]{2,1,0:T(8,128)(2,1)S(1)}, u32[]{:S(2)}, u32[]{:S(2)}) collective-permute-start(bf16[4,256,128]{2,1,0:T(8,128)(2,1)S(1)} %join.2.after_ref.refs_0_), channel_id=1, source_target_pairs={{0,2},{1,3},{2,0},{3,1},{4,6},{5,7},{6,4},{7,5},{8,10},{9,11},{10,... | collective-permute-start | bytes 786440 | tf_op jit(solution)/shard_map/ppermute | solution.py:653
  54.5 3.6 %project.2 = (f32[80,8192]{1,0:T(8,128)S(1)}, f32[8,128]{1,0:T(8,128)S(1)}) custom-call(bf16[128,80,256]{2,1,0:T(8,128)(2,1)S(1)} %bitcast.9, f32[128,256]{1,0:T(8,128)S(1)} %get-tuple-element.73.y_ref.refs_3_, bf16[2,256,128]{2,1,0:T(8,128)(2,1)S(1)} %copy-done.2, bf16[4,256,128]{2,1,0:T(8,128)(2,1)S(1)} %join.2.after_ref.refs_0_), custom_call_target="tpu_custom_call" | custom-call | flops 1342177280 | bytes 8000000 | tf_op jit(solution)/shard_map/project/pallas_call | solution.py:472
  64.2 1.6 %collective-permute-start.20 = (s16[272,256]{1,0:T(8,128)(2,1)S(1)}, s16[272,256]{1,0:T(8,128)(2,1)S(1)}, u32[]{:S(2)}, u32[]{:S(2)}) collective-permute-start(s16[272,256]{1,0:T(8,128)(2,1)S(1)} %get-tuple-element.83), channel_id=1, source_target_pairs={{0,2},{1,3},{2,0},{3,1},{4,6},{5,7},{6,4},{7,5},{8,10},{9,11},{10,... | collective-permute-start | bytes 417800 | tf_op jit(solution)/shard_map/ppermute | solution.py:653
  66.8 3.9 %collective-permute-done.20.p_ref = s16[272,256]{1,0:T(8,128)(2,1)S(1)} collective-permute-done((s16[272,256]{1,0:T(8,128)(2,1)S(1)}, s16[272,256]{1,0:T(8,128)(2,1)S(1)}, u32[]{:S(2)}, u32[]{:S(2)}) %collective-permute-start.20) | collective-permute-done | bytes 139296 | tf_op jit(solution)/shard_map/ppermute | solution.py:653
  71.1 2.2 %collective-permute-start.22 = (s16[144,256]{1,0:T(8,128)(2,1)S(1)}, s16[144,256]{1,0:T(8,128)(2,1)S(1)}, u32[]{:S(2)}, u32[]{:S(2)}) collective-permute-start(s16[144,256]{1,0:T(8,128)(2,1)S(1)} %get-tuple-element.88), channel_id=1, source_target_pairs={{0,12},{1,13},{2,14},{3,15},{4,8},{5,9},{6,10},{7,11},{8,4},{9,5},... | collective-permute-start | bytes 221192 | tf_op jit(solution)/shard_map/ppermute | solution.py:657
  74.6 3.8 %collective-permute-done.21.refs_0_ = s16[144,256]{1,0:T(8,128)(2,1)S(1)} collective-permute-done((s16[144,256]{1,0:T(8,128)(2,1)S(1)}, s16[144,256]{1,0:T(8,128)(2,1)S(1)}, u32[]{:S(2)}, u32[]{:S(2)}) %collective-permute-start.21) | collective-permute-done | bytes 73760 | tf_op jit(solution)/shard_map/ppermute | solution.py:657
  78.8 3.6 %coarse_second.1 = (bf16[256,128]{1,0:T(8,128)(2,1)S(1)}, f32[128,256]{1,0:T(8,128)S(1)}, f32[8,128]{1,0:T(8,128)S(1)}, f32[8,256]{1,0:T(8,128)S(1)}) custom-call(bf16[80,128,256]{2,1,0:T(8,128)(2,1)S(1)} %bitcast.12, bf16[256,256]{1,0:T(8,128)(2,1)S(1)} %copy-done.1, f32[128,256]{1,0:T(8,128)S(1)} %get-tuple-element.86.own_ref, ...), custom_call_target="tpu_custom_call" | custom-call | flops 1342177280 | bytes 5000000 | tf_op jit(solution)/shard_map/coarse_second/pallas_call | solution.py:434
  83.3 1.8 %collective-permute-start.25 = (bf16[256,128]{1,0:T(8,128)(2,1)S(1)}, bf16[256,128]{1,0:T(8,128)(2,1)S(1)}, u32[]{:S(2)}, u32[]{:S(2)}) collective-permute-start(bf16[256,128]{1,0:T(8,128)(2,1)S(1)} %get-tuple-element.91.refs_3_), channel_id=1, source_target_pairs={{0,12},{1,13},{2,14},{3,15},{4,8},{5,9},{6,10},{7,11},{8,4},{9,5},... | collective-permute-start | bytes 196616 | tf_op jit(solution)/shard_map/ppermute | solution.py:657
  87.0 2.5 %collective-permute-done.25.refs_1_ = bf16[256,128]{1,0:T(8,128)(2,1)S(1)} collective-permute-done((bf16[256,128]{1,0:T(8,128)(2,1)S(1)}, bf16[256,128]{1,0:T(8,128)(2,1)S(1)}, u32[]{:S(2)}, u32[]{:S(2)}) %collective-permute-start.25) | collective-permute-done | bytes 65568 | tf_op jit(solution)/shard_map/ppermute | solution.py:657
  89.5 2.2 %collective-permute-done.24.refs_0_ = bf16[256,128]{1,0:T(8,128)(2,1)S(1)} collective-permute-done((bf16[256,128]{1,0:T(8,128)(2,1)S(1)}, bf16[256,128]{1,0:T(8,128)(2,1)S(1)}, u32[]{:S(2)}, u32[]{:S(2)}) %collective-permute-start.24) | collective-permute-done | bytes 65568 | tf_op jit(solution)/shard_map/ppermute | solution.py:657
  91.7 1.6 %collective-permute-start.27 = (bf16[4,256,128]{2,1,0:T(8,128)(2,1)S(1)}, bf16[4,256,128]{2,1,0:T(8,128)(2,1)S(1)}, u32[]{:S(2)}, u32[]{:S(2)}) collective-permute-start(bf16[4,256,128]{2,1,0:T(8,128)(2,1)S(1)} %join.3.after_ref.refs_0_), channel_id=1, source_target_pairs={{0,2},{1,3},{2,0},{3,1},{4,6},{5,7},{6,4},{7,5},{8,10},{9,11},{10,... | collective-permute-start | bytes 786440 | tf_op jit(solution)/shard_map/ppermute | solution.py:653
  93.3 3.8 %project.3 = (f32[80,8192]{1,0:T(8,128)S(1)}, f32[8,128]{1,0:T(8,128)S(1)}) custom-call(bf16[128,80,256]{2,1,0:T(8,128)(2,1)S(1)} %bitcast.10, f32[128,256]{1,0:T(8,128)S(1)} %get-tuple-element.92.y_ref, bf16[2,256,128]{2,1,0:T(8,128)(2,1)S(1)} %copy-done.2, bf16[4,256,128]{2,1,0:T(8,128)(2,1)S(1)} %join.3.after_ref.refs_0_), custom_call_target="tpu_custom_call" | custom-call | flops 1342177280 | bytes 8000000 | tf_op jit(solution)/shard_map/project/pallas_call | solution.py:472
  97.2 1.7 %collective-permute-done.27.x_ref = bf16[4,256,128]{2,1,0:T(8,128)(2,1)S(1)} collective-permute-done((bf16[4,256,128]{2,1,0:T(8,128)(2,1)S(1)}, bf16[4,256,128]{2,1,0:T(8,128)(2,1)S(1)}, u32[]{:S(2)}, u32[]{:S(2)}) %collective-permute-start.27) | collective-permute-done | bytes 262176 | tf_op jit(solution)/shard_map/ppermute | solution.py:653
  104.1 2.1 %collective-permute-done.31 = f32[8,256]{1,0:T(8,128)S(1)} collective-permute-done((f32[8,256]{1,0:T(8,128)S(1)}, f32[8,256]{1,0:T(8,128)S(1)}, u32[]{:S(2)}, u32[]{:S(2)}) %collective-permute-start.31) | collective-permute-done | bytes 8224 | tf_op jit(solution)/shard_map/ppermute | solution.py:653
  106.2 1.9 %collective-permute-start.34 = (f32[8,256]{1,0:T(8,128)S(1)}, f32[8,256]{1,0:T(8,128)S(1)}, u32[]{:S(2)}, u32[]{:S(2)}) collective-permute-start(f32[8,256]{1,0:T(8,128)S(1)} %add.18.refs_0_), channel_id=1, source_target_pairs={{0,12},{1,13},{2,14},{3,15},{4,8},{5,9},{6,10},{7,11},{8,4},{9,5},... | collective-permute-start | bytes 24584 | tf_op jit(solution)/shard_map/ppermute | solution.py:657
  108.1 2.5 %collective-permute-start.32 = (f32[8,256]{1,0:T(8,128)S(1)}, f32[8,256]{1,0:T(8,128)S(1)}, u32[]{:S(2)}, u32[]{:S(2)}) collective-permute-start(f32[8,256]{1,0:T(8,128)S(1)} %add.18.refs_0_), channel_id=1, source_target_pairs={{0,4},{1,5},{2,6},{3,7},{4,0},{5,1},{6,2},{7,3},{8,12},{9,13},{10,... | collective-permute-start | bytes 24584 | tf_op jit(solution)/shard_map/ppermute | solution.py:657
  112.7 2.2 %result.1 = (f32[80,8192]{1,0:T(8,128)}, f32[1152,256]{1,0:T(8,128)}) custom-call(f32[8,128]{1,0:T(8,128)S(1)} %get-tuple-element.90.l0_ref, f32[8,256]{1,0:T(8,128)S(1)} %add.18.refs_0_, f32[8,256]{1,0:T(8,128)S(1)} %collective-permute-done.32.refs_1_, f32[8,256]{1,0:T(8,128)S(1)} %collective-permute-done.33.refs_2_, ...), custom_call_target="tpu_custom_call" | custom-call | flops 1966080 | bytes 10000000 | tf_op jit(solution)/shard_map/result/pallas_call | solution.py:632
  (92 shorter events, 32.8 us)
Async XLA Ops:
  3.4 4.4 %collective-permute-start.1 = (s32[8,128]{1,0:T(8,128)S(1)}, s32[8,128]{1,0:T(8,128)S(1)}, u32[]{:S(2)}, u32[]{:S(2)}) collective-permute-start(s32[8,128]{1,0:T(8,128)S(1)} %get-tuple-element.54), channel_id=1, source_target_pairs={{0,2},{1,3},{2,0},{3,1},{4,6},{5,7},{6,4},{7,5},{8,10},{9,11},{10,... | collective-permute-start | bytes 12296 | tf_op jit(solution)/shard_map/ppermute | solution.py:653
  7.8 3.7 %collective-permute-start.2 = (s32[8,128]{1,0:T(8,128)S(1)}, s32[8,128]{1,0:T(8,128)S(1)}, u32[]{:S(2)}, u32[]{:S(2)}) collective-permute-start(s32[8,128]{1,0:T(8,128)S(1)} %get-tuple-element.56), channel_id=1, source_target_pairs={{0,4},{1,5},{2,6},{3,7},{4,0},{5,1},{6,2},{7,3},{8,12},{9,13},{10,... | collective-permute-start | bytes 12296 | tf_op jit(solution)/shard_map/ppermute | solution.py:657
  11.6 4.6 %collective-permute-start.3 = (s32[8,128]{1,0:T(8,128)S(1)}, s32[8,128]{1,0:T(8,128)S(1)}, u32[]{:S(2)}, u32[]{:S(2)}) collective-permute-start(s32[8,128]{1,0:T(8,128)S(1)} %get-tuple-element.58), channel_id=1, source_target_pairs={{0,8},{1,9},{2,10},{3,11},{4,12},{5,13},{6,14},{7,15},{8,0},{9,1},... | collective-permute-start | bytes 12296 | tf_op jit(solution)/shard_map/ppermute | solution.py:657
  19.1 5.1 %collective-permute-start.5 = (f32[512,256]{1,0:T(8,128)S(1)}, f32[512,256]{1,0:T(8,128)S(1)}, u32[]{:S(2)}, u32[]{:S(2)}) collective-permute-start(f32[512,256]{1,0:T(8,128)S(1)} %get-tuple-element.65), channel_id=1, source_target_pairs={{0,1},{1,0},{2,3},{3,2},{4,5},{5,4},{6,7},{7,6},{8,9},{9,8},{10,11... | collective-permute-start | bytes 1572872 | tf_op jit(solution)/shard_map/ppermute | solution.py:649
  21.4 7.2 %collective-permute-start.4 = (f32[512,256]{1,0:T(8,128)S(1)}, f32[512,256]{1,0:T(8,128)S(1)}, u32[]{:S(2)}, u32[]{:S(2)}) collective-permute-start(f32[512,256]{1,0:T(8,128)S(1)} %get-tuple-element.63), channel_id=1, source_target_pairs={{0,1},{1,0},{2,3},{3,2},{4,5},{5,4},{6,7},{7,6},{8,9},{9,8},{10,11... | collective-permute-start | bytes 1572872 | tf_op jit(solution)/shard_map/ppermute | solution.py:649
  24.3 6.6 %collective-permute-start.7 = (s16[272,256]{1,0:T(8,128)(2,1)S(1)}, s16[272,256]{1,0:T(8,128)(2,1)S(1)}, u32[]{:S(2)}, u32[]{:S(2)}) collective-permute-start(s16[272,256]{1,0:T(8,128)(2,1)S(1)} %get-tuple-element.68), channel_id=1, source_target_pairs={{0,2},{1,3},{2,0},{3,1},{4,6},{5,7},{6,4},{7,5},{8,10},{9,11},{10,... | collective-permute-start | bytes 417800 | tf_op jit(solution)/shard_map/ppermute | solution.py:653
  26.2 9.1 %collective-permute-start.6 = (s16[272,256]{1,0:T(8,128)(2,1)S(1)}, s16[272,256]{1,0:T(8,128)(2,1)S(1)}, u32[]{:S(2)}, u32[]{:S(2)}) collective-permute-start(s16[272,256]{1,0:T(8,128)(2,1)S(1)} %get-tuple-element.66), channel_id=1, source_target_pairs={{0,2},{1,3},{2,0},{3,1},{4,6},{5,7},{6,4},{7,5},{8,10},{9,11},{10,... | collective-permute-start | bytes 417800 | tf_op jit(solution)/shard_map/ppermute | solution.py:653
  31.0 7.9 %collective-permute-start.8 = (s16[144,256]{1,0:T(8,128)(2,1)S(1)}, s16[144,256]{1,0:T(8,128)(2,1)S(1)}, u32[]{:S(2)}, u32[]{:S(2)}) collective-permute-start(s16[144,256]{1,0:T(8,128)(2,1)S(1)} %get-tuple-element.69), channel_id=1, source_target_pairs={{0,8},{1,9},{2,10},{3,11},{4,12},{5,13},{6,14},{7,15},{8,0},{9,1},... | collective-permute-start | bytes 221192 | tf_op jit(solution)/shard_map/ppermute | solution.py:657
  34.0 6.3 %collective-permute-start.9 = (s16[144,256]{1,0:T(8,128)(2,1)S(1)}, s16[144,256]{1,0:T(8,128)(2,1)S(1)}, u32[]{:S(2)}, u32[]{:S(2)}) collective-permute-start(s16[144,256]{1,0:T(8,128)(2,1)S(1)} %get-tuple-element.70), channel_id=1, source_target_pairs={{0,12},{1,13},{2,14},{3,15},{4,8},{5,9},{6,10},{7,11},{8,4},{9,5},... | collective-permute-start | bytes 221192 | tf_op jit(solution)/shard_map/ppermute | solution.py:657
  35.5 5.2 %collective-permute-start.10 = (s16[144,256]{1,0:T(8,128)(2,1)S(1)}, s16[144,256]{1,0:T(8,128)(2,1)S(1)}, u32[]{:S(2)}, u32[]{:S(2)}) collective-permute-start(s16[144,256]{1,0:T(8,128)(2,1)S(1)} %get-tuple-element.71), channel_id=1, source_target_pairs={{0,4},{1,5},{2,6},{3,7},{4,0},{5,1},{6,2},{7,3},{8,12},{9,13},{10,... | collective-permute-start | bytes 221192 | tf_op jit(solution)/shard_map/ppermute | solution.py:657
  44.1 4.3 %collective-permute-start.13 = (bf16[256,128]{1,0:T(8,128)(2,1)S(1)}, bf16[256,128]{1,0:T(8,128)(2,1)S(1)}, u32[]{:S(2)}, u32[]{:S(2)}) collective-permute-start(bf16[256,128]{1,0:T(8,128)(2,1)S(1)} %get-tuple-element.72.refs_3_), channel_id=1, source_target_pairs={{0,4},{1,5},{2,6},{3,7},{4,0},{5,1},{6,2},{7,3},{8,12},{9,13},{10,... | collective-permute-start | bytes 196616 | tf_op jit(solution)/shard_map/ppermute | solution.py:657
  44.4 6.2 %collective-permute-start.12 = (bf16[256,128]{1,0:T(8,128)(2,1)S(1)}, bf16[256,128]{1,0:T(8,128)(2,1)S(1)}, u32[]{:S(2)}, u32[]{:S(2)}) collective-permute-start(bf16[256,128]{1,0:T(8,128)(2,1)S(1)} %get-tuple-element.72.refs_3_), channel_id=1, source_target_pairs={{0,12},{1,13},{2,14},{3,15},{4,8},{5,9},{6,10},{7,11},{8,4},{9,5},... | collective-permute-start | bytes 196616 | tf_op jit(solution)/shard_map/ppermute | solution.py:657
  47.0 5.9 %collective-permute-start.11 = (bf16[256,128]{1,0:T(8,128)(2,1)S(1)}, bf16[256,128]{1,0:T(8,128)(2,1)S(1)}, u32[]{:S(2)}, u32[]{:S(2)}) collective-permute-start(bf16[256,128]{1,0:T(8,128)(2,1)S(1)} %get-tuple-element.72.refs_3_), channel_id=1, source_target_pairs={{0,8},{1,9},{2,10},{3,11},{4,12},{5,13},{6,14},{7,15},{8,0},{9,1},... | collective-permute-start | bytes 196616 | tf_op jit(solution)/shard_map/ppermute | solution.py:657
  52.9 6.4 %collective-permute-start.14 = (bf16[4,256,128]{2,1,0:T(8,128)(2,1)S(1)}, bf16[4,256,128]{2,1,0:T(8,128)(2,1)S(1)}, u32[]{:S(2)}, u32[]{:S(2)}) collective-permute-start(bf16[4,256,128]{2,1,0:T(8,128)(2,1)S(1)} %join.2.after_ref.refs_0_), channel_id=1, source_target_pairs={{0,2},{1,3},{2,0},{3,1},{4,6},{5,7},{6,4},{7,5},{8,10},{9,11},{10,... | collective-permute-start | bytes 786440 | tf_op jit(solution)/shard_map/ppermute | solution.py:653
  54.5 5.0 %collective-permute-start.16 = (bf16[4,256,128]{2,1,0:T(8,128)(2,1)S(1)}, bf16[4,256,128]{2,1,0:T(8,128)(2,1)S(1)}, u32[]{:S(2)}, u32[]{:S(2)}) collective-permute-start(bf16[4,256,128]{2,1,0:T(8,128)(2,1)S(1)} %join.2.after_ref.refs_0_), channel_id=1, source_target_pairs={{0,1},{1,0},{2,3},{3,2},{4,5},{5,4},{6,7},{7,6},{8,9},{9,8},{10,11... | collective-permute-start | bytes 786440 | tf_op jit(solution)/shard_map/ppermute | solution.py:649
  59.4 1.6 %collective-permute-start.15 = (bf16[4,256,128]{2,1,0:T(8,128)(2,1)S(1)}, bf16[4,256,128]{2,1,0:T(8,128)(2,1)S(1)}, u32[]{:S(2)}, u32[]{:S(2)}) collective-permute-start(bf16[4,256,128]{2,1,0:T(8,128)(2,1)S(1)} %relay.2.refs_1_), channel_id=1, source_target_pairs={{0,1},{1,0},{2,3},{3,2},{4,5},{5,4},{6,7},{7,6},{8,9},{9,8},{10,11... | collective-permute-start | bytes 786440 | tf_op jit(solution)/shard_map/ppermute | solution.py:649
  62.1 2.0 %collective-permute-start.18 = (f32[520,256]{1,0:T(8,128)S(1)}, f32[520,256]{1,0:T(8,128)S(1)}, u32[]{:S(2)}, u32[]{:S(2)}) collective-permute-start(f32[520,256]{1,0:T(8,128)S(1)} %get-tuple-element.80), channel_id=1, source_target_pairs={{0,1},{1,0},{2,3},{3,2},{4,5},{5,4},{6,7},{7,6},{8,9},{9,8},{10,11... | collective-permute-start | bytes 1597448 | tf_op jit(solution)/shard_map/ppermute | solution.py:649
  63.0 3.8 %collective-permute-start.17 = (f32[512,256]{1,0:T(8,128)S(1)}, f32[512,256]{1,0:T(8,128)S(1)}, u32[]{:S(2)}, u32[]{:S(2)}) collective-permute-start(f32[512,256]{1,0:T(8,128)S(1)} %back_side.1), channel_id=1, source_target_pairs={{0,1},{1,0},{2,3},{3,2},{4,5},{5,4},{6,7},{7,6},{8,9},{9,8},{10,11... | collective-permute-start | bytes 1572872 | tf_op jit(solution)/shard_map/ppermute | solution.py:649
  64.2 6.6 %collective-permute-start.20 = (s16[272,256]{1,0:T(8,128)(2,1)S(1)}, s16[272,256]{1,0:T(8,128)(2,1)S(1)}, u32[]{:S(2)}, u32[]{:S(2)}) collective-permute-start(s16[272,256]{1,0:T(8,128)(2,1)S(1)} %get-tuple-element.83), channel_id=1, source_target_pairs={{0,2},{1,3},{2,0},{3,1},{4,6},{5,7},{6,4},{7,5},{8,10},{9,11},{10,... | collective-permute-start | bytes 417800 | tf_op jit(solution)/shard_map/ppermute | solution.py:653
  65.8 7.5 %collective-permute-start.19 = (s16[272,256]{1,0:T(8,128)(2,1)S(1)}, s16[272,256]{1,0:T(8,128)(2,1)S(1)}, u32[]{:S(2)}, u32[]{:S(2)}) collective-permute-start(s16[272,256]{1,0:T(8,128)(2,1)S(1)} %get-tuple-element.82), channel_id=1, source_target_pairs={{0,2},{1,3},{2,0},{3,1},{4,6},{5,7},{6,4},{7,5},{8,10},{9,11},{10,... | collective-permute-start | bytes 417800 | tf_op jit(solution)/shard_map/ppermute | solution.py:653
  70.9 7.5 %collective-permute-start.21 = (s16[144,256]{1,0:T(8,128)(2,1)S(1)}, s16[144,256]{1,0:T(8,128)(2,1)S(1)}, u32[]{:S(2)}, u32[]{:S(2)}) collective-permute-start(s16[144,256]{1,0:T(8,128)(2,1)S(1)} %get-tuple-element.87), channel_id=1, source_target_pairs={{0,8},{1,9},{2,10},{3,11},{4,12},{5,13},{6,14},{7,15},{8,0},{9,1},... | collective-permute-start | bytes 221192 | tf_op jit(solution)/shard_map/ppermute | solution.py:657
  71.1 7.3 %collective-permute-start.22 = (s16[144,256]{1,0:T(8,128)(2,1)S(1)}, s16[144,256]{1,0:T(8,128)(2,1)S(1)}, u32[]{:S(2)}, u32[]{:S(2)}) collective-permute-start(s16[144,256]{1,0:T(8,128)(2,1)S(1)} %get-tuple-element.88), channel_id=1, source_target_pairs={{0,12},{1,13},{2,14},{3,15},{4,8},{5,9},{6,10},{7,11},{8,4},{9,5},... | collective-permute-start | bytes 221192 | tf_op jit(solution)/shard_map/ppermute | solution.py:657
  73.4 5.5 %collective-permute-start.23 = (s16[144,256]{1,0:T(8,128)(2,1)S(1)}, s16[144,256]{1,0:T(8,128)(2,1)S(1)}, u32[]{:S(2)}, u32[]{:S(2)}) collective-permute-start(s16[144,256]{1,0:T(8,128)(2,1)S(1)} %get-tuple-element.89), channel_id=1, source_target_pairs={{0,4},{1,5},{2,6},{3,7},{4,0},{5,1},{6,2},{7,3},{8,12},{9,13},{10,... | collective-permute-start | bytes 221192 | tf_op jit(solution)/shard_map/ppermute | solution.py:657
  82.4 4.6 %collective-permute-start.26 = (bf16[256,128]{1,0:T(8,128)(2,1)S(1)}, bf16[256,128]{1,0:T(8,128)(2,1)S(1)}, u32[]{:S(2)}, u32[]{:S(2)}) collective-permute-start(bf16[256,128]{1,0:T(8,128)(2,1)S(1)} %get-tuple-element.91.refs_3_), channel_id=1, source_target_pairs={{0,4},{1,5},{2,6},{3,7},{4,0},{5,1},{6,2},{7,3},{8,12},{9,13},{10,... | collective-permute-start | bytes 196616 | tf_op jit(solution)/shard_map/ppermute | solution.py:657
  83.3 6.2 %collective-permute-start.25 = (bf16[256,128]{1,0:T(8,128)(2,1)S(1)}, bf16[256,128]{1,0:T(8,128)(2,1)S(1)}, u32[]{:S(2)}, u32[]{:S(2)}) collective-permute-start(bf16[256,128]{1,0:T(8,128)(2,1)S(1)} %get-tuple-element.91.refs_3_), channel_id=1, source_target_pairs={{0,12},{1,13},{2,14},{3,15},{4,8},{5,9},{6,10},{7,11},{8,4},{9,5},... | collective-permute-start | bytes 196616 | tf_op jit(solution)/shard_map/ppermute | solution.py:657
  85.2 6.5 %collective-permute-start.24 = (bf16[256,128]{1,0:T(8,128)(2,1)S(1)}, bf16[256,128]{1,0:T(8,128)(2,1)S(1)}, u32[]{:S(2)}, u32[]{:S(2)}) collective-permute-start(bf16[256,128]{1,0:T(8,128)(2,1)S(1)} %get-tuple-element.91.refs_3_), channel_id=1, source_target_pairs={{0,8},{1,9},{2,10},{3,11},{4,12},{5,13},{6,14},{7,15},{8,0},{9,1},... | collective-permute-start | bytes 196616 | tf_op jit(solution)/shard_map/ppermute | solution.py:657
  91.7 7.2 %collective-permute-start.27 = (bf16[4,256,128]{2,1,0:T(8,128)(2,1)S(1)}, bf16[4,256,128]{2,1,0:T(8,128)(2,1)S(1)}, u32[]{:S(2)}, u32[]{:S(2)}) collective-permute-start(bf16[4,256,128]{2,1,0:T(8,128)(2,1)S(1)} %join.3.after_ref.refs_0_), channel_id=1, source_target_pairs={{0,2},{1,3},{2,0},{3,1},{4,6},{5,7},{6,4},{7,5},{8,10},{9,11},{10,... | collective-permute-start | bytes 786440 | tf_op jit(solution)/shard_map/ppermute | solution.py:653
  93.3 5.7 %collective-permute-start.29 = (bf16[4,256,128]{2,1,0:T(8,128)(2,1)S(1)}, bf16[4,256,128]{2,1,0:T(8,128)(2,1)S(1)}, u32[]{:S(2)}, u32[]{:S(2)}) collective-permute-start(bf16[4,256,128]{2,1,0:T(8,128)(2,1)S(1)} %join.3.after_ref.refs_0_), channel_id=1, source_target_pairs={{0,1},{1,0},{2,3},{3,2},{4,5},{5,4},{6,7},{7,6},{8,9},{9,8},{10,11... | collective-permute-start | bytes 786440 | tf_op jit(solution)/shard_map/ppermute | solution.py:649
  102.5 3.7 %collective-permute-start.31 = (f32[8,256]{1,0:T(8,128)S(1)}, f32[8,256]{1,0:T(8,128)S(1)}, u32[]{:S(2)}, u32[]{:S(2)}) collective-permute-start(f32[8,256]{1,0:T(8,128)S(1)} %add.17), channel_id=1, source_target_pairs={{0,2},{1,3},{2,0},{3,1},{4,6},{5,7},{6,4},{7,5},{8,10},{9,11},{10,... | collective-permute-start | bytes 24584 | tf_op jit(solution)/shard_map/ppermute | solution.py:653
  106.2 5.4 %collective-permute-start.34 = (f32[8,256]{1,0:T(8,128)S(1)}, f32[8,256]{1,0:T(8,128)S(1)}, u32[]{:S(2)}, u32[]{:S(2)}) collective-permute-start(f32[8,256]{1,0:T(8,128)S(1)} %add.18.refs_0_), channel_id=1, source_target_pairs={{0,12},{1,13},{2,14},{3,15},{4,8},{5,9},{6,10},{7,11},{8,4},{9,5},... | collective-permute-start | bytes 24584 | tf_op jit(solution)/shard_map/ppermute | solution.py:657
  108.1 4.5 %collective-permute-start.33 = (f32[8,256]{1,0:T(8,128)S(1)}, f32[8,256]{1,0:T(8,128)S(1)}, u32[]{:S(2)}, u32[]{:S(2)}) collective-permute-start(f32[8,256]{1,0:T(8,128)S(1)} %add.18.refs_0_), channel_id=1, source_target_pairs={{0,8},{1,9},{2,10},{3,11},{4,12},{5,13},{6,14},{7,15},{8,0},{9,1},... | collective-permute-start | bytes 24584 | tf_op jit(solution)/shard_map/ppermute | solution.py:657
  108.1 4.5 %collective-permute-start.32 = (f32[8,256]{1,0:T(8,128)S(1)}, f32[8,256]{1,0:T(8,128)S(1)}, u32[]{:S(2)}, u32[]{:S(2)}) collective-permute-start(f32[8,256]{1,0:T(8,128)S(1)} %add.18.refs_0_), channel_id=1, source_target_pairs={{0,4},{1,5},{2,6},{3,7},{4,0},{5,1},{6,2},{7,3},{8,12},{9,13},{10,... | collective-permute-start | bytes 24584 | tf_op jit(solution)/shard_map/ppermute | solution.py:657
  (11 other events, 69.9 us)

commit v12 on v11

--- a/solution.py
+++ b/solution.py
@@ -120,7 +120,8 @@
     build_rows(ids_ref, weight_ref, wh_ref, wl_ref, at_ref, [y_ref], lo_s, base)
 
 
-def near_kernel(base, ids_ref, weight_ref, wh_ref, wl_ref, at_ref, y_ref, lo_s):
+def near_kernel(base, ids_ref, weight_ref, wh_ref, wl_ref, *refs):
+    at_ref, y_ref, lo_s = refs[-3:]
     build_rows(ids_ref, weight_ref, wh_ref, wl_ref, at_ref, [y_ref], lo_s, base)
 
 
@@ -144,7 +145,7 @@
 
 
 def adjoint_near(slots, args, base):
-    fine, width = args[-1].shape
+    fine, width = args[2].shape
     rows = slots // 4
     return pl.pallas_call(
         functools.partial(near_kernel, base),
@@ -580,22 +581,22 @@
     )(xs[-1], *part, far, obs, g_sums)
 
 
-def back_kernel(at_ref, v_ref, out_ref):
-    out_ref[...] = dot(at_ref[...], v_ref[...])
-
-
-def back(at, v, name):
+def back_kernel(at_ref, v_ref, *refs):
+    refs[-1][...] = dot(at_ref[...], v_ref[...])
+
+
+def back(at, v, name, *after):
     rows, fine = at.shape
     width = v.shape[1]
     return pl.pallas_call(
         back_kernel,
-        in_specs=[VMEM] * 2,
+        in_specs=[VMEM] * (2 + len(after)),
         out_specs=VMEM,
         out_shape=shape((rows, width), F32),
         compiler_params=params(16),
         cost_estimate=cost(2 * rows * fine * width, 2e6),
         name=name,
-    )(at, v)
+    )(at, v, *after)
 
 
 OUT_CUTS = 4
@@ -660,8 +661,8 @@
 def scatter_sums(parts, sums=None):
     near, far_y, near_c, far_yc = parts
     got_yc = over_core(far_yc)
-    got_c = over_core(near_c)
     first, second, *s = merge_y(far_y, got_yc, sums)
+    got_c = over_core(near_c(first))
     first, second = over_y(first), over_y(second)
     two, three, *s = merge_z(False, near, got_c, first, s[0] if s else None)
     got = [over_z(two, 2), over_z(three, 3)]
@@ -721,6 +722,7 @@
             return x.reshape(slots, width)
 
         def scatter(parts, sums=None):
+            parts = [p(parts[0]) if callable(p) else p for p in parts]
             got = swap(jnp.concatenate([p[: slots // 4] for p in parts], axis=0))
             high = lax.reduce_precision(got, 8, 7)
             high, low = high.astype(BF), (got - high).astype(BF)
@@ -739,15 +741,20 @@
     )
     built = [ids, weight, wh, wl]
     near, n1 = adjoint_near(slots, built, slots // 4)
-    side, c0 = adjoint_near(slots, built, slots // 2)
     stay, n0 = adjoint_near(slots, built, 0)
-    quarters = [stay, near, side]
-    own, got, _ = scatter([n0, n1, c0, c1])
+    quarters = [stay, near]
+
+    def first_side(after):
+        side, c0 = adjoint_near(slots, built + [after], slots // 2)
+        quarters.append(side)
+        return c0
+
+    own, got, _ = scatter([n0, n1, first_side, c1])
     ens = jnp.transpose(ensemble, (1, 0, 2))
     x0, y0, g_sums = coarse_image(ensemble, kern, own, got, after=[ens])
     xs, g0 = gather(x0, lambda after: project(ens, y0, taps, after))
     im0, sums, v, c1 = image_of(xs, quarters, far, obs_weight, g_sums, True)
-    c0 = back(side, v, "back_side")
+    c0 = lambda after: back(quarters[2], v, "back_side", after)
     n1, n0 = back(near, v, "back_near"), back(stay, v, "back_stay")
     own, got, sums = scatter([n0, n1, c0, c1], sums)
     x1, y1, l0, g_sums = coarse_image(ensemble, kern, own, got, y0, sums)

time: 115 us -> 114 us (level)
  waiting for transfers between devices: 35.7 us -> 34.5 us
  transfers between devices with their start and end apart: 35 -> 35, of which waited for: 24 -> 24; matrix products, arithmetic and copies ran while one was open for 4% -> 4% of each run, Pallas kernels for 17% -> 14%
where the time goes in v12:
time: 114 us
  starting transfers between devices  39.3 us (34%)
  waiting for transfers between devices  34.5 us (30%)
  Pallas kernels  33.5 us (29%)
  local copies, waits for them, and re-layouts  3.89 us (3%)
  other arithmetic  1.62 us (1%)
  between operations  1.17 us (1%)
    ppermute x17, starting transfers between devices, over_z(): return lax.ppermute(x, 'space', [(i, i ^ 4 * k) for i in range(GROUP)])  24.9 us
    ppermute x17, waiting for transfers between devices, over_z(): return lax.ppermute(x, 'space', [(i, i ^ 4 * k) for i in range(GROUP)])  19.5 us
    ppermute x8, waiting for transfers between devices, over_y(): return lax.ppermute(x, 'space', [(i, i ^ 2) for i in range(GROUP)])  12.1 us
    ppermute x8, starting transfers between devices, over_y(): return lax.ppermute(x, 'space', [(i, i ^ 2) for i in range(GROUP)])  11.7 us
    pallas_call x2, Pallas kernels, project(): pl.pallas_call(project_kernel, in_specs=[VMEM] * 4, out_specs=[VMEM] * 2,...  7.48 us
    pallas_call x2, Pallas kernels, coarse_image(): pl.pallas_call(functools.partial(coarse_kernel, len(got), second, len(aft...  7.03 us
    pallas_call x3, Pallas kernels, adjoint_near(): pl.pallas_call(functools.partial(near_kernel, base), in_specs=[VMEM] * le...  6.57 us
    unnamed x17, local copies, waits for them, and re-layouts  3.89 us
  transfers between devices with their start and end apart: 35, of which 24 were waited for; matrix products, arithmetic and copies ran while one was open for 4% of the time, Pallas kernels for 14%

profile of v12, /device:TPU:0, one launch (start us, length us, event | category | flops | bytes accessed | tf_op | source)
XLA Modules:
  0.0 114.0 jit_solution(15935506208244964368)
XLA Ops:
  3.4 2.9 %collective-permute-start.1 = (s32[8,128]{1,0:T(8,128)S(1)}, s32[8,128]{1,0:T(8,128)S(1)}, u32[]{:S(2)}, u32[]{:S(2)}) collective-permute-start(s32[8,128]{1,0:T(8,128)S(1)} %get-tuple-element.54), channel_id=1, source_target_pairs={{0,2},{1,3},{2,0},{3,1},{4,6},{5,7},{6,4},{7,5},{8,10},{9,11},{10,... | collective-permute-start | bytes 12296 | tf_op jit(solution)/shard_map/ppermute | solution.py:654
  6.2 1.6 %collective-permute-done.1.got_ref = s32[8,128]{1,0:T(8,128)S(1)} collective-permute-done((s32[8,128]{1,0:T(8,128)S(1)}, s32[8,128]{1,0:T(8,128)S(1)}, u32[]{:S(2)}, u32[]{:S(2)}) %collective-permute-start.1) | collective-permute-done | bytes 4128 | tf_op jit(solution)/shard_map/ppermute | solution.py:654
  7.8 2.1 %collective-permute-start.2 = (s32[8,128]{1,0:T(8,128)S(1)}, s32[8,128]{1,0:T(8,128)S(1)}, u32[]{:S(2)}, u32[]{:S(2)}) collective-permute-start(s32[8,128]{1,0:T(8,128)S(1)} %get-tuple-element.56), channel_id=1, source_target_pairs={{0,4},{1,5},{2,6},{3,7},{4,0},{5,1},{6,2},{7,3},{8,12},{9,13},{10,... | collective-permute-start | bytes 12296 | tf_op jit(solution)/shard_map/ppermute | solution.py:658
  11.6 3.0 %collective-permute-start.3 = (s32[8,128]{1,0:T(8,128)S(1)}, s32[8,128]{1,0:T(8,128)S(1)}, u32[]{:S(2)}, u32[]{:S(2)}) collective-permute-start(s32[8,128]{1,0:T(8,128)S(1)} %get-tuple-element.58), channel_id=1, source_target_pairs={{0,8},{1,9},{2,10},{3,11},{4,12},{5,13},{6,14},{7,15},{8,0},{9,1},... | collective-permute-start | bytes 12296 | tf_op jit(solution)/shard_map/ppermute | solution.py:658
  14.6 1.6 %collective-permute-done.3.refs_1_ = s32[8,128]{1,0:T(8,128)S(1)} collective-permute-done((s32[8,128]{1,0:T(8,128)S(1)}, s32[8,128]{1,0:T(8,128)S(1)}, u32[]{:S(2)}, u32[]{:S(2)}) %collective-permute-start.3) | collective-permute-done | bytes 4128 | tf_op jit(solution)/shard_map/ppermute | solution.py:658
  16.2 2.9 %adjoint_far.1 = (s32[4,1152]{1,0:T(4,128)S(1)}, f32[4,1152]{1,0:T(4,128)S(1)}, bf16[512,1152]{1,0:T(8,128)(2,1)S(1)}, f32[512,256]{1,0:T(8,128)S(1)}) custom-call(s32[4]{0:T(128)S(1)} %pad_add_fusion.me_ref, s32[8,128]{1,0:T(8,128)S(1)} %get-tuple-element.57.refs_0_, s32[8,128]{1,0:T(8,128)S(1)} %collective-permute-done.3.refs_1_, ...), custom_call_target="tpu_custom_call" | custom-call | flops 905969664 | bytes 2000000 | tf_op jit(solution)/shard_map/adjoint_far/pallas_call | solution.py:135
  19.2 2.2 %adjoint_near.1 = (bf16[512,1152]{1,0:T(8,128)(2,1)S(1)}, f32[512,256]{1,0:T(8,128)S(1)}) custom-call(s32[4,1152]{1,0:T(4,128)S(1)} %get-tuple-element.59.ids_ref, f32[4,1152]{1,0:T(4,128)S(1)} %get-tuple-element.60.weight_ref, bf16[1152,256]{1,0:T(8,128)(2,1)S(1)} %get-tuple-element.101.refs_3_.wh_ref, bf16[1152,256]{1,0:T(8,128)(2,1)S(1)} %get-tuple-element.100.refs_4_.wl_ref), custom_call_target="tpu_custom_call" | custom-call | flops 905969664 | bytes 2000000 | tf_op jit(solution)/shard_map/adjoint_near/pallas_call | solution.py:150
  21.5 2.2 %adjoint_side.1 = (bf16[512,1152]{1,0:T(8,128)(2,1)S(1)}, f32[512,256]{1,0:T(8,128)S(1)}) custom-call(s32[4,1152]{1,0:T(4,128)S(1)} %get-tuple-element.59.ids_ref, f32[4,1152]{1,0:T(4,128)S(1)} %get-tuple-element.60.weight_ref, bf16[1152,256]{1,0:T(8,128)(2,1)S(1)} %get-tuple-element.101.refs_3_.wh_ref, ...), custom_call_target="tpu_custom_call" | custom-call | flops 905969664 | bytes 2000000 | tf_op jit(solution)/shard_map/adjoint_side/pallas_call | solution.py:150
  24.3 1.9 %collective-permute-start.7 = (s16[272,256]{1,0:T(8,128)(2,1)S(1)}, s16[272,256]{1,0:T(8,128)(2,1)S(1)}, u32[]{:S(2)}, u32[]{:S(2)}) collective-permute-start(s16[272,256]{1,0:T(8,128)(2,1)S(1)} %get-tuple-element.65.refs_0_), channel_id=1, source_target_pairs={{0,2},{1,3},{2,0},{3,1},{4,6},{5,7},{6,4},{7,5},{8,10},{9,11},{10,... | collective-permute-start | bytes 417800 | tf_op jit(solution)/shard_map/ppermute | solution.py:654
  26.3 2.2 %adjoint_stay.1 = (bf16[512,1152]{1,0:T(8,128)(2,1)S(1)}, f32[512,256]{1,0:T(8,128)S(1)}) custom-call(s32[4,1152]{1,0:T(4,128)S(1)} %get-tuple-element.59.ids_ref, f32[4,1152]{1,0:T(4,128)S(1)} %get-tuple-element.60.weight_ref, bf16[1152,256]{1,0:T(8,128)(2,1)S(1)} %get-tuple-element.101.refs_3_.wh_ref, bf16[1152,256]{1,0:T(8,128)(2,1)S(1)} %get-tuple-element.100.refs_4_.wl_ref), custom_call_target="tpu_custom_call" | custom-call | flops 905969664 | bytes 2000000 | tf_op jit(solution)/shard_map/adjoint_stay/pallas_call | solution.py:150
  28.5 2.3 %collective-permute-done.7.p_ref = s16[272,256]{1,0:T(8,128)(2,1)S(1)} collective-permute-done((s16[272,256]{1,0:T(8,128)(2,1)S(1)}, s16[272,256]{1,0:T(8,128)(2,1)S(1)}, u32[]{:S(2)}, u32[]{:S(2)}) %collective-permute-start.7) | collective-permute-done | bytes 139296 | tf_op jit(solution)/shard_map/ppermute | solution.py:654
  30.9 3.0 %collective-permute-start.8 = (s16[144,256]{1,0:T(8,128)(2,1)S(1)}, s16[144,256]{1,0:T(8,128)(2,1)S(1)}, u32[]{:S(2)}, u32[]{:S(2)}) collective-permute-start(s16[144,256]{1,0:T(8,128)(2,1)S(1)} %get-tuple-element.69), channel_id=1, source_target_pairs={{0,8},{1,9},{2,10},{3,11},{4,12},{5,13},{6,14},{7,15},{8,0},{9,1},... | collective-permute-start | bytes 221192 | tf_op jit(solution)/shard_map/ppermute | solution.py:658
  35.7 3.1 %copy.12 = bf16[80,128,256]{2,0,1:T(8,128)(2,1)S(1)} copy(bf16[80,128,256]{2,1,0:T(8,128)(2,1)S(1)} %bitcast.12) | data formatting | bytes 10485760 | tf_op args[0]
  40.6 3.5 %coarse_first.1 = (bf16[256,128]{1,0:T(8,128)(2,1)S(1)}, f32[128,256]{1,0:T(8,128)S(1)}, f32[8,256]{1,0:T(8,128)S(1)}) custom-call(bf16[80,128,256]{2,1,0:T(8,128)(2,1)S(1)} %bitcast.12, bf16[256,256]{1,0:T(8,128)(2,1)S(1)} %copy-done.1, f32[128,256]{1,0:T(8,128)S(1)} %get-tuple-element.68.own_ref, s16[144,256]{1,0:T(8,128)(2,1)S(1)} %collective-permute-done.8.refs_0_, ...), custom_call_target="tpu_custom_call" | custom-call | flops 1342177280 | bytes 5000000 | tf_op jit(solution)/shard_map/coarse_first/pallas_call | solution.py:435
  44.3 2.8 %collective-permute-start.12 = (bf16[256,128]{1,0:T(8,128)(2,1)S(1)}, bf16[256,128]{1,0:T(8,128)(2,1)S(1)}, u32[]{:S(2)}, u32[]{:S(2)}) collective-permute-start(bf16[256,128]{1,0:T(8,128)(2,1)S(1)} %get-tuple-element.72.refs_3_), channel_id=1, source_target_pairs={{0,12},{1,13},{2,14},{3,15},{4,8},{5,9},{6,10},{7,11},{8,4},{9,5},... | collective-permute-start | bytes 196616 | tf_op jit(solution)/shard_map/ppermute | solution.py:658
  48.7 1.8 %collective-permute-done.12.refs_1_ = bf16[256,128]{1,0:T(8,128)(2,1)S(1)} collective-permute-done((bf16[256,128]{1,0:T(8,128)(2,1)S(1)}, bf16[256,128]{1,0:T(8,128)(2,1)S(1)}, u32[]{:S(2)}, u32[]{:S(2)}) %collective-permute-start.12) | collective-permute-done | bytes 65568 | tf_op jit(solution)/shard_map/ppermute | solution.py:658
  50.5 2.3 %collective-permute-done.11.refs_0_ = bf16[256,128]{1,0:T(8,128)(2,1)S(1)} collective-permute-done((bf16[256,128]{1,0:T(8,128)(2,1)S(1)}, bf16[256,128]{1,0:T(8,128)(2,1)S(1)}, u32[]{:S(2)}, u32[]{:S(2)}) %collective-permute-start.11) | collective-permute-done | bytes 65568 | tf_op jit(solution)/shard_map/ppermute | solution.py:658
  52.8 1.6 %collective-permute-start.14 = (bf16[4,256,128]{2,1,0:T(8,128)(2,1)S(1)}, bf16[4,256,128]{2,1,0:T(8,128)(2,1)S(1)}, u32[]{:S(2)}, u32[]{:S(2)}) collective-permute-start(bf16[4,256,128]{2,1,0:T(8,128)(2,1)S(1)} %join.2.after_ref.refs_0_), channel_id=1, source_target_pairs={{0,2},{1,3},{2,0},{3,1},{4,6},{5,7},{6,4},{7,5},{8,10},{9,11},{10,... | collective-permute-start | bytes 786440 | tf_op jit(solution)/shard_map/ppermute | solution.py:654
  54.4 3.6 %project.2 = (f32[80,8192]{1,0:T(8,128)S(1)}, f32[8,128]{1,0:T(8,128)S(1)}) custom-call(bf16[128,80,256]{2,1,0:T(8,128)(2,1)S(1)} %bitcast.9, f32[128,256]{1,0:T(8,128)S(1)} %get-tuple-element.73.y_ref.refs_3_, bf16[2,256,128]{2,1,0:T(8,128)(2,1)S(1)} %copy-done.2, bf16[4,256,128]{2,1,0:T(8,128)(2,1)S(1)} %join.2.after_ref.refs_0_), custom_call_target="tpu_custom_call" | custom-call | flops 1342177280 | bytes 8000000 | tf_op jit(solution)/shard_map/project/pallas_call | solution.py:473
  67.6 4.0 %collective-permute-done.20.p_ref = s16[272,256]{1,0:T(8,128)(2,1)S(1)} collective-permute-done((s16[272,256]{1,0:T(8,128)(2,1)S(1)}, s16[272,256]{1,0:T(8,128)(2,1)S(1)}, u32[]{:S(2)}, u32[]{:S(2)}) %collective-permute-start.20) | collective-permute-done | bytes 139296 | tf_op jit(solution)/shard_map/ppermute | solution.py:654
  72.0 2.0 %collective-permute-start.22 = (s16[144,256]{1,0:T(8,128)(2,1)S(1)}, s16[144,256]{1,0:T(8,128)(2,1)S(1)}, u32[]{:S(2)}, u32[]{:S(2)}) collective-permute-start(s16[144,256]{1,0:T(8,128)(2,1)S(1)} %get-tuple-element.88), channel_id=1, source_target_pairs={{0,12},{1,13},{2,14},{3,15},{4,8},{5,9},{6,10},{7,11},{8,4},{9,5},... | collective-permute-start | bytes 221192 | tf_op jit(solution)/shard_map/ppermute | solution.py:658
  75.4 3.3 %collective-permute-done.21.refs_0_ = s16[144,256]{1,0:T(8,128)(2,1)S(1)} collective-permute-done((s16[144,256]{1,0:T(8,128)(2,1)S(1)}, s16[144,256]{1,0:T(8,128)(2,1)S(1)}, u32[]{:S(2)}, u32[]{:S(2)}) %collective-permute-start.21) | collective-permute-done | bytes 73760 | tf_op jit(solution)/shard_map/ppermute | solution.py:658
  79.4 3.6 %coarse_second.1 = (bf16[256,128]{1,0:T(8,128)(2,1)S(1)}, f32[128,256]{1,0:T(8,128)S(1)}, f32[8,128]{1,0:T(8,128)S(1)}, f32[8,256]{1,0:T(8,128)S(1)}) custom-call(bf16[80,128,256]{2,1,0:T(8,128)(2,1)S(1)} %bitcast.12, bf16[256,256]{1,0:T(8,128)(2,1)S(1)} %copy-done.1, f32[128,256]{1,0:T(8,128)S(1)} %get-tuple-element.86.own_ref, ...), custom_call_target="tpu_custom_call" | custom-call | flops 1342177280 | bytes 5000000 | tf_op jit(solution)/shard_map/coarse_second/pallas_call | solution.py:435
  83.6 1.8 %collective-permute-start.25 = (bf16[256,128]{1,0:T(8,128)(2,1)S(1)}, bf16[256,128]{1,0:T(8,128)(2,1)S(1)}, u32[]{:S(2)}, u32[]{:S(2)}) collective-permute-start(bf16[256,128]{1,0:T(8,128)(2,1)S(1)} %get-tuple-element.91.refs_3_), channel_id=1, source_target_pairs={{0,12},{1,13},{2,14},{3,15},{4,8},{5,9},{6,10},{7,11},{8,4},{9,5},... | collective-permute-start | bytes 196616 | tf_op jit(solution)/shard_map/ppermute | solution.py:658
  86.6 1.9 %collective-permute-done.26.refs_2_ = bf16[256,128]{1,0:T(8,128)(2,1)S(1)} collective-permute-done((bf16[256,128]{1,0:T(8,128)(2,1)S(1)}, bf16[256,128]{1,0:T(8,128)(2,1)S(1)}, u32[]{:S(2)}, u32[]{:S(2)}) %collective-permute-start.26) | collective-permute-done | bytes 65568 | tf_op jit(solution)/shard_map/ppermute | solution.py:658
  89.8 1.6 %collective-permute-done.24.refs_0_ = bf16[256,128]{1,0:T(8,128)(2,1)S(1)} collective-permute-done((bf16[256,128]{1,0:T(8,128)(2,1)S(1)}, bf16[256,128]{1,0:T(8,128)(2,1)S(1)}, u32[]{:S(2)}, u32[]{:S(2)}) %collective-permute-start.24) | collective-permute-done | bytes 65568 | tf_op jit(solution)/shard_map/ppermute | solution.py:658
  91.4 1.6 %collective-permute-start.27 = (bf16[4,256,128]{2,1,0:T(8,128)(2,1)S(1)}, bf16[4,256,128]{2,1,0:T(8,128)(2,1)S(1)}, u32[]{:S(2)}, u32[]{:S(2)}) collective-permute-start(bf16[4,256,128]{2,1,0:T(8,128)(2,1)S(1)} %join.3.after_ref.refs_0_), channel_id=1, source_target_pairs={{0,2},{1,3},{2,0},{3,1},{4,6},{5,7},{6,4},{7,5},{8,10},{9,11},{10,... | collective-permute-start | bytes 786440 | tf_op jit(solution)/shard_map/ppermute | solution.py:654
  93.0 3.8 %project.3 = (f32[80,8192]{1,0:T(8,128)S(1)}, f32[8,128]{1,0:T(8,128)S(1)}) custom-call(bf16[128,80,256]{2,1,0:T(8,128)(2,1)S(1)} %bitcast.10, f32[128,256]{1,0:T(8,128)S(1)} %get-tuple-element.92.y_ref, bf16[2,256,128]{2,1,0:T(8,128)(2,1)S(1)} %copy-done.2, bf16[4,256,128]{2,1,0:T(8,128)(2,1)S(1)} %join.3.after_ref.refs_0_), custom_call_target="tpu_custom_call" | custom-call | flops 1342177280 | bytes 8000000 | tf_op jit(solution)/shard_map/project/pallas_call | solution.py:473
  103.0 2.1 %collective-permute-done.31 = f32[8,256]{1,0:T(8,128)S(1)} collective-permute-done((f32[8,256]{1,0:T(8,128)S(1)}, f32[8,256]{1,0:T(8,128)S(1)}, u32[]{:S(2)}, u32[]{:S(2)}) %collective-permute-start.31) | collective-permute-done | bytes 8224 | tf_op jit(solution)/shard_map/ppermute | solution.py:654
  105.1 2.0 %collective-permute-start.34 = (f32[8,256]{1,0:T(8,128)S(1)}, f32[8,256]{1,0:T(8,128)S(1)}, u32[]{:S(2)}, u32[]{:S(2)}) collective-permute-start(f32[8,256]{1,0:T(8,128)S(1)} %add.18.refs_0_), channel_id=1, source_target_pairs={{0,12},{1,13},{2,14},{3,15},{4,8},{5,9},{6,10},{7,11},{8,4},{9,5},... | collective-permute-start | bytes 24584 | tf_op jit(solution)/shard_map/ppermute | solution.py:658
  107.0 2.4 %collective-permute-start.32 = (f32[8,256]{1,0:T(8,128)S(1)}, f32[8,256]{1,0:T(8,128)S(1)}, u32[]{:S(2)}, u32[]{:S(2)}) collective-permute-start(f32[8,256]{1,0:T(8,128)S(1)} %add.18.refs_0_), channel_id=1, source_target_pairs={{0,4},{1,5},{2,6},{3,7},{4,0},{5,1},{6,2},{7,3},{8,12},{9,13},{10,... | collective-permute-start | bytes 24584 | tf_op jit(solution)/shard_map/ppermute | solution.py:658
  111.6 2.2 %result.1 = (f32[80,8192]{1,0:T(8,128)}, f32[1152,256]{1,0:T(8,128)}) custom-call(f32[8,128]{1,0:T(8,128)S(1)} %get-tuple-element.90.l0_ref, f32[8,256]{1,0:T(8,128)S(1)} %add.18.refs_0_, f32[8,256]{1,0:T(8,128)S(1)} %collective-permute-done.32.refs_1_, f32[8,256]{1,0:T(8,128)S(1)} %collective-permute-done.33.refs_2_, ...), custom_call_target="tpu_custom_call" | custom-call | flops 1966080 | bytes 10000000 | tf_op jit(solution)/shard_map/result/pallas_call | solution.py:633
  (92 shorter events, 34.0 us)
Async XLA Ops:
  3.4 4.4 %collective-permute-start.1 = (s32[8,128]{1,0:T(8,128)S(1)}, s32[8,128]{1,0:T(8,128)S(1)}, u32[]{:S(2)}, u32[]{:S(2)}) collective-permute-start(s32[8,128]{1,0:T(8,128)S(1)} %get-tuple-element.54), channel_id=1, source_target_pairs={{0,2},{1,3},{2,0},{3,1},{4,6},{5,7},{6,4},{7,5},{8,10},{9,11},{10,... | collective-permute-start | bytes 12296 | tf_op jit(solution)/shard_map/ppermute | solution.py:654
  7.8 3.7 %collective-permute-start.2 = (s32[8,128]{1,0:T(8,128)S(1)}, s32[8,128]{1,0:T(8,128)S(1)}, u32[]{:S(2)}, u32[]{:S(2)}) collective-permute-start(s32[8,128]{1,0:T(8,128)S(1)} %get-tuple-element.56), channel_id=1, source_target_pairs={{0,4},{1,5},{2,6},{3,7},{4,0},{5,1},{6,2},{7,3},{8,12},{9,13},{10,... | collective-permute-start | bytes 12296 | tf_op jit(solution)/shard_map/ppermute | solution.py:658
  11.6 4.6 %collective-permute-start.3 = (s32[8,128]{1,0:T(8,128)S(1)}, s32[8,128]{1,0:T(8,128)S(1)}, u32[]{:S(2)}, u32[]{:S(2)}) collective-permute-start(s32[8,128]{1,0:T(8,128)S(1)} %get-tuple-element.58), channel_id=1, source_target_pairs={{0,8},{1,9},{2,10},{3,11},{4,12},{5,13},{6,14},{7,15},{8,0},{9,1},... | collective-permute-start | bytes 12296 | tf_op jit(solution)/shard_map/ppermute | solution.py:658
  19.1 2.3 %collective-permute-start.4 = (f32[512,256]{1,0:T(8,128)S(1)}, f32[512,256]{1,0:T(8,128)S(1)}, u32[]{:S(2)}, u32[]{:S(2)}) collective-permute-start(f32[512,256]{1,0:T(8,128)S(1)} %get-tuple-element.64), channel_id=1, source_target_pairs={{0,1},{1,0},{2,3},{3,2},{4,5},{5,4},{6,7},{7,6},{8,9},{9,8},{10,11... | collective-permute-start | bytes 1572872 | tf_op jit(solution)/shard_map/ppermute | solution.py:650
  23.7 7.1 %collective-permute-start.5 = (f32[512,256]{1,0:T(8,128)S(1)}, f32[512,256]{1,0:T(8,128)S(1)}, u32[]{:S(2)}, u32[]{:S(2)}) collective-permute-start(f32[512,256]{1,0:T(8,128)S(1)} %get-tuple-element.66), channel_id=1, source_target_pairs={{0,1},{1,0},{2,3},{3,2},{4,5},{5,4},{6,7},{7,6},{8,9},{9,8},{10,11... | collective-permute-start | bytes 1572872 | tf_op jit(solution)/shard_map/ppermute | solution.py:650
  24.3 6.5 %collective-permute-start.7 = (s16[272,256]{1,0:T(8,128)(2,1)S(1)}, s16[272,256]{1,0:T(8,128)(2,1)S(1)}, u32[]{:S(2)}, u32[]{:S(2)}) collective-permute-start(s16[272,256]{1,0:T(8,128)(2,1)S(1)} %get-tuple-element.65.refs_0_), channel_id=1, source_target_pairs={{0,2},{1,3},{2,0},{3,1},{4,6},{5,7},{6,4},{7,5},{8,10},{9,11},{10,... | collective-permute-start | bytes 417800 | tf_op jit(solution)/shard_map/ppermute | solution.py:654
  26.1 9.1 %collective-permute-start.6 = (s16[272,256]{1,0:T(8,128)(2,1)S(1)}, s16[272,256]{1,0:T(8,128)(2,1)S(1)}, u32[]{:S(2)}, u32[]{:S(2)}) collective-permute-start(s16[272,256]{1,0:T(8,128)(2,1)S(1)} %get-tuple-element.67), channel_id=1, source_target_pairs={{0,2},{1,3},{2,0},{3,1},{4,6},{5,7},{6,4},{7,5},{8,10},{9,11},{10,... | collective-permute-start | bytes 417800 | tf_op jit(solution)/shard_map/ppermute | solution.py:654
  30.9 7.9 %collective-permute-start.8 = (s16[144,256]{1,0:T(8,128)(2,1)S(1)}, s16[144,256]{1,0:T(8,128)(2,1)S(1)}, u32[]{:S(2)}, u32[]{:S(2)}) collective-permute-start(s16[144,256]{1,0:T(8,128)(2,1)S(1)} %get-tuple-element.69), channel_id=1, source_target_pairs={{0,8},{1,9},{2,10},{3,11},{4,12},{5,13},{6,14},{7,15},{8,0},{9,1},... | collective-permute-start | bytes 221192 | tf_op jit(solution)/shard_map/ppermute | solution.py:658
  33.9 6.3 %collective-permute-start.9 = (s16[144,256]{1,0:T(8,128)(2,1)S(1)}, s16[144,256]{1,0:T(8,128)(2,1)S(1)}, u32[]{:S(2)}, u32[]{:S(2)}) collective-permute-start(s16[144,256]{1,0:T(8,128)(2,1)S(1)} %get-tuple-element.70), channel_id=1, source_target_pairs={{0,12},{1,13},{2,14},{3,15},{4,8},{5,9},{6,10},{7,11},{8,4},{9,5},... | collective-permute-start | bytes 221192 | tf_op jit(solution)/shard_map/ppermute | solution.py:658
  35.4 5.2 %collective-permute-start.10 = (s16[144,256]{1,0:T(8,128)(2,1)S(1)}, s16[144,256]{1,0:T(8,128)(2,1)S(1)}, u32[]{:S(2)}, u32[]{:S(2)}) collective-permute-start(s16[144,256]{1,0:T(8,128)(2,1)S(1)} %get-tuple-element.71), channel_id=1, source_target_pairs={{0,4},{1,5},{2,6},{3,7},{4,0},{5,1},{6,2},{7,3},{8,12},{9,13},{10,... | collective-permute-start | bytes 221192 | tf_op jit(solution)/shard_map/ppermute | solution.py:658
  44.0 4.6 %collective-permute-start.13 = (bf16[256,128]{1,0:T(8,128)(2,1)S(1)}, bf16[256,128]{1,0:T(8,128)(2,1)S(1)}, u32[]{:S(2)}, u32[]{:S(2)}) collective-permute-start(bf16[256,128]{1,0:T(8,128)(2,1)S(1)} %get-tuple-element.72.refs_3_), channel_id=1, source_target_pairs={{0,4},{1,5},{2,6},{3,7},{4,0},{5,1},{6,2},{7,3},{8,12},{9,13},{10,... | collective-permute-start | bytes 196616 | tf_op jit(solution)/shard_map/ppermute | solution.py:658
  44.3 6.2 %collective-permute-start.12 = (bf16[256,128]{1,0:T(8,128)(2,1)S(1)}, bf16[256,128]{1,0:T(8,128)(2,1)S(1)}, u32[]{:S(2)}, u32[]{:S(2)}) collective-permute-start(bf16[256,128]{1,0:T(8,128)(2,1)S(1)} %get-tuple-element.72.refs_3_), channel_id=1, source_target_pairs={{0,12},{1,13},{2,14},{3,15},{4,8},{5,9},{6,10},{7,11},{8,4},{9,5},... | collective-permute-start | bytes 196616 | tf_op jit(solution)/shard_map/ppermute | solution.py:658
  47.1 5.7 %collective-permute-start.11 = (bf16[256,128]{1,0:T(8,128)(2,1)S(1)}, bf16[256,128]{1,0:T(8,128)(2,1)S(1)}, u32[]{:S(2)}, u32[]{:S(2)}) collective-permute-start(bf16[256,128]{1,0:T(8,128)(2,1)S(1)} %get-tuple-element.72.refs_3_), channel_id=1, source_target_pairs={{0,8},{1,9},{2,10},{3,11},{4,12},{5,13},{6,14},{7,15},{8,0},{9,1},... | collective-permute-start | bytes 196616 | tf_op jit(solution)/shard_map/ppermute | solution.py:658
  52.8 6.4 %collective-permute-start.14 = (bf16[4,256,128]{2,1,0:T(8,128)(2,1)S(1)}, bf16[4,256,128]{2,1,0:T(8,128)(2,1)S(1)}, u32[]{:S(2)}, u32[]{:S(2)}) collective-permute-start(bf16[4,256,128]{2,1,0:T(8,128)(2,1)S(1)} %join.2.after_ref.refs_0_), channel_id=1, source_target_pairs={{0,2},{1,3},{2,0},{3,1},{4,6},{5,7},{6,4},{7,5},{8,10},{9,11},{10,... | collective-permute-start | bytes 786440 | tf_op jit(solution)/shard_map/ppermute | solution.py:654
  54.4 5.0 %collective-permute-start.16 = (bf16[4,256,128]{2,1,0:T(8,128)(2,1)S(1)}, bf16[4,256,128]{2,1,0:T(8,128)(2,1)S(1)}, u32[]{:S(2)}, u32[]{:S(2)}) collective-permute-start(bf16[4,256,128]{2,1,0:T(8,128)(2,1)S(1)} %join.2.after_ref.refs_0_), channel_id=1, source_target_pairs={{0,1},{1,0},{2,3},{3,2},{4,5},{5,4},{6,7},{7,6},{8,9},{9,8},{10,11... | collective-permute-start | bytes 786440 | tf_op jit(solution)/shard_map/ppermute | solution.py:650
  59.3 1.6 %collective-permute-start.15 = (bf16[4,256,128]{2,1,0:T(8,128)(2,1)S(1)}, bf16[4,256,128]{2,1,0:T(8,128)(2,1)S(1)}, u32[]{:S(2)}, u32[]{:S(2)}) collective-permute-start(bf16[4,256,128]{2,1,0:T(8,128)(2,1)S(1)} %relay.2.refs_1_), channel_id=1, source_target_pairs={{0,1},{1,0},{2,3},{3,2},{4,5},{5,4},{6,7},{7,6},{8,9},{9,8},{10,11... | collective-permute-start | bytes 786440 | tf_op jit(solution)/shard_map/ppermute | solution.py:650
  62.0 2.0 %collective-permute-start.17 = (f32[520,256]{1,0:T(8,128)S(1)}, f32[520,256]{1,0:T(8,128)S(1)}, u32[]{:S(2)}, u32[]{:S(2)}) collective-permute-start(f32[520,256]{1,0:T(8,128)S(1)} %get-tuple-element.80), channel_id=1, source_target_pairs={{0,1},{1,0},{2,3},{3,2},{4,5},{5,4},{6,7},{7,6},{8,9},{9,8},{10,11... | collective-permute-start | bytes 1597448 | tf_op jit(solution)/shard_map/ppermute | solution.py:650
  64.6 7.0 %collective-permute-start.18 = (f32[512,256]{1,0:T(8,128)S(1)}, f32[512,256]{1,0:T(8,128)S(1)}, u32[]{:S(2)}, u32[]{:S(2)}) collective-permute-start(f32[512,256]{1,0:T(8,128)S(1)} %back_side.1), channel_id=1, source_target_pairs={{0,1},{1,0},{2,3},{3,2},{4,5},{5,4},{6,7},{7,6},{8,9},{9,8},{10,11... | collective-permute-start | bytes 1572872 | tf_op jit(solution)/shard_map/ppermute | solution.py:650
  65.1 6.5 %collective-permute-start.20 = (s16[272,256]{1,0:T(8,128)(2,1)S(1)}, s16[272,256]{1,0:T(8,128)(2,1)S(1)}, u32[]{:S(2)}, u32[]{:S(2)}) collective-permute-start(s16[272,256]{1,0:T(8,128)(2,1)S(1)} %get-tuple-element.82.refs_0_), channel_id=1, source_target_pairs={{0,2},{1,3},{2,0},{3,1},{4,6},{5,7},{6,4},{7,5},{8,10},{9,11},{10,... | collective-permute-start | bytes 417800 | tf_op jit(solution)/shard_map/ppermute | solution.py:654
  66.6 7.5 %collective-permute-start.19 = (s16[272,256]{1,0:T(8,128)(2,1)S(1)}, s16[272,256]{1,0:T(8,128)(2,1)S(1)}, u32[]{:S(2)}, u32[]{:S(2)}) collective-permute-start(s16[272,256]{1,0:T(8,128)(2,1)S(1)} %get-tuple-element.83), channel_id=1, source_target_pairs={{0,2},{1,3},{2,0},{3,1},{4,6},{5,7},{6,4},{7,5},{8,10},{9,11},{10,... | collective-permute-start | bytes 417800 | tf_op jit(solution)/shard_map/ppermute | solution.py:654
  71.7 7.0 %collective-permute-start.21 = (s16[144,256]{1,0:T(8,128)(2,1)S(1)}, s16[144,256]{1,0:T(8,128)(2,1)S(1)}, u32[]{:S(2)}, u32[]{:S(2)}) collective-permute-start(s16[144,256]{1,0:T(8,128)(2,1)S(1)} %get-tuple-element.87), channel_id=1, source_target_pairs={{0,8},{1,9},{2,10},{3,11},{4,12},{5,13},{6,14},{7,15},{8,0},{9,1},... | collective-permute-start | bytes 221192 | tf_op jit(solution)/shard_map/ppermute | solution.py:658
  72.0 6.7 %collective-permute-start.22 = (s16[144,256]{1,0:T(8,128)(2,1)S(1)}, s16[144,256]{1,0:T(8,128)(2,1)S(1)}, u32[]{:S(2)}, u32[]{:S(2)}) collective-permute-start(s16[144,256]{1,0:T(8,128)(2,1)S(1)} %get-tuple-element.88), channel_id=1, source_target_pairs={{0,12},{1,13},{2,14},{3,15},{4,8},{5,9},{6,10},{7,11},{8,4},{9,5},... | collective-permute-start | bytes 221192 | tf_op jit(solution)/shard_map/ppermute | solution.py:658
  74.1 5.3 %collective-permute-start.23 = (s16[144,256]{1,0:T(8,128)(2,1)S(1)}, s16[144,256]{1,0:T(8,128)(2,1)S(1)}, u32[]{:S(2)}, u32[]{:S(2)}) collective-permute-start(s16[144,256]{1,0:T(8,128)(2,1)S(1)} %get-tuple-element.89), channel_id=1, source_target_pairs={{0,4},{1,5},{2,6},{3,7},{4,0},{5,1},{6,2},{7,3},{8,12},{9,13},{10,... | collective-permute-start | bytes 221192 | tf_op jit(solution)/shard_map/ppermute | solution.py:658
  83.0 5.4 %collective-permute-start.26 = (bf16[256,128]{1,0:T(8,128)(2,1)S(1)}, bf16[256,128]{1,0:T(8,128)(2,1)S(1)}, u32[]{:S(2)}, u32[]{:S(2)}) collective-permute-start(bf16[256,128]{1,0:T(8,128)(2,1)S(1)} %get-tuple-element.91.refs_3_), channel_id=1, source_target_pairs={{0,4},{1,5},{2,6},{3,7},{4,0},{5,1},{6,2},{7,3},{8,12},{9,13},{10,... | collective-permute-start | bytes 196616 | tf_op jit(solution)/shard_map/ppermute | solution.py:658
  83.6 6.1 %collective-permute-start.25 = (bf16[256,128]{1,0:T(8,128)(2,1)S(1)}, bf16[256,128]{1,0:T(8,128)(2,1)S(1)}, u32[]{:S(2)}, u32[]{:S(2)}) collective-permute-start(bf16[256,128]{1,0:T(8,128)(2,1)S(1)} %get-tuple-element.91.refs_3_), channel_id=1, source_target_pairs={{0,12},{1,13},{2,14},{3,15},{4,8},{5,9},{6,10},{7,11},{8,4},{9,5},... | collective-permute-start | bytes 196616 | tf_op jit(solution)/shard_map/ppermute | solution.py:658
  85.5 5.9 %collective-permute-start.24 = (bf16[256,128]{1,0:T(8,128)(2,1)S(1)}, bf16[256,128]{1,0:T(8,128)(2,1)S(1)}, u32[]{:S(2)}, u32[]{:S(2)}) collective-permute-start(bf16[256,128]{1,0:T(8,128)(2,1)S(1)} %get-tuple-element.91.refs_3_), channel_id=1, source_target_pairs={{0,8},{1,9},{2,10},{3,11},{4,12},{5,13},{6,14},{7,15},{8,0},{9,1},... | collective-permute-start | bytes 196616 | tf_op jit(solution)/shard_map/ppermute | solution.py:658
  91.4 6.4 %collective-permute-start.27 = (bf16[4,256,128]{2,1,0:T(8,128)(2,1)S(1)}, bf16[4,256,128]{2,1,0:T(8,128)(2,1)S(1)}, u32[]{:S(2)}, u32[]{:S(2)}) collective-permute-start(bf16[4,256,128]{2,1,0:T(8,128)(2,1)S(1)} %join.3.after_ref.refs_0_), channel_id=1, source_target_pairs={{0,2},{1,3},{2,0},{3,1},{4,6},{5,7},{6,4},{7,5},{8,10},{9,11},{10,... | collective-permute-start | bytes 786440 | tf_op jit(solution)/shard_map/ppermute | solution.py:654
  93.0 4.9 %collective-permute-start.29 = (bf16[4,256,128]{2,1,0:T(8,128)(2,1)S(1)}, bf16[4,256,128]{2,1,0:T(8,128)(2,1)S(1)}, u32[]{:S(2)}, u32[]{:S(2)}) collective-permute-start(bf16[4,256,128]{2,1,0:T(8,128)(2,1)S(1)} %join.3.after_ref.refs_0_), channel_id=1, source_target_pairs={{0,1},{1,0},{2,3},{3,2},{4,5},{5,4},{6,7},{7,6},{8,9},{9,8},{10,11... | collective-permute-start | bytes 786440 | tf_op jit(solution)/shard_map/ppermute | solution.py:650
  101.4 3.7 %collective-permute-start.31 = (f32[8,256]{1,0:T(8,128)S(1)}, f32[8,256]{1,0:T(8,128)S(1)}, u32[]{:S(2)}, u32[]{:S(2)}) collective-permute-start(f32[8,256]{1,0:T(8,128)S(1)} %add.17), channel_id=1, source_target_pairs={{0,2},{1,3},{2,0},{3,1},{4,6},{5,7},{6,4},{7,5},{8,10},{9,11},{10,... | collective-permute-start | bytes 24584 | tf_op jit(solution)/shard_map/ppermute | solution.py:654
  105.1 5.4 %collective-permute-start.34 = (f32[8,256]{1,0:T(8,128)S(1)}, f32[8,256]{1,0:T(8,128)S(1)}, u32[]{:S(2)}, u32[]{:S(2)}) collective-permute-start(f32[8,256]{1,0:T(8,128)S(1)} %add.18.refs_0_), channel_id=1, source_target_pairs={{0,12},{1,13},{2,14},{3,15},{4,8},{5,9},{6,10},{7,11},{8,4},{9,5},... | collective-permute-start | bytes 24584 | tf_op jit(solution)/shard_map/ppermute | solution.py:658
  107.0 4.5 %collective-permute-start.33 = (f32[8,256]{1,0:T(8,128)S(1)}, f32[8,256]{1,0:T(8,128)S(1)}, u32[]{:S(2)}, u32[]{:S(2)}) collective-permute-start(f32[8,256]{1,0:T(8,128)S(1)} %add.18.refs_0_), channel_id=1, source_target_pairs={{0,8},{1,9},{2,10},{3,11},{4,12},{5,13},{6,14},{7,15},{8,0},{9,1},... | collective-permute-start | bytes 24584 | tf_op jit(solution)/shard_map/ppermute | solution.py:658
  107.0 4.5 %collective-permute-start.32 = (f32[8,256]{1,0:T(8,128)S(1)}, f32[8,256]{1,0:T(8,128)S(1)}, u32[]{:S(2)}, u32[]{:S(2)}) collective-permute-start(f32[8,256]{1,0:T(8,128)S(1)} %add.18.refs_0_), channel_id=1, source_target_pairs={{0,4},{1,5},{2,6},{3,7},{4,0},{5,1},{6,2},{7,3},{8,12},{9,13},{10,... | collective-permute-start | bytes 24584 | tf_op jit(solution)/shard_map/ppermute | solution.py:658
  (11 other events, 66.6 us)

commit v13 on v12

--- a/solution.py
+++ b/solution.py
@@ -370,7 +370,7 @@
 
 
 BATCH = 16
-SOME = 8
+SOME = 10
 
 
 def coarse_kernel(packed, second, after, e_ref, k_ref, own_ref, *refs):
@@ -599,7 +599,7 @@
     )(at, v, *after)
 
 
-OUT_CUTS = 4
+OUT_CUTS = 8
 
 
 def result_kernel(count, l0_ref, *refs):

time: 114 us -> 114 us (level)
  no operation moved by 1% of the time
where the time goes in v13:
time: 114 us
  starting transfers between devices  39.2 us (34%)
  waiting for transfers between devices  34.5 us (30%)
  Pallas kernels  33.5 us (29%)
  local copies, waits for them, and re-layouts  3.89 us (3%)
  other arithmetic  1.62 us (1%)
  between operations  1.17 us (1%)
    ppermute x17, starting transfers between devices, over_z(): return lax.ppermute(x, 'space', [(i, i ^ 4 * k) for i in range(GROUP)])  24.9 us
    ppermute x17, waiting for transfers between devices, over_z(): return lax.ppermute(x, 'space', [(i, i ^ 4 * k) for i in range(GROUP)])  19.5 us
    ppermute x8, waiting for transfers between devices, over_y(): return lax.ppermute(x, 'space', [(i, i ^ 2) for i in range(GROUP)])  12.1 us
    ppermute x8, starting transfers between devices, over_y(): return lax.ppermute(x, 'space', [(i, i ^ 2) for i in range(GROUP)])  11.7 us
    pallas_call x2, Pallas kernels, project(): pl.pallas_call(project_kernel, in_specs=[VMEM] * 4, out_specs=[VMEM] * 2,...  7.47 us
    pallas_call x2, Pallas kernels, coarse_image(): pl.pallas_call(functools.partial(coarse_kernel, len(got), second, len(aft...  6.96 us
    pallas_call x3, Pallas kernels, adjoint_near(): pl.pallas_call(functools.partial(near_kernel, base), in_specs=[VMEM] * le...  6.57 us
    unnamed x17, local copies, waits for them, and re-layouts  3.89 us
  transfers between devices with their start and end apart: 35, of which 24 were waited for; matrix products, arithmetic and copies ran while one was open for 4% of the time, Pallas kernels for 14%

profile of v13, /device:TPU:0, one launch (start us, length us, event | category | flops | bytes accessed | tf_op | source)
XLA Modules:
  0.0 113.9 jit_solution(8166730578578409774)
XLA Ops:
  3.4 2.9 %collective-permute-start.1 = (s32[8,128]{1,0:T(8,128)S(1)}, s32[8,128]{1,0:T(8,128)S(1)}, u32[]{:S(2)}, u32[]{:S(2)}) collective-permute-start(s32[8,128]{1,0:T(8,128)S(1)} %get-tuple-element.54), channel_id=1, source_target_pairs={{0,2},{1,3},{2,0},{3,1},{4,6},{5,7},{6,4},{7,5},{8,10},{9,11},{10,... | collective-permute-start | bytes 12296 | tf_op jit(solution)/shard_map/ppermute | solution.py:654
  6.2 1.6 %collective-permute-done.1.got_ref = s32[8,128]{1,0:T(8,128)S(1)} collective-permute-done((s32[8,128]{1,0:T(8,128)S(1)}, s32[8,128]{1,0:T(8,128)S(1)}, u32[]{:S(2)}, u32[]{:S(2)}) %collective-permute-start.1) | collective-permute-done | bytes 4128 | tf_op jit(solution)/shard_map/ppermute | solution.py:654
  7.8 2.1 %collective-permute-start.2 = (s32[8,128]{1,0:T(8,128)S(1)}, s32[8,128]{1,0:T(8,128)S(1)}, u32[]{:S(2)}, u32[]{:S(2)}) collective-permute-start(s32[8,128]{1,0:T(8,128)S(1)} %get-tuple-element.56), channel_id=1, source_target_pairs={{0,4},{1,5},{2,6},{3,7},{4,0},{5,1},{6,2},{7,3},{8,12},{9,13},{10,... | collective-permute-start | bytes 12296 | tf_op jit(solution)/shard_map/ppermute | solution.py:658
  11.6 3.0 %collective-permute-start.3 = (s32[8,128]{1,0:T(8,128)S(1)}, s32[8,128]{1,0:T(8,128)S(1)}, u32[]{:S(2)}, u32[]{:S(2)}) collective-permute-start(s32[8,128]{1,0:T(8,128)S(1)} %get-tuple-element.58), channel_id=1, source_target_pairs={{0,8},{1,9},{2,10},{3,11},{4,12},{5,13},{6,14},{7,15},{8,0},{9,1},... | collective-permute-start | bytes 12296 | tf_op jit(solution)/shard_map/ppermute | solution.py:658
  14.6 1.6 %collective-permute-done.3.refs_1_ = s32[8,128]{1,0:T(8,128)S(1)} collective-permute-done((s32[8,128]{1,0:T(8,128)S(1)}, s32[8,128]{1,0:T(8,128)S(1)}, u32[]{:S(2)}, u32[]{:S(2)}) %collective-permute-start.3) | collective-permute-done | bytes 4128 | tf_op jit(solution)/shard_map/ppermute | solution.py:658
  16.2 2.9 %adjoint_far.1 = (s32[4,1152]{1,0:T(4,128)S(1)}, f32[4,1152]{1,0:T(4,128)S(1)}, bf16[512,1152]{1,0:T(8,128)(2,1)S(1)}, f32[512,256]{1,0:T(8,128)S(1)}) custom-call(s32[4]{0:T(128)S(1)} %pad_add_fusion.me_ref, s32[8,128]{1,0:T(8,128)S(1)} %get-tuple-element.57.refs_0_, s32[8,128]{1,0:T(8,128)S(1)} %collective-permute-done.3.refs_1_, ...), custom_call_target="tpu_custom_call" | custom-call | flops 905969664 | bytes 2000000 | tf_op jit(solution)/shard_map/adjoint_far/pallas_call | solution.py:135
  19.2 2.2 %adjoint_near.1 = (bf16[512,1152]{1,0:T(8,128)(2,1)S(1)}, f32[512,256]{1,0:T(8,128)S(1)}) custom-call(s32[4,1152]{1,0:T(4,128)S(1)} %get-tuple-element.59.ids_ref, f32[4,1152]{1,0:T(4,128)S(1)} %get-tuple-element.60.weight_ref, bf16[1152,256]{1,0:T(8,128)(2,1)S(1)} %get-tuple-element.101.refs_3_.wh_ref, bf16[1152,256]{1,0:T(8,128)(2,1)S(1)} %get-tuple-element.100.refs_4_.wl_ref), custom_call_target="tpu_custom_call" | custom-call | flops 905969664 | bytes 2000000 | tf_op jit(solution)/shard_map/adjoint_near/pallas_call | solution.py:150
  21.5 2.2 %adjoint_side.1 = (bf16[512,1152]{1,0:T(8,128)(2,1)S(1)}, f32[512,256]{1,0:T(8,128)S(1)}) custom-call(s32[4,1152]{1,0:T(4,128)S(1)} %get-tuple-element.59.ids_ref, f32[4,1152]{1,0:T(4,128)S(1)} %get-tuple-element.60.weight_ref, bf16[1152,256]{1,0:T(8,128)(2,1)S(1)} %get-tuple-element.101.refs_3_.wh_ref, ...), custom_call_target="tpu_custom_call" | custom-call | flops 905969664 | bytes 2000000 | tf_op jit(solution)/shard_map/adjoint_side/pallas_call | solution.py:150
  24.3 1.9 %collective-permute-start.7 = (s16[272,256]{1,0:T(8,128)(2,1)S(1)}, s16[272,256]{1,0:T(8,128)(2,1)S(1)}, u32[]{:S(2)}, u32[]{:S(2)}) collective-permute-start(s16[272,256]{1,0:T(8,128)(2,1)S(1)} %get-tuple-element.65.refs_0_), channel_id=1, source_target_pairs={{0,2},{1,3},{2,0},{3,1},{4,6},{5,7},{6,4},{7,5},{8,10},{9,11},{10,... | collective-permute-start | bytes 417800 | tf_op jit(solution)/shard_map/ppermute | solution.py:654
  26.3 2.2 %adjoint_stay.1 = (bf16[512,1152]{1,0:T(8,128)(2,1)S(1)}, f32[512,256]{1,0:T(8,128)S(1)}) custom-call(s32[4,1152]{1,0:T(4,128)S(1)} %get-tuple-element.59.ids_ref, f32[4,1152]{1,0:T(4,128)S(1)} %get-tuple-element.60.weight_ref, bf16[1152,256]{1,0:T(8,128)(2,1)S(1)} %get-tuple-element.101.refs_3_.wh_ref, bf16[1152,256]{1,0:T(8,128)(2,1)S(1)} %get-tuple-element.100.refs_4_.wl_ref), custom_call_target="tpu_custom_call" | custom-call | flops 905969664 | bytes 2000000 | tf_op jit(solution)/shard_map/adjoint_stay/pallas_call | solution.py:150
  28.5 2.3 %collective-permute-done.7.p_ref = s16[272,256]{1,0:T(8,128)(2,1)S(1)} collective-permute-done((s16[272,256]{1,0:T(8,128)(2,1)S(1)}, s16[272,256]{1,0:T(8,128)(2,1)S(1)}, u32[]{:S(2)}, u32[]{:S(2)}) %collective-permute-start.7) | collective-permute-done | bytes 139296 | tf_op jit(solution)/shard_map/ppermute | solution.py:654
  30.9 3.0 %collective-permute-start.8 = (s16[144,256]{1,0:T(8,128)(2,1)S(1)}, s16[144,256]{1,0:T(8,128)(2,1)S(1)}, u32[]{:S(2)}, u32[]{:S(2)}) collective-permute-start(s16[144,256]{1,0:T(8,128)(2,1)S(1)} %get-tuple-element.69), channel_id=1, source_target_pairs={{0,8},{1,9},{2,10},{3,11},{4,12},{5,13},{6,14},{7,15},{8,0},{9,1},... | collective-permute-start | bytes 221192 | tf_op jit(solution)/shard_map/ppermute | solution.py:658
  35.7 3.1 %copy.12 = bf16[80,128,256]{2,0,1:T(8,128)(2,1)S(1)} copy(bf16[80,128,256]{2,1,0:T(8,128)(2,1)S(1)} %bitcast.12) | data formatting | bytes 10485760 | tf_op args[0]
  40.6 3.4 %coarse_first.1 = (bf16[256,128]{1,0:T(8,128)(2,1)S(1)}, f32[128,256]{1,0:T(8,128)S(1)}, f32[8,256]{1,0:T(8,128)S(1)}) custom-call(bf16[80,128,256]{2,1,0:T(8,128)(2,1)S(1)} %bitcast.12, bf16[256,256]{1,0:T(8,128)(2,1)S(1)} %copy-done.1, f32[128,256]{1,0:T(8,128)S(1)} %get-tuple-element.68.own_ref, s16[144,256]{1,0:T(8,128)(2,1)S(1)} %collective-permute-done.8.refs_0_, ...), custom_call_target="tpu_custom_call" | custom-call | flops 1342177280 | bytes 5000000 | tf_op jit(solution)/shard_map/coarse_first/pallas_call | solution.py:435
  44.3 2.8 %collective-permute-start.12 = (bf16[256,128]{1,0:T(8,128)(2,1)S(1)}, bf16[256,128]{1,0:T(8,128)(2,1)S(1)}, u32[]{:S(2)}, u32[]{:S(2)}) collective-permute-start(bf16[256,128]{1,0:T(8,128)(2,1)S(1)} %get-tuple-element.72.refs_3_), channel_id=1, source_target_pairs={{0,12},{1,13},{2,14},{3,15},{4,8},{5,9},{6,10},{7,11},{8,4},{9,5},... | collective-permute-start | bytes 196616 | tf_op jit(solution)/shard_map/ppermute | solution.py:658
  48.7 1.8 %collective-permute-done.12.refs_1_ = bf16[256,128]{1,0:T(8,128)(2,1)S(1)} collective-permute-done((bf16[256,128]{1,0:T(8,128)(2,1)S(1)}, bf16[256,128]{1,0:T(8,128)(2,1)S(1)}, u32[]{:S(2)}, u32[]{:S(2)}) %collective-permute-start.12) | collective-permute-done | bytes 65568 | tf_op jit(solution)/shard_map/ppermute | solution.py:658
  50.4 2.3 %collective-permute-done.11.refs_0_ = bf16[256,128]{1,0:T(8,128)(2,1)S(1)} collective-permute-done((bf16[256,128]{1,0:T(8,128)(2,1)S(1)}, bf16[256,128]{1,0:T(8,128)(2,1)S(1)}, u32[]{:S(2)}, u32[]{:S(2)}) %collective-permute-start.11) | collective-permute-done | bytes 65568 | tf_op jit(solution)/shard_map/ppermute | solution.py:658
  52.8 1.6 %collective-permute-start.14 = (bf16[4,256,128]{2,1,0:T(8,128)(2,1)S(1)}, bf16[4,256,128]{2,1,0:T(8,128)(2,1)S(1)}, u32[]{:S(2)}, u32[]{:S(2)}) collective-permute-start(bf16[4,256,128]{2,1,0:T(8,128)(2,1)S(1)} %join.2.after_ref.refs_0_), channel_id=1, source_target_pairs={{0,2},{1,3},{2,0},{3,1},{4,6},{5,7},{6,4},{7,5},{8,10},{9,11},{10,... | collective-permute-start | bytes 786440 | tf_op jit(solution)/shard_map/ppermute | solution.py:654
  54.4 3.6 %project.2 = (f32[80,8192]{1,0:T(8,128)S(1)}, f32[8,128]{1,0:T(8,128)S(1)}) custom-call(bf16[128,80,256]{2,1,0:T(8,128)(2,1)S(1)} %bitcast.9, f32[128,256]{1,0:T(8,128)S(1)} %get-tuple-element.73.y_ref.refs_3_, bf16[2,256,128]{2,1,0:T(8,128)(2,1)S(1)} %copy-done.2, bf16[4,256,128]{2,1,0:T(8,128)(2,1)S(1)} %join.2.after_ref.refs_0_), custom_call_target="tpu_custom_call" | custom-call | flops 1342177280 | bytes 8000000 | tf_op jit(solution)/shard_map/project/pallas_call | solution.py:473
  67.6 4.0 %collective-permute-done.20.p_ref = s16[272,256]{1,0:T(8,128)(2,1)S(1)} collective-permute-done((s16[272,256]{1,0:T(8,128)(2,1)S(1)}, s16[272,256]{1,0:T(8,128)(2,1)S(1)}, u32[]{:S(2)}, u32[]{:S(2)}) %collective-permute-start.20) | collective-permute-done | bytes 139296 | tf_op jit(solution)/shard_map/ppermute | solution.py:654
  72.0 2.0 %collective-permute-start.22 = (s16[144,256]{1,0:T(8,128)(2,1)S(1)}, s16[144,256]{1,0:T(8,128)(2,1)S(1)}, u32[]{:S(2)}, u32[]{:S(2)}) collective-permute-start(s16[144,256]{1,0:T(8,128)(2,1)S(1)} %get-tuple-element.88), channel_id=1, source_target_pairs={{0,12},{1,13},{2,14},{3,15},{4,8},{5,9},{6,10},{7,11},{8,4},{9,5},... | collective-permute-start | bytes 221192 | tf_op jit(solution)/shard_map/ppermute | solution.py:658
  75.4 3.3 %collective-permute-done.21.refs_0_ = s16[144,256]{1,0:T(8,128)(2,1)S(1)} collective-permute-done((s16[144,256]{1,0:T(8,128)(2,1)S(1)}, s16[144,256]{1,0:T(8,128)(2,1)S(1)}, u32[]{:S(2)}, u32[]{:S(2)}) %collective-permute-start.21) | collective-permute-done | bytes 73760 | tf_op jit(solution)/shard_map/ppermute | solution.py:658
  79.4 3.5 %coarse_second.1 = (bf16[256,128]{1,0:T(8,128)(2,1)S(1)}, f32[128,256]{1,0:T(8,128)S(1)}, f32[8,128]{1,0:T(8,128)S(1)}, f32[8,256]{1,0:T(8,128)S(1)}) custom-call(bf16[80,128,256]{2,1,0:T(8,128)(2,1)S(1)} %bitcast.12, bf16[256,256]{1,0:T(8,128)(2,1)S(1)} %copy-done.1, f32[128,256]{1,0:T(8,128)S(1)} %get-tuple-element.86.own_ref, ...), custom_call_target="tpu_custom_call" | custom-call | flops 1342177280 | bytes 5000000 | tf_op jit(solution)/shard_map/coarse_second/pallas_call | solution.py:435
  83.6 1.8 %collective-permute-start.25 = (bf16[256,128]{1,0:T(8,128)(2,1)S(1)}, bf16[256,128]{1,0:T(8,128)(2,1)S(1)}, u32[]{:S(2)}, u32[]{:S(2)}) collective-permute-start(bf16[256,128]{1,0:T(8,128)(2,1)S(1)} %get-tuple-element.91.refs_3_), channel_id=1, source_target_pairs={{0,12},{1,13},{2,14},{3,15},{4,8},{5,9},{6,10},{7,11},{8,4},{9,5},... | collective-permute-start | bytes 196616 | tf_op jit(solution)/shard_map/ppermute | solution.py:658
  86.5 1.9 %collective-permute-done.26.refs_2_ = bf16[256,128]{1,0:T(8,128)(2,1)S(1)} collective-permute-done((bf16[256,128]{1,0:T(8,128)(2,1)S(1)}, bf16[256,128]{1,0:T(8,128)(2,1)S(1)}, u32[]{:S(2)}, u32[]{:S(2)}) %collective-permute-start.26) | collective-permute-done | bytes 65568 | tf_op jit(solution)/shard_map/ppermute | solution.py:658
  89.7 1.6 %collective-permute-done.24.refs_0_ = bf16[256,128]{1,0:T(8,128)(2,1)S(1)} collective-permute-done((bf16[256,128]{1,0:T(8,128)(2,1)S(1)}, bf16[256,128]{1,0:T(8,128)(2,1)S(1)}, u32[]{:S(2)}, u32[]{:S(2)}) %collective-permute-start.24) | collective-permute-done | bytes 65568 | tf_op jit(solution)/shard_map/ppermute | solution.py:658
  91.3 1.6 %collective-permute-start.27 = (bf16[4,256,128]{2,1,0:T(8,128)(2,1)S(1)}, bf16[4,256,128]{2,1,0:T(8,128)(2,1)S(1)}, u32[]{:S(2)}, u32[]{:S(2)}) collective-permute-start(bf16[4,256,128]{2,1,0:T(8,128)(2,1)S(1)} %join.3.after_ref.refs_0_), channel_id=1, source_target_pairs={{0,2},{1,3},{2,0},{3,1},{4,6},{5,7},{6,4},{7,5},{8,10},{9,11},{10,... | collective-permute-start | bytes 786440 | tf_op jit(solution)/shard_map/ppermute | solution.py:654
  92.9 3.8 %project.3 = (f32[80,8192]{1,0:T(8,128)S(1)}, f32[8,128]{1,0:T(8,128)S(1)}) custom-call(bf16[128,80,256]{2,1,0:T(8,128)(2,1)S(1)} %bitcast.10, f32[128,256]{1,0:T(8,128)S(1)} %get-tuple-element.92.y_ref, bf16[2,256,128]{2,1,0:T(8,128)(2,1)S(1)} %copy-done.2, bf16[4,256,128]{2,1,0:T(8,128)(2,1)S(1)} %join.3.after_ref.refs_0_), custom_call_target="tpu_custom_call" | custom-call | flops 1342177280 | bytes 8000000 | tf_op jit(solution)/shard_map/project/pallas_call | solution.py:473
  102.9 2.1 %collective-permute-done.31 = f32[8,256]{1,0:T(8,128)S(1)} collective-permute-done((f32[8,256]{1,0:T(8,128)S(1)}, f32[8,256]{1,0:T(8,128)S(1)}, u32[]{:S(2)}, u32[]{:S(2)}) %collective-permute-start.31) | collective-permute-done | bytes 8224 | tf_op jit(solution)/shard_map/ppermute | solution.py:654
  105.0 2.0 %collective-permute-start.34 = (f32[8,256]{1,0:T(8,128)S(1)}, f32[8,256]{1,0:T(8,128)S(1)}, u32[]{:S(2)}, u32[]{:S(2)}) collective-permute-start(f32[8,256]{1,0:T(8,128)S(1)} %add.18.refs_0_), channel_id=1, source_target_pairs={{0,12},{1,13},{2,14},{3,15},{4,8},{5,9},{6,10},{7,11},{8,4},{9,5},... | collective-permute-start | bytes 24584 | tf_op jit(solution)/shard_map/ppermute | solution.py:658
  107.0 2.4 %collective-permute-start.32 = (f32[8,256]{1,0:T(8,128)S(1)}, f32[8,256]{1,0:T(8,128)S(1)}, u32[]{:S(2)}, u32[]{:S(2)}) collective-permute-start(f32[8,256]{1,0:T(8,128)S(1)} %add.18.refs_0_), channel_id=1, source_target_pairs={{0,4},{1,5},{2,6},{3,7},{4,0},{5,1},{6,2},{7,3},{8,12},{9,13},{10,... | collective-permute-start | bytes 24584 | tf_op jit(solution)/shard_map/ppermute | solution.py:658
  111.5 2.2 %result.1 = (f32[80,8192]{1,0:T(8,128)}, f32[1152,256]{1,0:T(8,128)}) custom-call(f32[8,128]{1,0:T(8,128)S(1)} %get-tuple-element.90.l0_ref, f32[8,256]{1,0:T(8,128)S(1)} %add.18.refs_0_, f32[8,256]{1,0:T(8,128)S(1)} %collective-permute-done.32.refs_1_, f32[8,256]{1,0:T(8,128)S(1)} %collective-permute-done.33.refs_2_, ...), custom_call_target="tpu_custom_call" | custom-call | flops 1966080 | bytes 10000000 | tf_op jit(solution)/shard_map/result/pallas_call | solution.py:633
  (92 shorter events, 34.0 us)
Async XLA Ops:
  3.4 4.4 %collective-permute-start.1 = (s32[8,128]{1,0:T(8,128)S(1)}, s32[8,128]{1,0:T(8,128)S(1)}, u32[]{:S(2)}, u32[]{:S(2)}) collective-permute-start(s32[8,128]{1,0:T(8,128)S(1)} %get-tuple-element.54), channel_id=1, source_target_pairs={{0,2},{1,3},{2,0},{3,1},{4,6},{5,7},{6,4},{7,5},{8,10},{9,11},{10,... | collective-permute-start | bytes 12296 | tf_op jit(solution)/shard_map/ppermute | solution.py:654
  7.8 3.7 %collective-permute-start.2 = (s32[8,128]{1,0:T(8,128)S(1)}, s32[8,128]{1,0:T(8,128)S(1)}, u32[]{:S(2)}, u32[]{:S(2)}) collective-permute-start(s32[8,128]{1,0:T(8,128)S(1)} %get-tuple-element.56), channel_id=1, source_target_pairs={{0,4},{1,5},{2,6},{3,7},{4,0},{5,1},{6,2},{7,3},{8,12},{9,13},{10,... | collective-permute-start | bytes 12296 | tf_op jit(solution)/shard_map/ppermute | solution.py:658
  11.6 4.6 %collective-permute-start.3 = (s32[8,128]{1,0:T(8,128)S(1)}, s32[8,128]{1,0:T(8,128)S(1)}, u32[]{:S(2)}, u32[]{:S(2)}) collective-permute-start(s32[8,128]{1,0:T(8,128)S(1)} %get-tuple-element.58), channel_id=1, source_target_pairs={{0,8},{1,9},{2,10},{3,11},{4,12},{5,13},{6,14},{7,15},{8,0},{9,1},... | collective-permute-start | bytes 12296 | tf_op jit(solution)/shard_map/ppermute | solution.py:658
  19.1 2.3 %collective-permute-start.4 = (f32[512,256]{1,0:T(8,128)S(1)}, f32[512,256]{1,0:T(8,128)S(1)}, u32[]{:S(2)}, u32[]{:S(2)}) collective-permute-start(f32[512,256]{1,0:T(8,128)S(1)} %get-tuple-element.64), channel_id=1, source_target_pairs={{0,1},{1,0},{2,3},{3,2},{4,5},{5,4},{6,7},{7,6},{8,9},{9,8},{10,11... | collective-permute-start | bytes 1572872 | tf_op jit(solution)/shard_map/ppermute | solution.py:650
  23.7 7.1 %collective-permute-start.5 = (f32[512,256]{1,0:T(8,128)S(1)}, f32[512,256]{1,0:T(8,128)S(1)}, u32[]{:S(2)}, u32[]{:S(2)}) collective-permute-start(f32[512,256]{1,0:T(8,128)S(1)} %get-tuple-element.66), channel_id=1, source_target_pairs={{0,1},{1,0},{2,3},{3,2},{4,5},{5,4},{6,7},{7,6},{8,9},{9,8},{10,11... | collective-permute-start | bytes 1572872 | tf_op jit(solution)/shard_map/ppermute | solution.py:650
  24.3 6.5 %collective-permute-start.7 = (s16[272,256]{1,0:T(8,128)(2,1)S(1)}, s16[272,256]{1,0:T(8,128)(2,1)S(1)}, u32[]{:S(2)}, u32[]{:S(2)}) collective-permute-start(s16[272,256]{1,0:T(8,128)(2,1)S(1)} %get-tuple-element.65.refs_0_), channel_id=1, source_target_pairs={{0,2},{1,3},{2,0},{3,1},{4,6},{5,7},{6,4},{7,5},{8,10},{9,11},{10,... | collective-permute-start | bytes 417800 | tf_op jit(solution)/shard_map/ppermute | solution.py:654
  26.1 9.1 %collective-permute-start.6 = (s16[272,256]{1,0:T(8,128)(2,1)S(1)}, s16[272,256]{1,0:T(8,128)(2,1)S(1)}, u32[]{:S(2)}, u32[]{:S(2)}) collective-permute-start(s16[272,256]{1,0:T(8,128)(2,1)S(1)} %get-tuple-element.67), channel_id=1, source_target_pairs={{0,2},{1,3},{2,0},{3,1},{4,6},{5,7},{6,4},{7,5},{8,10},{9,11},{10,... | collective-permute-start | bytes 417800 | tf_op jit(solution)/shard_map/ppermute | solution.py:654
  30.9 7.9 %collective-permute-start.8 = (s16[144,256]{1,0:T(8,128)(2,1)S(1)}, s16[144,256]{1,0:T(8,128)(2,1)S(1)}, u32[]{:S(2)}, u32[]{:S(2)}) collective-permute-start(s16[144,256]{1,0:T(8,128)(2,1)S(1)} %get-tuple-element.69), channel_id=1, source_target_pairs={{0,8},{1,9},{2,10},{3,11},{4,12},{5,13},{6,14},{7,15},{8,0},{9,1},... | collective-permute-start | bytes 221192 | tf_op jit(solution)/shard_map/ppermute | solution.py:658
  33.9 6.3 %collective-permute-start.9 = (s16[144,256]{1,0:T(8,128)(2,1)S(1)}, s16[144,256]{1,0:T(8,128)(2,1)S(1)}, u32[]{:S(2)}, u32[]{:S(2)}) collective-permute-start(s16[144,256]{1,0:T(8,128)(2,1)S(1)} %get-tuple-element.70), channel_id=1, source_target_pairs={{0,12},{1,13},{2,14},{3,15},{4,8},{5,9},{6,10},{7,11},{8,4},{9,5},... | collective-permute-start | bytes 221192 | tf_op jit(solution)/shard_map/ppermute | solution.py:658
  35.4 5.2 %collective-permute-start.10 = (s16[144,256]{1,0:T(8,128)(2,1)S(1)}, s16[144,256]{1,0:T(8,128)(2,1)S(1)}, u32[]{:S(2)}, u32[]{:S(2)}) collective-permute-start(s16[144,256]{1,0:T(8,128)(2,1)S(1)} %get-tuple-element.71), channel_id=1, source_target_pairs={{0,4},{1,5},{2,6},{3,7},{4,0},{5,1},{6,2},{7,3},{8,12},{9,13},{10,... | collective-permute-start | bytes 221192 | tf_op jit(solution)/shard_map/ppermute | solution.py:658
  44.0 4.6 %collective-permute-start.13 = (bf16[256,128]{1,0:T(8,128)(2,1)S(1)}, bf16[256,128]{1,0:T(8,128)(2,1)S(1)}, u32[]{:S(2)}, u32[]{:S(2)}) collective-permute-start(bf16[256,128]{1,0:T(8,128)(2,1)S(1)} %get-tuple-element.72.refs_3_), channel_id=1, source_target_pairs={{0,4},{1,5},{2,6},{3,7},{4,0},{5,1},{6,2},{7,3},{8,12},{9,13},{10,... | collective-permute-start | bytes 196616 | tf_op jit(solution)/shard_map/ppermute | solution.py:658
  44.3 6.2 %collective-permute-start.12 = (bf16[256,128]{1,0:T(8,128)(2,1)S(1)}, bf16[256,128]{1,0:T(8,128)(2,1)S(1)}, u32[]{:S(2)}, u32[]{:S(2)}) collective-permute-start(bf16[256,128]{1,0:T(8,128)(2,1)S(1)} %get-tuple-element.72.refs_3_), channel_id=1, source_target_pairs={{0,12},{1,13},{2,14},{3,15},{4,8},{5,9},{6,10},{7,11},{8,4},{9,5},... | collective-permute-start | bytes 196616 | tf_op jit(solution)/shard_map/ppermute | solution.py:658
  47.1 5.7 %collective-permute-start.11 = (bf16[256,128]{1,0:T(8,128)(2,1)S(1)}, bf16[256,128]{1,0:T(8,128)(2,1)S(1)}, u32[]{:S(2)}, u32[]{:S(2)}) collective-permute-start(bf16[256,128]{1,0:T(8,128)(2,1)S(1)} %get-tuple-element.72.refs_3_), channel_id=1, source_target_pairs={{0,8},{1,9},{2,10},{3,11},{4,12},{5,13},{6,14},{7,15},{8,0},{9,1},... | collective-permute-start | bytes 196616 | tf_op jit(solution)/shard_map/ppermute | solution.py:658
  52.8 6.4 %collective-permute-start.14 = (bf16[4,256,128]{2,1,0:T(8,128)(2,1)S(1)}, bf16[4,256,128]{2,1,0:T(8,128)(2,1)S(1)}, u32[]{:S(2)}, u32[]{:S(2)}) collective-permute-start(bf16[4,256,128]{2,1,0:T(8,128)(2,1)S(1)} %join.2.after_ref.refs_0_), channel_id=1, source_target_pairs={{0,2},{1,3},{2,0},{3,1},{4,6},{5,7},{6,4},{7,5},{8,10},{9,11},{10,... | collective-permute-start | bytes 786440 | tf_op jit(solution)/shard_map/ppermute | solution.py:654
  54.4 5.0 %collective-permute-start.16 = (bf16[4,256,128]{2,1,0:T(8,128)(2,1)S(1)}, bf16[4,256,128]{2,1,0:T(8,128)(2,1)S(1)}, u32[]{:S(2)}, u32[]{:S(2)}) collective-permute-start(bf16[4,256,128]{2,1,0:T(8,128)(2,1)S(1)} %join.2.after_ref.refs_0_), channel_id=1, source_target_pairs={{0,1},{1,0},{2,3},{3,2},{4,5},{5,4},{6,7},{7,6},{8,9},{9,8},{10,11... | collective-permute-start | bytes 786440 | tf_op jit(solution)/shard_map/ppermute | solution.py:650
  59.2 1.6 %collective-permute-start.15 = (bf16[4,256,128]{2,1,0:T(8,128)(2,1)S(1)}, bf16[4,256,128]{2,1,0:T(8,128)(2,1)S(1)}, u32[]{:S(2)}, u32[]{:S(2)}) collective-permute-start(bf16[4,256,128]{2,1,0:T(8,128)(2,1)S(1)} %relay.2.refs_1_), channel_id=1, source_target_pairs={{0,1},{1,0},{2,3},{3,2},{4,5},{5,4},{6,7},{7,6},{8,9},{9,8},{10,11... | collective-permute-start | bytes 786440 | tf_op jit(solution)/shard_map/ppermute | solution.py:650
  61.9 2.0 %collective-permute-start.17 = (f32[520,256]{1,0:T(8,128)S(1)}, f32[520,256]{1,0:T(8,128)S(1)}, u32[]{:S(2)}, u32[]{:S(2)}) collective-permute-start(f32[520,256]{1,0:T(8,128)S(1)} %get-tuple-element.80), channel_id=1, source_target_pairs={{0,1},{1,0},{2,3},{3,2},{4,5},{5,4},{6,7},{7,6},{8,9},{9,8},{10,11... | collective-permute-start | bytes 1597448 | tf_op jit(solution)/shard_map/ppermute | solution.py:650
  64.6 7.0 %collective-permute-start.18 = (f32[512,256]{1,0:T(8,128)S(1)}, f32[512,256]{1,0:T(8,128)S(1)}, u32[]{:S(2)}, u32[]{:S(2)}) collective-permute-start(f32[512,256]{1,0:T(8,128)S(1)} %back_side.1), channel_id=1, source_target_pairs={{0,1},{1,0},{2,3},{3,2},{4,5},{5,4},{6,7},{7,6},{8,9},{9,8},{10,11... | collective-permute-start | bytes 1572872 | tf_op jit(solution)/shard_map/ppermute | solution.py:650
  65.0 6.5 %collective-permute-start.20 = (s16[272,256]{1,0:T(8,128)(2,1)S(1)}, s16[272,256]{1,0:T(8,128)(2,1)S(1)}, u32[]{:S(2)}, u32[]{:S(2)}) collective-permute-start(s16[272,256]{1,0:T(8,128)(2,1)S(1)} %get-tuple-element.82.refs_0_), channel_id=1, source_target_pairs={{0,2},{1,3},{2,0},{3,1},{4,6},{5,7},{6,4},{7,5},{8,10},{9,11},{10,... | collective-permute-start | bytes 417800 | tf_op jit(solution)/shard_map/ppermute | solution.py:654
  66.6 7.5 %collective-permute-start.19 = (s16[272,256]{1,0:T(8,128)(2,1)S(1)}, s16[272,256]{1,0:T(8,128)(2,1)S(1)}, u32[]{:S(2)}, u32[]{:S(2)}) collective-permute-start(s16[272,256]{1,0:T(8,128)(2,1)S(1)} %get-tuple-element.83), channel_id=1, source_target_pairs={{0,2},{1,3},{2,0},{3,1},{4,6},{5,7},{6,4},{7,5},{8,10},{9,11},{10,... | collective-permute-start | bytes 417800 | tf_op jit(solution)/shard_map/ppermute | solution.py:654
  71.7 7.0 %collective-permute-start.21 = (s16[144,256]{1,0:T(8,128)(2,1)S(1)}, s16[144,256]{1,0:T(8,128)(2,1)S(1)}, u32[]{:S(2)}, u32[]{:S(2)}) collective-permute-start(s16[144,256]{1,0:T(8,128)(2,1)S(1)} %get-tuple-element.87), channel_id=1, source_target_pairs={{0,8},{1,9},{2,10},{3,11},{4,12},{5,13},{6,14},{7,15},{8,0},{9,1},... | collective-permute-start | bytes 221192 | tf_op jit(solution)/shard_map/ppermute | solution.py:658
  72.0 6.7 %collective-permute-start.22 = (s16[144,256]{1,0:T(8,128)(2,1)S(1)}, s16[144,256]{1,0:T(8,128)(2,1)S(1)}, u32[]{:S(2)}, u32[]{:S(2)}) collective-permute-start(s16[144,256]{1,0:T(8,128)(2,1)S(1)} %get-tuple-element.88), channel_id=1, source_target_pairs={{0,12},{1,13},{2,14},{3,15},{4,8},{5,9},{6,10},{7,11},{8,4},{9,5},... | collective-permute-start | bytes 221192 | tf_op jit(solution)/shard_map/ppermute | solution.py:658
  74.1 5.3 %collective-permute-start.23 = (s16[144,256]{1,0:T(8,128)(2,1)S(1)}, s16[144,256]{1,0:T(8,128)(2,1)S(1)}, u32[]{:S(2)}, u32[]{:S(2)}) collective-permute-start(s16[144,256]{1,0:T(8,128)(2,1)S(1)} %get-tuple-element.89), channel_id=1, source_target_pairs={{0,4},{1,5},{2,6},{3,7},{4,0},{5,1},{6,2},{7,3},{8,12},{9,13},{10,... | collective-permute-start | bytes 221192 | tf_op jit(solution)/shard_map/ppermute | solution.py:658
  82.9 5.4 %collective-permute-start.26 = (bf16[256,128]{1,0:T(8,128)(2,1)S(1)}, bf16[256,128]{1,0:T(8,128)(2,1)S(1)}, u32[]{:S(2)}, u32[]{:S(2)}) collective-permute-start(bf16[256,128]{1,0:T(8,128)(2,1)S(1)} %get-tuple-element.91.refs_3_), channel_id=1, source_target_pairs={{0,4},{1,5},{2,6},{3,7},{4,0},{5,1},{6,2},{7,3},{8,12},{9,13},{10,... | collective-permute-start | bytes 196616 | tf_op jit(solution)/shard_map/ppermute | solution.py:658
  83.6 6.1 %collective-permute-start.25 = (bf16[256,128]{1,0:T(8,128)(2,1)S(1)}, bf16[256,128]{1,0:T(8,128)(2,1)S(1)}, u32[]{:S(2)}, u32[]{:S(2)}) collective-permute-start(bf16[256,128]{1,0:T(8,128)(2,1)S(1)} %get-tuple-element.91.refs_3_), channel_id=1, source_target_pairs={{0,12},{1,13},{2,14},{3,15},{4,8},{5,9},{6,10},{7,11},{8,4},{9,5},... | collective-permute-start | bytes 196616 | tf_op jit(solution)/shard_map/ppermute | solution.py:658
  85.4 5.9 %collective-permute-start.24 = (bf16[256,128]{1,0:T(8,128)(2,1)S(1)}, bf16[256,128]{1,0:T(8,128)(2,1)S(1)}, u32[]{:S(2)}, u32[]{:S(2)}) collective-permute-start(bf16[256,128]{1,0:T(8,128)(2,1)S(1)} %get-tuple-element.91.refs_3_), channel_id=1, source_target_pairs={{0,8},{1,9},{2,10},{3,11},{4,12},{5,13},{6,14},{7,15},{8,0},{9,1},... | collective-permute-start | bytes 196616 | tf_op jit(solution)/shard_map/ppermute | solution.py:658
  91.3 6.4 %collective-permute-start.27 = (bf16[4,256,128]{2,1,0:T(8,128)(2,1)S(1)}, bf16[4,256,128]{2,1,0:T(8,128)(2,1)S(1)}, u32[]{:S(2)}, u32[]{:S(2)}) collective-permute-start(bf16[4,256,128]{2,1,0:T(8,128)(2,1)S(1)} %join.3.after_ref.refs_0_), channel_id=1, source_target_pairs={{0,2},{1,3},{2,0},{3,1},{4,6},{5,7},{6,4},{7,5},{8,10},{9,11},{10,... | collective-permute-start | bytes 786440 | tf_op jit(solution)/shard_map/ppermute | solution.py:654
  92.9 4.9 %collective-permute-start.29 = (bf16[4,256,128]{2,1,0:T(8,128)(2,1)S(1)}, bf16[4,256,128]{2,1,0:T(8,128)(2,1)S(1)}, u32[]{:S(2)}, u32[]{:S(2)}) collective-permute-start(bf16[4,256,128]{2,1,0:T(8,128)(2,1)S(1)} %join.3.after_ref.refs_0_), channel_id=1, source_target_pairs={{0,1},{1,0},{2,3},{3,2},{4,5},{5,4},{6,7},{7,6},{8,9},{9,8},{10,11... | collective-permute-start | bytes 786440 | tf_op jit(solution)/shard_map/ppermute | solution.py:650
  101.3 3.7 %collective-permute-start.31 = (f32[8,256]{1,0:T(8,128)S(1)}, f32[8,256]{1,0:T(8,128)S(1)}, u32[]{:S(2)}, u32[]{:S(2)}) collective-permute-start(f32[8,256]{1,0:T(8,128)S(1)} %add.17), channel_id=1, source_target_pairs={{0,2},{1,3},{2,0},{3,1},{4,6},{5,7},{6,4},{7,5},{8,10},{9,11},{10,... | collective-permute-start | bytes 24584 | tf_op jit(solution)/shard_map/ppermute | solution.py:654
  105.0 5.4 %collective-permute-start.34 = (f32[8,256]{1,0:T(8,128)S(1)}, f32[8,256]{1,0:T(8,128)S(1)}, u32[]{:S(2)}, u32[]{:S(2)}) collective-permute-start(f32[8,256]{1,0:T(8,128)S(1)} %add.18.refs_0_), channel_id=1, source_target_pairs={{0,12},{1,13},{2,14},{3,15},{4,8},{5,9},{6,10},{7,11},{8,4},{9,5},... | collective-permute-start | bytes 24584 | tf_op jit(solution)/shard_map/ppermute | solution.py:658
  107.0 4.5 %collective-permute-start.33 = (f32[8,256]{1,0:T(8,128)S(1)}, f32[8,256]{1,0:T(8,128)S(1)}, u32[]{:S(2)}, u32[]{:S(2)}) collective-permute-start(f32[8,256]{1,0:T(8,128)S(1)} %add.18.refs_0_), channel_id=1, source_target_pairs={{0,8},{1,9},{2,10},{3,11},{4,12},{5,13},{6,14},{7,15},{8,0},{9,1},... | collective-permute-start | bytes 24584 | tf_op jit(solution)/shard_map/ppermute | solution.py:658
  107.0 4.5 %collective-permute-start.32 = (f32[8,256]{1,0:T(8,128)S(1)}, f32[8,256]{1,0:T(8,128)S(1)}, u32[]{:S(2)}, u32[]{:S(2)}) collective-permute-start(f32[8,256]{1,0:T(8,128)S(1)} %add.18.refs_0_), channel_id=1, source_target_pairs={{0,4},{1,5},{2,6},{3,7},{4,0},{5,1},{6,2},{7,3},{8,12},{9,13},{10,... | collective-permute-start | bytes 24584 | tf_op jit(solution)/shard_map/ppermute | solution.py:658
  (11 other events, 66.6 us)

commit v14 on v12

--- a/solution.py
+++ b/solution.py
@@ -87,10 +87,10 @@
 def build_rows(ids_ref, weight_ref, wh_ref, wl_ref, at_ref, y_refs, lo_s, base):
     sources, fine = ids_ref.shape
     rows = at_ref.shape[0] // len(y_refs)
-    step = rows // 2
+    step = rows // 4
     row = lax.broadcasted_iota(jnp.int32, (step, LANES), 0)
     for n, y_ref in enumerate(y_refs):
-        for m in range(2):
+        for m in range(4):
             start = n * rows + m * step
             for j in range(fine // LANES):
                 lanes = pl.ds(j * LANES, LANES)

time: 114 us -> 114 us (level)
  no operation moved by 1% of the time
where the time goes in v14:
time: 114 us
  starting transfers between devices  39.3 us (34%)
  waiting for transfers between devices  34.5 us (30%)
  Pallas kernels  33.6 us (29%)
  local copies, waits for them, and re-layouts  3.89 us (3%)
  other arithmetic  1.62 us (1%)
  between operations  1.17 us (1%)
    ppermute x17, starting transfers between devices, over_z(): return lax.ppermute(x, 'space', [(i, i ^ 4 * k) for i in range(GROUP)])  24.9 us
    ppermute x17, waiting for transfers between devices, over_z(): return lax.ppermute(x, 'space', [(i, i ^ 4 * k) for i in range(GROUP)])  19.5 us
    ppermute x8, waiting for transfers between devices, over_y(): return lax.ppermute(x, 'space', [(i, i ^ 2) for i in range(GROUP)])  12.1 us
    ppermute x8, starting transfers between devices, over_y(): return lax.ppermute(x, 'space', [(i, i ^ 2) for i in range(GROUP)])  11.7 us
    pallas_call x2, Pallas kernels, project(): pl.pallas_call(project_kernel, in_specs=[VMEM] * 4, out_specs=[VMEM] * 2,...  7.48 us
    pallas_call x2, Pallas kernels, coarse_image(): pl.pallas_call(functools.partial(coarse_kernel, len(got), second, len(aft...  7.03 us
    pallas_call x3, Pallas kernels, adjoint_near(): pl.pallas_call(functools.partial(near_kernel, base), in_specs=[VMEM] * le...  6.57 us
    unnamed x17, local copies, waits for them, and re-layouts  3.89 us
  transfers between devices with their start and end apart: 35, of which 24 were waited for; matrix products, arithmetic and copies ran while one was open for 4% of the time, Pallas kernels for 14%

profile of v14, /device:TPU:0, one launch (start us, length us, event | category | flops | bytes accessed | tf_op | source)
XLA Modules:
  0.0 114.0 jit_solution(10748375228458531493)
XLA Ops:
  3.4 2.9 %collective-permute-start.1 = (s32[8,128]{1,0:T(8,128)S(1)}, s32[8,128]{1,0:T(8,128)S(1)}, u32[]{:S(2)}, u32[]{:S(2)}) collective-permute-start(s32[8,128]{1,0:T(8,128)S(1)} %get-tuple-element.54), channel_id=1, source_target_pairs={{0,2},{1,3},{2,0},{3,1},{4,6},{5,7},{6,4},{7,5},{8,10},{9,11},{10,... | collective-permute-start | bytes 12296 | tf_op jit(solution)/shard_map/ppermute | solution.py:654
  6.2 1.6 %collective-permute-done.1.got_ref = s32[8,128]{1,0:T(8,128)S(1)} collective-permute-done((s32[8,128]{1,0:T(8,128)S(1)}, s32[8,128]{1,0:T(8,128)S(1)}, u32[]{:S(2)}, u32[]{:S(2)}) %collective-permute-start.1) | collective-permute-done | bytes 4128 | tf_op jit(solution)/shard_map/ppermute | solution.py:654
  7.8 2.1 %collective-permute-start.2 = (s32[8,128]{1,0:T(8,128)S(1)}, s32[8,128]{1,0:T(8,128)S(1)}, u32[]{:S(2)}, u32[]{:S(2)}) collective-permute-start(s32[8,128]{1,0:T(8,128)S(1)} %get-tuple-element.56), channel_id=1, source_target_pairs={{0,4},{1,5},{2,6},{3,7},{4,0},{5,1},{6,2},{7,3},{8,12},{9,13},{10,... | collective-permute-start | bytes 12296 | tf_op jit(solution)/shard_map/ppermute | solution.py:658
  11.6 3.0 %collective-permute-start.3 = (s32[8,128]{1,0:T(8,128)S(1)}, s32[8,128]{1,0:T(8,128)S(1)}, u32[]{:S(2)}, u32[]{:S(2)}) collective-permute-start(s32[8,128]{1,0:T(8,128)S(1)} %get-tuple-element.58), channel_id=1, source_target_pairs={{0,8},{1,9},{2,10},{3,11},{4,12},{5,13},{6,14},{7,15},{8,0},{9,1},... | collective-permute-start | bytes 12296 | tf_op jit(solution)/shard_map/ppermute | solution.py:658
  14.6 1.6 %collective-permute-done.3.refs_1_ = s32[8,128]{1,0:T(8,128)S(1)} collective-permute-done((s32[8,128]{1,0:T(8,128)S(1)}, s32[8,128]{1,0:T(8,128)S(1)}, u32[]{:S(2)}, u32[]{:S(2)}) %collective-permute-start.3) | collective-permute-done | bytes 4128 | tf_op jit(solution)/shard_map/ppermute | solution.py:658
  16.2 2.9 %adjoint_far.1 = (s32[4,1152]{1,0:T(4,128)S(1)}, f32[4,1152]{1,0:T(4,128)S(1)}, bf16[512,1152]{1,0:T(8,128)(2,1)S(1)}, f32[512,256]{1,0:T(8,128)S(1)}) custom-call(s32[4]{0:T(128)S(1)} %pad_add_fusion.me_ref, s32[8,128]{1,0:T(8,128)S(1)} %get-tuple-element.57.refs_0_, s32[8,128]{1,0:T(8,128)S(1)} %collective-permute-done.3.refs_1_, ...), custom_call_target="tpu_custom_call" | custom-call | flops 905969664 | bytes 2000000 | tf_op jit(solution)/shard_map/adjoint_far/pallas_call | solution.py:135
  19.2 2.2 %adjoint_near.1 = (bf16[512,1152]{1,0:T(8,128)(2,1)S(1)}, f32[512,256]{1,0:T(8,128)S(1)}) custom-call(s32[4,1152]{1,0:T(4,128)S(1)} %get-tuple-element.59.ids_ref, f32[4,1152]{1,0:T(4,128)S(1)} %get-tuple-element.60.weight_ref, bf16[1152,256]{1,0:T(8,128)(2,1)S(1)} %get-tuple-element.101.refs_3_.wh_ref, bf16[1152,256]{1,0:T(8,128)(2,1)S(1)} %get-tuple-element.100.refs_4_.wl_ref), custom_call_target="tpu_custom_call" | custom-call | flops 905969664 | bytes 2000000 | tf_op jit(solution)/shard_map/adjoint_near/pallas_call | solution.py:150
  21.5 2.2 %adjoint_side.1 = (bf16[512,1152]{1,0:T(8,128)(2,1)S(1)}, f32[512,256]{1,0:T(8,128)S(1)}) custom-call(s32[4,1152]{1,0:T(4,128)S(1)} %get-tuple-element.59.ids_ref, f32[4,1152]{1,0:T(4,128)S(1)} %get-tuple-element.60.weight_ref, bf16[1152,256]{1,0:T(8,128)(2,1)S(1)} %get-tuple-element.101.refs_3_.wh_ref, ...), custom_call_target="tpu_custom_call" | custom-call | flops 905969664 | bytes 2000000 | tf_op jit(solution)/shard_map/adjoint_side/pallas_call | solution.py:150
  24.3 1.9 %collective-permute-start.7 = (s16[272,256]{1,0:T(8,128)(2,1)S(1)}, s16[272,256]{1,0:T(8,128)(2,1)S(1)}, u32[]{:S(2)}, u32[]{:S(2)}) collective-permute-start(s16[272,256]{1,0:T(8,128)(2,1)S(1)} %get-tuple-element.65.refs_0_), channel_id=1, source_target_pairs={{0,2},{1,3},{2,0},{3,1},{4,6},{5,7},{6,4},{7,5},{8,10},{9,11},{10,... | collective-permute-start | bytes 417800 | tf_op jit(solution)/shard_map/ppermute | solution.py:654
  26.3 2.2 %adjoint_stay.1 = (bf16[512,1152]{1,0:T(8,128)(2,1)S(1)}, f32[512,256]{1,0:T(8,128)S(1)}) custom-call(s32[4,1152]{1,0:T(4,128)S(1)} %get-tuple-element.59.ids_ref, f32[4,1152]{1,0:T(4,128)S(1)} %get-tuple-element.60.weight_ref, bf16[1152,256]{1,0:T(8,128)(2,1)S(1)} %get-tuple-element.101.refs_3_.wh_ref, bf16[1152,256]{1,0:T(8,128)(2,1)S(1)} %get-tuple-element.100.refs_4_.wl_ref), custom_call_target="tpu_custom_call" | custom-call | flops 905969664 | bytes 2000000 | tf_op jit(solution)/shard_map/adjoint_stay/pallas_call | solution.py:150
  28.5 2.3 %collective-permute-done.7.p_ref = s16[272,256]{1,0:T(8,128)(2,1)S(1)} collective-permute-done((s16[272,256]{1,0:T(8,128)(2,1)S(1)}, s16[272,256]{1,0:T(8,128)(2,1)S(1)}, u32[]{:S(2)}, u32[]{:S(2)}) %collective-permute-start.7) | collective-permute-done | bytes 139296 | tf_op jit(solution)/shard_map/ppermute | solution.py:654
  30.9 3.0 %collective-permute-start.8 = (s16[144,256]{1,0:T(8,128)(2,1)S(1)}, s16[144,256]{1,0:T(8,128)(2,1)S(1)}, u32[]{:S(2)}, u32[]{:S(2)}) collective-permute-start(s16[144,256]{1,0:T(8,128)(2,1)S(1)} %get-tuple-element.69), channel_id=1, source_target_pairs={{0,8},{1,9},{2,10},{3,11},{4,12},{5,13},{6,14},{7,15},{8,0},{9,1},... | collective-permute-start | bytes 221192 | tf_op jit(solution)/shard_map/ppermute | solution.py:658
  35.7 3.1 %copy.12 = bf16[80,128,256]{2,0,1:T(8,128)(2,1)S(1)} copy(bf16[80,128,256]{2,1,0:T(8,128)(2,1)S(1)} %bitcast.12) | data formatting | bytes 10485760 | tf_op args[0]
  40.6 3.5 %coarse_first.1 = (bf16[256,128]{1,0:T(8,128)(2,1)S(1)}, f32[128,256]{1,0:T(8,128)S(1)}, f32[8,256]{1,0:T(8,128)S(1)}) custom-call(bf16[80,128,256]{2,1,0:T(8,128)(2,1)S(1)} %bitcast.12, bf16[256,256]{1,0:T(8,128)(2,1)S(1)} %copy-done.1, f32[128,256]{1,0:T(8,128)S(1)} %get-tuple-element.68.own_ref, s16[144,256]{1,0:T(8,128)(2,1)S(1)} %collective-permute-done.8.refs_0_, ...), custom_call_target="tpu_custom_call" | custom-call | flops 1342177280 | bytes 5000000 | tf_op jit(solution)/shard_map/coarse_first/pallas_call | solution.py:435
  44.3 2.8 %collective-permute-start.12 = (bf16[256,128]{1,0:T(8,128)(2,1)S(1)}, bf16[256,128]{1,0:T(8,128)(2,1)S(1)}, u32[]{:S(2)}, u32[]{:S(2)}) collective-permute-start(bf16[256,128]{1,0:T(8,128)(2,1)S(1)} %get-tuple-element.72.refs_3_), channel_id=1, source_target_pairs={{0,12},{1,13},{2,14},{3,15},{4,8},{5,9},{6,10},{7,11},{8,4},{9,5},... | collective-permute-start | bytes 196616 | tf_op jit(solution)/shard_map/ppermute | solution.py:658
  48.7 1.8 %collective-permute-done.12.refs_1_ = bf16[256,128]{1,0:T(8,128)(2,1)S(1)} collective-permute-done((bf16[256,128]{1,0:T(8,128)(2,1)S(1)}, bf16[256,128]{1,0:T(8,128)(2,1)S(1)}, u32[]{:S(2)}, u32[]{:S(2)}) %collective-permute-start.12) | collective-permute-done | bytes 65568 | tf_op jit(solution)/shard_map/ppermute | solution.py:658
  50.5 2.3 %collective-permute-done.11.refs_0_ = bf16[256,128]{1,0:T(8,128)(2,1)S(1)} collective-permute-done((bf16[256,128]{1,0:T(8,128)(2,1)S(1)}, bf16[256,128]{1,0:T(8,128)(2,1)S(1)}, u32[]{:S(2)}, u32[]{:S(2)}) %collective-permute-start.11) | collective-permute-done | bytes 65568 | tf_op jit(solution)/shard_map/ppermute | solution.py:658
  52.8 1.6 %collective-permute-start.14 = (bf16[4,256,128]{2,1,0:T(8,128)(2,1)S(1)}, bf16[4,256,128]{2,1,0:T(8,128)(2,1)S(1)}, u32[]{:S(2)}, u32[]{:S(2)}) collective-permute-start(bf16[4,256,128]{2,1,0:T(8,128)(2,1)S(1)} %join.2.after_ref.refs_0_), channel_id=1, source_target_pairs={{0,2},{1,3},{2,0},{3,1},{4,6},{5,7},{6,4},{7,5},{8,10},{9,11},{10,... | collective-permute-start | bytes 786440 | tf_op jit(solution)/shard_map/ppermute | solution.py:654
  54.4 3.6 %project.2 = (f32[80,8192]{1,0:T(8,128)S(1)}, f32[8,128]{1,0:T(8,128)S(1)}) custom-call(bf16[128,80,256]{2,1,0:T(8,128)(2,1)S(1)} %bitcast.9, f32[128,256]{1,0:T(8,128)S(1)} %get-tuple-element.73.y_ref.refs_3_, bf16[2,256,128]{2,1,0:T(8,128)(2,1)S(1)} %copy-done.2, bf16[4,256,128]{2,1,0:T(8,128)(2,1)S(1)} %join.2.after_ref.refs_0_), custom_call_target="tpu_custom_call" | custom-call | flops 1342177280 | bytes 8000000 | tf_op jit(solution)/shard_map/project/pallas_call | solution.py:473
  67.6 4.0 %collective-permute-done.20.p_ref = s16[272,256]{1,0:T(8,128)(2,1)S(1)} collective-permute-done((s16[272,256]{1,0:T(8,128)(2,1)S(1)}, s16[272,256]{1,0:T(8,128)(2,1)S(1)}, u32[]{:S(2)}, u32[]{:S(2)}) %collective-permute-start.20) | collective-permute-done | bytes 139296 | tf_op jit(solution)/shard_map/ppermute | solution.py:654
  72.0 2.0 %collective-permute-start.22 = (s16[144,256]{1,0:T(8,128)(2,1)S(1)}, s16[144,256]{1,0:T(8,128)(2,1)S(1)}, u32[]{:S(2)}, u32[]{:S(2)}) collective-permute-start(s16[144,256]{1,0:T(8,128)(2,1)S(1)} %get-tuple-element.88), channel_id=1, source_target_pairs={{0,12},{1,13},{2,14},{3,15},{4,8},{5,9},{6,10},{7,11},{8,4},{9,5},... | collective-permute-start | bytes 221192 | tf_op jit(solution)/shard_map/ppermute | solution.py:658
  75.4 3.3 %collective-permute-done.21.refs_0_ = s16[144,256]{1,0:T(8,128)(2,1)S(1)} collective-permute-done((s16[144,256]{1,0:T(8,128)(2,1)S(1)}, s16[144,256]{1,0:T(8,128)(2,1)S(1)}, u32[]{:S(2)}, u32[]{:S(2)}) %collective-permute-start.21) | collective-permute-done | bytes 73760 | tf_op jit(solution)/shard_map/ppermute | solution.py:658
  79.4 3.6 %coarse_second.1 = (bf16[256,128]{1,0:T(8,128)(2,1)S(1)}, f32[128,256]{1,0:T(8,128)S(1)}, f32[8,128]{1,0:T(8,128)S(1)}, f32[8,256]{1,0:T(8,128)S(1)}) custom-call(bf16[80,128,256]{2,1,0:T(8,128)(2,1)S(1)} %bitcast.12, bf16[256,256]{1,0:T(8,128)(2,1)S(1)} %copy-done.1, f32[128,256]{1,0:T(8,128)S(1)} %get-tuple-element.86.own_ref, ...), custom_call_target="tpu_custom_call" | custom-call | flops 1342177280 | bytes 5000000 | tf_op jit(solution)/shard_map/coarse_second/pallas_call | solution.py:435
  83.7 1.8 %collective-permute-start.25 = (bf16[256,128]{1,0:T(8,128)(2,1)S(1)}, bf16[256,128]{1,0:T(8,128)(2,1)S(1)}, u32[]{:S(2)}, u32[]{:S(2)}) collective-permute-start(bf16[256,128]{1,0:T(8,128)(2,1)S(1)} %get-tuple-element.91.refs_3_), channel_id=1, source_target_pairs={{0,12},{1,13},{2,14},{3,15},{4,8},{5,9},{6,10},{7,11},{8,4},{9,5},... | collective-permute-start | bytes 196616 | tf_op jit(solution)/shard_map/ppermute | solution.py:658
  86.6 1.9 %collective-permute-done.26.refs_2_ = bf16[256,128]{1,0:T(8,128)(2,1)S(1)} collective-permute-done((bf16[256,128]{1,0:T(8,128)(2,1)S(1)}, bf16[256,128]{1,0:T(8,128)(2,1)S(1)}, u32[]{:S(2)}, u32[]{:S(2)}) %collective-permute-start.26) | collective-permute-done | bytes 65568 | tf_op jit(solution)/shard_map/ppermute | solution.py:658
  89.8 1.6 %collective-permute-done.24.refs_0_ = bf16[256,128]{1,0:T(8,128)(2,1)S(1)} collective-permute-done((bf16[256,128]{1,0:T(8,128)(2,1)S(1)}, bf16[256,128]{1,0:T(8,128)(2,1)S(1)}, u32[]{:S(2)}, u32[]{:S(2)}) %collective-permute-start.24) | collective-permute-done | bytes 65568 | tf_op jit(solution)/shard_map/ppermute | solution.py:658
  91.4 1.6 %collective-permute-start.27 = (bf16[4,256,128]{2,1,0:T(8,128)(2,1)S(1)}, bf16[4,256,128]{2,1,0:T(8,128)(2,1)S(1)}, u32[]{:S(2)}, u32[]{:S(2)}) collective-permute-start(bf16[4,256,128]{2,1,0:T(8,128)(2,1)S(1)} %join.3.after_ref.refs_0_), channel_id=1, source_target_pairs={{0,2},{1,3},{2,0},{3,1},{4,6},{5,7},{6,4},{7,5},{8,10},{9,11},{10,... | collective-permute-start | bytes 786440 | tf_op jit(solution)/shard_map/ppermute | solution.py:654
  93.0 3.8 %project.3 = (f32[80,8192]{1,0:T(8,128)S(1)}, f32[8,128]{1,0:T(8,128)S(1)}) custom-call(bf16[128,80,256]{2,1,0:T(8,128)(2,1)S(1)} %bitcast.10, f32[128,256]{1,0:T(8,128)S(1)} %get-tuple-element.92.y_ref, bf16[2,256,128]{2,1,0:T(8,128)(2,1)S(1)} %copy-done.2, bf16[4,256,128]{2,1,0:T(8,128)(2,1)S(1)} %join.3.after_ref.refs_0_), custom_call_target="tpu_custom_call" | custom-call | flops 1342177280 | bytes 8000000 | tf_op jit(solution)/shard_map/project/pallas_call | solution.py:473
  103.0 2.1 %collective-permute-done.31 = f32[8,256]{1,0:T(8,128)S(1)} collective-permute-done((f32[8,256]{1,0:T(8,128)S(1)}, f32[8,256]{1,0:T(8,128)S(1)}, u32[]{:S(2)}, u32[]{:S(2)}) %collective-permute-start.31) | collective-permute-done | bytes 8224 | tf_op jit(solution)/shard_map/ppermute | solution.py:654
  105.1 2.0 %collective-permute-start.34 = (f32[8,256]{1,0:T(8,128)S(1)}, f32[8,256]{1,0:T(8,128)S(1)}, u32[]{:S(2)}, u32[]{:S(2)}) collective-permute-start(f32[8,256]{1,0:T(8,128)S(1)} %add.18.refs_0_), channel_id=1, source_target_pairs={{0,12},{1,13},{2,14},{3,15},{4,8},{5,9},{6,10},{7,11},{8,4},{9,5},... | collective-permute-start | bytes 24584 | tf_op jit(solution)/shard_map/ppermute | solution.py:658
  107.1 2.4 %collective-permute-start.32 = (f32[8,256]{1,0:T(8,128)S(1)}, f32[8,256]{1,0:T(8,128)S(1)}, u32[]{:S(2)}, u32[]{:S(2)}) collective-permute-start(f32[8,256]{1,0:T(8,128)S(1)} %add.18.refs_0_), channel_id=1, source_target_pairs={{0,4},{1,5},{2,6},{3,7},{4,0},{5,1},{6,2},{7,3},{8,12},{9,13},{10,... | collective-permute-start | bytes 24584 | tf_op jit(solution)/shard_map/ppermute | solution.py:658
  111.6 2.2 %result.1 = (f32[80,8192]{1,0:T(8,128)}, f32[1152,256]{1,0:T(8,128)}) custom-call(f32[8,128]{1,0:T(8,128)S(1)} %get-tuple-element.90.l0_ref, f32[8,256]{1,0:T(8,128)S(1)} %add.18.refs_0_, f32[8,256]{1,0:T(8,128)S(1)} %collective-permute-done.32.refs_1_, f32[8,256]{1,0:T(8,128)S(1)} %collective-permute-done.33.refs_2_, ...), custom_call_target="tpu_custom_call" | custom-call | flops 1966080 | bytes 10000000 | tf_op jit(solution)/shard_map/result/pallas_call | solution.py:633
  (92 shorter events, 34.0 us)
Async XLA Ops:
  3.4 4.4 %collective-permute-start.1 = (s32[8,128]{1,0:T(8,128)S(1)}, s32[8,128]{1,0:T(8,128)S(1)}, u32[]{:S(2)}, u32[]{:S(2)}) collective-permute-start(s32[8,128]{1,0:T(8,128)S(1)} %get-tuple-element.54), channel_id=1, source_target_pairs={{0,2},{1,3},{2,0},{3,1},{4,6},{5,7},{6,4},{7,5},{8,10},{9,11},{10,... | collective-permute-start | bytes 12296 | tf_op jit(solution)/shard_map/ppermute | solution.py:654
  7.8 3.7 %collective-permute-start.2 = (s32[8,128]{1,0:T(8,128)S(1)}, s32[8,128]{1,0:T(8,128)S(1)}, u32[]{:S(2)}, u32[]{:S(2)}) collective-permute-start(s32[8,128]{1,0:T(8,128)S(1)} %get-tuple-element.56), channel_id=1, source_target_pairs={{0,4},{1,5},{2,6},{3,7},{4,0},{5,1},{6,2},{7,3},{8,12},{9,13},{10,... | collective-permute-start | bytes 12296 | tf_op jit(solution)/shard_map/ppermute | solution.py:658
  11.6 4.6 %collective-permute-start.3 = (s32[8,128]{1,0:T(8,128)S(1)}, s32[8,128]{1,0:T(8,128)S(1)}, u32[]{:S(2)}, u32[]{:S(2)}) collective-permute-start(s32[8,128]{1,0:T(8,128)S(1)} %get-tuple-element.58), channel_id=1, source_target_pairs={{0,8},{1,9},{2,10},{3,11},{4,12},{5,13},{6,14},{7,15},{8,0},{9,1},... | collective-permute-start | bytes 12296 | tf_op jit(solution)/shard_map/ppermute | solution.py:658
  19.1 2.3 %collective-permute-start.4 = (f32[512,256]{1,0:T(8,128)S(1)}, f32[512,256]{1,0:T(8,128)S(1)}, u32[]{:S(2)}, u32[]{:S(2)}) collective-permute-start(f32[512,256]{1,0:T(8,128)S(1)} %get-tuple-element.64), channel_id=1, source_target_pairs={{0,1},{1,0},{2,3},{3,2},{4,5},{5,4},{6,7},{7,6},{8,9},{9,8},{10,11... | collective-permute-start | bytes 1572872 | tf_op jit(solution)/shard_map/ppermute | solution.py:650
  23.7 7.1 %collective-permute-start.5 = (f32[512,256]{1,0:T(8,128)S(1)}, f32[512,256]{1,0:T(8,128)S(1)}, u32[]{:S(2)}, u32[]{:S(2)}) collective-permute-start(f32[512,256]{1,0:T(8,128)S(1)} %get-tuple-element.66), channel_id=1, source_target_pairs={{0,1},{1,0},{2,3},{3,2},{4,5},{5,4},{6,7},{7,6},{8,9},{9,8},{10,11... | collective-permute-start | bytes 1572872 | tf_op jit(solution)/shard_map/ppermute | solution.py:650
  24.3 6.5 %collective-permute-start.7 = (s16[272,256]{1,0:T(8,128)(2,1)S(1)}, s16[272,256]{1,0:T(8,128)(2,1)S(1)}, u32[]{:S(2)}, u32[]{:S(2)}) collective-permute-start(s16[272,256]{1,0:T(8,128)(2,1)S(1)} %get-tuple-element.65.refs_0_), channel_id=1, source_target_pairs={{0,2},{1,3},{2,0},{3,1},{4,6},{5,7},{6,4},{7,5},{8,10},{9,11},{10,... | collective-permute-start | bytes 417800 | tf_op jit(solution)/shard_map/ppermute | solution.py:654
  26.1 9.1 %collective-permute-start.6 = (s16[272,256]{1,0:T(8,128)(2,1)S(1)}, s16[272,256]{1,0:T(8,128)(2,1)S(1)}, u32[]{:S(2)}, u32[]{:S(2)}) collective-permute-start(s16[272,256]{1,0:T(8,128)(2,1)S(1)} %get-tuple-element.67), channel_id=1, source_target_pairs={{0,2},{1,3},{2,0},{3,1},{4,6},{5,7},{6,4},{7,5},{8,10},{9,11},{10,... | collective-permute-start | bytes 417800 | tf_op jit(solution)/shard_map/ppermute | solution.py:654
  30.9 7.9 %collective-permute-start.8 = (s16[144,256]{1,0:T(8,128)(2,1)S(1)}, s16[144,256]{1,0:T(8,128)(2,1)S(1)}, u32[]{:S(2)}, u32[]{:S(2)}) collective-permute-start(s16[144,256]{1,0:T(8,128)(2,1)S(1)} %get-tuple-element.69), channel_id=1, source_target_pairs={{0,8},{1,9},{2,10},{3,11},{4,12},{5,13},{6,14},{7,15},{8,0},{9,1},... | collective-permute-start | bytes 221192 | tf_op jit(solution)/shard_map/ppermute | solution.py:658
  33.9 6.3 %collective-permute-start.9 = (s16[144,256]{1,0:T(8,128)(2,1)S(1)}, s16[144,256]{1,0:T(8,128)(2,1)S(1)}, u32[]{:S(2)}, u32[]{:S(2)}) collective-permute-start(s16[144,256]{1,0:T(8,128)(2,1)S(1)} %get-tuple-element.70), channel_id=1, source_target_pairs={{0,12},{1,13},{2,14},{3,15},{4,8},{5,9},{6,10},{7,11},{8,4},{9,5},... | collective-permute-start | bytes 221192 | tf_op jit(solution)/shard_map/ppermute | solution.py:658
  35.4 5.2 %collective-permute-start.10 = (s16[144,256]{1,0:T(8,128)(2,1)S(1)}, s16[144,256]{1,0:T(8,128)(2,1)S(1)}, u32[]{:S(2)}, u32[]{:S(2)}) collective-permute-start(s16[144,256]{1,0:T(8,128)(2,1)S(1)} %get-tuple-element.71), channel_id=1, source_target_pairs={{0,4},{1,5},{2,6},{3,7},{4,0},{5,1},{6,2},{7,3},{8,12},{9,13},{10,... | collective-permute-start | bytes 221192 | tf_op jit(solution)/shard_map/ppermute | solution.py:658
  44.1 4.6 %collective-permute-start.13 = (bf16[256,128]{1,0:T(8,128)(2,1)S(1)}, bf16[256,128]{1,0:T(8,128)(2,1)S(1)}, u32[]{:S(2)}, u32[]{:S(2)}) collective-permute-start(bf16[256,128]{1,0:T(8,128)(2,1)S(1)} %get-tuple-element.72.refs_3_), channel_id=1, source_target_pairs={{0,4},{1,5},{2,6},{3,7},{4,0},{5,1},{6,2},{7,3},{8,12},{9,13},{10,... | collective-permute-start | bytes 196616 | tf_op jit(solution)/shard_map/ppermute | solution.py:658
  44.3 6.2 %collective-permute-start.12 = (bf16[256,128]{1,0:T(8,128)(2,1)S(1)}, bf16[256,128]{1,0:T(8,128)(2,1)S(1)}, u32[]{:S(2)}, u32[]{:S(2)}) collective-permute-start(bf16[256,128]{1,0:T(8,128)(2,1)S(1)} %get-tuple-element.72.refs_3_), channel_id=1, source_target_pairs={{0,12},{1,13},{2,14},{3,15},{4,8},{5,9},{6,10},{7,11},{8,4},{9,5},... | collective-permute-start | bytes 196616 | tf_op jit(solution)/shard_map/ppermute | solution.py:658
  47.1 5.7 %collective-permute-start.11 = (bf16[256,128]{1,0:T(8,128)(2,1)S(1)}, bf16[256,128]{1,0:T(8,128)(2,1)S(1)}, u32[]{:S(2)}, u32[]{:S(2)}) collective-permute-start(bf16[256,128]{1,0:T(8,128)(2,1)S(1)} %get-tuple-element.72.refs_3_), channel_id=1, source_target_pairs={{0,8},{1,9},{2,10},{3,11},{4,12},{5,13},{6,14},{7,15},{8,0},{9,1},... | collective-permute-start | bytes 196616 | tf_op jit(solution)/shard_map/ppermute | solution.py:658
  52.8 6.4 %collective-permute-start.14 = (bf16[4,256,128]{2,1,0:T(8,128)(2,1)S(1)}, bf16[4,256,128]{2,1,0:T(8,128)(2,1)S(1)}, u32[]{:S(2)}, u32[]{:S(2)}) collective-permute-start(bf16[4,256,128]{2,1,0:T(8,128)(2,1)S(1)} %join.2.after_ref.refs_0_), channel_id=1, source_target_pairs={{0,2},{1,3},{2,0},{3,1},{4,6},{5,7},{6,4},{7,5},{8,10},{9,11},{10,... | collective-permute-start | bytes 786440 | tf_op jit(solution)/shard_map/ppermute | solution.py:654
  54.4 5.0 %collective-permute-start.16 = (bf16[4,256,128]{2,1,0:T(8,128)(2,1)S(1)}, bf16[4,256,128]{2,1,0:T(8,128)(2,1)S(1)}, u32[]{:S(2)}, u32[]{:S(2)}) collective-permute-start(bf16[4,256,128]{2,1,0:T(8,128)(2,1)S(1)} %join.2.after_ref.refs_0_), channel_id=1, source_target_pairs={{0,1},{1,0},{2,3},{3,2},{4,5},{5,4},{6,7},{7,6},{8,9},{9,8},{10,11... | collective-permute-start | bytes 786440 | tf_op jit(solution)/shard_map/ppermute | solution.py:650
  59.3 1.6 %collective-permute-start.15 = (bf16[4,256,128]{2,1,0:T(8,128)(2,1)S(1)}, bf16[4,256,128]{2,1,0:T(8,128)(2,1)S(1)}, u32[]{:S(2)}, u32[]{:S(2)}) collective-permute-start(bf16[4,256,128]{2,1,0:T(8,128)(2,1)S(1)} %relay.2.refs_1_), channel_id=1, source_target_pairs={{0,1},{1,0},{2,3},{3,2},{4,5},{5,4},{6,7},{7,6},{8,9},{9,8},{10,11... | collective-permute-start | bytes 786440 | tf_op jit(solution)/shard_map/ppermute | solution.py:650
  62.0 2.0 %collective-permute-start.17 = (f32[520,256]{1,0:T(8,128)S(1)}, f32[520,256]{1,0:T(8,128)S(1)}, u32[]{:S(2)}, u32[]{:S(2)}) collective-permute-start(f32[520,256]{1,0:T(8,128)S(1)} %get-tuple-element.80), channel_id=1, source_target_pairs={{0,1},{1,0},{2,3},{3,2},{4,5},{5,4},{6,7},{7,6},{8,9},{9,8},{10,11... | collective-permute-start | bytes 1597448 | tf_op jit(solution)/shard_map/ppermute | solution.py:650
  64.6 7.0 %collective-permute-start.18 = (f32[512,256]{1,0:T(8,128)S(1)}, f32[512,256]{1,0:T(8,128)S(1)}, u32[]{:S(2)}, u32[]{:S(2)}) collective-permute-start(f32[512,256]{1,0:T(8,128)S(1)} %back_side.1), channel_id=1, source_target_pairs={{0,1},{1,0},{2,3},{3,2},{4,5},{5,4},{6,7},{7,6},{8,9},{9,8},{10,11... | collective-permute-start | bytes 1572872 | tf_op jit(solution)/shard_map/ppermute | solution.py:650
  65.1 6.5 %collective-permute-start.20 = (s16[272,256]{1,0:T(8,128)(2,1)S(1)}, s16[272,256]{1,0:T(8,128)(2,1)S(1)}, u32[]{:S(2)}, u32[]{:S(2)}) collective-permute-start(s16[272,256]{1,0:T(8,128)(2,1)S(1)} %get-tuple-element.82.refs_0_), channel_id=1, source_target_pairs={{0,2},{1,3},{2,0},{3,1},{4,6},{5,7},{6,4},{7,5},{8,10},{9,11},{10,... | collective-permute-start | bytes 417800 | tf_op jit(solution)/shard_map/ppermute | solution.py:654
  66.6 7.4 %collective-permute-start.19 = (s16[272,256]{1,0:T(8,128)(2,1)S(1)}, s16[272,256]{1,0:T(8,128)(2,1)S(1)}, u32[]{:S(2)}, u32[]{:S(2)}) collective-permute-start(s16[272,256]{1,0:T(8,128)(2,1)S(1)} %get-tuple-element.83), channel_id=1, source_target_pairs={{0,2},{1,3},{2,0},{3,1},{4,6},{5,7},{6,4},{7,5},{8,10},{9,11},{10,... | collective-permute-start | bytes 417800 | tf_op jit(solution)/shard_map/ppermute | solution.py:654
  71.7 7.0 %collective-permute-start.21 = (s16[144,256]{1,0:T(8,128)(2,1)S(1)}, s16[144,256]{1,0:T(8,128)(2,1)S(1)}, u32[]{:S(2)}, u32[]{:S(2)}) collective-permute-start(s16[144,256]{1,0:T(8,128)(2,1)S(1)} %get-tuple-element.87), channel_id=1, source_target_pairs={{0,8},{1,9},{2,10},{3,11},{4,12},{5,13},{6,14},{7,15},{8,0},{9,1},... | collective-permute-start | bytes 221192 | tf_op jit(solution)/shard_map/ppermute | solution.py:658
  72.0 6.7 %collective-permute-start.22 = (s16[144,256]{1,0:T(8,128)(2,1)S(1)}, s16[144,256]{1,0:T(8,128)(2,1)S(1)}, u32[]{:S(2)}, u32[]{:S(2)}) collective-permute-start(s16[144,256]{1,0:T(8,128)(2,1)S(1)} %get-tuple-element.88), channel_id=1, source_target_pairs={{0,12},{1,13},{2,14},{3,15},{4,8},{5,9},{6,10},{7,11},{8,4},{9,5},... | collective-permute-start | bytes 221192 | tf_op jit(solution)/shard_map/ppermute | solution.py:658
  74.2 5.3 %collective-permute-start.23 = (s16[144,256]{1,0:T(8,128)(2,1)S(1)}, s16[144,256]{1,0:T(8,128)(2,1)S(1)}, u32[]{:S(2)}, u32[]{:S(2)}) collective-permute-start(s16[144,256]{1,0:T(8,128)(2,1)S(1)} %get-tuple-element.89), channel_id=1, source_target_pairs={{0,4},{1,5},{2,6},{3,7},{4,0},{5,1},{6,2},{7,3},{8,12},{9,13},{10,... | collective-permute-start | bytes 221192 | tf_op jit(solution)/shard_map/ppermute | solution.py:658
  83.0 5.4 %collective-permute-start.26 = (bf16[256,128]{1,0:T(8,128)(2,1)S(1)}, bf16[256,128]{1,0:T(8,128)(2,1)S(1)}, u32[]{:S(2)}, u32[]{:S(2)}) collective-permute-start(bf16[256,128]{1,0:T(8,128)(2,1)S(1)} %get-tuple-element.91.refs_3_), channel_id=1, source_target_pairs={{0,4},{1,5},{2,6},{3,7},{4,0},{5,1},{6,2},{7,3},{8,12},{9,13},{10,... | collective-permute-start | bytes 196616 | tf_op jit(solution)/shard_map/ppermute | solution.py:658
  83.7 6.1 %collective-permute-start.25 = (bf16[256,128]{1,0:T(8,128)(2,1)S(1)}, bf16[256,128]{1,0:T(8,128)(2,1)S(1)}, u32[]{:S(2)}, u32[]{:S(2)}) collective-permute-start(bf16[256,128]{1,0:T(8,128)(2,1)S(1)} %get-tuple-element.91.refs_3_), channel_id=1, source_target_pairs={{0,12},{1,13},{2,14},{3,15},{4,8},{5,9},{6,10},{7,11},{8,4},{9,5},... | collective-permute-start | bytes 196616 | tf_op jit(solution)/shard_map/ppermute | solution.py:658
  85.5 5.9 %collective-permute-start.24 = (bf16[256,128]{1,0:T(8,128)(2,1)S(1)}, bf16[256,128]{1,0:T(8,128)(2,1)S(1)}, u32[]{:S(2)}, u32[]{:S(2)}) collective-permute-start(bf16[256,128]{1,0:T(8,128)(2,1)S(1)} %get-tuple-element.91.refs_3_), channel_id=1, source_target_pairs={{0,8},{1,9},{2,10},{3,11},{4,12},{5,13},{6,14},{7,15},{8,0},{9,1},... | collective-permute-start | bytes 196616 | tf_op jit(solution)/shard_map/ppermute | solution.py:658
  91.4 6.4 %collective-permute-start.27 = (bf16[4,256,128]{2,1,0:T(8,128)(2,1)S(1)}, bf16[4,256,128]{2,1,0:T(8,128)(2,1)S(1)}, u32[]{:S(2)}, u32[]{:S(2)}) collective-permute-start(bf16[4,256,128]{2,1,0:T(8,128)(2,1)S(1)} %join.3.after_ref.refs_0_), channel_id=1, source_target_pairs={{0,2},{1,3},{2,0},{3,1},{4,6},{5,7},{6,4},{7,5},{8,10},{9,11},{10,... | collective-permute-start | bytes 786440 | tf_op jit(solution)/shard_map/ppermute | solution.py:654
  93.0 4.9 %collective-permute-start.29 = (bf16[4,256,128]{2,1,0:T(8,128)(2,1)S(1)}, bf16[4,256,128]{2,1,0:T(8,128)(2,1)S(1)}, u32[]{:S(2)}, u32[]{:S(2)}) collective-permute-start(bf16[4,256,128]{2,1,0:T(8,128)(2,1)S(1)} %join.3.after_ref.refs_0_), channel_id=1, source_target_pairs={{0,1},{1,0},{2,3},{3,2},{4,5},{5,4},{6,7},{7,6},{8,9},{9,8},{10,11... | collective-permute-start | bytes 786440 | tf_op jit(solution)/shard_map/ppermute | solution.py:650
  101.4 3.7 %collective-permute-start.31 = (f32[8,256]{1,0:T(8,128)S(1)}, f32[8,256]{1,0:T(8,128)S(1)}, u32[]{:S(2)}, u32[]{:S(2)}) collective-permute-start(f32[8,256]{1,0:T(8,128)S(1)} %add.17), channel_id=1, source_target_pairs={{0,2},{1,3},{2,0},{3,1},{4,6},{5,7},{6,4},{7,5},{8,10},{9,11},{10,... | collective-permute-start | bytes 24584 | tf_op jit(solution)/shard_map/ppermute | solution.py:654
  105.1 5.4 %collective-permute-start.34 = (f32[8,256]{1,0:T(8,128)S(1)}, f32[8,256]{1,0:T(8,128)S(1)}, u32[]{:S(2)}, u32[]{:S(2)}) collective-permute-start(f32[8,256]{1,0:T(8,128)S(1)} %add.18.refs_0_), channel_id=1, source_target_pairs={{0,12},{1,13},{2,14},{3,15},{4,8},{5,9},{6,10},{7,11},{8,4},{9,5},... | collective-permute-start | bytes 24584 | tf_op jit(solution)/shard_map/ppermute | solution.py:658
  107.0 4.5 %collective-permute-start.33 = (f32[8,256]{1,0:T(8,128)S(1)}, f32[8,256]{1,0:T(8,128)S(1)}, u32[]{:S(2)}, u32[]{:S(2)}) collective-permute-start(f32[8,256]{1,0:T(8,128)S(1)} %add.18.refs_0_), channel_id=1, source_target_pairs={{0,8},{1,9},{2,10},{3,11},{4,12},{5,13},{6,14},{7,15},{8,0},{9,1},... | collective-permute-start | bytes 24584 | tf_op jit(solution)/shard_map/ppermute | solution.py:658
  107.1 4.5 %collective-permute-start.32 = (f32[8,256]{1,0:T(8,128)S(1)}, f32[8,256]{1,0:T(8,128)S(1)}, u32[]{:S(2)}, u32[]{:S(2)}) collective-permute-start(f32[8,256]{1,0:T(8,128)S(1)} %add.18.refs_0_), channel_id=1, source_target_pairs={{0,4},{1,5},{2,6},{3,7},{4,0},{5,1},{6,2},{7,3},{8,12},{9,13},{10,... | collective-permute-start | bytes 24584 | tf_op jit(solution)/shard_map/ppermute | solution.py:658
  (11 other events, 66.6 us)
